TPU v7x, 32 devices: a whole 2x2x4 slice. The times are simulated.
32 devices in a mesh: groups: 2 (over x), wide: 8 (over z, y), narrow: 2 (over core).
Axes of the slice: x: 2, y: 2, z: 4, core: 2. Of those that a mesh axis runs over, the one named last changes fastest.
Arguments:
- volume: bfloat16 [32, 128, 16, 32], P(None, ('groups', 'wide'), None, 'narrow'), parts along dimension 1, may hold values from -6 to 6
- cotangent: bfloat16 [32, 128, 16, 32], P(None, ('groups', 'wide'), None, 'narrow'), parts along dimension 1, may hold values from -6 to 6
- fine_weight: bfloat16 [27, 32, 32], replicated, may hold values from -0.21875 to 0.21875
- merge_weight: bfloat16 [16384, 1024], P('wide'), may hold values from -0.046875 to 0.046875
- hidden_weight: bfloat16 [27, 1024, 2048], P(None, None, 'wide'), may hold values from -0.0390625 to 0.0390625
- step_table: float32 [1000, 2048], P(None, 'wide'), may hold values from -6 to 6
- output_weight: bfloat16 [27, 2048, 1024], P(None, 'wide'), may hold values from -0.02734375 to 0.02734375
- expand_weight: bfloat16 [1024, 16384], P(None, 'wide'), may hold values from -0.1875 to 0.1875
- timestep: int32 [2], P('groups'), parts along dimension 0, may hold values from 0 to 999
Outputs:
- input_grad: bfloat16 [32, 128, 16, 32], P(None, ('groups', 'wide'), None, 'narrow'), parts along dimension 1
There are 2 independent parts, one for each index of `groups`. A program takes and returns all parts, laid end to end along the dimension named above; an argument that names none is the same for every part. Nothing has to cross between parts.
All inputs are finite; a program needn't handle non-finite values.
Results may differ from a plain program's by a relative error of at most 0.012.
Values may be sent and summed in bfloat16 or wider, within the bound.
No kernel may reach another device: no remote copies, remote signals or barrier semaphores. Data moves between devices by JAX's collectives and lax.ppermute only.
A program may use at most 128 MiB of HBM per device.

v0:
```python
import jax
import jax.numpy as jnp
from jax import lax
from jax.sharding import PartitionSpec as P

PATCH = 8


def extended(cells, sides, width):
    for axis, dim in sides:
        count = lax.axis_size(axis)
        ends = count - 1
        head = lax.slice_in_dim(cells, 0, width, axis=dim)
        tail = lax.slice_in_dim(cells, cells.shape[dim] - width, cells.shape[dim], axis=dim)
        cells = jnp.concatenate(
            [
                lax.ppermute(tail, axis, [(i, (i + 1) % count) for i in range(ends)]),
                cells,
                lax.ppermute(head, axis, [((i + 1) % count, i) for i in range(ends)]),
            ],
            axis=dim,
        )
    return cells


def shifts(transposed):
    return [
        (2 - i, 2 - j, 2 - k) if transposed else (i, j, k)
        for i in range(3)
        for j in range(3)
        for k in range(3)
    ]


def silu_slope(values):
    logistic = jax.nn.sigmoid(values)
    return logistic * (1.0 + values * (1.0 - logistic))


def fine_conv(fine_field, weight, transposed):
    grown = extended(fine_field, (("wide", 1), ("narrow", 3)), 1)
    padded = jnp.pad(grown, ((0, 0), (0, 0), (1, 1), (0, 0)))
    kernel = weight.reshape(3, 3, 3, weight.shape[1], weight.shape[2])
    if transposed:
        kernel = kernel[::-1, ::-1, ::-1]
    result = lax.conv_general_dilated(
        padded[None],
        kernel,
        (1, 1, 1),
        "VALID",
        dimension_numbers=("NCDHW", "DHWIO", "NCDHW"),
        preferred_element_type=jnp.float32,
    )
    return result[0]


def to_patches(fine_field):
    channels = fine_field.shape[0]
    shaped = fine_field.reshape(
        channels, PATCH, fine_field.shape[2] // PATCH, PATCH, fine_field.shape[3] // PATCH, PATCH
    )
    return shaped.transpose(2, 4, 1, 3, 5, 0).reshape(-1, PATCH**3 * channels)


def send_patches(fine_field):
    return lax.all_to_all(to_patches(fine_field), "wide", split_axis=1, concat_axis=0, tiled=True)


def return_patches(patch_rows, fine_height, fine_depth, channels):
    returned = lax.all_to_all(patch_rows, "wide", split_axis=0, concat_axis=1, tiled=True)
    shaped = returned.reshape(
        fine_height // PATCH, fine_depth // PATCH, PATCH, PATCH, PATCH, channels
    )
    return shaped.transpose(5, 2, 0, 3, 1, 4).reshape(channels, PATCH, fine_height, fine_depth)


def coarse_faces(coarse_block):
    return extended(coarse_block, (("narrow", 2),), 1)


def wide_input_conv(coarse_block, weight_mat, out_count, transposed):
    grown = coarse_faces(coarse_block)
    products = jnp.einsum("xyzd,dk->xyzk", grown, weight_mat, preferred_element_type=jnp.float32)
    padded = jnp.pad(products, ((1, 1), (1, 1), (0, 0), (0, 0)))
    extent = coarse_block.shape[:3]
    summed = jnp.zeros(extent + (out_count,), jnp.float32)
    for tap_index, (a, b, c) in enumerate(shifts(transposed)):
        summed = (
            summed
            + padded[
                a : a + extent[0],
                b : b + extent[1],
                c : c + extent[2],
                tap_index * out_count : (tap_index + 1) * out_count,
            ]
        )
    return summed


def narrow_input_conv(coarse_block, weight_mat, transposed):
    grown = coarse_faces(coarse_block)
    padded = jnp.pad(grown, ((1, 1), (1, 1), (0, 0), (0, 0)))
    extent = coarse_block.shape[:3]
    columns = jnp.concatenate(
        [
            padded[a : a + extent[0], b : b + extent[1], c : c + extent[2]]
            for a, b, c in shifts(transposed)
        ],
        axis=3,
    )
    return jnp.einsum("xyzk,kd->xyzd", columns, weight_mat, preferred_element_type=jnp.float32)


def shards(
    volume,
    cotangent,
    fine_weight,
    merge_weight,
    hidden_weight,
    step_table,
    output_weight,
    expand_weight,
    timestep,
):
    channels = volume.shape[0]
    fine_height = volume.shape[2]
    fine_depth = volume.shape[3]
    wide_count = lax.axis_size("wide")
    features = merge_weight.shape[1]
    hidden_local = hidden_weight.shape[2]
    coarse_grid = (wide_count, fine_height // PATCH, fine_depth // PATCH)
    hidden_mat = hidden_weight.transpose(1, 0, 2).reshape(features, 27 * hidden_local)
    output_mat = output_weight.reshape(27 * hidden_local, features)
    output_back = output_weight.transpose(2, 0, 1).reshape(features, 27 * hidden_local)
    hidden_back = hidden_weight.transpose(0, 2, 1).reshape(27 * hidden_local, features)

    def total_rows(partial_value):
        return lax.psum(partial_value, "wide")

    pre_act = fine_conv(volume, fine_weight, False)
    activated = jax.nn.silu(pre_act).astype(jnp.bfloat16)
    received = send_patches(activated)
    merged = total_rows(jnp.dot(received, merge_weight, preferred_element_type=jnp.float32))
    coarse_in = merged.astype(jnp.bfloat16).reshape(coarse_grid + (features,))
    bias_row = step_table[timestep[0]]
    gate_pre = wide_input_conv(coarse_in, hidden_mat, hidden_local, False) + bias_row
    hidden_act = jax.nn.silu(gate_pre).astype(jnp.bfloat16)
    branch = total_rows(narrow_input_conv(hidden_act, output_mat, False).reshape(-1, features))
    residual_sum = (merged + branch).astype(jnp.bfloat16)
    expanded = jnp.dot(residual_sum, expand_weight, preferred_element_type=jnp.float32).astype(
        jnp.bfloat16
    )
    expanded_field = return_patches(expanded, fine_height, fine_depth, channels)
    combined = activated.astype(jnp.float32) + expanded_field.astype(jnp.float32)
    grad_comb = (cotangent.astype(jnp.float32) * silu_slope(combined)).astype(jnp.bfloat16)
    grad_res = total_rows(
        jnp.einsum(
            "nk,dk->nd", send_patches(grad_comb), expand_weight, preferred_element_type=jnp.float32
        )
    )
    grad_res_b = grad_res.astype(jnp.bfloat16).reshape(coarse_grid + (features,))
    grad_hidden = wide_input_conv(grad_res_b, output_back, hidden_local, True)
    grad_gate = (grad_hidden * silu_slope(gate_pre)).astype(jnp.bfloat16)
    grad_conv = total_rows(narrow_input_conv(grad_gate, hidden_back, True).reshape(-1, features))
    grad_merged = (grad_res + grad_conv).astype(jnp.bfloat16)
    grad_cells = jnp.einsum(
        "nd,kd->nk", grad_merged, merge_weight, preferred_element_type=jnp.float32
    ).astype(jnp.bfloat16)
    grad_act = return_patches(grad_cells, fine_height, fine_depth, channels).astype(
        jnp.float32
    ) + grad_comb.astype(jnp.float32)
    grad_pre = (grad_act * silu_slope(pre_act)).astype(jnp.bfloat16)
    return fine_conv(grad_pre, fine_weight.transpose(0, 2, 1), True).astype(jnp.bfloat16)


def solution(mesh):
    in_specs = (
        P(None, ("groups", "wide"), None, "narrow"),
        P(None, ("groups", "wide"), None, "narrow"),
        P(),
        P("wide", None),
        P(None, None, "wide"),
        P(None, "wide"),
        P(None, "wide", None),
        P(None, "wide"),
        P("groups"),
    )
    out_specs = P(None, ("groups", "wide"), None, "narrow")
    return jax.shard_map(shards, mesh=mesh, in_specs=in_specs, out_specs=out_specs, check_vma=False)
```

profile of v0, /device:TPU:0, one launch (start us, length us, event | category | flops | bytes accessed | tf_op | source)
XLA Modules:
  0.0 473.5 jit_solution(18221159646353453401)
XLA Ops:
  7.5 4.9 %collective-permute-start = (bf16[32,1,16,16]{0,3,2,1:T(8,128)(2,1)S(1)}, bf16[32,1,16,16]{0,3,2,1:T(8,128)(2,1)S(1)}, u32[]{:S(2)}, u32[]{:S(2)}) collective-permute-start(bf16[32,1,16,16]{0,3,2,1:T(8,128)(2,1)S(1)} %get-tuple-element.14), channel_id=1, source_target_pairs={{0,2},{2,4},{4,6},{6,8},{8,10},{10,12},{12,14},{1,3},{3,5},{5,7},{... | collective-permute-start | bytes 49160 | tf_op jit(solution)/shard_map/ppermute | solution.py:17
  15.4 3.2 collective-permute-done.1
  21.3 1.9 collective-permute-done.3
  25.0 2.8 reshape.76
  28.8 2.4 fusion.20
  32.6 12.9 %all_to_all.64 = bf16[4,8,2048]{2,0,1:T(4,128)(2,1)S(1)} all-to-all(bf16[4,8,2048]{2,0,1:T(4,128)(2,1)S(1)} %copy.53), channel_id=1, replica_groups=mesh['groups'=2,'wide'=8,'narrow'=2] {'wide'}, dimensions={1} | all-to-all | bytes 262144 | tf_op jit(solution)/shard_map/all_to_all | solution.py:66
  45.5 3.7 fusion.129
  50.0 67.2 %all-reduce.11.cloned.1.call-done = f32[32,1024]{1,0:T(8,128)} async-done(((f32[32,1024]{1,0:T(8,128)}), f32[32,1024]{1,0:T(8,128)}) %all-reduce.11.cloned.1.call-update) | async-done | bytes 131088 | tf_op jit(solution)/shard_map/psum | solution.py:138
  120.7 18.6 %copy.57 = bf16[27,1024,256]{1,2,0:T(8,128)(2,1)} copy(bf16[27,1024,256]{2,1,0:T(8,128)(2,1)} %param.13) | data formatting | bytes 28311552 | tf_op args[4]
  139.4 9.4 %fusion.50 = f32[8,2,4,6912]{3,0,2,1:T(8,128)S(1)} fusion(bf16[1024,6912,1,1]{0,1,3,2:T(8,128)(2,1)} %bitcast.118, bf16[8,2,1,1024]{3,0,2,1:T(8,128)(2,1)S(1)} %collective-permute-done.5, bf16[8,2,2,1024]{3,0,2,1:T(8,128)(2,1)S(1)} %copy.54, bf16[8,2,1,1024]{3,0,2,1:T(8,128)(2,1)S(1)} %collective-permute-done.4), kind=kOutput, calls=%fused_computation.119 | convolution fusion | flops 906100736 | bytes 16056320 | tf_op jit(solution)/shard_map/xyzd,dk->xyzk/dot_general | solution.py:83
  148.9 3.0 collective-permute-start.6
  153.4 1.6 collective-permute-done.7
  155.9 8.3 %fusion.130 = f32[32,1024]{1,0:T(8,128)} fusion(bf16[32,6912]{1,0:T(8,128)(2,1)S(1)} %dot_general.30, bf16[6912,1024]{1,0:T(8,128)(2,1)} %bitcast.120), kind=kOutput, calls=%fused_computation.271 | convolution fusion | flops 452984832 | bytes 14729216 | tf_op jit(solution)/shard_map/xyzk,kd->xyzd/dot_general | solution.py:111
  164.3 69.0 %all-reduce.13.cloned.1.call-done = f32[32,1024]{1,0:T(8,128)} async-done(((f32[32,1024]{1,0:T(8,128)}), f32[32,1024]{1,0:T(8,128)}) %all-reduce.13.cloned.1.call-update) | async-done | bytes 131088 | tf_op jit(solution)/shard_map/psum | solution.py:138
  233.3 3.1 convolution_convert_fusion.1
  236.4 11.1 %all_to_all.65 = bf16[8,4,2048]{2,1,0:T(4,128)(2,1)S(1)} all-to-all(bf16[8,4,2048]{2,1,0:T(4,128)(2,1)S(1)} %all_to_all.52), channel_id=1, replica_groups=mesh['groups'=2,'wide'=8,'narrow'=2] {'wide'}, dimensions={0} | all-to-all | bytes 262144 | tf_op jit(solution)/shard_map/all_to_all | solution.py:70
  251.9 9.7 %all_to_all.66 = bf16[4,8,2048]{2,0,1:T(4,128)(2,1)S(1)} all-to-all(bf16[4,8,2048]{2,0,1:T(4,128)(2,1)S(1)} %copy.62), channel_id=1, replica_groups=mesh['groups'=2,'wide'=8,'narrow'=2] {'wide'}, dimensions={1} | all-to-all | bytes 262144 | tf_op jit(solution)/shard_map/all_to_all | solution.py:66
  261.6 4.2 fusion.131
  265.9 67.4 %all-reduce.15.cloned.1.call-done = f32[32,1024]{1,0:T(8,128)} async-done(((f32[32,1024]{1,0:T(8,128)}), f32[32,1024]{1,0:T(8,128)}) %all-reduce.15.cloned.1.call-update) | async-done | bytes 131088 | tf_op jit(solution)/shard_map/psum | solution.py:138
  336.9 1.8 collective-permute-done.9
  338.7 9.4 %fusion.56 = f32[8,2,4,6912]{3,0,2,1:T(8,128)S(1)} fusion(bf16[1024,6912,1,1]{0,1,3,2:T(8,128)(2,1)} %bitcast.121, bf16[8,2,1,1024]{3,0,2,1:T(8,128)(2,1)S(1)} %collective-permute-done.9, bf16[8,2,2,1024]{3,0,2,1:T(8,128)(2,1)S(1)} %copy.63, bf16[8,2,1,1024]{3,0,2,1:T(8,128)(2,1)S(1)} %collective-permute-done.8), kind=kOutput, calls=%fused_computation.125 | convolution fusion | flops 906100736 | bytes 16056320 | tf_op jit(solution)/shard_map/xyzd,dk->xyzk/dot_general | solution.py:83
  348.2 2.1 collective-permute-start.10
  350.3 1.5 collective-permute-start.11
  351.8 1.5 collective-permute-done.11
  354.3 8.2 %fusion.132 = f32[32,1024]{1,0:T(8,128)} fusion(bf16[32,6912]{1,0:T(8,128)(2,1)S(1)} %dot_general.35, bf16[6912,1024]{1,0:T(8,128)(2,1)} %bitcast.119), kind=kOutput, calls=%fused_computation.273 | convolution fusion | flops 452984832 | bytes 14729216 | tf_op jit(solution)/shard_map/xyzk,kd->xyzd/dot_general | solution.py:111
  362.6 69.0 %all-reduce.17.cloned.1.call-done = f32[32,1024]{1,0:T(8,128)} async-done(((f32[32,1024]{1,0:T(8,128)}), f32[32,1024]{1,0:T(8,128)}) %all-reduce.17.cloned.1.call-update) | async-done | bytes 131088 | tf_op jit(solution)/shard_map/psum | solution.py:138
  431.6 3.6 convolution_convert_fusion
  435.3 11.0 %all_to_all.67 = bf16[8,4,2048]{2,1,0:T(4,128)(2,1)S(1)} all-to-all(bf16[8,4,2048]{2,1,0:T(4,128)(2,1)S(1)} %all_to_all.58), channel_id=1, replica_groups=mesh['groups'=2,'wide'=8,'narrow'=2] {'wide'}, dimensions={0} | all-to-all | bytes 262144 | tf_op jit(solution)/shard_map/all_to_all | solution.py:70
  449.5 2.1 collective-permute-start.12
  453.6 4.3 collective-permute-done.13
  460.5 1.8 collective-permute-done.15
  463.5 2.3 select_convert_fusion
  (153 shorter events, 35.8 us)
Async XLA Ops:
  6.5 114.2 %copy-start = (f32[1000,256]{1,0:T(8,128)S(1)}, f32[1000,256]{1,0:T(8,128)}, u32[]{:S(2)}) copy-start(f32[1000,256]{1,0:T(8,128)} %param.14) | copy-start | bytes 3072004
  6.5 110.6 %all-reduce.11.cloned.1.call-start = ((), (), s32[]{:S(2)}) async-start(), calls=%async_computation.4 | async-start | bytes 262144 | tf_op jit(solution)/shard_map/psum | solution.py:138
  7.5 6.8 %collective-permute-start = (bf16[32,1,16,16]{0,3,2,1:T(8,128)(2,1)S(1)}, bf16[32,1,16,16]{0,3,2,1:T(8,128)(2,1)S(1)}, u32[]{:S(2)}, u32[]{:S(2)}) collective-permute-start(bf16[32,1,16,16]{0,3,2,1:T(8,128)(2,1)S(1)} %get-tuple-element.14), channel_id=1, source_target_pairs={{0,2},{2,4},{4,6},{6,8},{8,10},{10,12},{12,14},{1,3},{3,5},{5,7},{... | collective-permute-start | bytes 49160 | tf_op jit(solution)/shard_map/ppermute | solution.py:17
  12.4 6.2 %collective-permute-start.1 = (bf16[32,1,16,16]{0,3,2,1:T(8,128)(2,1)S(1)}, bf16[32,1,16,16]{0,3,2,1:T(8,128)(2,1)S(1)}, u32[]{:S(2)}, u32[]{:S(2)}) collective-permute-start(bf16[32,1,16,16]{0,3,2,1:T(8,128)(2,1)S(1)} %get-tuple-element.13), channel_id=1, source_target_pairs={{2,0},{4,2},{6,4},{8,6},{10,8},{12,10},{14,12},{3,1},{5,3},{7,5},{... | collective-permute-start | bytes 49160 | tf_op jit(solution)/shard_map/ppermute | solution.py:19
  18.7 2.6 collective-permute-start.2
  20.0 3.2 collective-permute-start.3
  27.8 0.9 copy-start.5
  27.9 0.9 copy-start.6
  49.3 184.0 %all-reduce.13.cloned.1.call-start = ((), (), s32[]{:S(2)}) async-start(), calls=%async_computation.5 | async-start | bytes 262144 | tf_op jit(solution)/shard_map/psum | solution.py:138
  118.1 21.3 %collective-permute-start.4 = (bf16[8,2,1,1024]{3,0,2,1:T(8,128)(2,1)S(1)}, bf16[8,2,1,1024]{3,0,2,1:T(8,128)(2,1)S(1)}, u32[]{:S(2)}, u32[]{:S(2)}) collective-permute-start(bf16[8,2,1,1024]{3,0,2,1:T(8,128)(2,1)S(1)} %get-tuple-element.17), channel_id=1, source_target_pairs={{0,1},{2,3},{4,5},{6,7},{8,9},{10,11},{12,13},{14,15},{16,17},{18,... | collective-permute-start | bytes 98312 | tf_op jit(solution)/shard_map/ppermute | solution.py:17
  119.4 20.0 %collective-permute-start.5 = (bf16[8,2,1,1024]{3,0,2,1:T(8,128)(2,1)S(1)}, bf16[8,2,1,1024]{3,0,2,1:T(8,128)(2,1)S(1)}, u32[]{:S(2)}, u32[]{:S(2)}) collective-permute-start(bf16[8,2,1,1024]{3,0,2,1:T(8,128)(2,1)S(1)} %get-tuple-element.18), channel_id=1, source_target_pairs={{1,0},{3,2},{5,4},{7,6},{9,8},{11,10},{13,12},{15,14},{17,16},{19,... | collective-permute-start | bytes 98312 | tf_op jit(solution)/shard_map/ppermute | solution.py:19
  148.9 4.5 collective-permute-start.6
  151.9 3.1 collective-permute-start.7
  155.9 77.3 %copy-start.2 = (f32[32,1024]{1,0:T(8,128)S(1)}, f32[32,1024]{1,0:T(8,128)}, u32[]{:S(2)}) copy-start(f32[32,1024]{1,0:T(8,128)} %all-reduce.11.cloned.1.call-done) | copy-start | bytes 393220
  164.2 169.1 %all-reduce.15.cloned.1.call-start = ((), (), s32[]{:S(2)}) async-start(), calls=%async_computation.6 | async-start | bytes 262144 | tf_op jit(solution)/shard_map/psum | solution.py:138
  236.4 14.0 %copy-start.4 = (bf16[32,8,16,16]{0,3,2,1:T(8,128)(2,1)S(1)}, bf16[32,8,16,16]{0,3,2,1:T(8,128)(2,1)}, u32[]{:S(2)}) copy-start(bf16[32,8,16,16]{0,3,2,1:T(8,128)(2,1)} %param.10) | copy-start | bytes 393220
  265.8 165.8 %all-reduce.17.cloned.1.call-start = ((), (), s32[]{:S(2)}) async-start(), calls=%async_computation.7 | async-start | bytes 262144 | tf_op jit(solution)/shard_map/psum | solution.py:138
  334.3 2.6 collective-permute-start.8
  335.6 3.1 collective-permute-start.9
  348.2 3.6 collective-permute-start.10
  350.3 3.1 collective-permute-start.11
  354.3 77.3 %copy-start.3 = (f32[32,1024]{1,0:T(8,128)S(1)}, f32[32,1024]{1,0:T(8,128)}, u32[]{:S(2)}) copy-start(f32[32,1024]{1,0:T(8,128)} %all-reduce.15.cloned.1.call-done) | copy-start | bytes 393220
  449.5 4.0 collective-permute-start.12
  451.7 6.2 %collective-permute-start.13 = (bf16[32,1,16,16]{0,2,3,1:T(8,128)(2,1)S(1)}, bf16[32,1,16,16]{0,2,3,1:T(8,128)(2,1)S(1)}, u32[]{:S(2)}, u32[]{:S(2)}) collective-permute-start(bf16[32,1,16,16]{0,2,3,1:T(8,128)(2,1)S(1)} %get-tuple-element.12), channel_id=1, source_target_pairs={{2,0},{4,2},{6,4},{8,6},{10,8},{12,10},{14,12},{3,1},{5,3},{7,5},{... | collective-permute-start | bytes 49160 | tf_op jit(solution)/shard_map/ppermute | solution.py:19
  457.9 2.6 collective-permute-start.14
  459.2 3.1 collective-permute-start.15
  463.5 3.4 copy-start.1
Sparse Core Ops, SparseCore 0:
  49.4 67.6 all-reduce.10
  164.3 68.8 all-reduce.12
  266.0 67.3 all-reduce.14
  362.7 68.8 all-reduce.16
where the time goes:
time: 475 us; the launch traced here: 473 us
  waiting for transfers between devices  290 us (61%)
  matrix products  54.5 us (11%)
  blocking collectives  44.8 us (9%)
  local copies, waits for them, and re-layouts  36.7 us (8%)
  starting transfers between devices  28.1 us (6%)
  between operations  14.8 us (3%)
  other arithmetic  4.77 us (1%)
    psum x4, waiting for transfers between devices, total_rows(): return lax.psum(partial_value, 'wide')  273 us
    all_to_all x2, blocking collectives, send_patches(): lax.all_to_all(to_patches(fine_field), 'wide', split_axis=1, concat_axis=...  22.6 us
    all_to_all x2, blocking collectives, return_patches(): lax.all_to_all(patch_rows, 'wide', split_axis=0, concat_axis=1, tiled=True)  22.2 us
    unnamed x65, local copies, waits for them, and re-layouts  20.7 us
    dot_general x2, matrix products, wide_input_conv(): jnp.einsum('xyzd,dk->xyzk', grown, weight_mat, preferred_element_type=jnp...  18.8 us
    ppermute x8, starting transfers between devices, extended(): lax.ppermute(tail, axis, [(i, (i + 1) % count) for i in range(ends)])  17.3 us
    dot_general x2, matrix products, narrow_input_conv(): jnp.einsum('xyzk,kd->xyzd', columns, weight_mat, preferred_element_type=j...  16.5 us
    ppermute x8, waiting for transfers between devices, extended(): lax.ppermute(head, axis, [((i + 1) % count, i) for i in range(ends)])  16 us
  transfers between devices with their start and end apart: 20, of which 13 were waited for; matrix products, arithmetic and copies ran while one was open for 4% of the time, Pallas kernels for 0%

commit v1 on v0

--- a/solution.py
+++ b/solution.py
@@ -1,6 +1,10 @@
+import functools
+
 import jax
 import jax.numpy as jnp
 from jax import lax
+from jax.experimental import pallas as pl
+from jax.experimental.pallas import tpu as pltpu
 from jax.sharding import PartitionSpec as P
 
 PATCH = 8
@@ -109,6 +113,425 @@
         axis=3,
     )
     return jnp.einsum("xyzk,kd->xyzd", columns, weight_mat, preferred_element_type=jnp.float32)
+
+
+BF = jnp.bfloat16
+F32 = jnp.float32
+LIMIT = 48 * 1024 * 1024
+
+
+def nn_dot(lhs, rhs):
+    return jnp.dot(lhs, rhs, preferred_element_type=F32)
+
+
+def nt_dot(lhs, rhs):
+    return lax.dot_general(lhs, rhs, (((1,), (1,)), ((), ())), preferred_element_type=F32)
+
+
+def banded(weight):
+    taps = weight.reshape(9, 3, 32, 32)
+    band = jnp.concatenate([taps[:, 2], taps[:, 1], taps[:, 0]], axis=2)
+    wide_band = jnp.pad(band, ((0, 0), (0, 0), (224, 224)))
+    starts = [224 - 32 * (d - 1) for d in range(8)] + [288, 0]
+    return jnp.concatenate([wide_band[:, :, s : s + 256] for s in starts], axis=1)
+
+
+def fine_taps(planes_ref, band_ref):
+    total = None
+    for i in range(3):
+        for j in range(3):
+            lhs = planes_ref[i, j : j + 16].reshape(256, 320)
+            part = nn_dot(lhs, band_ref[3 * i + j])
+            total = part if total is None else total + part
+    return total
+
+
+def cell_rows(ref, b):
+    low = ref[pl.ds(pl.multiple_of(b * 16, 16), 16), :]
+    high = ref[pl.ds(pl.multiple_of(b * 16 + 128, 16), 16), :]
+    return jnp.concatenate([low, high], axis=0)
+
+
+def put_rows(ref, b, value):
+    ref[pl.ds(pl.multiple_of(b * 16, 16), 16), :] = value[:16]
+    ref[pl.ds(pl.multiple_of(b * 16 + 128, 16), 16), :] = value[16:]
+
+
+def add_up(step, ref, value):
+    @pl.when(step == 0)
+    def _():
+        ref[...] = value
+
+    @pl.when(step > 0)
+    def _():
+        ref[...] += value
+
+
+def merge_kernel(planes_ref, band_ref, merge_ref, pre_ref, act_ref, sum_ref, sum_b_ref):
+    b = pl.program_id(0)
+
+    @pl.when(b == 0)
+    def _():
+        pre = fine_taps(planes_ref, band_ref)
+        pre_ref[...] = pre
+        act_ref[...] = (pre * jax.nn.sigmoid(pre)).astype(BF)
+
+    add_up(b, sum_ref, nn_dot(cell_rows(act_ref, b), merge_ref[...]))
+
+    @pl.when(b == pl.num_programs(0) - 1)
+    def _():
+        sum_b_ref[...] = sum_ref[...].astype(BF)
+
+
+def whole(shape):
+    return pl.BlockSpec(shape, lambda *_: (0,) * len(shape))
+
+
+def params():
+    return pltpu.CompilerParams(vmem_limit_bytes=LIMIT)
+
+
+def merge_call(planes, band, merge_weight):
+    features = merge_weight.shape[1]
+    return pl.pallas_call(
+        merge_kernel,
+        grid=(8,),
+        in_specs=[
+            whole(planes.shape),
+            whole(band.shape),
+            pl.BlockSpec((256, features), lambda b: (b, 0)),
+        ],
+        out_specs=[whole((256, 256)), whole((256, 256)), whole((32, features)), whole((32, features))],
+        out_shape=[
+            jax.ShapeDtypeStruct((256, 256), F32),
+            jax.ShapeDtypeStruct((256, 256), BF),
+            jax.ShapeDtypeStruct((32, features), F32),
+            jax.ShapeDtypeStruct((32, features), BF),
+        ],
+        compiler_params=params(),
+    )(planes, band, merge_weight)
+
+
+def final_kernel(planes_ref, band_ref, out_ref):
+    out_ref[...] = fine_taps(planes_ref, band_ref).astype(BF)
+
+
+def final_call(planes, band):
+    return pl.pallas_call(
+        final_kernel,
+        out_shape=jax.ShapeDtypeStruct((256, 256), BF),
+        compiler_params=params(),
+    )(planes, band)
+
+
+def put_columns(cols_ref, cells):
+    row = lax.broadcasted_iota(jnp.int32, (64, 1), 0)
+    in_half, along_x, half = row & 1, (row >> 1) & 7, row >> 5
+    zero = jnp.zeros_like(cells)
+    below = jnp.where(
+        in_half == 1,
+        pltpu.roll(cells, 1, 0),
+        jnp.where(half == 1, pltpu.roll(cells, 31, 0), zero),
+    )
+    above = jnp.where(
+        in_half == 0,
+        pltpu.roll(cells, 63, 0),
+        jnp.where(half == 0, pltpu.roll(cells, 33, 0), zero),
+    )
+    none = jnp.zeros((16, cells.shape[1]), BF)
+    for k, along_z in enumerate((below, cells, above)):
+        before = jnp.where(along_x > 0, pltpu.roll(along_z, 2, 0), zero)
+        after = jnp.where(along_x < 7, pltpu.roll(along_z, 62, 0), zero)
+        for i, moved in enumerate((before, along_z, after)):
+            rows = moved.astype(BF)
+            blocks = [rows[16 * q : 16 * q + 16] for q in range(4)]
+            cols_ref[9 * i + k] = jnp.concatenate([none, blocks[0], none, blocks[2]], axis=0)
+            cols_ref[9 * i + 3 + k] = rows
+            cols_ref[9 * i + 6 + k] = jnp.concatenate([blocks[1], none, blocks[3], none], axis=0)
+
+
+def conv_steps(weight_ref, sum_ref, cols_ref, flipped, dot):
+    step = pl.program_id(0)
+    taps = weight_ref.shape[0]
+    total = None
+    for q in range(taps):
+        t = step * taps + q
+        part = dot(cols_ref[26 - t if flipped else t], weight_ref[q])
+        total = part if total is None else total + part
+    add_up(step, sum_ref, total)
+
+
+def both_halves(n_ref, mine_ref, got_ref):
+    mine, got = mine_ref[...].astype(F32), got_ref[...].astype(F32)
+    first = n_ref[0] == 0
+    return jnp.concatenate([jnp.where(first, mine, got), jnp.where(first, got, mine)], axis=0)
+
+
+def outer_kernel(n_ref, mine_ref, got_ref, weight_ref, sum_ref, cols_ref, *, flipped, dot):
+    @pl.when(pl.program_id(0) == 0)
+    def _():
+        put_columns(cols_ref, both_halves(n_ref, mine_ref, got_ref))
+
+    conv_steps(weight_ref, sum_ref, cols_ref, flipped, dot)
+
+
+def inner_forward_kernel(
+    n_ref, mine_ref, got_ref, bias_ref, weight_ref, gate_ref, sum_ref, sum_b_ref, cols_ref
+):
+    @pl.when(pl.program_id(0) == 0)
+    def _():
+        gate = mine_ref[...] + got_ref[...] + bias_ref[...]
+        gate_ref[...] = gate
+        put_columns(cols_ref, gate * jax.nn.sigmoid(gate))
+
+    conv_steps(weight_ref, sum_ref, cols_ref, False, nn_dot)
+
+    @pl.when(pl.program_id(0) == pl.num_programs(0) - 1)
+    def _():
+        sum_b_ref[...] = sum_ref[...].astype(BF)
+
+
+def inner_backward_kernel(
+    n_ref, mine_ref, got_ref, gate_ref, weight_ref, sum_ref, sum_b_ref, cols_ref
+):
+    @pl.when(pl.program_id(0) == 0)
+    def _():
+        grad = (mine_ref[...] + got_ref[...]) * silu_slope(gate_ref[...])
+        put_columns(cols_ref, grad)
+
+    conv_steps(weight_ref, sum_ref, cols_ref, True, nt_dot)
+
+    @pl.when(pl.program_id(0) == pl.num_programs(0) - 1)
+    def _():
+        sum_b_ref[...] = sum_ref[...].astype(BF)
+
+
+def conv_call(kernel, n, small, weight, block, place, depth, outs):
+    taps = block[0]
+    return pl.pallas_call(
+        kernel,
+        grid_spec=pltpu.PrefetchScalarGridSpec(
+            num_scalar_prefetch=1,
+            grid=(27 // taps,),
+            in_specs=[whole(a.shape) for a in small] + [pl.BlockSpec(block, place)],
+            out_specs=[whole(o.shape) for o in outs],
+            scratch_shapes=[pltpu.VMEM((27, 64, depth), BF)],
+        ),
+        out_shape=outs,
+        compiler_params=params(),
+    )(n, *small, weight)
+
+
+def expand_kernel(
+    n_ref, merged_ref, mine_ref, got_ref, act_ref, cot_ref, expand_ref, grad_ref, sum_ref, sum_b_ref, res_ref
+):
+    b = pl.program_id(0)
+
+    @pl.when(b == 0)
+    def _():
+        mine, got = mine_ref[...].astype(F32), got_ref[...].astype(F32)
+        first = n_ref[0] == 0
+        branch = jnp.concatenate([jnp.where(first, mine, got), jnp.where(first, got, mine)], axis=1)
+        res_ref[...] = (merged_ref[...] + branch).astype(BF)
+
+    expanded = nn_dot(res_ref[...], expand_ref[...]).astype(BF)
+    combined = cell_rows(act_ref, b).astype(F32) + expanded.astype(F32)
+    grad = (cell_rows(cot_ref, b).astype(F32) * silu_slope(combined)).astype(BF)
+    put_rows(grad_ref, b, grad)
+    add_up(b, sum_ref, nt_dot(grad, expand_ref[...]))
+
+    @pl.when(b == pl.num_programs(0) - 1)
+    def _():
+        sum_b_ref[...] = sum_ref[...].astype(BF)
+
+
+def expand_call(n, merged, mine, got, act, cot, expand_weight):
+    features = expand_weight.shape[0]
+    small = (merged, mine, got, act, cot)
+    outs = [
+        jax.ShapeDtypeStruct((256, 256), BF),
+        jax.ShapeDtypeStruct((32, features), F32),
+        jax.ShapeDtypeStruct((32, features), BF),
+    ]
+    return pl.pallas_call(
+        expand_kernel,
+        grid_spec=pltpu.PrefetchScalarGridSpec(
+            num_scalar_prefetch=1,
+            grid=(8,),
+            in_specs=[whole(a.shape) for a in small]
+            + [pl.BlockSpec((features, 256), lambda b, n: (0, b))],
+            out_specs=[whole(o.shape) for o in outs],
+            scratch_shapes=[pltpu.VMEM((32, features), BF)],
+        ),
+        out_shape=outs,
+        compiler_params=params(),
+    )(n, *small, expand_weight)
+
+
+def grad_kernel(n_ref, res_ref, mine_ref, got_ref, comb_ref, pre_ref, merge_ref, out_ref, sum_ref):
+    b = pl.program_id(0)
+
+    @pl.when(b == 0)
+    def _():
+        mine, got = mine_ref[...].astype(F32), got_ref[...].astype(F32)
+        first = n_ref[0] == 0
+        conv = jnp.concatenate([jnp.where(first, mine, got), jnp.where(first, got, mine)], axis=1)
+        sum_ref[...] = (res_ref[...] + conv).astype(BF)
+
+    cells = nt_dot(sum_ref[...], merge_ref[...]).astype(BF)
+    grad = cells.astype(F32) + cell_rows(comb_ref, b).astype(F32)
+    put_rows(out_ref, b, (grad * silu_slope(cell_rows(pre_ref, b))).astype(BF))
+
+
+def grad_call(n, grad_res, mine, got, grad_comb, pre_act, merge_weight):
+    features = merge_weight.shape[1]
+    small = (grad_res, mine, got, grad_comb, pre_act)
+    return pl.pallas_call(
+        grad_kernel,
+        grid_spec=pltpu.PrefetchScalarGridSpec(
+            num_scalar_prefetch=1,
+            grid=(8,),
+            in_specs=[whole(a.shape) for a in small]
+            + [pl.BlockSpec((256, features), lambda b, n: (b, 0))],
+            out_specs=whole((256, 256)),
+            scratch_shapes=[pltpu.VMEM((32, features), BF)],
+        ),
+        out_shape=jax.ShapeDtypeStruct((256, 256), BF),
+        compiler_params=params(),
+    )(n, *small, merge_weight)
+
+
+def swap_narrow(value):
+    return lax.ppermute(value, "narrow", [(0, 1), (1, 0)])
+
+
+def summed_wide(part, part_b):
+    def partner(value, mask):
+        return lax.ppermute(value, "wide", [(i, i ^ mask) for i in range(8)])
+
+    pair = part + partner(part_b, 1).astype(F32)
+    pair_b = pair.astype(BF)
+    others = [partner(pair_b, mask) for mask in (2, 4, 6)]
+    return pair + others[0].astype(F32) + others[1].astype(F32) + others[2].astype(F32)
+
+
+def to_feature_halves(n, cells):
+    half = cells.shape[1] // 2
+    low, high = cells[:, :half], cells[:, half:]
+    return jnp.where(n == 0, low, high), swap_narrow(jnp.where(n == 0, high, low))
+
+
+def to_cell_halves(n, rows):
+    half = rows.shape[0] // 2
+    low, high = rows[:half], rows[half:]
+    return jnp.where(n == 0, low, high), swap_narrow(jnp.where(n == 0, high, low).astype(BF))
+
+
+def with_edges(n, planes):
+    low, high = planes[..., 0, :32], planes[..., 1, 224:]
+    got = swap_narrow(jnp.where(n == 0, high, low))
+    none = jnp.zeros_like(got)
+    before = jnp.stack([jnp.where(n == 0, none, got), planes[..., 0, 224:]], axis=3)
+    after = jnp.stack([planes[..., 1, :32], jnp.where(n == 0, got, none)], axis=3)
+    rows = jnp.concatenate([planes, before, after], axis=4).reshape(3, 16, 16, 320)
+    return jnp.pad(rows, ((0, 0), (1, 1), (0, 0), (0, 0)))
+
+
+def along_x(planes, step):
+    none = jnp.zeros_like(planes[:, :1])
+    if step > 0:
+        return jnp.concatenate([none, planes[:, :-1]], axis=1)
+    return jnp.concatenate([planes[:, 1:], none], axis=1)
+
+
+def eight_shards(
+    volume,
+    cotangent,
+    fine_weight,
+    merge_weight,
+    hidden_weight,
+    step_table,
+    output_weight,
+    expand_weight,
+    timestep,
+):
+    features = merge_weight.shape[1]
+    hidden = hidden_weight.shape[2]
+    half = features // 2
+    w, n = lax.axis_index("wide"), lax.axis_index("narrow")
+    n_arr = n.astype(jnp.int32).reshape(1)
+
+    def row_form(fine_field):
+        return fine_field.transpose(1, 2, 3, 0).reshape(8, 16, 2, 256)
+
+    field = row_form(volume)
+    outgoing = jnp.stack(
+        [jnp.roll(field, 1, 0), field, jnp.roll(field, -1, 0), row_form(cotangent)], axis=1
+    )
+    arrived = lax.all_to_all(
+        outgoing.reshape(8, 128, 256), "wide", split_axis=0, concat_axis=0, tiled=True
+    )
+    planes = arrived.reshape(8, 4, 16, 2, 256).transpose(1, 2, 0, 3, 4)
+    planes_in = jnp.stack(
+        [
+            jnp.where(w == 0, along_x(planes[0], 1), planes[0]),
+            planes[1],
+            jnp.where(w == 7, along_x(planes[2], -1), planes[2]),
+        ]
+    )
+    cot = planes[3].reshape(256, 256)
+    pre_act, act, merged_part, merged_part_b = merge_call(
+        with_edges(n, planes_in), banded(fine_weight), merge_weight
+    )
+    merged = summed_wide(merged_part, merged_part_b)
+    mine, got = to_feature_halves(n, merged.astype(BF))
+
+    gate_shape = jax.ShapeDtypeStruct((64, hidden), F32)
+    sum_shapes = [jax.ShapeDtypeStruct((64, half), F32), jax.ShapeDtypeStruct((64, half), BF)]
+    hidden_block = ((3, half, hidden), lambda s, n: (s, n[0], 0))
+    output_block = ((3, hidden, half), lambda s, n: (s, 0, n[0]))
+
+    (gate_part,) = conv_call(
+        functools.partial(outer_kernel, flipped=False, dot=nn_dot),
+        n_arr, (mine, got), hidden_weight, *hidden_block, half, [gate_shape],
+    )
+    bias = lax.dynamic_slice_in_dim(step_table, timestep[0], 1, axis=0)
+    gate_pre, branch_part, branch_part_b = conv_call(
+        inner_forward_kernel,
+        n_arr, (gate_part, swap_narrow(gate_part), bias), output_weight, *output_block, hidden,
+        [gate_shape] + sum_shapes,
+    )
+    branch = summed_wide(branch_part, branch_part_b)
+    mine, got = to_cell_halves(n, branch)
+    grad_comb, res_part, res_part_b = expand_call(n_arr, merged, mine, got, act, cot, expand_weight)
+    grad_res = summed_wide(res_part, res_part_b)
+    mine, got = to_feature_halves(n, grad_res.astype(BF))
+    (hidden_part,) = conv_call(
+        functools.partial(outer_kernel, flipped=True, dot=nt_dot),
+        n_arr, (mine, got), output_weight, *output_block, half, [gate_shape],
+    )
+    conv_part, conv_part_b = conv_call(
+        inner_backward_kernel,
+        n_arr, (hidden_part, swap_narrow(hidden_part), gate_pre), hidden_weight, *hidden_block, hidden,
+        sum_shapes,
+    )
+    grad_conv = summed_wide(conv_part, conv_part_b)
+    mine, got = to_cell_halves(n, grad_conv)
+    grad_pre = grad_call(n_arr, grad_res, mine, got, grad_comb, pre_act, merge_weight)
+
+    plane = grad_pre.reshape(16, 8, 2, 256)
+    none = jnp.zeros_like(plane)
+    beside = jnp.where(
+        w == 0, along_x(plane, -1), jnp.where(w == 7, along_x(plane, 1), none)
+    )
+    leaving = jnp.stack([plane, beside]).transpose(2, 0, 1, 3, 4).reshape(8, 64, 256)
+    returned = lax.all_to_all(leaving, "wide", split_axis=0, concat_axis=0, tiled=True)
+    returned = returned.reshape(8, 2, 16, 2, 256)
+    grown = jnp.concatenate([returned[7:, 1], returned[:, 0], returned[:1, 1]], axis=0)
+    windows = jnp.stack([grown[i : i + 8].transpose(1, 0, 2, 3) for i in range(3)])
+    back = fine_weight[::-1].transpose(0, 2, 1)
+    result = final_call(with_edges(n, windows), banded(back))
+    return result.reshape(16, 8, 2, 8, 32).transpose(4, 1, 0, 2, 3).reshape(32, 8, 16, 16)
 
 
 def shards(
@@ -186,4 +609,7 @@
         P("groups"),
     )
     out_specs = P(None, ("groups", "wide"), None, "narrow")
-    return jax.shard_map(shards, mesh=mesh, in_specs=in_specs, out_specs=out_specs, check_vma=False)
+    sizes = dict(mesh.shape)
+    fits = sizes["wide"] == PATCH and sizes["narrow"] == 2
+    body = eight_shards if fits else shards
+    return jax.shard_map(body, mesh=mesh, in_specs=in_specs, out_specs=out_specs, check_vma=False)

time: 475 us -> 163 us (0.34)
  waiting for transfers between devices: 290 us -> 56.5 us
  matrix products: 54.5 us -> 0 us
  blocking collectives: 44.8 us -> 0 us
  Pallas kernels: 0 us -> 44.6 us
  local copies, waits for them, and re-layouts: 36.7 us -> 18.5 us
  between operations: 14.8 us -> 1.41 us
  starting transfers between devices: 28.1 us -> 36.8 us
    psum x4 -> x0, waiting for transfers between devices: 273 us -> none  [total_rows(): return lax.psum(partial_value, 'wide')]
    dot_general x8 -> x0, matrix products: 49.8 us -> none  [the longest x2 18.8 us: wide_input_conv(): jnp.einsum('xyzd,dk->xyzk', grown, weight_mat, preferred_element_type=jnp...]
    all_to_all x4 -> x0, blocking collectives: 44.8 us -> none  [the longest x2 22.6 us: send_patches(): lax.all_to_all(to_patches(fine_field), 'wide', split_axis=1, concat_axis=...]
    pallas_call x0 -> x8, Pallas kernels: none -> 44.6 us  [the longest x4 30.4 us: conv_call(): pl.pallas_call(kernel, grid_spec=pltpu.PrefetchScalarGridSpec(num_scalar_...]
    all_to_all x0 -> x2, waiting for transfers between devices: none -> 22.5 us  [the longest x1 13.4 us: eight_shards(): lax.all_to_all(outgoing.reshape(8, 128, 256), 'wide', split_axis=0, conca...]
    ppermute x16 -> x24, waiting for transfers between devices: 17.2 us -> 34.1 us  [the longest x16 25.5 us: partner(): return lax.ppermute(value, 'wide', [(i, i ^ mask) for i in range(8)])]
    unnamed x65 -> x42, local copies, waits for them, and re-layouts: 20.7 us -> 4.08 us
    all_to_all x0 -> x2, starting transfers between devices: none -> 11.6 us  [the longest x1 7.28 us: eight_shards(): lax.all_to_all(outgoing.reshape(8, 128, 256), 'wide', split_axis=0, conca...]
  transfers between devices with their start and end apart: 20 -> 26, of which waited for: 13 -> 21; matrix products, arithmetic and copies ran while one was open for 4% -> 1% of each run, Pallas kernels for 0% -> 0%
where the time goes in v1:
time: 163 us; the launch traced here: 162 us
  waiting for transfers between devices  56.5 us (35%)
  Pallas kernels  44.6 us (27%)
  starting transfers between devices  36.8 us (23%)
  local copies, waits for them, and re-layouts  18.5 us (11%)
  other arithmetic  4.37 us (3%)
    pallas_call x4, Pallas kernels, conv_call(): pl.pallas_call(kernel, grid_spec=pltpu.PrefetchScalarGridSpec(num_scalar_...  30.4 us
    ppermute x16, waiting for transfers between devices, partner(): return lax.ppermute(value, 'wide', [(i, i ^ mask) for i in range(8)])  25.5 us
    ppermute x16, starting transfers between devices, partner(): return lax.ppermute(value, 'wide', [(i, i ^ mask) for i in range(8)])  24.3 us
    all_to_all x1, waiting for transfers between devices, eight_shards(): lax.all_to_all(outgoing.reshape(8, 128, 256), 'wide', split_axis=0, conca...  13.4 us
    all_to_all x1, waiting for transfers between devices, eight_shards(): lax.all_to_all(leaving, 'wide', split_axis=0, concat_axis=0, tiled=True)  9.01 us
    ppermute x8, waiting for transfers between devices, swap_narrow(): return lax.ppermute(value, 'narrow', [(0, 1), (1, 0)])  8.56 us
    all_to_all x1, starting transfers between devices, eight_shards(): lax.all_to_all(outgoing.reshape(8, 128, 256), 'wide', split_axis=0, conca...  7.28 us
    pallas_call x1, Pallas kernels, merge_call(): pl.pallas_call(merge_kernel, grid=(8,), in_specs=[whole(planes.shape), wh...  6.16 us
  transfers between devices with their start and end apart: 26, of which 21 were waited for; matrix products, arithmetic and copies ran while one was open for 1% of the time, Pallas kernels for 0%

profile of v1, /device:TPU:0, one launch (start us, length us, event | category | flops | bytes accessed | tf_op | source)
XLA Modules:
  0.0 162.2 jit_solution(15390374826816285340)
XLA Ops:
  5.9 7.3 %all-to-all-start = ((bf16[8,128,256]{2,1,0:T(8,128)(2,1)}), bf16[8,128,256]{2,1,0:T(8,128)(2,1)S(1)}, u32[]{:S(2)}, u32[]{:S(2)}) async-start(bf16[8,128,256]{2,1,0:T(8,128)(2,1)} %copy.75), calls=%async_computation | async-start | bytes 1048576 | tf_op jit(solution)/shard_map/all_to_all | solution.py:471
  14.2 13.4 %all-to-all-done = bf16[8,128,256]{2,1,0:T(8,128)(2,1)S(1)} async-done(((bf16[8,128,256]{2,1,0:T(8,128)(2,1)}), bf16[8,128,256]{2,1,0:T(8,128)(2,1)S(1)}, u32[]{:S(2)}, u32[]{:S(2)}) %all-to-all-start) | async-done | bytes 524320 | tf_op jit(solution)/shard_map/all_to_all | solution.py:471
  33.4 6.2 %shard_map.91 = (f32[256,256]{1,0:T(8,128)S(1)}, bf16[256,256]{1,0:T(8,128)(2,1)S(1)}, f32[32,1024]{1,0:T(8,128)S(1)}, bf16[32,1024]{1,0:T(8,128)(2,1)S(1)}) custom-call(bf16[3,18,16,320]{3,2,1,0:T(8,128)(2,1)S(1)} %pad.18.planes_ref, bf16[9,320,256]{2,1,0:T(8,128)(2,1)S(1)} %slice_dynamic-update-slice_fusion.10.band_ref, bf16[2048,1024]{1,0:T(8,128)(2,1)} %merge_ref.3), custom_call_target="tpu_custom_call" | custom-call | tf_op jit(solution)/shard_map/pallas_call | solution.py:196
  39.5 1.5 collective-permute-start.1
  41.1 2.8 %collective-permute-done.1 = bf16[32,1024]{1,0:T(8,128)(2,1)S(1)} collective-permute-done((bf16[32,1024]{1,0:T(8,128)(2,1)S(1)}, bf16[32,1024]{1,0:T(8,128)(2,1)S(1)}, u32[]{:S(2)}, u32[]{:S(2)}) %collective-permute-start.1) | collective-permute-done | bytes 65568 | tf_op jit(solution)/shard_map/ppermute | solution.py:410
  45.7 2.6 %collective-permute-start.4 = (bf16[32,1024]{1,0:T(8,128)(2,1)S(1)}, bf16[32,1024]{1,0:T(8,128)(2,1)S(1)}, u32[]{:S(2)}, u32[]{:S(2)}) collective-permute-start(bf16[32,1024]{1,0:T(8,128)(2,1)S(1)} %fusion.7), channel_id=1, source_target_pairs={{0,12},{2,14},{4,8},{6,10},{8,4},{10,6},{12,0},{14,2},{1,13},{3,15... | collective-permute-start | bytes 196616 | tf_op jit(solution)/shard_map/ppermute | solution.py:410
  48.5 3.3 %collective-permute-done.3 = bf16[32,1024]{1,0:T(8,128)(2,1)S(1)} collective-permute-done((bf16[32,1024]{1,0:T(8,128)(2,1)S(1)}, bf16[32,1024]{1,0:T(8,128)(2,1)S(1)}, u32[]{:S(2)}, u32[]{:S(2)}) %collective-permute-start.3) | collective-permute-done | bytes 65568 | tf_op jit(solution)/shard_map/ppermute | solution.py:410
  53.2 7.3 %shard_map.92.mine_ref = f32[64,256]{1,0:T(8,128)S(1)} custom-call(s32[1]{0:T(128)} %bitcast.n_ref, bf16[32,512]{1,0:T(8,128)(2,1)S(1)} %get-tuple-element.69.mine_ref, bf16[32,512]{1,0:T(8,128)(2,1)S(1)} %collective-permute-done.5.got_ref, bf16[27,1024,256]{2,1,0:T(8,128)(2,1)} %weight_ref.7), custom_call_target="tpu_custom_call" | custom-call | tf_op jit(solution)/shard_map/pallas_call | solution.py:311
  61.8 7.3 %shard_map.93 = (f32[64,256]{1,0:T(8,128)S(1)}, f32[64,512]{1,0:T(8,128)S(1)}, bf16[64,512]{1,0:T(8,128)(2,1)S(1)}) custom-call(s32[1]{0:T(128)} %bitcast.n_ref, f32[64,256]{1,0:T(8,128)S(1)} %shard_map.92.mine_ref, f32[64,256]{1,0:T(8,128)S(1)} %collective-permute-done.6.got_ref, f32[1,256]{1,0:T(1,128)S(1)} %constant_dynamic-slice_fusion.bias_ref, ...), custom_call_target="tpu_custom_call" | custom-call | tf_op jit(solution)/shard_map/pallas_call | solution.py:311
  69.1 1.8 %collective-permute-start.7 = (bf16[64,512]{1,0:T(8,128)(2,1)S(1)}, bf16[64,512]{1,0:T(8,128)(2,1)S(1)}, u32[]{:S(2)}, u32[]{:S(2)}) collective-permute-start(bf16[64,512]{1,0:T(8,128)(2,1)S(1)} %get-tuple-element.20), channel_id=1, source_target_pairs={{0,2},{2,0},{4,6},{6,4},{8,10},{10,8},{12,14},{14,12},{1,3},{3,1},... | collective-permute-start | bytes 196616 | tf_op jit(solution)/shard_map/ppermute | solution.py:410
  71.1 2.4 %collective-permute-done.7 = bf16[64,512]{1,0:T(8,128)(2,1)S(1)} collective-permute-done((bf16[64,512]{1,0:T(8,128)(2,1)S(1)}, bf16[64,512]{1,0:T(8,128)(2,1)S(1)}, u32[]{:S(2)}, u32[]{:S(2)}) %collective-permute-start.7) | collective-permute-done | bytes 65568 | tf_op jit(solution)/shard_map/ppermute | solution.py:410
  74.1 2.6 %collective-permute-start.10 = (bf16[64,512]{1,0:T(8,128)(2,1)}, bf16[64,512]{1,0:T(8,128)(2,1)}, u32[]{:S(2)}, u32[]{:S(2)}) collective-permute-start(bf16[64,512]{1,0:T(8,128)(2,1)} %fusion.8), channel_id=1, source_target_pairs={{0,12},{2,14},{4,8},{6,10},{8,4},{10,6},{12,0},{14,2},{1,13},{3,15... | collective-permute-start | bytes 196616 | tf_op jit(solution)/shard_map/ppermute | solution.py:410
  76.6 1.8 %collective-permute-start.9 = (bf16[64,512]{1,0:T(8,128)(2,1)}, bf16[64,512]{1,0:T(8,128)(2,1)}, u32[]{:S(2)}, u32[]{:S(2)}) collective-permute-start(bf16[64,512]{1,0:T(8,128)(2,1)} %fusion.8), channel_id=1, source_target_pairs={{0,8},{2,10},{4,12},{6,14},{8,0},{10,2},{12,4},{14,6},{1,9},{3,11}... | collective-permute-start | bytes 196616 | tf_op jit(solution)/shard_map/ppermute | solution.py:410
  78.7 2.0 %collective-permute-done.10 = bf16[64,512]{1,0:T(8,128)(2,1)} collective-permute-done((bf16[64,512]{1,0:T(8,128)(2,1)}, bf16[64,512]{1,0:T(8,128)(2,1)}, u32[]{:S(2)}, u32[]{:S(2)}) %collective-permute-start.10) | collective-permute-done | bytes 65568 | tf_op jit(solution)/shard_map/ppermute | solution.py:410
  84.5 2.2 %copy-done.2 = bf16[1024,2048]{1,0:T(8,128)(2,1)S(1)} copy-done((bf16[1024,2048]{1,0:T(8,128)(2,1)S(1)}, bf16[1024,2048]{1,0:T(8,128)(2,1)}, u32[]{:S(2)}) %copy-start.2) | copy-done | bytes 4194328
  86.7 5.0 %shard_map.94 = (bf16[256,256]{1,0:T(8,128)(2,1)S(1)}, f32[32,1024]{1,0:T(8,128)S(1)}, bf16[32,1024]{1,0:T(8,128)(2,1)S(1)}) custom-call(s32[1]{0:T(128)} %bitcast.n_ref, f32[32,1024]{1,0:T(8,128)S(1)} %get-tuple-element.32.merged_ref, f32[32,512]{1,0:T(8,128)S(1)} %slice_select_fusion.2.mine_ref, bf16[32,512]{1,0:T(8,128)(2,1)S(1)} %collective-permute-done.11.got_ref, ...), custom_call_target="tpu_custom_call" | custom-call | tf_op jit(solution)/shard_map/pallas_call | solution.py:356
  91.7 1.7 %collective-permute-start.12 = (bf16[32,1024]{1,0:T(8,128)(2,1)S(1)}, bf16[32,1024]{1,0:T(8,128)(2,1)S(1)}, u32[]{:S(2)}, u32[]{:S(2)}) collective-permute-start(bf16[32,1024]{1,0:T(8,128)(2,1)S(1)} %get-tuple-element.23), channel_id=1, source_target_pairs={{0,2},{2,0},{4,6},{6,4},{8,10},{10,8},{12,14},{14,12},{1,3},{3,1},... | collective-permute-start | bytes 196616 | tf_op jit(solution)/shard_map/ppermute | solution.py:410
  93.5 2.5 %collective-permute-done.12 = bf16[32,1024]{1,0:T(8,128)(2,1)S(1)} collective-permute-done((bf16[32,1024]{1,0:T(8,128)(2,1)S(1)}, bf16[32,1024]{1,0:T(8,128)(2,1)S(1)}, u32[]{:S(2)}, u32[]{:S(2)}) %collective-permute-start.12) | collective-permute-done | bytes 65568 | tf_op jit(solution)/shard_map/ppermute | solution.py:410
  96.1 1.9 %collective-permute-start.13 = (bf16[32,1024]{1,0:T(8,128)(2,1)S(1)}, bf16[32,1024]{1,0:T(8,128)(2,1)S(1)}, u32[]{:S(2)}, u32[]{:S(2)}) collective-permute-start(bf16[32,1024]{1,0:T(8,128)(2,1)S(1)} %fusion.9), channel_id=1, source_target_pairs={{0,4},{2,6},{4,0},{6,2},{8,12},{10,14},{12,8},{14,10},{1,5},{3,7},... | collective-permute-start | bytes 196616 | tf_op jit(solution)/shard_map/ppermute | solution.py:410
  98.3 2.2 %collective-permute-start.15 = (bf16[32,1024]{1,0:T(8,128)(2,1)S(1)}, bf16[32,1024]{1,0:T(8,128)(2,1)S(1)}, u32[]{:S(2)}, u32[]{:S(2)}) collective-permute-start(bf16[32,1024]{1,0:T(8,128)(2,1)S(1)} %fusion.9), channel_id=1, source_target_pairs={{0,12},{2,14},{4,8},{6,10},{8,4},{10,6},{12,0},{14,2},{1,13},{3,15... | collective-permute-start | bytes 196616 | tf_op jit(solution)/shard_map/ppermute | solution.py:410
  100.7 4.3 %collective-permute-done.14 = bf16[32,1024]{1,0:T(8,128)(2,1)S(1)} collective-permute-done((bf16[32,1024]{1,0:T(8,128)(2,1)S(1)}, bf16[32,1024]{1,0:T(8,128)(2,1)S(1)}, u32[]{:S(2)}, u32[]{:S(2)}) %collective-permute-start.14) | collective-permute-done | bytes 65568 | tf_op jit(solution)/shard_map/ppermute | solution.py:410
  106.3 7.8 %shard_map.95.mine_ref = f32[64,256]{1,0:T(8,128)S(1)} custom-call(s32[1]{0:T(128)} %bitcast.n_ref, bf16[32,512]{1,0:T(8,128)(2,1)S(1)} %get-tuple-element.67.mine_ref, bf16[32,512]{1,0:T(8,128)(2,1)S(1)} %collective-permute-done.16.got_ref, bf16[27,256,1024]{2,1,0:T(8,128)(2,1)} %weight_ref.6), custom_call_target="tpu_custom_call" | custom-call | tf_op jit(solution)/shard_map/pallas_call | solution.py:311
  115.5 8.0 %shard_map.96 = (f32[64,512]{1,0:T(8,128)S(1)}, bf16[64,512]{1,0:T(8,128)(2,1)S(1)}) custom-call(s32[1]{0:T(128)} %bitcast.n_ref, f32[64,256]{1,0:T(8,128)S(1)} %shard_map.95.mine_ref, f32[64,256]{1,0:T(8,128)S(1)} %collective-permute-done.17.got_ref, f32[64,256]{1,0:T(8,128)S(1)} %get-tuple-element.24.gate_ref, bf16[27,1024,256]{2,1,0:T(8,128)(2,1)} %weight_ref.7), custom_call_target="tpu_custom_call" | custom-call | tf_op jit(solution)/shard_map/pallas_call | solution.py:311
  123.4 1.5 collective-permute-start.18
  125.1 2.7 %collective-permute-done.18 = bf16[64,512]{1,0:T(8,128)(2,1)S(1)} collective-permute-done((bf16[64,512]{1,0:T(8,128)(2,1)S(1)}, bf16[64,512]{1,0:T(8,128)(2,1)S(1)}, u32[]{:S(2)}, u32[]{:S(2)}) %collective-permute-start.18) | collective-permute-done | bytes 65568 | tf_op jit(solution)/shard_map/ppermute | solution.py:410
  130.1 2.1 %collective-permute-start.21 = (bf16[64,512]{1,0:T(8,128)(2,1)S(1)}, bf16[64,512]{1,0:T(8,128)(2,1)S(1)}, u32[]{:S(2)}, u32[]{:S(2)}) collective-permute-start(bf16[64,512]{1,0:T(8,128)(2,1)S(1)} %fusion.10), channel_id=1, source_target_pairs={{0,12},{2,14},{4,8},{6,10},{8,4},{10,6},{12,0},{14,2},{1,13},{3,15... | collective-permute-start | bytes 196616 | tf_op jit(solution)/shard_map/ppermute | solution.py:410
  132.4 3.2 %collective-permute-done.20 = bf16[64,512]{1,0:T(8,128)(2,1)S(1)} collective-permute-done((bf16[64,512]{1,0:T(8,128)(2,1)S(1)}, bf16[64,512]{1,0:T(8,128)(2,1)S(1)}, u32[]{:S(2)}, u32[]{:S(2)}) %collective-permute-start.20) | collective-permute-done | bytes 65568 | tf_op jit(solution)/shard_map/ppermute | solution.py:410
  137.6 2.2 %shard_map.97 = bf16[256,256]{1,0:T(8,128)(2,1)S(1)} custom-call(s32[1]{0:T(128)} %bitcast.n_ref, f32[32,1024]{1,0:T(8,128)S(1)} %get-tuple-element.30.res_ref, f32[32,512]{1,0:T(8,128)S(1)} %slice_select_fusion.1.mine_ref, bf16[32,512]{1,0:T(8,128)(2,1)S(1)} %collective-permute-done.22.got_ref, bf16[256,256]{1,0:T(8,128)(2,1)S(1)} %get-tuple-element.27.comb_ref, ...), custom_call_target="tpu_custom_call" | custom-call | tf_op jit(solution)/shard_map/pallas_call | solution.py:389
  141.1 4.3 %all-to-all-start.1 = ((bf16[8,64,256]{2,1,0:T(8,128)(2,1)}), bf16[8,64,256]{2,1,0:T(8,128)(2,1)S(1)}, u32[]{:S(2)}, u32[]{:S(2)}) async-start(bf16[8,64,256]{2,1,0:T(8,128)(2,1)} %copy.89), calls=%async_computation.1 | async-start | bytes 524288 | tf_op jit(solution)/shard_map/all_to_all | solution.py:528
  145.6 9.0 %all-to-all-done.1 = bf16[8,64,256]{2,1,0:T(8,128)(2,1)S(1)} async-done(((bf16[8,64,256]{2,1,0:T(8,128)(2,1)}), bf16[8,64,256]{2,1,0:T(8,128)(2,1)S(1)}, u32[]{:S(2)}, u32[]{:S(2)}) %all-to-all-start.1) | async-done | bytes 262176 | tf_op jit(solution)/shard_map/all_to_all | solution.py:528
  156.8 1.4 copy.98
  158.3 2.0 %reshape.53 = bf16[3,16,16,320]{3,2,1,0:T(8,128)(2,1)S(1)} reshape(bf16[3,16,8,2,320]{4,3,2,1,0:T(2,128)(2,1)} %copy.98) | data formatting | bytes 983040 | tf_op jit(solution)/shard_map/reshape | solution.py:436
  (141 shorter events, 34.2 us)
Async XLA Ops:
  0.0 60.8 %copy-start = (f32[1000,256]{1,0:T(8,128)S(1)}, f32[1000,256]{1,0:T(8,128)}, u32[]{:S(2)}) copy-start(f32[1000,256]{1,0:T(8,128)} %param.14) | copy-start | bytes 3072004
  4.4 8.8 %copy-start.7 = (bf16[27,32,32]{2,1,0:T(8,128)(2,1)S(1)}, bf16[27,32,32]{2,1,0:T(8,128)(2,1)}, u32[]{:S(2)}) copy-start(bf16[27,32,32]{2,1,0:T(8,128)(2,1)} %param.11) | copy-start | bytes 165892
  5.9 21.8 %all-to-all-start = ((bf16[8,128,256]{2,1,0:T(8,128)(2,1)}), bf16[8,128,256]{2,1,0:T(8,128)(2,1)S(1)}, u32[]{:S(2)}, u32[]{:S(2)}) async-start(bf16[8,128,256]{2,1,0:T(8,128)(2,1)} %copy.75), calls=%async_computation | async-start | bytes 1048576 | tf_op jit(solution)/shard_map/all_to_all | solution.py:471
  28.9 1.4 collective-permute-start
  39.5 4.3 %collective-permute-start.1 = (bf16[32,1024]{1,0:T(8,128)(2,1)S(1)}, bf16[32,1024]{1,0:T(8,128)(2,1)S(1)}, u32[]{:S(2)}, u32[]{:S(2)}) collective-permute-start(bf16[32,1024]{1,0:T(8,128)(2,1)S(1)} %get-tuple-element.18), channel_id=1, source_target_pairs={{0,2},{2,0},{4,6},{6,4},{8,10},{10,8},{12,14},{14,12},{1,3},{3,1},... | collective-permute-start | bytes 196616 | tf_op jit(solution)/shard_map/ppermute | solution.py:410
  43.9 4.6 %collective-permute-start.2 = (bf16[32,1024]{1,0:T(8,128)(2,1)S(1)}, bf16[32,1024]{1,0:T(8,128)(2,1)S(1)}, u32[]{:S(2)}, u32[]{:S(2)}) collective-permute-start(bf16[32,1024]{1,0:T(8,128)(2,1)S(1)} %fusion.7), channel_id=1, source_target_pairs={{0,4},{2,6},{4,0},{6,2},{8,12},{10,14},{12,8},{14,10},{1,5},{3,7},... | collective-permute-start | bytes 196616 | tf_op jit(solution)/shard_map/ppermute | solution.py:410
  44.7 7.1 %collective-permute-start.3 = (bf16[32,1024]{1,0:T(8,128)(2,1)S(1)}, bf16[32,1024]{1,0:T(8,128)(2,1)S(1)}, u32[]{:S(2)}, u32[]{:S(2)}) collective-permute-start(bf16[32,1024]{1,0:T(8,128)(2,1)S(1)} %fusion.7), channel_id=1, source_target_pairs={{0,8},{2,10},{4,12},{6,14},{8,0},{10,2},{12,4},{14,6},{1,9},{3,11}... | collective-permute-start | bytes 196616 | tf_op jit(solution)/shard_map/ppermute | solution.py:410
  45.7 6.1 %collective-permute-start.4 = (bf16[32,1024]{1,0:T(8,128)(2,1)S(1)}, bf16[32,1024]{1,0:T(8,128)(2,1)S(1)}, u32[]{:S(2)}, u32[]{:S(2)}) collective-permute-start(bf16[32,1024]{1,0:T(8,128)(2,1)S(1)} %fusion.7), channel_id=1, source_target_pairs={{0,12},{2,14},{4,8},{6,10},{8,4},{10,6},{12,0},{14,2},{1,13},{3,15... | collective-permute-start | bytes 196616 | tf_op jit(solution)/shard_map/ppermute | solution.py:410
  51.9 1.3 collective-permute-start.5
  60.5 1.3 collective-permute-start.6
  60.8 17.7 %copy-start.9 = (bf16[1,16,8,2,256]{4,2,3,1,0:T(8,128)(2,1)S(1)}, bf16[1,16,8,2,256]{4,2,3,1,0:T(8,128)(2,1)}, u32[]{:S(2)}) copy-start(bf16[1,16,8,2,256]{4,2,3,1,0:T(8,128)(2,1)} %get-tuple-element.33) | copy-start | bytes 393220
  69.1 4.3 %collective-permute-start.7 = (bf16[64,512]{1,0:T(8,128)(2,1)S(1)}, bf16[64,512]{1,0:T(8,128)(2,1)S(1)}, u32[]{:S(2)}, u32[]{:S(2)}) collective-permute-start(bf16[64,512]{1,0:T(8,128)(2,1)S(1)} %get-tuple-element.20), channel_id=1, source_target_pairs={{0,2},{2,0},{4,6},{6,4},{8,10},{10,8},{12,14},{14,12},{1,3},{3,1},... | collective-permute-start | bytes 196616 | tf_op jit(solution)/shard_map/ppermute | solution.py:410
  71.1 7.4 %copy-start.3 = (bf16[9,32,544]{2,1,0:T(8,128)(2,1)}, bf16[9,32,544]{2,1,0:T(8,128)(2,1)S(1)}, u32[]{:S(2)}) copy-start(bf16[9,32,544]{2,1,0:T(8,128)(2,1)S(1)} %select_maximum_fusion) | copy-start | bytes 940036
  74.1 6.6 %collective-permute-start.10 = (bf16[64,512]{1,0:T(8,128)(2,1)}, bf16[64,512]{1,0:T(8,128)(2,1)}, u32[]{:S(2)}, u32[]{:S(2)}) collective-permute-start(bf16[64,512]{1,0:T(8,128)(2,1)} %fusion.8), channel_id=1, source_target_pairs={{0,12},{2,14},{4,8},{6,10},{8,4},{10,6},{12,0},{14,2},{1,13},{3,15... | collective-permute-start | bytes 196616 | tf_op jit(solution)/shard_map/ppermute | solution.py:410
  76.6 5.0 %collective-permute-start.8 = (bf16[64,512]{1,0:T(8,128)(2,1)}, bf16[64,512]{1,0:T(8,128)(2,1)}, u32[]{:S(2)}, u32[]{:S(2)}) collective-permute-start(bf16[64,512]{1,0:T(8,128)(2,1)} %fusion.8), channel_id=1, source_target_pairs={{0,4},{2,6},{4,0},{6,2},{8,12},{10,14},{12,8},{14,10},{1,5},{3,7},... | collective-permute-start | bytes 196616 | tf_op jit(solution)/shard_map/ppermute | solution.py:410
  76.6 5.6 %collective-permute-start.9 = (bf16[64,512]{1,0:T(8,128)(2,1)}, bf16[64,512]{1,0:T(8,128)(2,1)}, u32[]{:S(2)}, u32[]{:S(2)}) collective-permute-start(bf16[64,512]{1,0:T(8,128)(2,1)} %fusion.8), channel_id=1, source_target_pairs={{0,8},{2,10},{4,12},{6,14},{8,0},{10,2},{12,4},{14,6},{1,9},{3,11}... | collective-permute-start | bytes 196616 | tf_op jit(solution)/shard_map/ppermute | solution.py:410
  83.2 1.3 collective-permute-start.11
  86.7 6.7 %copy-start.4 = (bf16[9,32,544]{2,1,0:T(8,128)(2,1)S(1)}, bf16[9,32,544]{2,1,0:T(8,128)(2,1)}, u32[]{:S(2)}) copy-start(bf16[9,32,544]{2,1,0:T(8,128)(2,1)} %copy-done.3) | copy-start | bytes 940036
  91.7 4.3 %collective-permute-start.12 = (bf16[32,1024]{1,0:T(8,128)(2,1)S(1)}, bf16[32,1024]{1,0:T(8,128)(2,1)S(1)}, u32[]{:S(2)}, u32[]{:S(2)}) collective-permute-start(bf16[32,1024]{1,0:T(8,128)(2,1)S(1)} %get-tuple-element.23), channel_id=1, source_target_pairs={{0,2},{2,0},{4,6},{6,4},{8,10},{10,8},{12,14},{14,12},{1,3},{3,1},... | collective-permute-start | bytes 196616 | tf_op jit(solution)/shard_map/ppermute | solution.py:410
  96.1 4.6 %collective-permute-start.13 = (bf16[32,1024]{1,0:T(8,128)(2,1)S(1)}, bf16[32,1024]{1,0:T(8,128)(2,1)S(1)}, u32[]{:S(2)}, u32[]{:S(2)}) collective-permute-start(bf16[32,1024]{1,0:T(8,128)(2,1)S(1)} %fusion.9), channel_id=1, source_target_pairs={{0,4},{2,6},{4,0},{6,2},{8,12},{10,14},{12,8},{14,10},{1,5},{3,7},... | collective-permute-start | bytes 196616 | tf_op jit(solution)/shard_map/ppermute | solution.py:410
  98.0 6.9 %collective-permute-start.14 = (bf16[32,1024]{1,0:T(8,128)(2,1)S(1)}, bf16[32,1024]{1,0:T(8,128)(2,1)S(1)}, u32[]{:S(2)}, u32[]{:S(2)}) collective-permute-start(bf16[32,1024]{1,0:T(8,128)(2,1)S(1)} %fusion.9), channel_id=1, source_target_pairs={{0,8},{2,10},{4,12},{6,14},{8,0},{10,2},{12,4},{14,6},{1,9},{3,11}... | collective-permute-start | bytes 196616 | tf_op jit(solution)/shard_map/ppermute | solution.py:410
  98.3 6.6 %collective-permute-start.15 = (bf16[32,1024]{1,0:T(8,128)(2,1)S(1)}, bf16[32,1024]{1,0:T(8,128)(2,1)S(1)}, u32[]{:S(2)}, u32[]{:S(2)}) collective-permute-start(bf16[32,1024]{1,0:T(8,128)(2,1)S(1)} %fusion.9), channel_id=1, source_target_pairs={{0,12},{2,14},{4,8},{6,10},{8,4},{10,6},{12,0},{14,2},{1,13},{3,15... | collective-permute-start | bytes 196616 | tf_op jit(solution)/shard_map/ppermute | solution.py:410
  105.0 1.3 collective-permute-start.16
  114.1 1.3 collective-permute-start.17
  115.5 22.2 %copy-start.1 = (bf16[2048,1024]{1,0:T(8,128)(2,1)S(1)}, bf16[2048,1024]{1,0:T(8,128)(2,1)}, u32[]{:S(2)}) copy-start(bf16[2048,1024]{1,0:T(8,128)(2,1)} %merge_ref.3) | copy-start | bytes 12582916
  123.4 4.3 %collective-permute-start.18 = (bf16[64,512]{1,0:T(8,128)(2,1)S(1)}, bf16[64,512]{1,0:T(8,128)(2,1)S(1)}, u32[]{:S(2)}, u32[]{:S(2)}) collective-permute-start(bf16[64,512]{1,0:T(8,128)(2,1)S(1)} %get-tuple-element.26), channel_id=1, source_target_pairs={{0,2},{2,0},{4,6},{6,4},{8,10},{10,8},{12,14},{14,12},{1,3},{3,1},... | collective-permute-start | bytes 196616 | tf_op jit(solution)/shard_map/ppermute | solution.py:410
  127.8 4.6 %collective-permute-start.19 = (bf16[64,512]{1,0:T(8,128)(2,1)S(1)}, bf16[64,512]{1,0:T(8,128)(2,1)S(1)}, u32[]{:S(2)}, u32[]{:S(2)}) collective-permute-start(bf16[64,512]{1,0:T(8,128)(2,1)S(1)} %fusion.10), channel_id=1, source_target_pairs={{0,4},{2,6},{4,0},{6,2},{8,12},{10,14},{12,8},{14,10},{1,5},{3,7},... | collective-permute-start | bytes 196616 | tf_op jit(solution)/shard_map/ppermute | solution.py:410
  129.1 6.4 %collective-permute-start.20 = (bf16[64,512]{1,0:T(8,128)(2,1)S(1)}, bf16[64,512]{1,0:T(8,128)(2,1)S(1)}, u32[]{:S(2)}, u32[]{:S(2)}) collective-permute-start(bf16[64,512]{1,0:T(8,128)(2,1)S(1)} %fusion.10), channel_id=1, source_target_pairs={{0,8},{2,10},{4,12},{6,14},{8,0},{10,2},{12,4},{14,6},{1,9},{3,11}... | collective-permute-start | bytes 196616 | tf_op jit(solution)/shard_map/ppermute | solution.py:410
  130.1 6.2 %collective-permute-start.21 = (bf16[64,512]{1,0:T(8,128)(2,1)S(1)}, bf16[64,512]{1,0:T(8,128)(2,1)S(1)}, u32[]{:S(2)}, u32[]{:S(2)}) collective-permute-start(bf16[64,512]{1,0:T(8,128)(2,1)S(1)} %fusion.10), channel_id=1, source_target_pairs={{0,12},{2,14},{4,8},{6,10},{8,4},{10,6},{12,0},{14,2},{1,13},{3,15... | collective-permute-start | bytes 196616 | tf_op jit(solution)/shard_map/ppermute | solution.py:410
  136.3 1.3 collective-permute-start.22
  141.1 13.6 %all-to-all-start.1 = ((bf16[8,64,256]{2,1,0:T(8,128)(2,1)}), bf16[8,64,256]{2,1,0:T(8,128)(2,1)S(1)}, u32[]{:S(2)}, u32[]{:S(2)}) async-start(bf16[8,64,256]{2,1,0:T(8,128)(2,1)} %copy.89), calls=%async_computation.1 | async-start | bytes 524288 | tf_op jit(solution)/shard_map/all_to_all | solution.py:528
  155.3 1.4 collective-permute-start.23
  (4 other events, 10.1 us)

commit v2 on v0

--- a/solution.py
+++ b/solution.py
@@ -1,6 +1,10 @@
+import functools
+
 import jax
 import jax.numpy as jnp
 from jax import lax
+from jax.experimental import pallas as pl
+from jax.experimental.pallas import tpu as pltpu
 from jax.sharding import PartitionSpec as P
 
 PATCH = 8
@@ -111,6 +115,386 @@
     return jnp.einsum("xyzk,kd->xyzd", columns, weight_mat, preferred_element_type=jnp.float32)
 
 
+BF = jnp.bfloat16
+F32 = jnp.float32
+LIMIT = 16 * 1024 * 1024
+VMEM = pl.BlockSpec(memory_space=pltpu.VMEM)
+SMEM = pl.BlockSpec(memory_space=pltpu.SMEM)
+
+
+def nn_dot(lhs, rhs):
+    return jnp.dot(lhs, rhs, preferred_element_type=F32)
+
+
+def nt_dot(lhs, rhs):
+    return lax.dot_general(lhs, rhs, (((1,), (1,)), ((), ())), preferred_element_type=F32)
+
+
+def shape_of(dims, dtype):
+    return jax.ShapeDtypeStruct(dims, dtype)
+
+
+def kernel_call(kernel, places, arrays, outs, scratch=()):
+    return pl.pallas_call(
+        kernel,
+        in_specs=[SMEM] * len(places) + [VMEM] * len(arrays),
+        out_specs=[VMEM] * len(outs),
+        out_shape=outs,
+        scratch_shapes=list(scratch),
+        compiler_params=pltpu.CompilerParams(vmem_limit_bytes=LIMIT),
+    )(*places, *arrays)
+
+
+def banded(weight):
+    taps = weight.reshape(9, 3, 32, 32)
+    band = jnp.concatenate([taps[:, 2], taps[:, 1], taps[:, 0]], axis=2)
+    wide_band = jnp.pad(band, ((0, 0), (0, 0), (224, 224)))
+
+    def placed(start):
+        return wide_band[:, :, start : start + 256]
+
+    planes = jnp.concatenate([placed(224 - 32 * (d - 1)) for d in range(8)], axis=1)
+    sides = jnp.concatenate([placed(288), placed(0)], axis=1)
+    planes = planes.reshape(3, 3, 256, 256)
+    sides = sides.reshape(3, 3, 64, 256)
+    columns = []
+    for j in range(3):
+        columns.append(
+            jnp.concatenate(
+                [planes[:, j].reshape(768, 256), sides[:, j].reshape(192, 256), jnp.zeros((64, 256), BF)],
+                axis=0,
+            )
+        )
+    return jnp.concatenate(columns, axis=1)
+
+
+def pack_kernel(field_ref, cot_ref, out_ref):
+    for a in range(8):
+        out_ref[a, 0:32] = field_ref[(a + 7) % 8]
+        out_ref[a, 32:64] = field_ref[a]
+        out_ref[a, 64:96] = field_ref[(a + 1) % 8]
+        out_ref[a, 96:128] = cot_ref[a]
+
+
+def arrived_planes(w, arrived_ref):
+    none = jnp.zeros((32, 256), BF)
+    before, own, after = [
+        arrived_ref[:, 32 * s : 32 * s + 32, :].reshape(256, 256) for s in range(3)
+    ]
+    before = jnp.where(w == 0, jnp.concatenate([none, before[:224]], axis=0), before)
+    after = jnp.where(w == 7, jnp.concatenate([after[32:], none], axis=0), after)
+    return before, own, after
+
+
+def returned_planes(w, returned_ref):
+    rows = [returned_ref[7, 32:64]] + [returned_ref[a, 0:32] for a in range(8)] + [returned_ref[0, 32:64]]
+    grown = jnp.concatenate(rows, axis=0)
+    return grown[0:256], grown[32:288], grown[64:320]
+
+
+def side_kernel(w_ref, planes_ref, own_ref, send_ref, *, planes_of):
+    planes = planes_of(w_ref[0], planes_ref)
+    source = lax.broadcasted_iota(jnp.int32, (256, 256), 0)
+    target = lax.broadcasted_iota(jnp.int32, (256, 256), 1)
+    sides = None
+    for i, plane in enumerate(planes):
+        high = (source >= 224) & (target == source - 224 + 64 * i)
+        low = (source < 32) & (target == source + 64 * i + 32)
+        part = nn_dot(plane, (high | low).astype(BF))
+        sides = part if sides is None else sides + part
+    even = (source & 1) == 0
+    sides = jnp.where(even, pltpu.roll(sides, 255, 0), pltpu.roll(sides, 1, 0))
+    low_side = (target & 32) != 0
+    own = even == low_side
+    zero = jnp.zeros_like(sides)
+    own_ref[...] = jnp.where(own, sides, zero).astype(BF)
+    send_ref[...] = jnp.where(own, zero, sides).astype(BF)
+
+
+def side_call(w, planes, planes_of):
+    shape = shape_of((256, 256), BF)
+    return kernel_call(
+        functools.partial(side_kernel, planes_of=planes_of), (w,), (planes,), [shape, shape]
+    )
+
+
+def fine_sum(n, planes, own_ref, got_ref, band_ref):
+    lane = lax.broadcasted_iota(jnp.int32, (256, 256), 1)
+    keep = ((lane & 32) != 0) == (n == 0)
+    got = jnp.where(keep, got_ref[...].astype(F32), jnp.zeros((256, 256), F32))
+    sides = (own_ref[...].astype(F32) + got).astype(BF)
+    lhs = jnp.concatenate([*planes, sides], axis=1)
+    total = nn_dot(lhs, band_ref[:, 256:512])
+    y = (lax.broadcasted_iota(jnp.int32, (256, 1), 0) >> 1) & 15
+    zero = jnp.zeros_like(total)
+    below = pltpu.roll(nn_dot(lhs, band_ref[:, 0:256]), 2, 0)
+    above = pltpu.roll(nn_dot(lhs, band_ref[:, 512:768]), 254, 0)
+    return total + jnp.where(y > 0, below, zero) + jnp.where(y < 15, above, zero)
+
+
+def cell_rows(ref, b):
+    return jnp.concatenate([ref[pl.ds(2 * b + z, 16, stride=16), :] for z in range(2)], axis=0)
+
+
+def merge_kernel(
+    n_ref, w_ref, planes_ref, own_ref, got_ref, band_ref, merge_ref, pre_ref, act_ref, sum_ref, sum_b_ref, rows_ref
+):
+    n = n_ref[0]
+    planes = arrived_planes(w_ref[0], planes_ref)
+    wide_rows = fine_sum(n, planes, own_ref, got_ref, band_ref)
+    rows_ref[0] = wide_rows[:, :128]
+    rows_ref[1] = wide_rows[:, 128:]
+    total = None
+    for b in range(8):
+        pre = jnp.concatenate([cell_rows(rows_ref.at[h], b) for h in range(2)], axis=1)
+        pre_ref[b] = pre
+        act = (pre * jax.nn.sigmoid(pre)).astype(BF)
+        act_ref[b] = act
+        part = nn_dot(act, merge_ref[256 * b : 256 * b + 256])
+        total = part if total is None else total + part
+    sum_ref[...] = total
+    sum_b_ref[...] = total.astype(BF)
+
+
+def cot_kernel(planes_ref, cot_ref, rows_ref):
+    rows = planes_ref[:, 96:128, :].reshape(256, 256).astype(F32)
+    rows_ref[0] = rows[:, :128]
+    rows_ref[1] = rows[:, 128:]
+    for b in range(8):
+        cot_ref[b] = jnp.concatenate([cell_rows(rows_ref.at[h], b) for h in range(2)], axis=1).astype(BF)
+
+
+def final_kernel(n_ref, w_ref, planes_ref, own_ref, got_ref, band_ref, out_ref):
+    planes = returned_planes(w_ref[0], planes_ref)
+    out_ref[...] = fine_sum(n_ref[0], planes, own_ref, got_ref, band_ref).astype(BF)
+
+
+def put_columns(cols_ref, cells):
+    row = lax.broadcasted_iota(jnp.int32, (64, 1), 0)
+    along_y, along_x = row & 1, (row >> 1) & 7
+    zero = jnp.zeros_like(cells)
+    none = jnp.zeros((16, cells.shape[1]), BF)
+    below = jnp.where(along_y == 1, pltpu.roll(cells, 1, 0), zero)
+    above = jnp.where(along_y == 0, pltpu.roll(cells, 63, 0), zero)
+    for j, moved_y in enumerate((below, cells, above)):
+        before = jnp.where(along_x > 0, pltpu.roll(moved_y, 2, 0), zero)
+        after = jnp.where(along_x < 7, pltpu.roll(moved_y, 62, 0), zero)
+        for i, moved in enumerate((before, moved_y, after)):
+            rows = moved.astype(BF)
+            cols_ref[9 * i + 3 * j] = jnp.concatenate([none, rows[:48]], axis=0)
+            cols_ref[9 * i + 3 * j + 1] = rows
+            cols_ref[9 * i + 3 * j + 2] = jnp.concatenate([rows[16:], none], axis=0)
+
+
+def both_halves(n, mine, got, axis):
+    first = n == 0
+    return jnp.concatenate([jnp.where(first, mine, got), jnp.where(first, got, mine)], axis=axis)
+
+
+def conv_sum(cols_ref, weight_of, flipped, dot):
+    total = None
+    for t in range(27):
+        part = dot(cols_ref[26 - t if flipped else t], weight_of(t))
+        total = part if total is None else total + part
+    return total
+
+
+def feature_rows(n, ref):
+    half = ref.shape[1] // 2
+    return lambda t: ref[t, pl.ds(pl.multiple_of(n * half, half), half), :]
+
+
+def feature_columns(n, ref):
+    half = ref.shape[2] // 2
+    return lambda t: ref[t, :, pl.ds(pl.multiple_of(n * half, half), half)]
+
+
+def outer_kernel(n_ref, mine_ref, got_ref, weight_ref, sum_ref, cols_ref, *, flipped, dot, part_of):
+    n = n_ref[0]
+    put_columns(cols_ref, both_halves(n, mine_ref[...].astype(F32), got_ref[...].astype(F32), 0))
+    sum_ref[...] = conv_sum(cols_ref, part_of(n, weight_ref), flipped, dot)
+
+
+def inner_forward_kernel(
+    n_ref, mine_ref, got_ref, bias_ref, weight_ref, gate_ref, sum_ref, sum_b_ref, cols_ref
+):
+    gate = mine_ref[...] + got_ref[...] + bias_ref[...]
+    gate_ref[...] = gate
+    put_columns(cols_ref, gate * jax.nn.sigmoid(gate))
+    total = conv_sum(cols_ref, feature_columns(n_ref[0], weight_ref), False, nn_dot)
+    sum_ref[...] = total
+    sum_b_ref[...] = total.astype(BF)
+
+
+def inner_backward_kernel(
+    n_ref, mine_ref, got_ref, gate_ref, weight_ref, sum_ref, sum_b_ref, cols_ref
+):
+    put_columns(cols_ref, (mine_ref[...] + got_ref[...]) * silu_slope(gate_ref[...]))
+    total = conv_sum(cols_ref, feature_rows(n_ref[0], weight_ref), True, nt_dot)
+    sum_ref[...] = total
+    sum_b_ref[...] = total.astype(BF)
+
+
+def expand_kernel(
+    n_ref, merged_ref, mine_ref, got_ref, act_ref, cot_ref, expand_ref, grad_ref, sum_ref, sum_b_ref
+):
+    branch = both_halves(n_ref[0], mine_ref[...].astype(F32), got_ref[...].astype(F32), 1)
+    residual = (merged_ref[...] + branch).astype(BF)
+    total = None
+    for b in range(8):
+        part = expand_ref[:, 256 * b : 256 * b + 256]
+        expanded = nn_dot(residual, part).astype(BF)
+        combined = act_ref[b].astype(F32) + expanded.astype(F32)
+        grad = (cot_ref[b].astype(F32) * silu_slope(combined)).astype(BF)
+        grad_ref[b] = grad
+        more = nt_dot(grad, part)
+        total = more if total is None else total + more
+    sum_ref[...] = total
+    sum_b_ref[...] = total.astype(BF)
+
+
+def grad_kernel(
+    n_ref, w_ref, res_ref, mine_ref, got_ref, comb_ref, pre_ref, merge_ref, out_ref, rows_ref
+):
+    w = w_ref[0]
+    conv = both_halves(n_ref[0], mine_ref[...].astype(F32), got_ref[...].astype(F32), 1)
+    merged_grad = (res_ref[...] + conv).astype(BF)
+    for b in range(8):
+        cells = nt_dot(merged_grad, merge_ref[256 * b : 256 * b + 256]).astype(BF)
+        grad = cells.astype(F32) + comb_ref[b].astype(F32)
+        grad = grad * silu_slope(pre_ref[b])
+        for z in range(2):
+            for h in range(2):
+                rows_ref[h, pl.ds(2 * b + z, 16, stride=16), :] = grad[
+                    16 * z : 16 * z + 16, 128 * h : 128 * h + 128
+                ]
+    rows = jnp.concatenate([rows_ref[0], rows_ref[1]], axis=1).astype(BF)
+    none = jnp.zeros((32, 256), BF)
+    for x in range(8):
+        ahead = rows[32 * x + 32 : 32 * x + 64] if x < 7 else none
+        behind = rows[32 * x - 32 : 32 * x] if x > 0 else none
+        out_ref[x, 0:32] = rows[32 * x : 32 * x + 32]
+        out_ref[x, 32:64] = jnp.where(w == 0, ahead, behind)
+
+
+def swap_narrow(value):
+    return lax.ppermute(value, "narrow", [(0, 1), (1, 0)])
+
+
+def summed_wide(part, part_b):
+    def partner(value, mask):
+        return lax.ppermute(value, "wide", [(i, i ^ mask) for i in range(8)])
+
+    pair = part + partner(part_b, 1).astype(F32)
+    pair_b = pair.astype(BF)
+    others = [partner(pair_b, mask) for mask in (2, 4, 6)]
+    return pair + others[0].astype(F32) + others[1].astype(F32) + others[2].astype(F32)
+
+
+def to_feature_halves(n, cells):
+    half = cells.shape[1] // 2
+    low, high = cells[:, :half], cells[:, half:]
+    return jnp.where(n == 0, low, high), swap_narrow(jnp.where(n == 0, high, low))
+
+
+def to_cell_halves(n, rows):
+    half = rows.shape[0] // 2
+    low, high = rows[:half], rows[half:]
+    return jnp.where(n == 0, low, high), swap_narrow(jnp.where(n == 0, high, low).astype(BF))
+
+
+def across_wide(value):
+    return lax.all_to_all(value, "wide", split_axis=0, concat_axis=0, tiled=True)
+
+
+def eight_shards(
+    volume,
+    cotangent,
+    fine_weight,
+    merge_weight,
+    hidden_weight,
+    step_table,
+    output_weight,
+    expand_weight,
+    timestep,
+):
+    features = merge_weight.shape[1]
+    hidden = hidden_weight.shape[2]
+    half = features // 2
+    w = lax.axis_index("wide").astype(jnp.int32).reshape(1)
+    n_index = lax.axis_index("narrow")
+    n = n_index.astype(jnp.int32).reshape(1)
+
+    def row_form(fine_field):
+        return fine_field.transpose(1, 2, 3, 0).reshape(8, 32, 256)
+
+    (outgoing,) = kernel_call(
+        pack_kernel, (), (row_form(volume), row_form(cotangent)), [shape_of((8, 128, 256), BF)]
+    )
+    arrived = across_wide(outgoing)
+    sides, sent = side_call(w, arrived, arrived_planes)
+    fine_rows = pltpu.VMEM((2, 256, 128), F32)
+    sum_shapes = [shape_of((32, features), F32), shape_of((32, features), BF)]
+    pre_act, act, merged_part, merged_part_b = kernel_call(
+        merge_kernel,
+        (n, w),
+        (arrived, sides, swap_narrow(sent), banded(fine_weight), merge_weight),
+        [shape_of((8, 32, 256), F32), shape_of((8, 32, 256), BF)] + sum_shapes,
+        [fine_rows],
+    )
+    (cot,) = kernel_call(cot_kernel, (), (arrived,), [shape_of((8, 32, 256), BF)], [fine_rows])
+    merged = summed_wide(merged_part, merged_part_b)
+    mine, got = to_feature_halves(n_index, merged.astype(BF))
+
+    gate_shape = shape_of((64, hidden), F32)
+    half_shapes = [shape_of((64, half), F32), shape_of((64, half), BF)]
+    outer_columns = [pltpu.VMEM((27, 64, half), BF)]
+    inner_columns = [pltpu.VMEM((27, 64, hidden), BF)]
+
+    (gate_part,) = kernel_call(
+        functools.partial(outer_kernel, flipped=False, dot=nn_dot, part_of=feature_rows),
+        (n,), (mine, got, hidden_weight), [gate_shape], outer_columns,
+    )
+    bias = lax.dynamic_slice_in_dim(step_table, timestep[0], 1, axis=0)
+    gate_pre, branch_part, branch_part_b = kernel_call(
+        inner_forward_kernel,
+        (n,), (gate_part, swap_narrow(gate_part), bias, output_weight),
+        [gate_shape] + half_shapes, inner_columns,
+    )
+    mine, got = to_cell_halves(n_index, summed_wide(branch_part, branch_part_b))
+    grad_comb, res_part, res_part_b = kernel_call(
+        expand_kernel,
+        (n,), (merged, mine, got, act, cot, expand_weight),
+        [shape_of((8, 32, 256), BF)] + sum_shapes,
+    )
+    grad_res = summed_wide(res_part, res_part_b)
+    mine, got = to_feature_halves(n_index, grad_res.astype(BF))
+    (hidden_part,) = kernel_call(
+        functools.partial(outer_kernel, flipped=True, dot=nt_dot, part_of=feature_columns),
+        (n,), (mine, got, output_weight), [gate_shape], outer_columns,
+    )
+    conv_part, conv_part_b = kernel_call(
+        inner_backward_kernel,
+        (n,), (hidden_part, swap_narrow(hidden_part), gate_pre, hidden_weight),
+        half_shapes, inner_columns,
+    )
+    mine, got = to_cell_halves(n_index, summed_wide(conv_part, conv_part_b))
+    (leaving,) = kernel_call(
+        grad_kernel,
+        (n, w), (grad_res, mine, got, grad_comb, pre_act, merge_weight),
+        [shape_of((8, 64, 256), BF)], [fine_rows],
+    )
+    returned = across_wide(leaving)
+    sides, sent = side_call(w, returned, returned_planes)
+    back = fine_weight[::-1].transpose(0, 2, 1)
+    (result,) = kernel_call(
+        final_kernel,
+        (n, w), (returned, sides, swap_narrow(sent), banded(back)),
+        [shape_of((256, 256), BF)],
+    )
+    return result.reshape(8, 16, 16, 32).transpose(3, 0, 1, 2)
+
+
 def shards(
     volume,
     cotangent,
@@ -186,4 +570,7 @@
         P("groups"),
     )
     out_specs = P(None, ("groups", "wide"), None, "narrow")
-    return jax.shard_map(shards, mesh=mesh, in_specs=in_specs, out_specs=out_specs, check_vma=False)
+    sizes = dict(mesh.shape)
+    fits = sizes["wide"] == PATCH and sizes["narrow"] == 2
+    body = eight_shards if fits else shards
+    return jax.shard_map(body, mesh=mesh, in_specs=in_specs, out_specs=out_specs, check_vma=False)

time: 475 us -> 147 us (0.31)
  waiting for transfers between devices: 290 us -> 41.4 us
  matrix products: 54.5 us -> 0 us
  blocking collectives: 44.8 us -> 13.6 us
  Pallas kernels: 0 us -> 15.5 us
  between operations: 14.8 us -> 1.08 us
  other arithmetic: 4.77 us -> 10.5 us
    psum x4 -> x0, waiting for transfers between devices: 273 us -> none  [total_rows(): return lax.psum(partial_value, 'wide')]
    dot_general x8 -> x0, matrix products: 49.8 us -> none  [the longest x2 18.8 us: wide_input_conv(): jnp.einsum('xyzd,dk->xyzk', grown, weight_mat, preferred_element_type=jnp...]
    all_to_all x4 -> x1, blocking collectives: 44.8 us -> 13.6 us  [across_wide(): lax.all_to_all(value, 'wide', split_axis=0, concat_axis=0, tiled=True)]
    ppermute x16 -> x24, waiting for transfers between devices: 17.2 us -> 35.8 us  [the longest x16 28.2 us: partner(): return lax.ppermute(value, 'wide', [(i, i ^ mask) for i in range(8)])]
    pallas_call x0 -> x12, Pallas kernels: none -> 15.5 us  [kernel_call(): pl.pallas_call(kernel, in_specs=[SMEM] * len(places) + [VMEM] * len(array...]
    concatenate x2 -> x5, other arithmetic: 0.07 us -> 8.66 us  [the longest x1 7.44 us: banded(): return jnp.concatenate(columns, axis=1)]
    all_to_all x0 -> x1, starting transfers between devices: none -> 7.28 us  [across_wide(): lax.all_to_all(value, 'wide', split_axis=0, concat_axis=0, tiled=True)]
    convert_element_type x7 -> x0, local copies, waits for them, and re-layouts: 6.6 us -> none  [the longest x2 2.77 us: shards(): expanded_field.astype(jnp.float32)]
  transfers between devices with their start and end apart: 20 -> 25, of which waited for: 13 -> 22; matrix products, arithmetic and copies ran while one was open for 4% -> 10% of each run, Pallas kernels for 0% -> 0%
where the time goes in v2:
time: 147 us; the launch traced here: 146 us
  waiting for transfers between devices  41.4 us (28%)
  local copies, waits for them, and re-layouts  32.5 us (22%)
  starting transfers between devices  31.4 us (21%)
  Pallas kernels  15.5 us (11%)
  blocking collectives  13.6 us (9%)
  other arithmetic  10.5 us (7%)
    ppermute x16, waiting for transfers between devices, partner(): return lax.ppermute(value, 'wide', [(i, i ^ mask) for i in range(8)])  28.2 us
    unnamed x53, local copies, waits for them, and re-layouts  23.3 us
    ppermute x16, starting transfers between devices, partner(): return lax.ppermute(value, 'wide', [(i, i ^ mask) for i in range(8)])  23.3 us
    pallas_call x12, Pallas kernels, kernel_call(): pl.pallas_call(kernel, in_specs=[SMEM] * len(places) + [VMEM] * len(array...  15.5 us
    all_to_all x1, blocking collectives, across_wide(): lax.all_to_all(value, 'wide', split_axis=0, concat_axis=0, tiled=True)  13.6 us
    ppermute x8, waiting for transfers between devices, swap_narrow(): return lax.ppermute(value, 'narrow', [(0, 1), (1, 0)])  7.61 us
    concatenate x1, other arithmetic, banded(): return jnp.concatenate(columns, axis=1)  7.44 us
    all_to_all x1, starting transfers between devices, across_wide(): lax.all_to_all(value, 'wide', split_axis=0, concat_axis=0, tiled=True)  7.28 us
  transfers between devices with their start and end apart: 25, of which 22 were waited for; matrix products, arithmetic and copies ran while one was open for 10% of the time, Pallas kernels for 0%

profile of v2, /device:TPU:0, one launch (start us, length us, event | category | flops | bytes accessed | tf_op | source)
XLA Modules:
  0.0 146.0 jit_solution(11868193615063760926)
XLA Ops:
  0.0 1.5 %reshape.35.field_ref = bf16[8,32,256]{2,1,0:T(8,128)(2,1)S(1)} reshape(bf16[8,16,16,32]{3,2,1,0:T(8,128)(2,1)} %bitcast.65) | data formatting | bytes 262144 | tf_op jit(solution)/shard_map/reshape | solution.py:429
  1.5 1.4 reshape.36.cot_ref
  3.8 7.3 %all-to-all-start = ((bf16[8,128,256]{2,1,0:T(8,128)(2,1)}), bf16[8,128,256]{2,1,0:T(8,128)(2,1)S(1)}, u32[]{:S(2)}, u32[]{:S(2)}) async-start(bf16[8,128,256]{2,1,0:T(8,128)(2,1)} %shard_map.91), calls=%async_computation | async-start | bytes 1048576 | tf_op jit(solution)/shard_map/all_to_all | solution.py:407
  20.0 5.6 %all-to-all-done.planes_ref = bf16[8,128,256]{2,1,0:T(8,128)(2,1)S(1)} async-done(((bf16[8,128,256]{2,1,0:T(8,128)(2,1)}), bf16[8,128,256]{2,1,0:T(8,128)(2,1)S(1)}, u32[]{:S(2)}, u32[]{:S(2)}) %all-to-all-start) | async-done | bytes 524320 | tf_op jit(solution)/shard_map/all_to_all | solution.py:407
  26.0 7.4 %fusion.3 = (bf16[1024,768]{1,0:T(8,128)(2,1)S(1)}, bf16[1024,768]{1,0:T(8,128)(2,1)}) fusion(bf16[64,256]{1,0:T(8,128)(2,1)S(1)} %broadcast.7, bf16[192,256]{1,0:T(8,128)(2,1)} %bitcast.71, bf16[768,256]{1,0:T(8,128)(2,1)} %bitcast.57, bf16[192,256]{1,0:T(8,128)(2,1)} %bitcast.72, bf16[768,256]{1,0:T(8,128)(2,1)} %bitcast.58, bf16[192,256]{1,0:T(8,128)(2,1)} %bitcast.70, ...), kind=kLoop, calls=%fused_computation.9 | loop fusion | flops 25952256 | bytes 6127616 | tf_op jit(solution)/shard_map/concatenate | solution.py:168
  34.1 2.2 %copy-done.5 = bf16[2048,1024]{1,0:T(8,128)(2,1)S(1)} copy-done((bf16[2048,1024]{1,0:T(8,128)(2,1)S(1)}, bf16[2048,1024]{1,0:T(8,128)(2,1)}, u32[]{:S(2)}) %copy-start.5) | copy-done | bytes 4194328
  38.6 2.1 %shard_map.93 = (f32[8,32,256]{2,1,0:T(8,128)S(1)}, bf16[8,32,256]{2,1,0:T(8,128)(2,1)S(1)}, f32[32,1024]{1,0:T(8,128)S(1)}, bf16[32,1024]{1,0:T(8,128)(2,1)S(1)}) custom-call(s32[1]{0:T(128)} %bitcast.n_ref, s32[1]{0:T(128)} %bitcast.1.w_ref, bf16[8,128,256]{2,1,0:T(8,128)(2,1)S(1)} %all-to-all-done.planes_ref, ...), custom_call_target="tpu_custom_call" | custom-call | tf_op jit(solution)/shard_map/pallas_call | solution.py:138
  41.4 1.5 %collective-permute-start.1 = (bf16[32,1024]{1,0:T(8,128)(2,1)S(1)}, bf16[32,1024]{1,0:T(8,128)(2,1)S(1)}, u32[]{:S(2)}, u32[]{:S(2)}) collective-permute-start(bf16[32,1024]{1,0:T(8,128)(2,1)S(1)} %get-tuple-element.24), channel_id=1, source_target_pairs={{0,2},{2,0},{4,6},{6,4},{8,10},{10,8},{12,14},{14,12},{1,3},{3,1},... | collective-permute-start | bytes 196616 | tf_op jit(solution)/shard_map/ppermute | solution.py:386
  42.9 3.0 %collective-permute-done.1 = bf16[32,1024]{1,0:T(8,128)(2,1)S(1)} collective-permute-done((bf16[32,1024]{1,0:T(8,128)(2,1)S(1)}, bf16[32,1024]{1,0:T(8,128)(2,1)S(1)}, u32[]{:S(2)}, u32[]{:S(2)}) %collective-permute-start.1) | collective-permute-done | bytes 65568 | tf_op jit(solution)/shard_map/ppermute | solution.py:386
  48.3 2.6 %collective-permute-start.4 = (bf16[32,1024]{1,0:T(8,128)(2,1)}, bf16[32,1024]{1,0:T(8,128)(2,1)}, u32[]{:S(2)}, u32[]{:S(2)}) collective-permute-start(bf16[32,1024]{1,0:T(8,128)(2,1)} %fusion.6), channel_id=1, source_target_pairs={{0,12},{2,14},{4,8},{6,10},{8,4},{10,6},{12,0},{14,2},{1,13},{3,15... | collective-permute-start | bytes 196616 | tf_op jit(solution)/shard_map/ppermute | solution.py:386
  51.7 3.7 %collective-permute-done.3 = bf16[32,1024]{1,0:T(8,128)(2,1)} collective-permute-done((bf16[32,1024]{1,0:T(8,128)(2,1)}, bf16[32,1024]{1,0:T(8,128)(2,1)}, u32[]{:S(2)}, u32[]{:S(2)}) %collective-permute-start.3) | collective-permute-done | bytes 65568 | tf_op jit(solution)/shard_map/ppermute | solution.py:386
  57.7 5.0 %copy-done.3 = bf16[27,1024,256]{2,1,0:T(8,128)(2,1)S(1)} copy-done((bf16[27,1024,256]{2,1,0:T(8,128)(2,1)S(1)}, bf16[27,1024,256]{2,1,0:T(8,128)(2,1)}, u32[]{:S(2)}) %copy-start.3) | copy-done | bytes 14155800
  65.4 5.0 %copy-done.1 = bf16[27,256,1024]{2,1,0:T(8,128)(2,1)S(1)} copy-done((bf16[27,256,1024]{2,1,0:T(8,128)(2,1)S(1)}, bf16[27,256,1024]{2,1,0:T(8,128)(2,1)}, u32[]{:S(2)}) %copy-start.1) | copy-done | bytes 14155800
  72.8 3.3 %collective-permute-done.7 = bf16[64,512]{1,0:T(8,128)(2,1)S(1)} collective-permute-done((bf16[64,512]{1,0:T(8,128)(2,1)S(1)}, bf16[64,512]{1,0:T(8,128)(2,1)S(1)}, u32[]{:S(2)}, u32[]{:S(2)}) %collective-permute-start.7) | collective-permute-done | bytes 65568 | tf_op jit(solution)/shard_map/ppermute | solution.py:386
  76.1 1.9 %collective-permute-start.10 = (bf16[64,512]{1,0:T(8,128)(2,1)S(1)}, bf16[64,512]{1,0:T(8,128)(2,1)S(1)}, u32[]{:S(2)}, u32[]{:S(2)}) collective-permute-start(bf16[64,512]{1,0:T(8,128)(2,1)S(1)} %fusion.7), channel_id=1, source_target_pairs={{0,12},{2,14},{4,8},{6,10},{8,4},{10,6},{12,0},{14,2},{1,13},{3,15... | collective-permute-start | bytes 196616 | tf_op jit(solution)/shard_map/ppermute | solution.py:386
  78.1 2.5 %collective-permute-start.9 = (bf16[64,512]{1,0:T(8,128)(2,1)S(1)}, bf16[64,512]{1,0:T(8,128)(2,1)S(1)}, u32[]{:S(2)}, u32[]{:S(2)}) collective-permute-start(bf16[64,512]{1,0:T(8,128)(2,1)S(1)} %fusion.7), channel_id=1, source_target_pairs={{0,8},{2,10},{4,12},{6,14},{8,0},{10,2},{12,4},{14,6},{1,9},{3,11}... | collective-permute-start | bytes 196616 | tf_op jit(solution)/shard_map/ppermute | solution.py:386
  80.7 2.3 %collective-permute-done.10 = bf16[64,512]{1,0:T(8,128)(2,1)S(1)} collective-permute-done((bf16[64,512]{1,0:T(8,128)(2,1)S(1)}, bf16[64,512]{1,0:T(8,128)(2,1)S(1)}, u32[]{:S(2)}, u32[]{:S(2)}) %collective-permute-start.10) | collective-permute-done | bytes 65568 | tf_op jit(solution)/shard_map/ppermute | solution.py:386
  85.1 2.7 %shard_map.97 = (bf16[8,32,256]{2,1,0:T(8,128)(2,1)S(1)}, f32[32,1024]{1,0:T(8,128)S(1)}, bf16[32,1024]{1,0:T(8,128)(2,1)S(1)}) custom-call(s32[1]{0:T(128)} %bitcast.n_ref, f32[32,1024]{1,0:T(8,128)S(1)} %get-tuple-element.40.merged_ref, f32[32,512]{1,0:T(8,128)S(1)} %slice_select_fusion.1.mine_ref, bf16[32,512]{1,0:T(8,128)(2,1)S(1)} %collective-permute-done.11.got_ref, ...), custom_call_target="tpu_custom_call" | custom-call | tf_op jit(solution)/shard_map/pallas_call | solution.py:138
  89.1 3.1 %collective-permute-done.12 = bf16[32,1024]{1,0:T(8,128)(2,1)S(1)} collective-permute-done((bf16[32,1024]{1,0:T(8,128)(2,1)S(1)}, bf16[32,1024]{1,0:T(8,128)(2,1)S(1)}, u32[]{:S(2)}, u32[]{:S(2)}) %collective-permute-start.12) | collective-permute-done | bytes 65568 | tf_op jit(solution)/shard_map/ppermute | solution.py:386
  92.2 1.5 %collective-permute-start.13 = (bf16[32,1024]{1,0:T(8,128)(2,1)S(1)}, bf16[32,1024]{1,0:T(8,128)(2,1)S(1)}, u32[]{:S(2)}, u32[]{:S(2)}) collective-permute-start(bf16[32,1024]{1,0:T(8,128)(2,1)S(1)} %fusion.8), channel_id=1, source_target_pairs={{0,4},{2,6},{4,0},{6,2},{8,12},{10,14},{12,8},{14,10},{1,5},{3,7},... | collective-permute-start | bytes 196616 | tf_op jit(solution)/shard_map/ppermute | solution.py:386
  93.7 1.4 collective-permute-start.14
  95.1 1.5 %collective-permute-start.15 = (bf16[32,1024]{1,0:T(8,128)(2,1)S(1)}, bf16[32,1024]{1,0:T(8,128)(2,1)S(1)}, u32[]{:S(2)}, u32[]{:S(2)}) collective-permute-start(bf16[32,1024]{1,0:T(8,128)(2,1)S(1)} %fusion.8), channel_id=1, source_target_pairs={{0,12},{2,14},{4,8},{6,10},{8,4},{10,6},{12,0},{14,2},{1,13},{3,15... | collective-permute-start | bytes 196616 | tf_op jit(solution)/shard_map/ppermute | solution.py:386
  96.7 3.6 %collective-permute-done.14 = bf16[32,1024]{1,0:T(8,128)(2,1)S(1)} collective-permute-done((bf16[32,1024]{1,0:T(8,128)(2,1)S(1)}, bf16[32,1024]{1,0:T(8,128)(2,1)S(1)}, u32[]{:S(2)}, u32[]{:S(2)}) %collective-permute-start.14) | collective-permute-done | bytes 65568 | tf_op jit(solution)/shard_map/ppermute | solution.py:386
  102.6 2.3 %shard_map.98.mine_ref = f32[64,256]{1,0:T(8,128)S(1)} custom-call(s32[1]{0:T(128)} %bitcast.n_ref, bf16[32,512]{1,0:T(8,128)(2,1)S(1)} %get-tuple-element.66.mine_ref, bf16[32,512]{1,0:T(8,128)(2,1)S(1)} %collective-permute-done.16.got_ref, bf16[27,256,1024]{2,1,0:T(8,128)(2,1)S(1)} %copy-done.2), custom_call_target="tpu_custom_call" | custom-call | tf_op jit(solution)/shard_map/pallas_call | solution.py:138
  106.2 5.0 %copy-done.4 = bf16[27,1024,256]{2,1,0:T(8,128)(2,1)S(1)} copy-done((bf16[27,1024,256]{2,1,0:T(8,128)(2,1)S(1)}, bf16[27,1024,256]{2,1,0:T(8,128)(2,1)}, u32[]{:S(2)}) %copy-start.4) | copy-done | bytes 14155800
  111.3 2.2 %shard_map.99 = (f32[64,512]{1,0:T(8,128)S(1)}, bf16[64,512]{1,0:T(8,128)(2,1)S(1)}) custom-call(s32[1]{0:T(128)} %bitcast.n_ref, f32[64,256]{1,0:T(8,128)S(1)} %shard_map.98.mine_ref, f32[64,256]{1,0:T(8,128)S(1)} %collective-permute-done.17.got_ref, f32[64,256]{1,0:T(8,128)S(1)} %get-tuple-element.30.gate_ref, bf16[27,1024,256]{2,1,0:T(8,128)(2,1)S(1)} %copy-done.4), custom_call_target="tpu_custom_call" | custom-call | tf_op jit(solution)/shard_map/pallas_call | solution.py:138
  113.5 1.8 %collective-permute-start.18 = (bf16[64,512]{1,0:T(8,128)(2,1)S(1)}, bf16[64,512]{1,0:T(8,128)(2,1)S(1)}, u32[]{:S(2)}, u32[]{:S(2)}) collective-permute-start(bf16[64,512]{1,0:T(8,128)(2,1)S(1)} %get-tuple-element.32), channel_id=1, source_target_pairs={{0,2},{2,0},{4,6},{6,4},{8,10},{10,8},{12,14},{14,12},{1,3},{3,1},... | collective-permute-start | bytes 196616 | tf_op jit(solution)/shard_map/ppermute | solution.py:386
  115.3 2.5 %collective-permute-done.18 = bf16[64,512]{1,0:T(8,128)(2,1)S(1)} collective-permute-done((bf16[64,512]{1,0:T(8,128)(2,1)S(1)}, bf16[64,512]{1,0:T(8,128)(2,1)S(1)}, u32[]{:S(2)}, u32[]{:S(2)}) %collective-permute-start.18) | collective-permute-done | bytes 65568 | tf_op jit(solution)/shard_map/ppermute | solution.py:386
  120.1 2.2 %collective-permute-start.21 = (bf16[64,512]{1,0:T(8,128)(2,1)S(1)}, bf16[64,512]{1,0:T(8,128)(2,1)S(1)}, u32[]{:S(2)}, u32[]{:S(2)}) collective-permute-start(bf16[64,512]{1,0:T(8,128)(2,1)S(1)} %fusion.9), channel_id=1, source_target_pairs={{0,12},{2,14},{4,8},{6,10},{8,4},{10,6},{12,0},{14,2},{1,13},{3,15... | collective-permute-start | bytes 196616 | tf_op jit(solution)/shard_map/ppermute | solution.py:386
  122.4 2.9 %collective-permute-done.20 = bf16[64,512]{1,0:T(8,128)(2,1)S(1)} collective-permute-done((bf16[64,512]{1,0:T(8,128)(2,1)S(1)}, bf16[64,512]{1,0:T(8,128)(2,1)S(1)}, u32[]{:S(2)}, u32[]{:S(2)}) %collective-permute-start.20) | collective-permute-done | bytes 65568 | tf_op jit(solution)/shard_map/ppermute | solution.py:386
  127.6 1.4 shard_map.100
  129.1 13.6 %all_to_all.10.planes_ref = bf16[8,64,256]{2,1,0:T(8,128)(2,1)S(1)} all-to-all(bf16[8,64,256]{2,1,0:T(8,128)(2,1)S(1)} %shard_map.100), channel_id=1, replica_groups=mesh['groups'=2,'wide'=8,'narrow'=2] {'wide'}, dimensions={0} | all-to-all | bytes 524288 | tf_op jit(solution)/shard_map/all_to_all | solution.py:407
  (117 shorter events, 38.6 us)
Async XLA Ops:
  0.0 64.3 %copy-start = (f32[1000,256]{1,0:T(8,128)S(1)}, f32[1000,256]{1,0:T(8,128)}, u32[]{:S(2)}) copy-start(f32[1000,256]{1,0:T(8,128)} %param.14) | copy-start | bytes 3072004
  0.0 11.1 %copy-start.15 = (bf16[27,32,32]{2,1,0:T(8,128)(2,1)S(1)}, bf16[27,32,32]{2,1,0:T(8,128)(2,1)}, u32[]{:S(2)}) copy-start(bf16[27,32,32]{2,1,0:T(8,128)(2,1)} %param.11) | copy-start | bytes 165892
  3.8 21.8 %all-to-all-start = ((bf16[8,128,256]{2,1,0:T(8,128)(2,1)}), bf16[8,128,256]{2,1,0:T(8,128)(2,1)S(1)}, u32[]{:S(2)}, u32[]{:S(2)}) async-start(bf16[8,128,256]{2,1,0:T(8,128)(2,1)} %shard_map.91), calls=%async_computation | async-start | bytes 1048576 | tf_op jit(solution)/shard_map/all_to_all | solution.py:407
  25.9 7.5 %collective-permute-start = (bf16[256,256]{1,0:T(8,128)(2,1)S(1)}, bf16[256,256]{1,0:T(8,128)(2,1)S(1)}, u32[]{:S(2)}, u32[]{:S(2)}) collective-permute-start(bf16[256,256]{1,0:T(8,128)(2,1)S(1)} %get-tuple-element.22), channel_id=1, source_target_pairs={{0,1},{1,0},{2,3},{3,2},{4,5},{5,4},{6,7},{7,6},{8,9},{9,8},{10,11... | collective-permute-start | bytes 393224 | tf_op jit(solution)/shard_map/ppermute | solution.py:381
  41.4 4.5 %collective-permute-start.1 = (bf16[32,1024]{1,0:T(8,128)(2,1)S(1)}, bf16[32,1024]{1,0:T(8,128)(2,1)S(1)}, u32[]{:S(2)}, u32[]{:S(2)}) collective-permute-start(bf16[32,1024]{1,0:T(8,128)(2,1)S(1)} %get-tuple-element.24), channel_id=1, source_target_pairs={{0,2},{2,0},{4,6},{6,4},{8,10},{10,8},{12,14},{14,12},{1,3},{3,1},... | collective-permute-start | bytes 196616 | tf_op jit(solution)/shard_map/ppermute | solution.py:386
  45.9 9.5 %copy-start.17 = (bf16[32,1024]{1,0:T(8,128)(2,1)}, bf16[32,1024]{1,0:T(8,128)(2,1)S(1)}, u32[]{:S(2)}) copy-start(bf16[32,1024]{1,0:T(8,128)(2,1)S(1)} %collective-permute-done.1) | copy-start | bytes 196612
  46.5 5.2 %collective-permute-start.2 = (bf16[32,1024]{1,0:T(8,128)(2,1)}, bf16[32,1024]{1,0:T(8,128)(2,1)S(1)}, u32[]{:S(2)}, u32[]{:S(2)}) collective-permute-start(bf16[32,1024]{1,0:T(8,128)(2,1)} %fusion.6), channel_id=1, source_target_pairs={{0,4},{2,6},{4,0},{6,2},{8,12},{10,14},{12,8},{14,10},{1,5},{3,7},... | collective-permute-start | bytes 196616 | tf_op jit(solution)/shard_map/ppermute | solution.py:386
  47.3 8.1 %collective-permute-start.3 = (bf16[32,1024]{1,0:T(8,128)(2,1)}, bf16[32,1024]{1,0:T(8,128)(2,1)}, u32[]{:S(2)}, u32[]{:S(2)}) collective-permute-start(bf16[32,1024]{1,0:T(8,128)(2,1)} %fusion.6), channel_id=1, source_target_pairs={{0,8},{2,10},{4,12},{6,14},{8,0},{10,2},{12,4},{14,6},{1,9},{3,11}... | collective-permute-start | bytes 196616 | tf_op jit(solution)/shard_map/ppermute | solution.py:386
  48.3 7.2 %collective-permute-start.4 = (bf16[32,1024]{1,0:T(8,128)(2,1)}, bf16[32,1024]{1,0:T(8,128)(2,1)}, u32[]{:S(2)}, u32[]{:S(2)}) collective-permute-start(bf16[32,1024]{1,0:T(8,128)(2,1)} %fusion.6), channel_id=1, source_target_pairs={{0,12},{2,14},{4,8},{6,10},{8,4},{10,6},{12,0},{14,2},{1,13},{3,15... | collective-permute-start | bytes 196616 | tf_op jit(solution)/shard_map/ppermute | solution.py:386
  56.4 1.3 collective-permute-start.5
  62.7 22.4 %copy-start.8 = (bf16[1024,2048]{1,0:T(8,128)(2,1)S(1)}, bf16[1024,2048]{1,0:T(8,128)(2,1)}, u32[]{:S(2)}) copy-start(bf16[1024,2048]{1,0:T(8,128)(2,1)} %expand_ref.1) | copy-start | bytes 12582916
  64.1 1.3 collective-permute-start.6
  70.4 32.2 %copy-start.2 = (bf16[27,256,1024]{2,1,0:T(8,128)(2,1)S(1)}, bf16[27,256,1024]{2,1,0:T(8,128)(2,1)}, u32[]{:S(2)}) copy-start(bf16[27,256,1024]{2,1,0:T(8,128)(2,1)} %weight_ref.6) | copy-start | bytes 42467332
  71.8 4.3 %collective-permute-start.7 = (bf16[64,512]{1,0:T(8,128)(2,1)S(1)}, bf16[64,512]{1,0:T(8,128)(2,1)S(1)}, u32[]{:S(2)}, u32[]{:S(2)}) collective-permute-start(bf16[64,512]{1,0:T(8,128)(2,1)S(1)} %get-tuple-element.26), channel_id=1, source_target_pairs={{0,2},{2,0},{4,6},{6,4},{8,10},{10,8},{12,14},{14,12},{1,3},{3,1},... | collective-permute-start | bytes 196616 | tf_op jit(solution)/shard_map/ppermute | solution.py:386
  76.1 6.9 %collective-permute-start.10 = (bf16[64,512]{1,0:T(8,128)(2,1)S(1)}, bf16[64,512]{1,0:T(8,128)(2,1)S(1)}, u32[]{:S(2)}, u32[]{:S(2)}) collective-permute-start(bf16[64,512]{1,0:T(8,128)(2,1)S(1)} %fusion.7), channel_id=1, source_target_pairs={{0,12},{2,14},{4,8},{6,10},{8,4},{10,6},{12,0},{14,2},{1,13},{3,15... | collective-permute-start | bytes 196616 | tf_op jit(solution)/shard_map/ppermute | solution.py:386
  78.1 5.0 %collective-permute-start.8 = (bf16[64,512]{1,0:T(8,128)(2,1)S(1)}, bf16[64,512]{1,0:T(8,128)(2,1)S(1)}, u32[]{:S(2)}, u32[]{:S(2)}) collective-permute-start(bf16[64,512]{1,0:T(8,128)(2,1)S(1)} %fusion.7), channel_id=1, source_target_pairs={{0,4},{2,6},{4,0},{6,2},{8,12},{10,14},{12,8},{14,10},{1,5},{3,7},... | collective-permute-start | bytes 196616 | tf_op jit(solution)/shard_map/ppermute | solution.py:386
  78.1 5.7 %collective-permute-start.9 = (bf16[64,512]{1,0:T(8,128)(2,1)S(1)}, bf16[64,512]{1,0:T(8,128)(2,1)S(1)}, u32[]{:S(2)}, u32[]{:S(2)}) collective-permute-start(bf16[64,512]{1,0:T(8,128)(2,1)S(1)} %fusion.7), channel_id=1, source_target_pairs={{0,8},{2,10},{4,12},{6,14},{8,0},{10,2},{12,4},{14,6},{1,9},{3,11}... | collective-permute-start | bytes 196616 | tf_op jit(solution)/shard_map/ppermute | solution.py:386
  83.9 1.3 collective-permute-start.11
  87.9 4.3 %collective-permute-start.12 = (bf16[32,1024]{1,0:T(8,128)(2,1)S(1)}, bf16[32,1024]{1,0:T(8,128)(2,1)S(1)}, u32[]{:S(2)}, u32[]{:S(2)}) collective-permute-start(bf16[32,1024]{1,0:T(8,128)(2,1)S(1)} %get-tuple-element.29), channel_id=1, source_target_pairs={{0,2},{2,0},{4,6},{6,4},{8,10},{10,8},{12,14},{14,12},{1,3},{3,1},... | collective-permute-start | bytes 196616 | tf_op jit(solution)/shard_map/ppermute | solution.py:386
  92.2 4.5 %collective-permute-start.13 = (bf16[32,1024]{1,0:T(8,128)(2,1)S(1)}, bf16[32,1024]{1,0:T(8,128)(2,1)S(1)}, u32[]{:S(2)}, u32[]{:S(2)}) collective-permute-start(bf16[32,1024]{1,0:T(8,128)(2,1)S(1)} %fusion.8), channel_id=1, source_target_pairs={{0,4},{2,6},{4,0},{6,2},{8,12},{10,14},{12,8},{14,10},{1,5},{3,7},... | collective-permute-start | bytes 196616 | tf_op jit(solution)/shard_map/ppermute | solution.py:386
  93.7 6.6 %collective-permute-start.14 = (bf16[32,1024]{1,0:T(8,128)(2,1)S(1)}, bf16[32,1024]{1,0:T(8,128)(2,1)S(1)}, u32[]{:S(2)}, u32[]{:S(2)}) collective-permute-start(bf16[32,1024]{1,0:T(8,128)(2,1)S(1)} %fusion.8), channel_id=1, source_target_pairs={{0,8},{2,10},{4,12},{6,14},{8,0},{10,2},{12,4},{14,6},{1,9},{3,11}... | collective-permute-start | bytes 196616 | tf_op jit(solution)/shard_map/ppermute | solution.py:386
  95.1 6.2 %collective-permute-start.15 = (bf16[32,1024]{1,0:T(8,128)(2,1)S(1)}, bf16[32,1024]{1,0:T(8,128)(2,1)S(1)}, u32[]{:S(2)}, u32[]{:S(2)}) collective-permute-start(bf16[32,1024]{1,0:T(8,128)(2,1)S(1)} %fusion.8), channel_id=1, source_target_pairs={{0,12},{2,14},{4,8},{6,10},{8,4},{10,6},{12,0},{14,2},{1,13},{3,15... | collective-permute-start | bytes 196616 | tf_op jit(solution)/shard_map/ppermute | solution.py:386
  101.4 1.3 collective-permute-start.16
  104.9 1.3 collective-permute-start.17
  111.3 16.4 %copy-start.6 = (bf16[2048,1024]{1,0:T(8,128)(2,1)S(1)}, bf16[2048,1024]{1,0:T(8,128)(2,1)}, u32[]{:S(2)}) copy-start(bf16[2048,1024]{1,0:T(8,128)(2,1)} %merge_ref.3) | copy-start | bytes 12582916
  111.3 16.4 %copy-start.10 = (f32[8,32,256]{2,1,0:T(8,128)S(1)}, f32[8,32,256]{2,1,0:T(8,128)}, u32[]{:S(2)}) copy-start(f32[8,32,256]{2,1,0:T(8,128)} %copy-done.9) | copy-start | bytes 786436
  113.5 4.3 %collective-permute-start.18 = (bf16[64,512]{1,0:T(8,128)(2,1)S(1)}, bf16[64,512]{1,0:T(8,128)(2,1)S(1)}, u32[]{:S(2)}, u32[]{:S(2)}) collective-permute-start(bf16[64,512]{1,0:T(8,128)(2,1)S(1)} %get-tuple-element.32), channel_id=1, source_target_pairs={{0,2},{2,0},{4,6},{6,4},{8,10},{10,8},{12,14},{14,12},{1,3},{3,1},... | collective-permute-start | bytes 196616 | tf_op jit(solution)/shard_map/ppermute | solution.py:386
  117.8 4.6 %collective-permute-start.19 = (bf16[64,512]{1,0:T(8,128)(2,1)S(1)}, bf16[64,512]{1,0:T(8,128)(2,1)S(1)}, u32[]{:S(2)}, u32[]{:S(2)}) collective-permute-start(bf16[64,512]{1,0:T(8,128)(2,1)S(1)} %fusion.9), channel_id=1, source_target_pairs={{0,4},{2,6},{4,0},{6,2},{8,12},{10,14},{12,8},{14,10},{1,5},{3,7},... | collective-permute-start | bytes 196616 | tf_op jit(solution)/shard_map/ppermute | solution.py:386
  118.9 6.4 %collective-permute-start.20 = (bf16[64,512]{1,0:T(8,128)(2,1)S(1)}, bf16[64,512]{1,0:T(8,128)(2,1)S(1)}, u32[]{:S(2)}, u32[]{:S(2)}) collective-permute-start(bf16[64,512]{1,0:T(8,128)(2,1)S(1)} %fusion.9), channel_id=1, source_target_pairs={{0,8},{2,10},{4,12},{6,14},{8,0},{10,2},{12,4},{14,6},{1,9},{3,11}... | collective-permute-start | bytes 196616 | tf_op jit(solution)/shard_map/ppermute | solution.py:386
  120.1 6.2 %collective-permute-start.21 = (bf16[64,512]{1,0:T(8,128)(2,1)S(1)}, bf16[64,512]{1,0:T(8,128)(2,1)S(1)}, u32[]{:S(2)}, u32[]{:S(2)}) collective-permute-start(bf16[64,512]{1,0:T(8,128)(2,1)S(1)} %fusion.9), channel_id=1, source_target_pairs={{0,12},{2,14},{4,8},{6,10},{8,4},{10,6},{12,0},{14,2},{1,13},{3,15... | collective-permute-start | bytes 196616 | tf_op jit(solution)/shard_map/ppermute | solution.py:386
  126.4 1.3 collective-permute-start.22
  143.0 1.4 collective-permute-start.23
  (12 other events, 30.0 us)

commit v3 on v2

--- a/solution.py
+++ b/solution.py
@@ -117,7 +117,8 @@
 
 BF = jnp.bfloat16
 F32 = jnp.float32
-LIMIT = 16 * 1024 * 1024
+LIMIT = 10 * 1024 * 1024
+BESIDE = 32 * 1024 * 1024
 VMEM = pl.BlockSpec(memory_space=pltpu.VMEM)
 SMEM = pl.BlockSpec(memory_space=pltpu.SMEM)
 
@@ -134,38 +135,51 @@
     return jax.ShapeDtypeStruct(dims, dtype)
 
 
-def kernel_call(kernel, places, arrays, outs, scratch=()):
+def kernel_call(kernel, places, arrays, outs, scratch=(), cost=None, rest=()):
     return pl.pallas_call(
         kernel,
-        in_specs=[SMEM] * len(places) + [VMEM] * len(arrays),
+        in_specs=[SMEM] * len(places) + [VMEM] * len(arrays) + [pl.BlockSpec(memory_space=pl.ANY)] * len(rest),
         out_specs=[VMEM] * len(outs),
         out_shape=outs,
         scratch_shapes=list(scratch),
+        cost_estimate=cost and pl.CostEstimate(flops=0, bytes_accessed=cost, transcendentals=0),
         compiler_params=pltpu.CompilerParams(vmem_limit_bytes=LIMIT),
-    )(*places, *arrays)
-
-
-def banded(weight):
-    taps = weight.reshape(9, 3, 32, 32)
-    band = jnp.concatenate([taps[:, 2], taps[:, 1], taps[:, 0]], axis=2)
-    wide_band = jnp.pad(band, ((0, 0), (0, 0), (224, 224)))
-
-    def placed(start):
-        return wide_band[:, :, start : start + 256]
-
-    planes = jnp.concatenate([placed(224 - 32 * (d - 1)) for d in range(8)], axis=1)
-    sides = jnp.concatenate([placed(288), placed(0)], axis=1)
-    planes = planes.reshape(3, 3, 256, 256)
-    sides = sides.reshape(3, 3, 64, 256)
-    columns = []
-    for j in range(3):
-        columns.append(
-            jnp.concatenate(
-                [planes[:, j].reshape(768, 256), sides[:, j].reshape(192, 256), jnp.zeros((64, 256), BF)],
-                axis=0,
-            )
-        )
-    return jnp.concatenate(columns, axis=1)
+    )(*places, *arrays, *rest)
+
+
+def band_kernel(weight_ref, out_ref, *, back):
+    row = lax.broadcasted_iota(jnp.int32, (32, 256), 0)
+    lane = lax.broadcasted_iota(jnp.int32, (32, 256), 1)
+    places = [(lane == row + 32 * (2 - k)).astype(BF) for k in range(3)]
+    same = (
+        lax.broadcasted_iota(jnp.int32, (32, 32), 0) == lax.broadcasted_iota(jnp.int32, (32, 32), 1)
+    ).astype(BF)
+    for i in range(3):
+        for j in range(3):
+            taps = None
+            for k in range(3):
+                t = 9 * i + 3 * j + k
+                tap = nt_dot(same, weight_ref[26 - t]).astype(BF) if back else weight_ref[t]
+                part = nn_dot(tap, places[k])
+                taps = part if taps is None else taps + part
+            columns = slice(256 * j, 256 * j + 256)
+
+            def placed(start):
+                moved = pltpu.roll(taps, start % 256, 1)
+                return jnp.where((lane >= start) & (lane < start + 96), moved, 0.0).astype(BF)
+
+            for d in range(8):
+                out_ref[256 * i + 32 * d : 256 * i + 32 * d + 32, columns] = placed(32 * (d - 1))
+            out_ref[768 + 64 * i : 800 + 64 * i, columns] = placed(-64)
+            out_ref[800 + 64 * i : 832 + 64 * i, columns] = placed(224)
+    out_ref[960:1024, :] = jnp.zeros((64, 768), BF)
+
+
+def banded(weight, back):
+    (out,) = kernel_call(
+        functools.partial(band_kernel, back=back), (), (weight,), [shape_of((1024, 768), BF)], cost=BESIDE
+    )
+    return out
 
 
 def pack_kernel(field_ref, cot_ref, out_ref):
@@ -192,7 +206,8 @@
     return grown[0:256], grown[32:288], grown[64:320]
 
 
-def side_kernel(w_ref, planes_ref, own_ref, send_ref, *, planes_of):
+def side_kernel(w_ref, planes_ref, band_ref, own_ref, send_ref, *, planes_of):
+    del band_ref
     planes = planes_of(w_ref[0], planes_ref)
     source = lax.broadcasted_iota(jnp.int32, (256, 256), 0)
     target = lax.broadcasted_iota(jnp.int32, (256, 256), 1)
@@ -211,10 +226,10 @@
     send_ref[...] = jnp.where(own, zero, sides).astype(BF)
 
 
-def side_call(w, planes, planes_of):
+def side_call(w, planes, band, planes_of):
     shape = shape_of((256, 256), BF)
     return kernel_call(
-        functools.partial(side_kernel, planes_of=planes_of), (w,), (planes,), [shape, shape]
+        functools.partial(side_kernel, planes_of=planes_of), (w,), (planes, band), [shape, shape]
     )
 
 
@@ -316,9 +331,17 @@
 
 
 def inner_forward_kernel(
-    n_ref, mine_ref, got_ref, bias_ref, weight_ref, gate_ref, sum_ref, sum_b_ref, cols_ref
+    n_ref, step_ref, mine_ref, got_ref, weight_ref, table_ref, gate_ref, sum_ref, sum_b_ref, cols_ref, bias_ref, sem
 ):
-    gate = mine_ref[...] + got_ref[...] + bias_ref[...]
+    step = step_ref[0]
+    group = pl.ds(pl.multiple_of(step // 8 * 8, 8), 8)
+    fetch = pltpu.make_async_copy(table_ref.at[group], bias_ref, sem)
+    fetch.start()
+    fetch.wait()
+    rows = bias_ref[...]
+    chosen = lax.broadcasted_iota(jnp.int32, rows.shape, 0) == step % 8
+    bias = jnp.sum(jnp.where(chosen, rows, jnp.zeros_like(rows)), axis=0, keepdims=True)
+    gate = mine_ref[...] + got_ref[...] + bias
     gate_ref[...] = gate
     put_columns(cols_ref, gate * jax.nn.sigmoid(gate))
     total = conv_sum(cols_ref, feature_columns(n_ref[0], weight_ref), False, nn_dot)
@@ -381,12 +404,20 @@
     return lax.ppermute(value, "narrow", [(0, 1), (1, 0)])
 
 
+def pair_kernel(part_ref, got_ref, pair_ref, pair_b_ref):
+    pair = part_ref[...] + got_ref[...].astype(F32)
+    pair_ref[...] = pair
+    pair_b_ref[...] = pair.astype(BF)
+
+
 def summed_wide(part, part_b):
     def partner(value, mask):
         return lax.ppermute(value, "wide", [(i, i ^ mask) for i in range(8)])
 
-    pair = part + partner(part_b, 1).astype(F32)
-    pair_b = pair.astype(BF)
+    shape = part.shape
+    pair, pair_b = kernel_call(
+        pair_kernel, (), (part, partner(part_b, 1)), [shape_of(shape, F32), shape_of(shape, BF)], cost=BESIDE
+    )
     others = [partner(pair_b, mask) for mask in (2, 4, 6)]
     return pair + others[0].astype(F32) + others[1].astype(F32) + others[2].astype(F32)
 
@@ -432,13 +463,14 @@
         pack_kernel, (), (row_form(volume), row_form(cotangent)), [shape_of((8, 128, 256), BF)]
     )
     arrived = across_wide(outgoing)
-    sides, sent = side_call(w, arrived, arrived_planes)
+    band = banded(fine_weight, False)
+    sides, sent = side_call(w, arrived, band, arrived_planes)
     fine_rows = pltpu.VMEM((2, 256, 128), F32)
     sum_shapes = [shape_of((32, features), F32), shape_of((32, features), BF)]
     pre_act, act, merged_part, merged_part_b = kernel_call(
         merge_kernel,
         (n, w),
-        (arrived, sides, swap_narrow(sent), banded(fine_weight), merge_weight),
+        (arrived, sides, swap_narrow(sent), band, merge_weight),
         [shape_of((8, 32, 256), F32), shape_of((8, 32, 256), BF)] + sum_shapes,
         [fine_rows],
     )
@@ -455,11 +487,10 @@
         functools.partial(outer_kernel, flipped=False, dot=nn_dot, part_of=feature_rows),
         (n,), (mine, got, hidden_weight), [gate_shape], outer_columns,
     )
-    bias = lax.dynamic_slice_in_dim(step_table, timestep[0], 1, axis=0)
     gate_pre, branch_part, branch_part_b = kernel_call(
         inner_forward_kernel,
-        (n,), (gate_part, swap_narrow(gate_part), bias, output_weight),
-        [gate_shape] + half_shapes, inner_columns,
+        (n, timestep), (gate_part, swap_narrow(gate_part), output_weight), [gate_shape] + half_shapes,
+        inner_columns + [pltpu.VMEM((8, hidden), F32), pltpu.SemaphoreType.DMA], rest=(step_table,),
     )
     mine, got = to_cell_halves(n_index, summed_wide(branch_part, branch_part_b))
     grad_comb, res_part, res_part_b = kernel_call(
@@ -485,11 +516,11 @@
         [shape_of((8, 64, 256), BF)], [fine_rows],
     )
     returned = across_wide(leaving)
-    sides, sent = side_call(w, returned, returned_planes)
-    back = fine_weight[::-1].transpose(0, 2, 1)
+    band = banded(fine_weight, True)
+    sides, sent = side_call(w, returned, band, returned_planes)
     (result,) = kernel_call(
         final_kernel,
-        (n, w), (returned, sides, swap_narrow(sent), banded(back)),
+        (n, w), (returned, sides, swap_narrow(sent), band),
         [shape_of((256, 256), BF)],
     )
     return result.reshape(8, 16, 16, 32).transpose(3, 0, 1, 2)

time: 147 us -> 130 us (0.88)
  local copies, waits for them, and re-layouts: 32.5 us -> 17.4 us
  waiting for transfers between devices: 41.4 us -> 55.6 us
  blocking collectives: 13.6 us -> 0 us
  other arithmetic: 10.5 us -> 0.19 us
  starting transfers between devices: 31.4 us -> 36.7 us
  Pallas kernels: 15.5 us -> 18.1 us
    all_to_all x1 -> x2, waiting for transfers between devices: 5.63 us -> 20.9 us  [across_wide(): lax.all_to_all(value, 'wide', split_axis=0, concat_axis=0, tiled=True)]
    all_to_all x1 -> x0, blocking collectives: 13.6 us -> none  [across_wide(): lax.all_to_all(value, 'wide', split_axis=0, concat_axis=0, tiled=True)]
    unnamed x53 -> x32, local copies, waits for them, and re-layouts: 23.3 us -> 13.4 us
    concatenate x5 -> x0, other arithmetic: 8.66 us -> none  [the longest x1 7.44 us: banded(): return jnp.concatenate(columns, axis=1)]
    all_to_all x1 -> x2, starting transfers between devices: 7.28 us -> 11.6 us  [across_wide(): lax.all_to_all(value, 'wide', split_axis=0, concat_axis=0, tiled=True)]
    slice x4 -> x0, local copies, waits for them, and re-layouts: 3.55 us -> none  [the longest x2 2.1 us: banded(): planes[:, j].reshape(768, 256)]
    pallas_call x12 -> x18, Pallas kernels: 15.5 us -> 18.1 us  [kernel_call(): pl.pallas_call(kernel, in_specs=[SMEM] * len(places) + [VMEM] * len(array...]
    ppermute x16, waiting for transfers between devices: 28.2 us -> 26.1 us  [partner(): return lax.ppermute(value, 'wide', [(i, i ^ mask) for i in range(8)])]
  transfers between devices with their start and end apart: 25 -> 26, of which waited for: 22 -> 21; matrix products, arithmetic and copies ran while one was open for 10% -> 0% of each run, Pallas kernels for 0% -> 1%
where the time goes in v3:
time: 130 us
  waiting for transfers between devices  55.6 us (43%)
  starting transfers between devices  36.7 us (28%)
  Pallas kernels  18.1 us (14%)
  local copies, waits for them, and re-layouts  17.4 us (13%)
  between operations  1.58 us (1%)
    ppermute x16, waiting for transfers between devices, partner(): return lax.ppermute(value, 'wide', [(i, i ^ mask) for i in range(8)])  26.1 us
    ppermute x16, starting transfers between devices, partner(): return lax.ppermute(value, 'wide', [(i, i ^ mask) for i in range(8)])  24.3 us
    all_to_all x2, waiting for transfers between devices, across_wide(): lax.all_to_all(value, 'wide', split_axis=0, concat_axis=0, tiled=True)  20.9 us
    pallas_call x18, Pallas kernels, kernel_call(): pl.pallas_call(kernel, in_specs=[SMEM] * len(places) + [VMEM] * len(array...  18.1 us
    unnamed x32, local copies, waits for them, and re-layouts  13.4 us
    all_to_all x2, starting transfers between devices, across_wide(): lax.all_to_all(value, 'wide', split_axis=0, concat_axis=0, tiled=True)  11.6 us
    ppermute x8, waiting for transfers between devices, swap_narrow(): return lax.ppermute(value, 'narrow', [(0, 1), (1, 0)])  8.51 us
    reshape x2, local copies, waits for them, and re-layouts, row_form(): return fine_field.transpose(1, 2, 3, 0).reshape(8, 32, 256)  2.88 us
  transfers between devices with their start and end apart: 26, of which 21 were waited for; matrix products, arithmetic and copies ran while one was open for 0% of the time, Pallas kernels for 1%

profile of v3, /device:TPU:0, one launch (start us, length us, event | category | flops | bytes accessed | tf_op | source)
XLA Modules:
  0.0 129.6 jit_solution(4359630261181458832)
XLA Ops:
  1.4 1.4 %reshape.18.cot_ref = bf16[8,32,256]{2,1,0:T(8,128)(2,1)S(1)} reshape(bf16[8,16,16,32]{3,2,1,0:T(8,128)(2,1)} %bitcast.12) | data formatting | bytes 262144 | tf_op jit(solution)/shard_map/reshape | solution.py:460
  3.7 7.3 %all-to-all-start = ((bf16[8,128,256]{2,1,0:T(8,128)(2,1)}), bf16[8,128,256]{2,1,0:T(8,128)(2,1)S(1)}, u32[]{:S(2)}, u32[]{:S(2)}) async-start(bf16[8,128,256]{2,1,0:T(8,128)(2,1)} %shard_map.91), calls=%async_computation | async-start | bytes 1048576 | tf_op jit(solution)/shard_map/all_to_all | solution.py:438
  12.3 13.2 %all-to-all-done.planes_ref = bf16[8,128,256]{2,1,0:T(8,128)(2,1)S(1)} async-done(((bf16[8,128,256]{2,1,0:T(8,128)(2,1)}), bf16[8,128,256]{2,1,0:T(8,128)(2,1)S(1)}, u32[]{:S(2)}, u32[]{:S(2)}) %all-to-all-start) | async-done | bytes 524320 | tf_op jit(solution)/shard_map/all_to_all | solution.py:438
  28.4 2.2 %copy-done.2 = bf16[2048,1024]{1,0:T(8,128)(2,1)S(1)} copy-done((bf16[2048,1024]{1,0:T(8,128)(2,1)S(1)}, bf16[2048,1024]{1,0:T(8,128)(2,1)}, u32[]{:S(2)}) %copy-start.2) | copy-done | bytes 4194328
  32.4 2.1 %shard_map.94 = (f32[8,32,256]{2,1,0:T(8,128)S(1)}, bf16[8,32,256]{2,1,0:T(8,128)(2,1)S(1)}, f32[32,1024]{1,0:T(8,128)S(1)}, bf16[32,1024]{1,0:T(8,128)(2,1)S(1)}) custom-call(s32[1]{0:T(128)} %bitcast.n_ref, s32[1]{0:T(128)} %bitcast.1.w_ref, bf16[8,128,256]{2,1,0:T(8,128)(2,1)S(1)} %all-to-all-done.planes_ref, bf16[256,256]{1,0:T(8,128)(2,1)S(1)} %copy-done.9, ...), custom_call_target="tpu_custom_call" | custom-call | tf_op jit(solution)/shard_map/pallas_call | solution.py:139
  34.5 1.5 %collective-permute-start.1 = (bf16[32,1024]{1,0:T(8,128)(2,1)S(1)}, bf16[32,1024]{1,0:T(8,128)(2,1)S(1)}, u32[]{:S(2)}, u32[]{:S(2)}) collective-permute-start(bf16[32,1024]{1,0:T(8,128)(2,1)S(1)} %get-tuple-element.32), channel_id=1, source_target_pairs={{0,2},{2,0},{4,6},{6,4},{8,10},{10,8},{12,14},{14,12},{1,3},{3,1},... | collective-permute-start | bytes 196616 | tf_op jit(solution)/shard_map/ppermute | solution.py:415
  36.0 2.8 %collective-permute-done.1.got_ref = bf16[32,1024]{1,0:T(8,128)(2,1)S(1)} collective-permute-done((bf16[32,1024]{1,0:T(8,128)(2,1)S(1)}, bf16[32,1024]{1,0:T(8,128)(2,1)S(1)}, u32[]{:S(2)}, u32[]{:S(2)}) %collective-permute-start.1) | collective-permute-done | bytes 65568 | tf_op jit(solution)/shard_map/ppermute | solution.py:415
  40.7 2.6 %collective-permute-start.4 = (bf16[32,1024]{1,0:T(8,128)(2,1)S(1)}, bf16[32,1024]{1,0:T(8,128)(2,1)S(1)}, u32[]{:S(2)}, u32[]{:S(2)}) collective-permute-start(bf16[32,1024]{1,0:T(8,128)(2,1)S(1)} %get-tuple-element.34), channel_id=1, source_target_pairs={{0,12},{2,14},{4,8},{6,10},{8,4},{10,6},{12,0},{14,2},{1,13},{3,15... | collective-permute-start | bytes 196616 | tf_op jit(solution)/shard_map/ppermute | solution.py:415
  43.3 3.5 %collective-permute-done.3 = bf16[32,1024]{1,0:T(8,128)(2,1)S(1)} collective-permute-done((bf16[32,1024]{1,0:T(8,128)(2,1)S(1)}, bf16[32,1024]{1,0:T(8,128)(2,1)S(1)}, u32[]{:S(2)}, u32[]{:S(2)}) %collective-permute-start.3) | collective-permute-done | bytes 65568 | tf_op jit(solution)/shard_map/ppermute | solution.py:415
  48.2 5.0 %copy-done.1 = bf16[27,1024,256]{2,1,0:T(8,128)(2,1)S(1)} copy-done((bf16[27,1024,256]{2,1,0:T(8,128)(2,1)S(1)}, bf16[27,1024,256]{2,1,0:T(8,128)(2,1)}, u32[]{:S(2)}) %copy-start.1) | copy-done | bytes 14155800
  56.1 2.1 %copy-done = bf16[27,256,1024]{2,1,0:T(8,128)(2,1)S(1)} copy-done((bf16[27,256,1024]{2,1,0:T(8,128)(2,1)S(1)}, bf16[27,256,1024]{2,1,0:T(8,128)(2,1)}, u32[]{:S(2)}) %copy-start) | copy-done | bytes 14155800
  59.6 1.8 %collective-permute-start.7 = (bf16[64,512]{1,0:T(8,128)(2,1)S(1)}, bf16[64,512]{1,0:T(8,128)(2,1)S(1)}, u32[]{:S(2)}, u32[]{:S(2)}) collective-permute-start(bf16[64,512]{1,0:T(8,128)(2,1)S(1)} %get-tuple-element.36), channel_id=1, source_target_pairs={{0,2},{2,0},{4,6},{6,4},{8,10},{10,8},{12,14},{14,12},{1,3},{3,1},... | collective-permute-start | bytes 196616 | tf_op jit(solution)/shard_map/ppermute | solution.py:415
  61.4 2.5 %collective-permute-done.7.got_ref = bf16[64,512]{1,0:T(8,128)(2,1)S(1)} collective-permute-done((bf16[64,512]{1,0:T(8,128)(2,1)S(1)}, bf16[64,512]{1,0:T(8,128)(2,1)S(1)}, u32[]{:S(2)}, u32[]{:S(2)}) %collective-permute-start.7) | collective-permute-done | bytes 65568 | tf_op jit(solution)/shard_map/ppermute | solution.py:415
  64.0 2.6 %collective-permute-start.10 = (bf16[64,512]{1,0:T(8,128)(2,1)S(1)}, bf16[64,512]{1,0:T(8,128)(2,1)S(1)}, u32[]{:S(2)}, u32[]{:S(2)}) collective-permute-start(bf16[64,512]{1,0:T(8,128)(2,1)S(1)} %get-tuple-element.38), channel_id=1, source_target_pairs={{0,12},{2,14},{4,8},{6,10},{8,4},{10,6},{12,0},{14,2},{1,13},{3,15... | collective-permute-start | bytes 196616 | tf_op jit(solution)/shard_map/ppermute | solution.py:415
  66.6 1.8 %collective-permute-start.9 = (bf16[64,512]{1,0:T(8,128)(2,1)S(1)}, bf16[64,512]{1,0:T(8,128)(2,1)S(1)}, u32[]{:S(2)}, u32[]{:S(2)}) collective-permute-start(bf16[64,512]{1,0:T(8,128)(2,1)S(1)} %get-tuple-element.38), channel_id=1, source_target_pairs={{0,8},{2,10},{4,12},{6,14},{8,0},{10,2},{12,4},{14,6},{1,9},{3,11}... | collective-permute-start | bytes 196616 | tf_op jit(solution)/shard_map/ppermute | solution.py:415
  68.5 1.8 %collective-permute-done.10 = bf16[64,512]{1,0:T(8,128)(2,1)S(1)} collective-permute-done((bf16[64,512]{1,0:T(8,128)(2,1)S(1)}, bf16[64,512]{1,0:T(8,128)(2,1)S(1)}, u32[]{:S(2)}, u32[]{:S(2)}) %collective-permute-start.10) | collective-permute-done | bytes 65568 | tf_op jit(solution)/shard_map/ppermute | solution.py:415
  73.2 2.7 %shard_map.100 = (bf16[8,32,256]{2,1,0:T(8,128)(2,1)S(1)}, f32[32,1024]{1,0:T(8,128)S(1)}, bf16[32,1024]{1,0:T(8,128)(2,1)S(1)}) custom-call(s32[1]{0:T(128)} %bitcast.n_ref, f32[32,1024]{1,0:T(8,128)S(1)} %get-tuple-element.56.merged_ref, f32[32,512]{1,0:T(8,128)S(1)} %slice_select_fusion.1.mine_ref, bf16[32,512]{1,0:T(8,128)(2,1)S(1)} %collective-permute-done.11.got_ref, ...), custom_call_target="tpu_custom_call" | custom-call | tf_op jit(solution)/shard_map/pallas_call | solution.py:139
  76.0 1.6 %collective-permute-start.12 = (bf16[32,1024]{1,0:T(8,128)(2,1)S(1)}, bf16[32,1024]{1,0:T(8,128)(2,1)S(1)}, u32[]{:S(2)}, u32[]{:S(2)}) collective-permute-start(bf16[32,1024]{1,0:T(8,128)(2,1)S(1)} %get-tuple-element.41), channel_id=1, source_target_pairs={{0,2},{2,0},{4,6},{6,4},{8,10},{10,8},{12,14},{14,12},{1,3},{3,1},... | collective-permute-start | bytes 196616 | tf_op jit(solution)/shard_map/ppermute | solution.py:415
  77.6 2.7 %collective-permute-done.12.got_ref = bf16[32,1024]{1,0:T(8,128)(2,1)S(1)} collective-permute-done((bf16[32,1024]{1,0:T(8,128)(2,1)S(1)}, bf16[32,1024]{1,0:T(8,128)(2,1)S(1)}, u32[]{:S(2)}, u32[]{:S(2)}) %collective-permute-start.12) | collective-permute-done | bytes 65568 | tf_op jit(solution)/shard_map/ppermute | solution.py:415
  80.3 1.9 %collective-permute-start.13 = (bf16[32,1024]{1,0:T(8,128)(2,1)S(1)}, bf16[32,1024]{1,0:T(8,128)(2,1)S(1)}, u32[]{:S(2)}, u32[]{:S(2)}) collective-permute-start(bf16[32,1024]{1,0:T(8,128)(2,1)S(1)} %get-tuple-element.43), channel_id=1, source_target_pairs={{0,4},{2,6},{4,0},{6,2},{8,12},{10,14},{12,8},{14,10},{1,5},{3,7},... | collective-permute-start | bytes 196616 | tf_op jit(solution)/shard_map/ppermute | solution.py:415
  82.5 2.2 %collective-permute-start.15 = (bf16[32,1024]{1,0:T(8,128)(2,1)S(1)}, bf16[32,1024]{1,0:T(8,128)(2,1)S(1)}, u32[]{:S(2)}, u32[]{:S(2)}) collective-permute-start(bf16[32,1024]{1,0:T(8,128)(2,1)S(1)} %get-tuple-element.43), channel_id=1, source_target_pairs={{0,12},{2,14},{4,8},{6,10},{8,4},{10,6},{12,0},{14,2},{1,13},{3,15... | collective-permute-start | bytes 196616 | tf_op jit(solution)/shard_map/ppermute | solution.py:415
  84.8 4.4 %collective-permute-done.14 = bf16[32,1024]{1,0:T(8,128)(2,1)S(1)} collective-permute-done((bf16[32,1024]{1,0:T(8,128)(2,1)S(1)}, bf16[32,1024]{1,0:T(8,128)(2,1)S(1)}, u32[]{:S(2)}, u32[]{:S(2)}) %collective-permute-start.14) | collective-permute-done | bytes 65568 | tf_op jit(solution)/shard_map/ppermute | solution.py:415
  90.5 2.3 %shard_map.102.mine_ref = f32[64,256]{1,0:T(8,128)S(1)} custom-call(s32[1]{0:T(128)} %bitcast.n_ref, bf16[32,512]{1,0:T(8,128)(2,1)S(1)} %get-tuple-element.58.mine_ref, bf16[32,512]{1,0:T(8,128)(2,1)S(1)} %collective-permute-done.16.got_ref, bf16[27,256,1024]{2,1,0:T(8,128)(2,1)S(1)} %copy-done), custom_call_target="tpu_custom_call" | custom-call | tf_op jit(solution)/shard_map/pallas_call | solution.py:139
  94.1 2.2 %shard_map.103 = (f32[64,512]{1,0:T(8,128)S(1)}, bf16[64,512]{1,0:T(8,128)(2,1)S(1)}) custom-call(s32[1]{0:T(128)} %bitcast.n_ref, f32[64,256]{1,0:T(8,128)S(1)} %shard_map.102.mine_ref, f32[64,256]{1,0:T(8,128)S(1)} %collective-permute-done.17.got_ref, f32[64,256]{1,0:T(8,128)S(1)} %get-tuple-element.44.gate_ref, bf16[27,1024,256]{2,1,0:T(8,128)(2,1)S(1)} %bitcast.10), custom_call_target="tpu_custom_call" | custom-call | tf_op jit(solution)/shard_map/pallas_call | solution.py:139
  96.4 1.5 %collective-permute-start.18 = (bf16[64,512]{1,0:T(8,128)(2,1)S(1)}, bf16[64,512]{1,0:T(8,128)(2,1)S(1)}, u32[]{:S(2)}, u32[]{:S(2)}) collective-permute-start(bf16[64,512]{1,0:T(8,128)(2,1)S(1)} %get-tuple-element.46), channel_id=1, source_target_pairs={{0,2},{2,0},{4,6},{6,4},{8,10},{10,8},{12,14},{14,12},{1,3},{3,1},... | collective-permute-start | bytes 196616 | tf_op jit(solution)/shard_map/ppermute | solution.py:415
  97.9 2.8 %collective-permute-done.18.got_ref = bf16[64,512]{1,0:T(8,128)(2,1)S(1)} collective-permute-done((bf16[64,512]{1,0:T(8,128)(2,1)S(1)}, bf16[64,512]{1,0:T(8,128)(2,1)S(1)}, u32[]{:S(2)}, u32[]{:S(2)}) %collective-permute-start.18) | collective-permute-done | bytes 65568 | tf_op jit(solution)/shard_map/ppermute | solution.py:415
  103.1 2.1 %collective-permute-start.21 = (bf16[64,512]{1,0:T(8,128)(2,1)S(1)}, bf16[64,512]{1,0:T(8,128)(2,1)S(1)}, u32[]{:S(2)}, u32[]{:S(2)}) collective-permute-start(bf16[64,512]{1,0:T(8,128)(2,1)S(1)} %get-tuple-element.48), channel_id=1, source_target_pairs={{0,12},{2,14},{4,8},{6,10},{8,4},{10,6},{12,0},{14,2},{1,13},{3,15... | collective-permute-start | bytes 196616 | tf_op jit(solution)/shard_map/ppermute | solution.py:415
  105.3 3.2 %collective-permute-done.20 = bf16[64,512]{1,0:T(8,128)(2,1)S(1)} collective-permute-done((bf16[64,512]{1,0:T(8,128)(2,1)S(1)}, bf16[64,512]{1,0:T(8,128)(2,1)S(1)}, u32[]{:S(2)}, u32[]{:S(2)}) %collective-permute-start.20) | collective-permute-done | bytes 65568 | tf_op jit(solution)/shard_map/ppermute | solution.py:415
  110.6 2.1 %shard_map.105 = bf16[8,64,256]{2,1,0:T(8,128)(2,1)} custom-call(s32[1]{0:T(128)} %bitcast.n_ref, s32[1]{0:T(128)} %bitcast.1.w_ref, f32[32,1024]{1,0:T(8,128)S(1)} %get-tuple-element.54.res_ref, f32[32,512]{1,0:T(8,128)S(1)} %slice_select_fusion.mine_ref, bf16[32,512]{1,0:T(8,128)(2,1)S(1)} %collective-permute-done.22.got_ref, ...), custom_call_target="tpu_custom_call" | custom-call | tf_op jit(solution)/shard_map/pallas_call | solution.py:139
  112.7 4.3 %all-to-all-start.1 = ((bf16[8,64,256]{2,1,0:T(8,128)(2,1)}), bf16[8,64,256]{2,1,0:T(8,128)(2,1)S(1)}, u32[]{:S(2)}, u32[]{:S(2)}) async-start(bf16[8,64,256]{2,1,0:T(8,128)(2,1)} %shard_map.105), calls=%async_computation.1 | async-start | bytes 524288 | tf_op jit(solution)/shard_map/all_to_all | solution.py:438
  117.0 1.4 %shard_map.106.band_ref = bf16[1024,768]{1,0:T(8,128)(2,1)S(1)} custom-call(bf16[27,32,32]{2,1,0:T(8,128)(2,1)S(1)} %copy-done.7), custom_call_target="tpu_custom_call" | custom-call | bytes 33554432 | tf_op jit(solution)/shard_map/pallas_call | solution.py:139
  118.5 7.8 %all-to-all-done.1.planes_ref = bf16[8,64,256]{2,1,0:T(8,128)(2,1)S(1)} async-done(((bf16[8,64,256]{2,1,0:T(8,128)(2,1)}), bf16[8,64,256]{2,1,0:T(8,128)(2,1)S(1)}, u32[]{:S(2)}, u32[]{:S(2)}) %all-to-all-start.1) | async-done | bytes 262176 | tf_op jit(solution)/shard_map/all_to_all | solution.py:438
  (84 shorter events, 28.2 us)
Async XLA Ops:
  3.7 21.8 %all-to-all-start = ((bf16[8,128,256]{2,1,0:T(8,128)(2,1)}), bf16[8,128,256]{2,1,0:T(8,128)(2,1)S(1)}, u32[]{:S(2)}, u32[]{:S(2)}) async-start(bf16[8,128,256]{2,1,0:T(8,128)(2,1)} %shard_map.91), calls=%async_computation | async-start | bytes 1048576 | tf_op jit(solution)/shard_map/all_to_all | solution.py:438
  26.4 1.3 %collective-permute-start = (bf16[256,256]{1,0:T(8,128)(2,1)S(1)}, bf16[256,256]{1,0:T(8,128)(2,1)S(1)}, u32[]{:S(2)}, u32[]{:S(2)}) collective-permute-start(bf16[256,256]{1,0:T(8,128)(2,1)S(1)} %get-tuple-element.30), channel_id=1, source_target_pairs={{0,1},{1,0},{2,3},{3,2},{4,5},{5,4},{6,7},{7,6},{8,9},{9,8},{10,11... | collective-permute-start | bytes 393224 | tf_op jit(solution)/shard_map/ppermute | solution.py:404
  32.4 23.6 %copy-start.5 = (f32[1000,256]{1,0:T(8,128)S(1)}, f32[1000,256]{1,0:T(8,128)}, u32[]{:S(2)}) copy-start(f32[1000,256]{1,0:T(8,128)} %table_ref.1) | copy-start | bytes 3072004
  34.5 4.3 %collective-permute-start.1 = (bf16[32,1024]{1,0:T(8,128)(2,1)S(1)}, bf16[32,1024]{1,0:T(8,128)(2,1)S(1)}, u32[]{:S(2)}, u32[]{:S(2)}) collective-permute-start(bf16[32,1024]{1,0:T(8,128)(2,1)S(1)} %get-tuple-element.32), channel_id=1, source_target_pairs={{0,2},{2,0},{4,6},{6,4},{8,10},{10,8},{12,14},{14,12},{1,3},{3,1},... | collective-permute-start | bytes 196616 | tf_op jit(solution)/shard_map/ppermute | solution.py:415
  38.9 4.5 %collective-permute-start.2 = (bf16[32,1024]{1,0:T(8,128)(2,1)S(1)}, bf16[32,1024]{1,0:T(8,128)(2,1)S(1)}, u32[]{:S(2)}, u32[]{:S(2)}) collective-permute-start(bf16[32,1024]{1,0:T(8,128)(2,1)S(1)} %get-tuple-element.34), channel_id=1, source_target_pairs={{0,4},{2,6},{4,0},{6,2},{8,12},{10,14},{12,8},{14,10},{1,5},{3,7},... | collective-permute-start | bytes 196616 | tf_op jit(solution)/shard_map/ppermute | solution.py:415
  39.7 7.1 %collective-permute-start.3 = (bf16[32,1024]{1,0:T(8,128)(2,1)S(1)}, bf16[32,1024]{1,0:T(8,128)(2,1)S(1)}, u32[]{:S(2)}, u32[]{:S(2)}) collective-permute-start(bf16[32,1024]{1,0:T(8,128)(2,1)S(1)} %get-tuple-element.34), channel_id=1, source_target_pairs={{0,8},{2,10},{4,12},{6,14},{8,0},{10,2},{12,4},{14,6},{1,9},{3,11}... | collective-permute-start | bytes 196616 | tf_op jit(solution)/shard_map/ppermute | solution.py:415
  40.7 6.1 %collective-permute-start.4 = (bf16[32,1024]{1,0:T(8,128)(2,1)S(1)}, bf16[32,1024]{1,0:T(8,128)(2,1)S(1)}, u32[]{:S(2)}, u32[]{:S(2)}) collective-permute-start(bf16[32,1024]{1,0:T(8,128)(2,1)S(1)} %get-tuple-element.34), channel_id=1, source_target_pairs={{0,12},{2,14},{4,8},{6,10},{8,4},{10,6},{12,0},{14,2},{1,13},{3,15... | collective-permute-start | bytes 196616 | tf_op jit(solution)/shard_map/ppermute | solution.py:415
  46.9 1.3 collective-permute-start.5
  54.5 1.5 %collective-permute-start.6 = (f32[64,256]{1,0:T(8,128)S(1)}, f32[64,256]{1,0:T(8,128)S(1)}, u32[]{:S(2)}, u32[]{:S(2)}) collective-permute-start(f32[64,256]{1,0:T(8,128)S(1)} %shard_map.96.mine_ref), channel_id=1, source_target_pairs={{0,1},{1,0},{2,3},{3,2},{4,5},{5,4},{6,7},{7,6},{8,9},{9,8},{10,11... | collective-permute-start | bytes 196616 | tf_op jit(solution)/shard_map/ppermute | solution.py:404
  58.2 35.9 %slice-start = ((s8[14155776]{0:T(1024)(128)(4,1)}), s8[4194304]{0:T(1024)(128)(4,1)S(1)}, s32[]{:S(2)}) async-start(s8[14155776]{0:T(1024)(128)(4,1)} %bitcast.9), calls=%async_computation.2 | async-start | bytes 8388608
  58.2 35.9 %slice-start.1 = ((s8[14155776]{0:T(1024)(128)(4,1)}), s8[4194304]{0:T(1024)(128)(4,1)S(1)}, s32[]{:S(2)}) async-start(s8[14155776]{0:T(1024)(128)(4,1)} %bitcast.9), calls=%async_computation.3 | async-start | bytes 8388608
  59.6 4.3 %collective-permute-start.7 = (bf16[64,512]{1,0:T(8,128)(2,1)S(1)}, bf16[64,512]{1,0:T(8,128)(2,1)S(1)}, u32[]{:S(2)}, u32[]{:S(2)}) collective-permute-start(bf16[64,512]{1,0:T(8,128)(2,1)S(1)} %get-tuple-element.36), channel_id=1, source_target_pairs={{0,2},{2,0},{4,6},{6,4},{8,10},{10,8},{12,14},{14,12},{1,3},{3,1},... | collective-permute-start | bytes 196616 | tf_op jit(solution)/shard_map/ppermute | solution.py:415
  64.0 6.4 %collective-permute-start.10 = (bf16[64,512]{1,0:T(8,128)(2,1)S(1)}, bf16[64,512]{1,0:T(8,128)(2,1)S(1)}, u32[]{:S(2)}, u32[]{:S(2)}) collective-permute-start(bf16[64,512]{1,0:T(8,128)(2,1)S(1)} %get-tuple-element.38), channel_id=1, source_target_pairs={{0,12},{2,14},{4,8},{6,10},{8,4},{10,6},{12,0},{14,2},{1,13},{3,15... | collective-permute-start | bytes 196616 | tf_op jit(solution)/shard_map/ppermute | solution.py:415
  66.6 4.6 %collective-permute-start.8 = (bf16[64,512]{1,0:T(8,128)(2,1)S(1)}, bf16[64,512]{1,0:T(8,128)(2,1)S(1)}, u32[]{:S(2)}, u32[]{:S(2)}) collective-permute-start(bf16[64,512]{1,0:T(8,128)(2,1)S(1)} %get-tuple-element.38), channel_id=1, source_target_pairs={{0,4},{2,6},{4,0},{6,2},{8,12},{10,14},{12,8},{14,10},{1,5},{3,7},... | collective-permute-start | bytes 196616 | tf_op jit(solution)/shard_map/ppermute | solution.py:415
  66.6 5.3 %collective-permute-start.9 = (bf16[64,512]{1,0:T(8,128)(2,1)S(1)}, bf16[64,512]{1,0:T(8,128)(2,1)S(1)}, u32[]{:S(2)}, u32[]{:S(2)}) collective-permute-start(bf16[64,512]{1,0:T(8,128)(2,1)S(1)} %get-tuple-element.38), channel_id=1, source_target_pairs={{0,8},{2,10},{4,12},{6,14},{8,0},{10,2},{12,4},{14,6},{1,9},{3,11}... | collective-permute-start | bytes 196616 | tf_op jit(solution)/shard_map/ppermute | solution.py:415
  71.9 1.3 collective-permute-start.11
  73.2 20.9 %slice-start.2 = ((s8[14155776]{0:T(1024)(128)(4,1)}), s8[4194304]{0:T(1024)(128)(4,1)S(1)}, s32[]{:S(2)}) async-start(s8[14155776]{0:T(1024)(128)(4,1)} %bitcast.9), calls=%async_computation.4 | async-start | bytes 8388608
  76.0 4.3 %collective-permute-start.12 = (bf16[32,1024]{1,0:T(8,128)(2,1)S(1)}, bf16[32,1024]{1,0:T(8,128)(2,1)S(1)}, u32[]{:S(2)}, u32[]{:S(2)}) collective-permute-start(bf16[32,1024]{1,0:T(8,128)(2,1)S(1)} %get-tuple-element.41), channel_id=1, source_target_pairs={{0,2},{2,0},{4,6},{6,4},{8,10},{10,8},{12,14},{14,12},{1,3},{3,1},... | collective-permute-start | bytes 196616 | tf_op jit(solution)/shard_map/ppermute | solution.py:415
  80.3 4.5 %collective-permute-start.13 = (bf16[32,1024]{1,0:T(8,128)(2,1)S(1)}, bf16[32,1024]{1,0:T(8,128)(2,1)S(1)}, u32[]{:S(2)}, u32[]{:S(2)}) collective-permute-start(bf16[32,1024]{1,0:T(8,128)(2,1)S(1)} %get-tuple-element.43), channel_id=1, source_target_pairs={{0,4},{2,6},{4,0},{6,2},{8,12},{10,14},{12,8},{14,10},{1,5},{3,7},... | collective-permute-start | bytes 196616 | tf_op jit(solution)/shard_map/ppermute | solution.py:415
  82.2 6.9 %collective-permute-start.14 = (bf16[32,1024]{1,0:T(8,128)(2,1)S(1)}, bf16[32,1024]{1,0:T(8,128)(2,1)S(1)}, u32[]{:S(2)}, u32[]{:S(2)}) collective-permute-start(bf16[32,1024]{1,0:T(8,128)(2,1)S(1)} %get-tuple-element.43), channel_id=1, source_target_pairs={{0,8},{2,10},{4,12},{6,14},{8,0},{10,2},{12,4},{14,6},{1,9},{3,11}... | collective-permute-start | bytes 196616 | tf_op jit(solution)/shard_map/ppermute | solution.py:415
  82.5 6.6 %collective-permute-start.15 = (bf16[32,1024]{1,0:T(8,128)(2,1)S(1)}, bf16[32,1024]{1,0:T(8,128)(2,1)S(1)}, u32[]{:S(2)}, u32[]{:S(2)}) collective-permute-start(bf16[32,1024]{1,0:T(8,128)(2,1)S(1)} %get-tuple-element.43), channel_id=1, source_target_pairs={{0,12},{2,14},{4,8},{6,10},{8,4},{10,6},{12,0},{14,2},{1,13},{3,15... | collective-permute-start | bytes 196616 | tf_op jit(solution)/shard_map/ppermute | solution.py:415
  89.2 1.3 collective-permute-start.16
  92.8 1.3 %collective-permute-start.17 = (f32[64,256]{1,0:T(8,128)S(1)}, f32[64,256]{1,0:T(8,128)S(1)}, u32[]{:S(2)}, u32[]{:S(2)}) collective-permute-start(f32[64,256]{1,0:T(8,128)S(1)} %shard_map.102.mine_ref), channel_id=1, source_target_pairs={{0,1},{1,0},{2,3},{3,2},{4,5},{5,4},{6,7},{7,6},{8,9},{9,8},{10,11... | collective-permute-start | bytes 196616 | tf_op jit(solution)/shard_map/ppermute | solution.py:404
  94.1 16.4 %copy-start.3 = (bf16[2048,1024]{1,0:T(8,128)(2,1)S(1)}, bf16[2048,1024]{1,0:T(8,128)(2,1)}, u32[]{:S(2)}) copy-start(bf16[2048,1024]{1,0:T(8,128)(2,1)} %merge_ref.3) | copy-start | bytes 12582916
  96.4 20.6 %copy-start.7 = (bf16[27,32,32]{2,1,0:T(8,128)(2,1)S(1)}, bf16[27,32,32]{2,1,0:T(8,128)(2,1)}, u32[]{:S(2)}) copy-start(bf16[27,32,32]{2,1,0:T(8,128)(2,1)} %weight_ref.11) | copy-start | bytes 165892
  96.4 4.3 %collective-permute-start.18 = (bf16[64,512]{1,0:T(8,128)(2,1)S(1)}, bf16[64,512]{1,0:T(8,128)(2,1)S(1)}, u32[]{:S(2)}, u32[]{:S(2)}) collective-permute-start(bf16[64,512]{1,0:T(8,128)(2,1)S(1)} %get-tuple-element.46), channel_id=1, source_target_pairs={{0,2},{2,0},{4,6},{6,4},{8,10},{10,8},{12,14},{14,12},{1,3},{3,1},... | collective-permute-start | bytes 196616 | tf_op jit(solution)/shard_map/ppermute | solution.py:415
  100.7 4.6 %collective-permute-start.19 = (bf16[64,512]{1,0:T(8,128)(2,1)S(1)}, bf16[64,512]{1,0:T(8,128)(2,1)S(1)}, u32[]{:S(2)}, u32[]{:S(2)}) collective-permute-start(bf16[64,512]{1,0:T(8,128)(2,1)S(1)} %get-tuple-element.48), channel_id=1, source_target_pairs={{0,4},{2,6},{4,0},{6,2},{8,12},{10,14},{12,8},{14,10},{1,5},{3,7},... | collective-permute-start | bytes 196616 | tf_op jit(solution)/shard_map/ppermute | solution.py:415
  102.1 6.4 %collective-permute-start.20 = (bf16[64,512]{1,0:T(8,128)(2,1)S(1)}, bf16[64,512]{1,0:T(8,128)(2,1)S(1)}, u32[]{:S(2)}, u32[]{:S(2)}) collective-permute-start(bf16[64,512]{1,0:T(8,128)(2,1)S(1)} %get-tuple-element.48), channel_id=1, source_target_pairs={{0,8},{2,10},{4,12},{6,14},{8,0},{10,2},{12,4},{14,6},{1,9},{3,11}... | collective-permute-start | bytes 196616 | tf_op jit(solution)/shard_map/ppermute | solution.py:415
  103.1 6.2 %collective-permute-start.21 = (bf16[64,512]{1,0:T(8,128)(2,1)S(1)}, bf16[64,512]{1,0:T(8,128)(2,1)S(1)}, u32[]{:S(2)}, u32[]{:S(2)}) collective-permute-start(bf16[64,512]{1,0:T(8,128)(2,1)S(1)} %get-tuple-element.48), channel_id=1, source_target_pairs={{0,12},{2,14},{4,8},{6,10},{8,4},{10,6},{12,0},{14,2},{1,13},{3,15... | collective-permute-start | bytes 196616 | tf_op jit(solution)/shard_map/ppermute | solution.py:415
  109.3 1.3 collective-permute-start.22
  112.7 13.6 %all-to-all-start.1 = ((bf16[8,64,256]{2,1,0:T(8,128)(2,1)}), bf16[8,64,256]{2,1,0:T(8,128)(2,1)S(1)}, u32[]{:S(2)}, u32[]{:S(2)}) async-start(bf16[8,64,256]{2,1,0:T(8,128)(2,1)} %shard_map.105), calls=%async_computation.1 | async-start | bytes 524288 | tf_op jit(solution)/shard_map/all_to_all | solution.py:438
  126.5 1.4 %collective-permute-start.23 = (bf16[256,256]{1,0:T(8,128)(2,1)S(1)}, bf16[256,256]{1,0:T(8,128)(2,1)S(1)}, u32[]{:S(2)}, u32[]{:S(2)}) collective-permute-start(bf16[256,256]{1,0:T(8,128)(2,1)S(1)} %get-tuple-element.52), channel_id=1, source_target_pairs={{0,1},{1,0},{2,3},{3,2},{4,5},{5,4},{6,7},{7,6},{8,9},{9,8},{10,11... | collective-permute-start | bytes 393224 | tf_op jit(solution)/shard_map/ppermute | solution.py:404
  (10 other events, 34.9 us)

commit v4 on v3

--- a/solution.py
+++ b/solution.py
@@ -144,7 +144,7 @@
         scratch_shapes=list(scratch),
         cost_estimate=cost and pl.CostEstimate(flops=0, bytes_accessed=cost, transcendentals=0),
         compiler_params=pltpu.CompilerParams(vmem_limit_bytes=LIMIT),
-    )(*places, *arrays, *rest)
+    )(*places, *arrays, *[pltpu.with_memory_space_constraint(a, pltpu.HBM) for a in rest])
 
 
 def band_kernel(weight_ref, out_ref, *, back):
@@ -182,7 +182,8 @@
     return out
 
 
-def pack_kernel(field_ref, cot_ref, out_ref):
+def pack_kernel(n_ref, w_ref, step_ref, field_ref, cot_ref, out_ref):
+    del n_ref, w_ref, step_ref
     for a in range(8):
         out_ref[a, 0:32] = field_ref[(a + 7) % 8]
         out_ref[a, 32:64] = field_ref[a]
@@ -252,9 +253,15 @@
 
 
 def merge_kernel(
-    n_ref, w_ref, planes_ref, own_ref, got_ref, band_ref, merge_ref, pre_ref, act_ref, sum_ref, sum_b_ref, rows_ref
+    n_ref, w_ref, planes_ref, own_ref, got_ref, band_ref, merge_ref, pre_ref, act_ref, sum_ref, sum_b_ref,
+    rows_ref, weight_ref, sems
 ):
     n = n_ref[0]
+    copies = []
+    for b in range(8):
+        place = pl.ds(256 * b, 256)
+        copies.append(pltpu.make_async_copy(merge_ref.at[place], weight_ref.at[place], sems.at[b]))
+        copies[b].start()
     planes = arrived_planes(w_ref[0], planes_ref)
     wide_rows = fine_sum(n, planes, own_ref, got_ref, band_ref)
     rows_ref[0] = wide_rows[:, :128]
@@ -265,7 +272,8 @@
         pre_ref[b] = pre
         act = (pre * jax.nn.sigmoid(pre)).astype(BF)
         act_ref[b] = act
-        part = nn_dot(act, merge_ref[256 * b : 256 * b + 256])
+        copies[b].wait()
+        part = nn_dot(act, weight_ref[256 * b : 256 * b + 256])
         total = part if total is None else total + part
     sum_ref[...] = total
     sum_b_ref[...] = total.astype(BF)
@@ -404,34 +412,60 @@
     return lax.ppermute(value, "narrow", [(0, 1), (1, 0)])
 
 
-def pair_kernel(part_ref, got_ref, pair_ref, pair_b_ref):
+def pair_kernel(part_ref, got_ref, *refs):
+    pair_ref, pair_b_ref = refs[-2:]
     pair = part_ref[...] + got_ref[...].astype(F32)
     pair_ref[...] = pair
     pair_b_ref[...] = pair.astype(BF)
 
 
-def summed_wide(part, part_b):
+def features_kernel(n_ref, pair_ref, one_ref, two_ref, three_ref, *refs):
+    sum_ref, mine_ref, send_ref = refs[-3:]
+    total = pair_ref[...] + one_ref[...].astype(F32) + two_ref[...].astype(F32) + three_ref[...].astype(F32)
+    sum_ref[...] = total
+    half = total.shape[1] // 2
+    low, high = total[:, :half], total[:, half:]
+    first = n_ref[0] == 0
+    mine_ref[...] = jnp.where(first, low, high).astype(BF)
+    send_ref[...] = jnp.where(first, high, low).astype(BF)
+
+
+def cells_kernel(n_ref, pair_ref, one_ref, two_ref, three_ref, mine_ref, send_ref):
+    total = pair_ref[...] + one_ref[...].astype(F32) + two_ref[...].astype(F32) + three_ref[...].astype(F32)
+    half = total.shape[0] // 2
+    low, high = total[:half], total[half:]
+    first = n_ref[0] == 0
+    mine_ref[...] = jnp.where(first, low, high)
+    send_ref[...] = jnp.where(first, high, low).astype(BF)
+
+
+def wide_terms(part, part_b, rest=()):
     def partner(value, mask):
         return lax.ppermute(value, "wide", [(i, i ^ mask) for i in range(8)])
 
     shape = part.shape
     pair, pair_b = kernel_call(
-        pair_kernel, (), (part, partner(part_b, 1)), [shape_of(shape, F32), shape_of(shape, BF)], cost=BESIDE
-    )
-    others = [partner(pair_b, mask) for mask in (2, 4, 6)]
-    return pair + others[0].astype(F32) + others[1].astype(F32) + others[2].astype(F32)
-
-
-def to_feature_halves(n, cells):
-    half = cells.shape[1] // 2
-    low, high = cells[:, :half], cells[:, half:]
-    return jnp.where(n == 0, low, high), swap_narrow(jnp.where(n == 0, high, low))
-
-
-def to_cell_halves(n, rows):
-    half = rows.shape[0] // 2
-    low, high = rows[:half], rows[half:]
-    return jnp.where(n == 0, low, high), swap_narrow(jnp.where(n == 0, high, low).astype(BF))
+        pair_kernel, (), (part, partner(part_b, 1)), [shape_of(shape, F32), shape_of(shape, BF)], rest=rest
+    )
+    return (pair, *[partner(pair_b, mask) for mask in (2, 4, 6)])
+
+
+def to_feature_halves(n, part, part_b, rest=()):
+    terms = wide_terms(part, part_b, rest)
+    cells, features = part.shape
+    half_shape = shape_of((cells, features // 2), BF)
+    total, mine, send = kernel_call(
+        features_kernel, (n,), terms, [shape_of(part.shape, F32), half_shape, half_shape], rest=rest
+    )
+    return total, mine, swap_narrow(send)
+
+
+def to_cell_halves(n, part, part_b):
+    terms = wide_terms(part, part_b)
+    cells, features = part.shape
+    half = (cells // 2, features)
+    mine, send = kernel_call(cells_kernel, (n,), terms, [shape_of(half, F32), shape_of(half, BF)])
+    return mine, swap_narrow(send)
 
 
 def across_wide(value):
@@ -453,14 +487,13 @@
     hidden = hidden_weight.shape[2]
     half = features // 2
     w = lax.axis_index("wide").astype(jnp.int32).reshape(1)
-    n_index = lax.axis_index("narrow")
-    n = n_index.astype(jnp.int32).reshape(1)
+    n = lax.axis_index("narrow").astype(jnp.int32).reshape(1)
 
     def row_form(fine_field):
         return fine_field.transpose(1, 2, 3, 0).reshape(8, 32, 256)
 
     (outgoing,) = kernel_call(
-        pack_kernel, (), (row_form(volume), row_form(cotangent)), [shape_of((8, 128, 256), BF)]
+        pack_kernel, (n, w, timestep), (row_form(volume), row_form(cotangent)), [shape_of((8, 128, 256), BF)]
     )
     arrived = across_wide(outgoing)
     band = banded(fine_weight, False)
@@ -470,13 +503,13 @@
     pre_act, act, merged_part, merged_part_b = kernel_call(
         merge_kernel,
         (n, w),
-        (arrived, sides, swap_narrow(sent), band, merge_weight),
+        (arrived, sides, swap_narrow(sent), band),
         [shape_of((8, 32, 256), F32), shape_of((8, 32, 256), BF)] + sum_shapes,
-        [fine_rows],
+        [fine_rows, pltpu.VMEM(merge_weight.shape, BF), pltpu.SemaphoreType.DMA((8,))],
+        rest=(merge_weight,),
     )
     (cot,) = kernel_call(cot_kernel, (), (arrived,), [shape_of((8, 32, 256), BF)], [fine_rows])
-    merged = summed_wide(merged_part, merged_part_b)
-    mine, got = to_feature_halves(n_index, merged.astype(BF))
+    merged, mine, got = to_feature_halves(n, merged_part, merged_part_b, (hidden_weight,))
 
     gate_shape = shape_of((64, hidden), F32)
     half_shapes = [shape_of((64, half), F32), shape_of((64, half), BF)]
@@ -492,14 +525,13 @@
         (n, timestep), (gate_part, swap_narrow(gate_part), output_weight), [gate_shape] + half_shapes,
         inner_columns + [pltpu.VMEM((8, hidden), F32), pltpu.SemaphoreType.DMA], rest=(step_table,),
     )
-    mine, got = to_cell_halves(n_index, summed_wide(branch_part, branch_part_b))
+    mine, got = to_cell_halves(n, branch_part, branch_part_b)
     grad_comb, res_part, res_part_b = kernel_call(
         expand_kernel,
         (n,), (merged, mine, got, act, cot, expand_weight),
         [shape_of((8, 32, 256), BF)] + sum_shapes,
     )
-    grad_res = summed_wide(res_part, res_part_b)
-    mine, got = to_feature_halves(n_index, grad_res.astype(BF))
+    grad_res, mine, got = to_feature_halves(n, res_part, res_part_b)
     (hidden_part,) = kernel_call(
         functools.partial(outer_kernel, flipped=True, dot=nt_dot, part_of=feature_columns),
         (n,), (mine, got, output_weight), [gate_shape], outer_columns,
@@ -509,7 +541,7 @@
         (n,), (hidden_part, swap_narrow(hidden_part), gate_pre, hidden_weight),
         half_shapes, inner_columns,
     )
-    mine, got = to_cell_halves(n_index, summed_wide(conv_part, conv_part_b))
+    mine, got = to_cell_halves(n, conv_part, conv_part_b)
     (leaving,) = kernel_call(
         grad_kernel,
         (n, w), (grad_res, mine, got, grad_comb, pre_act, merge_weight),

time: 130 us -> 122 us (0.938)
  local copies, waits for them, and re-layouts: 17.4 us -> 6.57 us
  Pallas kernels: 18.1 us -> 20.6 us
    unnamed x32 -> x24, local copies, waits for them, and re-layouts: 13.4 us -> 2.66 us
    pallas_call x18 -> x22, Pallas kernels: 18.1 us -> 20.6 us  [kernel_call(): pl.pallas_call(kernel, in_specs=[SMEM] * len(places) + [VMEM] * len(array...]
  transfers between devices with their start and end apart: 26 -> 26, of which waited for: 21 -> 21; matrix products, arithmetic and copies ran while one was open for 0% -> 0% of each run, Pallas kernels for 1% -> 2%
where the time goes in v4:
time: 122 us
  waiting for transfers between devices  56.7 us (46%)
  starting transfers between devices  36.8 us (30%)
  Pallas kernels  20.6 us (17%)
  local copies, waits for them, and re-layouts  6.57 us (5%)
    ppermute x16, waiting for transfers between devices, partner(): return lax.ppermute(value, 'wide', [(i, i ^ mask) for i in range(8)])  26.2 us
    ppermute x16, starting transfers between devices, partner(): return lax.ppermute(value, 'wide', [(i, i ^ mask) for i in range(8)])  24.3 us
    all_to_all x2, waiting for transfers between devices, across_wide(): lax.all_to_all(value, 'wide', split_axis=0, concat_axis=0, tiled=True)  20.9 us
    pallas_call x22, Pallas kernels, kernel_call(): pl.pallas_call(kernel, in_specs=[SMEM] * len(places) + [VMEM] * len(array...  20.6 us
    all_to_all x2, starting transfers between devices, across_wide(): lax.all_to_all(value, 'wide', split_axis=0, concat_axis=0, tiled=True)  11.6 us
    ppermute x8, waiting for transfers between devices, swap_narrow(): return lax.ppermute(value, 'narrow', [(0, 1), (1, 0)])  9.56 us
    reshape x2, local copies, waits for them, and re-layouts, row_form(): return fine_field.transpose(1, 2, 3, 0).reshape(8, 32, 256)  2.88 us
    unnamed x24, local copies, waits for them, and re-layouts  2.66 us
  transfers between devices with their start and end apart: 26, of which 21 were waited for; matrix products, arithmetic and copies ran while one was open for 0% of the time, Pallas kernels for 2%

profile of v4, /device:TPU:0, one launch (start us, length us, event | category | flops | bytes accessed | tf_op | source)
XLA Modules:
  0.0 121.5 jit_solution(12079990621880676762)
XLA Ops:
  0.7 1.4 %reshape.17.field_ref = bf16[8,32,256]{2,1,0:T(8,128)(2,1)S(1)} reshape(bf16[8,16,16,32]{3,2,1,0:T(8,128)(2,1)} %bitcast.13) | data formatting | bytes 262144 | tf_op jit(solution)/shard_map/reshape | solution.py:493
  2.1 1.4 %reshape.18.cot_ref = bf16[8,32,256]{2,1,0:T(8,128)(2,1)S(1)} reshape(bf16[8,16,16,32]{3,2,1,0:T(8,128)(2,1)} %bitcast.14) | data formatting | bytes 262144 | tf_op jit(solution)/shard_map/reshape | solution.py:493
  4.4 7.3 %all-to-all-start = ((bf16[8,128,256]{2,1,0:T(8,128)(2,1)}), bf16[8,128,256]{2,1,0:T(8,128)(2,1)S(1)}, u32[]{:S(2)}, u32[]{:S(2)}) async-start(bf16[8,128,256]{2,1,0:T(8,128)(2,1)} %shard_map.91), calls=%async_computation | async-start | bytes 1048576 | tf_op jit(solution)/shard_map/all_to_all | solution.py:472
  13.0 13.2 %all-to-all-done.planes_ref = bf16[8,128,256]{2,1,0:T(8,128)(2,1)S(1)} async-done(((bf16[8,128,256]{2,1,0:T(8,128)(2,1)}), bf16[8,128,256]{2,1,0:T(8,128)(2,1)S(1)}, u32[]{:S(2)}, u32[]{:S(2)}) %all-to-all-start) | async-done | bytes 524320 | tf_op jit(solution)/shard_map/all_to_all | solution.py:472
  27.8 3.7 %shard_map.94 = (f32[8,32,256]{2,1,0:T(8,128)S(1)}, bf16[8,32,256]{2,1,0:T(8,128)(2,1)S(1)}, f32[32,1024]{1,0:T(8,128)S(1)}, bf16[32,1024]{1,0:T(8,128)(2,1)S(1)}) custom-call(s32[1]{0:T(128)} %bitcast.n_ref, s32[1]{0:T(128)} %bitcast.1.w_ref, bf16[8,128,256]{2,1,0:T(8,128)(2,1)S(1)} %all-to-all-done.planes_ref, ...), custom_call_target="tpu_custom_call" | custom-call | tf_op jit(solution)/shard_map/pallas_call | solution.py:139
  31.5 1.5 %collective-permute-start.1 = (bf16[32,1024]{1,0:T(8,128)(2,1)S(1)}, bf16[32,1024]{1,0:T(8,128)(2,1)S(1)}, u32[]{:S(2)}, u32[]{:S(2)}) collective-permute-start(bf16[32,1024]{1,0:T(8,128)(2,1)S(1)} %get-tuple-element.42), channel_id=1, source_target_pairs={{0,2},{2,0},{4,6},{6,4},{8,10},{10,8},{12,14},{14,12},{1,3},{3,1},... | collective-permute-start | bytes 196616 | tf_op jit(solution)/shard_map/ppermute | solution.py:444
  33.1 2.8 %collective-permute-done.1.got_ref = bf16[32,1024]{1,0:T(8,128)(2,1)S(1)} collective-permute-done((bf16[32,1024]{1,0:T(8,128)(2,1)S(1)}, bf16[32,1024]{1,0:T(8,128)(2,1)S(1)}, u32[]{:S(2)}, u32[]{:S(2)}) %collective-permute-start.1) | collective-permute-done | bytes 65568 | tf_op jit(solution)/shard_map/ppermute | solution.py:444
  37.7 2.6 %collective-permute-start.4 = (bf16[32,1024]{1,0:T(8,128)(2,1)S(1)}, bf16[32,1024]{1,0:T(8,128)(2,1)S(1)}, u32[]{:S(2)}, u32[]{:S(2)}) collective-permute-start(bf16[32,1024]{1,0:T(8,128)(2,1)S(1)} %get-tuple-element.44), channel_id=1, source_target_pairs={{0,12},{2,14},{4,8},{6,10},{8,4},{10,6},{12,0},{14,2},{1,13},{3,15... | collective-permute-start | bytes 196616 | tf_op jit(solution)/shard_map/ppermute | solution.py:444
  40.4 3.5 %collective-permute-done.3.two_ref = bf16[32,1024]{1,0:T(8,128)(2,1)S(1)} collective-permute-done((bf16[32,1024]{1,0:T(8,128)(2,1)S(1)}, bf16[32,1024]{1,0:T(8,128)(2,1)S(1)}, u32[]{:S(2)}, u32[]{:S(2)}) %collective-permute-start.3) | collective-permute-done | bytes 65568 | tf_op jit(solution)/shard_map/ppermute | solution.py:444
  45.3 1.3 %shard_map.97.mine_ref = f32[64,256]{1,0:T(8,128)S(1)} custom-call(s32[1]{0:T(128)} %bitcast.n_ref, bf16[32,512]{1,0:T(8,128)(2,1)S(1)} %get-tuple-element.46.mine_ref, bf16[32,512]{1,0:T(8,128)(2,1)S(1)} %collective-permute-done.5.got_ref, bf16[27,1024,256]{2,1,0:T(8,128)(2,1)S(1)} %bitcast.10), custom_call_target="tpu_custom_call" | custom-call | tf_op jit(solution)/shard_map/pallas_call | solution.py:139
  49.6 2.1 %shard_map.98 = (f32[64,256]{1,0:T(8,128)S(1)}, f32[64,512]{1,0:T(8,128)S(1)}, bf16[64,512]{1,0:T(8,128)(2,1)S(1)}) custom-call(s32[1]{0:T(128)} %bitcast.n_ref, s32[1]{0:T(128)S(6)} %copy.10.step_ref, f32[64,256]{1,0:T(8,128)S(1)} %shard_map.97.mine_ref, f32[64,256]{1,0:T(8,128)S(1)} %collective-permute-done.6.got_ref, bf16[27,256,1024]{2,1,0:T(8,128)(2,1)S(1)} %bitcast.12, ...), custom_call_target="tpu_custom_call" | custom-call | tf_op jit(solution)/shard_map/pallas_call | solution.py:139
  51.7 1.8 %collective-permute-start.7 = (bf16[64,512]{1,0:T(8,128)(2,1)S(1)}, bf16[64,512]{1,0:T(8,128)(2,1)S(1)}, u32[]{:S(2)}, u32[]{:S(2)}) collective-permute-start(bf16[64,512]{1,0:T(8,128)(2,1)S(1)} %get-tuple-element.49), channel_id=1, source_target_pairs={{0,2},{2,0},{4,6},{6,4},{8,10},{10,8},{12,14},{14,12},{1,3},{3,1},... | collective-permute-start | bytes 196616 | tf_op jit(solution)/shard_map/ppermute | solution.py:444
  53.5 2.5 %collective-permute-done.7.got_ref = bf16[64,512]{1,0:T(8,128)(2,1)S(1)} collective-permute-done((bf16[64,512]{1,0:T(8,128)(2,1)S(1)}, bf16[64,512]{1,0:T(8,128)(2,1)S(1)}, u32[]{:S(2)}, u32[]{:S(2)}) %collective-permute-start.7) | collective-permute-done | bytes 65568 | tf_op jit(solution)/shard_map/ppermute | solution.py:444
  56.0 2.6 %collective-permute-start.10 = (bf16[64,512]{1,0:T(8,128)(2,1)S(1)}, bf16[64,512]{1,0:T(8,128)(2,1)S(1)}, u32[]{:S(2)}, u32[]{:S(2)}) collective-permute-start(bf16[64,512]{1,0:T(8,128)(2,1)S(1)} %get-tuple-element.51), channel_id=1, source_target_pairs={{0,12},{2,14},{4,8},{6,10},{8,4},{10,6},{12,0},{14,2},{1,13},{3,15... | collective-permute-start | bytes 196616 | tf_op jit(solution)/shard_map/ppermute | solution.py:444
  58.6 1.8 %collective-permute-start.9 = (bf16[64,512]{1,0:T(8,128)(2,1)S(1)}, bf16[64,512]{1,0:T(8,128)(2,1)S(1)}, u32[]{:S(2)}, u32[]{:S(2)}) collective-permute-start(bf16[64,512]{1,0:T(8,128)(2,1)S(1)} %get-tuple-element.51), channel_id=1, source_target_pairs={{0,8},{2,10},{4,12},{6,14},{8,0},{10,2},{12,4},{14,6},{1,9},{3,11}... | collective-permute-start | bytes 196616 | tf_op jit(solution)/shard_map/ppermute | solution.py:444
  60.5 1.7 %collective-permute-done.10.three_ref = bf16[64,512]{1,0:T(8,128)(2,1)S(1)} collective-permute-done((bf16[64,512]{1,0:T(8,128)(2,1)S(1)}, bf16[64,512]{1,0:T(8,128)(2,1)S(1)}, u32[]{:S(2)}, u32[]{:S(2)}) %collective-permute-start.10) | collective-permute-done | bytes 65568 | tf_op jit(solution)/shard_map/ppermute | solution.py:444
  65.1 2.7 %shard_map.102 = (bf16[8,32,256]{2,1,0:T(8,128)(2,1)S(1)}, f32[32,1024]{1,0:T(8,128)S(1)}, bf16[32,1024]{1,0:T(8,128)(2,1)S(1)}) custom-call(s32[1]{0:T(128)} %bitcast.n_ref, f32[32,1024]{1,0:T(8,128)S(1)} %get-tuple-element.45.merged_ref, f32[32,512]{1,0:T(8,128)S(1)} %get-tuple-element.52.mine_ref, bf16[32,512]{1,0:T(8,128)(2,1)S(1)} %collective-permute-done.11.got_ref, ...), custom_call_target="tpu_custom_call" | custom-call | tf_op jit(solution)/shard_map/pallas_call | solution.py:139
  67.9 1.5 %collective-permute-start.12 = (bf16[32,1024]{1,0:T(8,128)(2,1)S(1)}, bf16[32,1024]{1,0:T(8,128)(2,1)S(1)}, u32[]{:S(2)}, u32[]{:S(2)}) collective-permute-start(bf16[32,1024]{1,0:T(8,128)(2,1)S(1)} %get-tuple-element.56), channel_id=1, source_target_pairs={{0,2},{2,0},{4,6},{6,4},{8,10},{10,8},{12,14},{14,12},{1,3},{3,1},... | collective-permute-start | bytes 196616 | tf_op jit(solution)/shard_map/ppermute | solution.py:444
  69.4 2.8 %collective-permute-done.12.got_ref = bf16[32,1024]{1,0:T(8,128)(2,1)S(1)} collective-permute-done((bf16[32,1024]{1,0:T(8,128)(2,1)S(1)}, bf16[32,1024]{1,0:T(8,128)(2,1)S(1)}, u32[]{:S(2)}, u32[]{:S(2)}) %collective-permute-start.12) | collective-permute-done | bytes 65568 | tf_op jit(solution)/shard_map/ppermute | solution.py:444
  72.2 2.1 %collective-permute-start.13 = (bf16[32,1024]{1,0:T(8,128)(2,1)S(1)}, bf16[32,1024]{1,0:T(8,128)(2,1)S(1)}, u32[]{:S(2)}, u32[]{:S(2)}) collective-permute-start(bf16[32,1024]{1,0:T(8,128)(2,1)S(1)} %get-tuple-element.58), channel_id=1, source_target_pairs={{0,4},{2,6},{4,0},{6,2},{8,12},{10,14},{12,8},{14,10},{1,5},{3,7},... | collective-permute-start | bytes 196616 | tf_op jit(solution)/shard_map/ppermute | solution.py:444
  74.6 2.1 %collective-permute-start.15 = (bf16[32,1024]{1,0:T(8,128)(2,1)S(1)}, bf16[32,1024]{1,0:T(8,128)(2,1)S(1)}, u32[]{:S(2)}, u32[]{:S(2)}) collective-permute-start(bf16[32,1024]{1,0:T(8,128)(2,1)S(1)} %get-tuple-element.58), channel_id=1, source_target_pairs={{0,12},{2,14},{4,8},{6,10},{8,4},{10,6},{12,0},{14,2},{1,13},{3,15... | collective-permute-start | bytes 196616 | tf_op jit(solution)/shard_map/ppermute | solution.py:444
  76.7 4.5 %collective-permute-done.14.two_ref = bf16[32,1024]{1,0:T(8,128)(2,1)S(1)} collective-permute-done((bf16[32,1024]{1,0:T(8,128)(2,1)S(1)}, bf16[32,1024]{1,0:T(8,128)(2,1)S(1)}, u32[]{:S(2)}, u32[]{:S(2)}) %collective-permute-start.14) | collective-permute-done | bytes 65568 | tf_op jit(solution)/shard_map/ppermute | solution.py:444
  82.5 2.3 %shard_map.105.mine_ref = f32[64,256]{1,0:T(8,128)S(1)} custom-call(s32[1]{0:T(128)} %bitcast.n_ref, bf16[32,512]{1,0:T(8,128)(2,1)S(1)} %get-tuple-element.60.mine_ref, bf16[32,512]{1,0:T(8,128)(2,1)S(1)} %collective-permute-done.16.got_ref, bf16[27,256,1024]{2,1,0:T(8,128)(2,1)S(1)} %bitcast.12), custom_call_target="tpu_custom_call" | custom-call | tf_op jit(solution)/shard_map/pallas_call | solution.py:139
  86.1 2.2 %shard_map.106 = (f32[64,512]{1,0:T(8,128)S(1)}, bf16[64,512]{1,0:T(8,128)(2,1)S(1)}) custom-call(s32[1]{0:T(128)} %bitcast.n_ref, f32[64,256]{1,0:T(8,128)S(1)} %shard_map.105.mine_ref, f32[64,256]{1,0:T(8,128)S(1)} %collective-permute-done.17.got_ref, f32[64,256]{1,0:T(8,128)S(1)} %get-tuple-element.62.gate_ref, bf16[27,1024,256]{2,1,0:T(8,128)(2,1)S(1)} %bitcast.10), custom_call_target="tpu_custom_call" | custom-call | tf_op jit(solution)/shard_map/pallas_call | solution.py:139
  88.4 1.5 %collective-permute-start.18 = (bf16[64,512]{1,0:T(8,128)(2,1)S(1)}, bf16[64,512]{1,0:T(8,128)(2,1)S(1)}, u32[]{:S(2)}, u32[]{:S(2)}) collective-permute-start(bf16[64,512]{1,0:T(8,128)(2,1)S(1)} %get-tuple-element.64), channel_id=1, source_target_pairs={{0,2},{2,0},{4,6},{6,4},{8,10},{10,8},{12,14},{14,12},{1,3},{3,1},... | collective-permute-start | bytes 196616 | tf_op jit(solution)/shard_map/ppermute | solution.py:444
  89.9 2.8 %collective-permute-done.18.got_ref = bf16[64,512]{1,0:T(8,128)(2,1)S(1)} collective-permute-done((bf16[64,512]{1,0:T(8,128)(2,1)S(1)}, bf16[64,512]{1,0:T(8,128)(2,1)S(1)}, u32[]{:S(2)}, u32[]{:S(2)}) %collective-permute-start.18) | collective-permute-done | bytes 65568 | tf_op jit(solution)/shard_map/ppermute | solution.py:444
  95.0 2.2 %collective-permute-start.21 = (bf16[64,512]{1,0:T(8,128)(2,1)S(1)}, bf16[64,512]{1,0:T(8,128)(2,1)S(1)}, u32[]{:S(2)}, u32[]{:S(2)}) collective-permute-start(bf16[64,512]{1,0:T(8,128)(2,1)S(1)} %get-tuple-element.66), channel_id=1, source_target_pairs={{0,12},{2,14},{4,8},{6,10},{8,4},{10,6},{12,0},{14,2},{1,13},{3,15... | collective-permute-start | bytes 196616 | tf_op jit(solution)/shard_map/ppermute | solution.py:444
  97.3 3.9 %collective-permute-done.20.two_ref = bf16[64,512]{1,0:T(8,128)(2,1)S(1)} collective-permute-done((bf16[64,512]{1,0:T(8,128)(2,1)S(1)}, bf16[64,512]{1,0:T(8,128)(2,1)S(1)}, u32[]{:S(2)}, u32[]{:S(2)}) %collective-permute-start.20) | collective-permute-done | bytes 65568 | tf_op jit(solution)/shard_map/ppermute | solution.py:444
  102.5 2.1 %shard_map.109 = bf16[8,64,256]{2,1,0:T(8,128)(2,1)} custom-call(s32[1]{0:T(128)} %bitcast.n_ref, s32[1]{0:T(128)} %bitcast.1.w_ref, f32[32,1024]{1,0:T(8,128)S(1)} %get-tuple-element.59.res_ref, f32[32,512]{1,0:T(8,128)S(1)} %get-tuple-element.67.mine_ref, bf16[32,512]{1,0:T(8,128)(2,1)S(1)} %collective-permute-done.22.got_ref, ...), custom_call_target="tpu_custom_call" | custom-call | tf_op jit(solution)/shard_map/pallas_call | solution.py:139
  104.6 4.3 %all-to-all-start.1 = ((bf16[8,64,256]{2,1,0:T(8,128)(2,1)}), bf16[8,64,256]{2,1,0:T(8,128)(2,1)S(1)}, u32[]{:S(2)}, u32[]{:S(2)}) async-start(bf16[8,64,256]{2,1,0:T(8,128)(2,1)} %shard_map.109), calls=%async_computation.1 | async-start | bytes 524288 | tf_op jit(solution)/shard_map/all_to_all | solution.py:472
  109.0 1.4 %shard_map.110.band_ref = bf16[1024,768]{1,0:T(8,128)(2,1)S(1)} custom-call(bf16[27,32,32]{2,1,0:T(8,128)(2,1)S(1)} %copy-done.3), custom_call_target="tpu_custom_call" | custom-call | bytes 33554432 | tf_op jit(solution)/shard_map/pallas_call | solution.py:139
  110.4 7.8 %all-to-all-done.1.planes_ref = bf16[8,64,256]{2,1,0:T(8,128)(2,1)S(1)} async-done(((bf16[8,64,256]{2,1,0:T(8,128)(2,1)}), bf16[8,64,256]{2,1,0:T(8,128)(2,1)S(1)}, u32[]{:S(2)}, u32[]{:S(2)}) %all-to-all-start.1) | async-done | bytes 262176 | tf_op jit(solution)/shard_map/all_to_all | solution.py:472
  (71 shorter events, 22.9 us)
Async XLA Ops:
  4.4 21.8 %all-to-all-start = ((bf16[8,128,256]{2,1,0:T(8,128)(2,1)}), bf16[8,128,256]{2,1,0:T(8,128)(2,1)S(1)}, u32[]{:S(2)}, u32[]{:S(2)}) async-start(bf16[8,128,256]{2,1,0:T(8,128)(2,1)} %shard_map.91), calls=%async_computation | async-start | bytes 1048576 | tf_op jit(solution)/shard_map/all_to_all | solution.py:472
  26.4 1.4 %collective-permute-start = (bf16[256,256]{1,0:T(8,128)(2,1)S(1)}, bf16[256,256]{1,0:T(8,128)(2,1)S(1)}, u32[]{:S(2)}, u32[]{:S(2)}) collective-permute-start(bf16[256,256]{1,0:T(8,128)(2,1)S(1)} %get-tuple-element.40), channel_id=1, source_target_pairs={{0,1},{1,0},{2,3},{3,2},{4,5},{5,4},{6,7},{7,6},{8,9},{9,8},{10,11... | collective-permute-start | bytes 393224 | tf_op jit(solution)/shard_map/ppermute | solution.py:412
  27.8 17.4 %slice-start = ((s8[14155776]{0:T(1024)(128)(4,1)}), s8[4194304]{0:T(1024)(128)(4,1)S(1)}, s32[]{:S(2)}) async-start(s8[14155776]{0:T(1024)(128)(4,1)} %bitcast.9), calls=%async_computation.2 | async-start | bytes 8388608
  31.5 4.3 %collective-permute-start.1 = (bf16[32,1024]{1,0:T(8,128)(2,1)S(1)}, bf16[32,1024]{1,0:T(8,128)(2,1)S(1)}, u32[]{:S(2)}, u32[]{:S(2)}) collective-permute-start(bf16[32,1024]{1,0:T(8,128)(2,1)S(1)} %get-tuple-element.42), channel_id=1, source_target_pairs={{0,2},{2,0},{4,6},{6,4},{8,10},{10,8},{12,14},{14,12},{1,3},{3,1},... | collective-permute-start | bytes 196616 | tf_op jit(solution)/shard_map/ppermute | solution.py:444
  35.9 9.3 %slice-start.1 = ((s8[14155776]{0:T(1024)(128)(4,1)}), s8[4194304]{0:T(1024)(128)(4,1)S(1)}, s32[]{:S(2)}) async-start(s8[14155776]{0:T(1024)(128)(4,1)} %bitcast.9), calls=%async_computation.3 | async-start | bytes 8388608
  35.9 9.3 %slice-start.2 = ((s8[14155776]{0:T(1024)(128)(4,1)}), s8[4194304]{0:T(1024)(128)(4,1)S(1)}, s32[]{:S(2)}) async-start(s8[14155776]{0:T(1024)(128)(4,1)} %bitcast.9), calls=%async_computation.4 | async-start | bytes 8388608
  35.9 4.5 %collective-permute-start.2 = (bf16[32,1024]{1,0:T(8,128)(2,1)S(1)}, bf16[32,1024]{1,0:T(8,128)(2,1)S(1)}, u32[]{:S(2)}, u32[]{:S(2)}) collective-permute-start(bf16[32,1024]{1,0:T(8,128)(2,1)S(1)} %get-tuple-element.44), channel_id=1, source_target_pairs={{0,4},{2,6},{4,0},{6,2},{8,12},{10,14},{12,8},{14,10},{1,5},{3,7},... | collective-permute-start | bytes 196616 | tf_op jit(solution)/shard_map/ppermute | solution.py:444
  36.7 7.1 %collective-permute-start.3 = (bf16[32,1024]{1,0:T(8,128)(2,1)S(1)}, bf16[32,1024]{1,0:T(8,128)(2,1)S(1)}, u32[]{:S(2)}, u32[]{:S(2)}) collective-permute-start(bf16[32,1024]{1,0:T(8,128)(2,1)S(1)} %get-tuple-element.44), channel_id=1, source_target_pairs={{0,8},{2,10},{4,12},{6,14},{8,0},{10,2},{12,4},{14,6},{1,9},{3,11}... | collective-permute-start | bytes 196616 | tf_op jit(solution)/shard_map/ppermute | solution.py:444
  37.7 6.1 %collective-permute-start.4 = (bf16[32,1024]{1,0:T(8,128)(2,1)S(1)}, bf16[32,1024]{1,0:T(8,128)(2,1)S(1)}, u32[]{:S(2)}, u32[]{:S(2)}) collective-permute-start(bf16[32,1024]{1,0:T(8,128)(2,1)S(1)} %get-tuple-element.44), channel_id=1, source_target_pairs={{0,12},{2,14},{4,8},{6,10},{8,4},{10,6},{12,0},{14,2},{1,13},{3,15... | collective-permute-start | bytes 196616 | tf_op jit(solution)/shard_map/ppermute | solution.py:444
  43.9 1.3 %collective-permute-start.5 = (bf16[32,512]{1,0:T(8,128)(2,1)S(1)}, bf16[32,512]{1,0:T(8,128)(2,1)S(1)}, u32[]{:S(2)}, u32[]{:S(2)}) collective-permute-start(bf16[32,512]{1,0:T(8,128)(2,1)S(1)} %get-tuple-element.47), channel_id=1, source_target_pairs={{0,1},{1,0},{2,3},{3,2},{4,5},{5,4},{6,7},{7,6},{8,9},{9,8},{10,11... | collective-permute-start | bytes 98312 | tf_op jit(solution)/shard_map/ppermute | solution.py:412
  46.6 18.5 %copy-start.1 = (bf16[1024,2048]{1,0:T(8,128)(2,1)S(1)}, bf16[1024,2048]{1,0:T(8,128)(2,1)}, u32[]{:S(2)}) copy-start(bf16[1024,2048]{1,0:T(8,128)(2,1)} %expand_ref.1) | copy-start | bytes 12582916
  46.6 1.3 %collective-permute-start.6 = (f32[64,256]{1,0:T(8,128)S(1)}, f32[64,256]{1,0:T(8,128)S(1)}, u32[]{:S(2)}, u32[]{:S(2)}) collective-permute-start(f32[64,256]{1,0:T(8,128)S(1)} %shard_map.97.mine_ref), channel_id=1, source_target_pairs={{0,1},{1,0},{2,3},{3,2},{4,5},{5,4},{6,7},{7,6},{8,9},{9,8},{10,11... | collective-permute-start | bytes 196616 | tf_op jit(solution)/shard_map/ppermute | solution.py:412
  51.7 4.3 %collective-permute-start.7 = (bf16[64,512]{1,0:T(8,128)(2,1)S(1)}, bf16[64,512]{1,0:T(8,128)(2,1)S(1)}, u32[]{:S(2)}, u32[]{:S(2)}) collective-permute-start(bf16[64,512]{1,0:T(8,128)(2,1)S(1)} %get-tuple-element.49), channel_id=1, source_target_pairs={{0,2},{2,0},{4,6},{6,4},{8,10},{10,8},{12,14},{14,12},{1,3},{3,1},... | collective-permute-start | bytes 196616 | tf_op jit(solution)/shard_map/ppermute | solution.py:444
  56.0 6.2 %collective-permute-start.10 = (bf16[64,512]{1,0:T(8,128)(2,1)S(1)}, bf16[64,512]{1,0:T(8,128)(2,1)S(1)}, u32[]{:S(2)}, u32[]{:S(2)}) collective-permute-start(bf16[64,512]{1,0:T(8,128)(2,1)S(1)} %get-tuple-element.51), channel_id=1, source_target_pairs={{0,12},{2,14},{4,8},{6,10},{8,4},{10,6},{12,0},{14,2},{1,13},{3,15... | collective-permute-start | bytes 196616 | tf_op jit(solution)/shard_map/ppermute | solution.py:444
  58.6 4.3 %collective-permute-start.8 = (bf16[64,512]{1,0:T(8,128)(2,1)S(1)}, bf16[64,512]{1,0:T(8,128)(2,1)S(1)}, u32[]{:S(2)}, u32[]{:S(2)}) collective-permute-start(bf16[64,512]{1,0:T(8,128)(2,1)S(1)} %get-tuple-element.51), channel_id=1, source_target_pairs={{0,4},{2,6},{4,0},{6,2},{8,12},{10,14},{12,8},{14,10},{1,5},{3,7},... | collective-permute-start | bytes 196616 | tf_op jit(solution)/shard_map/ppermute | solution.py:444
  58.6 5.2 %collective-permute-start.9 = (bf16[64,512]{1,0:T(8,128)(2,1)S(1)}, bf16[64,512]{1,0:T(8,128)(2,1)S(1)}, u32[]{:S(2)}, u32[]{:S(2)}) collective-permute-start(bf16[64,512]{1,0:T(8,128)(2,1)S(1)} %get-tuple-element.51), channel_id=1, source_target_pairs={{0,8},{2,10},{4,12},{6,14},{8,0},{10,2},{12,4},{14,6},{1,9},{3,11}... | collective-permute-start | bytes 196616 | tf_op jit(solution)/shard_map/ppermute | solution.py:444
  63.8 1.3 %collective-permute-start.11 = (bf16[32,512]{1,0:T(8,128)(2,1)S(1)}, bf16[32,512]{1,0:T(8,128)(2,1)S(1)}, u32[]{:S(2)}, u32[]{:S(2)}) collective-permute-start(bf16[32,512]{1,0:T(8,128)(2,1)S(1)} %get-tuple-element.53), channel_id=1, source_target_pairs={{0,1},{1,0},{2,3},{3,2},{4,5},{5,4},{6,7},{7,6},{8,9},{9,8},{10,11... | collective-permute-start | bytes 98312 | tf_op jit(solution)/shard_map/ppermute | solution.py:412
  67.9 4.3 %collective-permute-start.12 = (bf16[32,1024]{1,0:T(8,128)(2,1)S(1)}, bf16[32,1024]{1,0:T(8,128)(2,1)S(1)}, u32[]{:S(2)}, u32[]{:S(2)}) collective-permute-start(bf16[32,1024]{1,0:T(8,128)(2,1)S(1)} %get-tuple-element.56), channel_id=1, source_target_pairs={{0,2},{2,0},{4,6},{6,4},{8,10},{10,8},{12,14},{14,12},{1,3},{3,1},... | collective-permute-start | bytes 196616 | tf_op jit(solution)/shard_map/ppermute | solution.py:444
  72.2 4.5 %collective-permute-start.13 = (bf16[32,1024]{1,0:T(8,128)(2,1)S(1)}, bf16[32,1024]{1,0:T(8,128)(2,1)S(1)}, u32[]{:S(2)}, u32[]{:S(2)}) collective-permute-start(bf16[32,1024]{1,0:T(8,128)(2,1)S(1)} %get-tuple-element.58), channel_id=1, source_target_pairs={{0,4},{2,6},{4,0},{6,2},{8,12},{10,14},{12,8},{14,10},{1,5},{3,7},... | collective-permute-start | bytes 196616 | tf_op jit(solution)/shard_map/ppermute | solution.py:444
  74.3 6.9 %collective-permute-start.14 = (bf16[32,1024]{1,0:T(8,128)(2,1)S(1)}, bf16[32,1024]{1,0:T(8,128)(2,1)S(1)}, u32[]{:S(2)}, u32[]{:S(2)}) collective-permute-start(bf16[32,1024]{1,0:T(8,128)(2,1)S(1)} %get-tuple-element.58), channel_id=1, source_target_pairs={{0,8},{2,10},{4,12},{6,14},{8,0},{10,2},{12,4},{14,6},{1,9},{3,11}... | collective-permute-start | bytes 196616 | tf_op jit(solution)/shard_map/ppermute | solution.py:444
  74.6 6.6 %collective-permute-start.15 = (bf16[32,1024]{1,0:T(8,128)(2,1)S(1)}, bf16[32,1024]{1,0:T(8,128)(2,1)S(1)}, u32[]{:S(2)}, u32[]{:S(2)}) collective-permute-start(bf16[32,1024]{1,0:T(8,128)(2,1)S(1)} %get-tuple-element.58), channel_id=1, source_target_pairs={{0,12},{2,14},{4,8},{6,10},{8,4},{10,6},{12,0},{14,2},{1,13},{3,15... | collective-permute-start | bytes 196616 | tf_op jit(solution)/shard_map/ppermute | solution.py:444
  81.3 1.3 %collective-permute-start.16 = (bf16[32,512]{1,0:T(8,128)(2,1)S(1)}, bf16[32,512]{1,0:T(8,128)(2,1)S(1)}, u32[]{:S(2)}, u32[]{:S(2)}) collective-permute-start(bf16[32,512]{1,0:T(8,128)(2,1)S(1)} %get-tuple-element.61), channel_id=1, source_target_pairs={{0,1},{1,0},{2,3},{3,2},{4,5},{5,4},{6,7},{7,6},{8,9},{9,8},{10,11... | collective-permute-start | bytes 98312 | tf_op jit(solution)/shard_map/ppermute | solution.py:412
  84.8 1.3 %collective-permute-start.17 = (f32[64,256]{1,0:T(8,128)S(1)}, f32[64,256]{1,0:T(8,128)S(1)}, u32[]{:S(2)}, u32[]{:S(2)}) collective-permute-start(f32[64,256]{1,0:T(8,128)S(1)} %shard_map.105.mine_ref), channel_id=1, source_target_pairs={{0,1},{1,0},{2,3},{3,2},{4,5},{5,4},{6,7},{7,6},{8,9},{9,8},{10,11... | collective-permute-start | bytes 196616 | tf_op jit(solution)/shard_map/ppermute | solution.py:412
  86.1 16.4 %copy-start = (bf16[2048,1024]{1,0:T(8,128)(2,1)S(1)}, bf16[2048,1024]{1,0:T(8,128)(2,1)}, u32[]{:S(2)}) copy-start(bf16[2048,1024]{1,0:T(8,128)(2,1)} %merge_ref.3) | copy-start | bytes 12582916
  88.4 20.6 %copy-start.3 = (bf16[27,32,32]{2,1,0:T(8,128)(2,1)S(1)}, bf16[27,32,32]{2,1,0:T(8,128)(2,1)}, u32[]{:S(2)}) copy-start(bf16[27,32,32]{2,1,0:T(8,128)(2,1)} %weight_ref.11) | copy-start | bytes 165892
  88.4 4.3 %collective-permute-start.18 = (bf16[64,512]{1,0:T(8,128)(2,1)S(1)}, bf16[64,512]{1,0:T(8,128)(2,1)S(1)}, u32[]{:S(2)}, u32[]{:S(2)}) collective-permute-start(bf16[64,512]{1,0:T(8,128)(2,1)S(1)} %get-tuple-element.64), channel_id=1, source_target_pairs={{0,2},{2,0},{4,6},{6,4},{8,10},{10,8},{12,14},{14,12},{1,3},{3,1},... | collective-permute-start | bytes 196616 | tf_op jit(solution)/shard_map/ppermute | solution.py:444
  92.7 4.6 %collective-permute-start.19 = (bf16[64,512]{1,0:T(8,128)(2,1)S(1)}, bf16[64,512]{1,0:T(8,128)(2,1)S(1)}, u32[]{:S(2)}, u32[]{:S(2)}) collective-permute-start(bf16[64,512]{1,0:T(8,128)(2,1)S(1)} %get-tuple-element.66), channel_id=1, source_target_pairs={{0,4},{2,6},{4,0},{6,2},{8,12},{10,14},{12,8},{14,10},{1,5},{3,7},... | collective-permute-start | bytes 196616 | tf_op jit(solution)/shard_map/ppermute | solution.py:444
  94.0 7.1 %collective-permute-start.20 = (bf16[64,512]{1,0:T(8,128)(2,1)S(1)}, bf16[64,512]{1,0:T(8,128)(2,1)S(1)}, u32[]{:S(2)}, u32[]{:S(2)}) collective-permute-start(bf16[64,512]{1,0:T(8,128)(2,1)S(1)} %get-tuple-element.66), channel_id=1, source_target_pairs={{0,8},{2,10},{4,12},{6,14},{8,0},{10,2},{12,4},{14,6},{1,9},{3,11}... | collective-permute-start | bytes 196616 | tf_op jit(solution)/shard_map/ppermute | solution.py:444
  95.0 6.2 %collective-permute-start.21 = (bf16[64,512]{1,0:T(8,128)(2,1)S(1)}, bf16[64,512]{1,0:T(8,128)(2,1)S(1)}, u32[]{:S(2)}, u32[]{:S(2)}) collective-permute-start(bf16[64,512]{1,0:T(8,128)(2,1)S(1)} %get-tuple-element.66), channel_id=1, source_target_pairs={{0,12},{2,14},{4,8},{6,10},{8,4},{10,6},{12,0},{14,2},{1,13},{3,15... | collective-permute-start | bytes 196616 | tf_op jit(solution)/shard_map/ppermute | solution.py:444
  101.2 1.3 %collective-permute-start.22 = (bf16[32,512]{1,0:T(8,128)(2,1)S(1)}, bf16[32,512]{1,0:T(8,128)(2,1)S(1)}, u32[]{:S(2)}, u32[]{:S(2)}) collective-permute-start(bf16[32,512]{1,0:T(8,128)(2,1)S(1)} %get-tuple-element.68), channel_id=1, source_target_pairs={{0,1},{1,0},{2,3},{3,2},{4,5},{5,4},{6,7},{7,6},{8,9},{9,8},{10,11... | collective-permute-start | bytes 98312 | tf_op jit(solution)/shard_map/ppermute | solution.py:412
  104.6 13.6 %all-to-all-start.1 = ((bf16[8,64,256]{2,1,0:T(8,128)(2,1)}), bf16[8,64,256]{2,1,0:T(8,128)(2,1)S(1)}, u32[]{:S(2)}, u32[]{:S(2)}) async-start(bf16[8,64,256]{2,1,0:T(8,128)(2,1)} %shard_map.109), calls=%async_computation.1 | async-start | bytes 524288 | tf_op jit(solution)/shard_map/all_to_all | solution.py:472
  118.5 1.4 %collective-permute-start.23 = (bf16[256,256]{1,0:T(8,128)(2,1)S(1)}, bf16[256,256]{1,0:T(8,128)(2,1)S(1)}, u32[]{:S(2)}, u32[]{:S(2)}) collective-permute-start(bf16[256,256]{1,0:T(8,128)(2,1)S(1)} %get-tuple-element.72), channel_id=1, source_target_pairs={{0,1},{1,0},{2,3},{3,2},{4,5},{5,4},{6,7},{7,6},{8,9},{9,8},{10,11... | collective-permute-start | bytes 393224 | tf_op jit(solution)/shard_map/ppermute | solution.py:412
  (6 other events, 19.9 us)

commit v5 on v4

--- a/solution.py
+++ b/solution.py
@@ -175,6 +175,18 @@
     out_ref[960:1024, :] = jnp.zeros((64, 768), BF)
 
 
+def band_and_bias_kernel(step_ref, weight_ref, table_ref, out_ref, bias_ref, rows_ref, sem):
+    step = step_ref[0]
+    group = pl.ds(pl.multiple_of(step // 8 * 8, 8), 8)
+    fetch = pltpu.make_async_copy(table_ref.at[group], rows_ref, sem)
+    fetch.start()
+    band_kernel(weight_ref, out_ref, back=False)
+    fetch.wait()
+    rows = rows_ref[...]
+    chosen = lax.broadcasted_iota(jnp.int32, rows.shape, 0) == step % 8
+    bias_ref[...] = jnp.sum(jnp.where(chosen, rows, jnp.zeros_like(rows)), axis=0, keepdims=True)
+
+
 def banded(weight, back):
     (out,) = kernel_call(
         functools.partial(band_kernel, back=back), (), (weight,), [shape_of((1024, 768), BF)], cost=BESIDE
@@ -182,13 +194,31 @@
     return out
 
 
-def pack_kernel(n_ref, w_ref, step_ref, field_ref, cot_ref, out_ref):
+def lane_place(d):
+    row = lax.broadcasted_iota(jnp.int32, (32, 256), 0)
+    lane = lax.broadcasted_iota(jnp.int32, (32, 256), 1)
+    return (lane == row + 32 * d).astype(BF)
+
+
+def to_rows(field_ref, cells_ref):
+    cells_ref[...] = field_ref[...].astype(F32).reshape(2048, 32)
+    rows = None
+    for d in range(8):
+        part = nn_dot(cells_ref[pl.ds(d, 256, stride=8), :].astype(BF), lane_place(d))
+        rows = part if rows is None else rows + part
+    return rows.astype(BF)
+
+
+def pack_kernel(n_ref, w_ref, step_ref, field_ref, cot_ref, out_ref, cells_ref, other_ref):
     del n_ref, w_ref, step_ref
+    field = to_rows(field_ref, cells_ref)
+    cot = to_rows(cot_ref, other_ref)
     for a in range(8):
-        out_ref[a, 0:32] = field_ref[(a + 7) % 8]
-        out_ref[a, 32:64] = field_ref[a]
-        out_ref[a, 64:96] = field_ref[(a + 1) % 8]
-        out_ref[a, 96:128] = cot_ref[a]
+        before, after = (a + 7) % 8, (a + 1) % 8
+        out_ref[a, 0:32] = field[32 * before : 32 * before + 32]
+        out_ref[a, 32:64] = field[32 * a : 32 * a + 32]
+        out_ref[a, 64:96] = field[32 * after : 32 * after + 32]
+        out_ref[a, 96:128] = cot[32 * a : 32 * a + 32]
 
 
 def arrived_planes(w, arrived_ref):
@@ -207,8 +237,9 @@
     return grown[0:256], grown[32:288], grown[64:320]
 
 
-def side_kernel(w_ref, planes_ref, band_ref, own_ref, send_ref, *, planes_of):
+def side_kernel(w_ref, planes_ref, band_ref, *refs, planes_of):
     del band_ref
+    own_ref, send_ref = refs[-2:]
     planes = planes_of(w_ref[0], planes_ref)
     source = lax.broadcasted_iota(jnp.int32, (256, 256), 0)
     target = lax.broadcasted_iota(jnp.int32, (256, 256), 1)
@@ -227,10 +258,10 @@
     send_ref[...] = jnp.where(own, zero, sides).astype(BF)
 
 
-def side_call(w, planes, band, planes_of):
+def side_call(w, planes, band, planes_of, rest=()):
     shape = shape_of((256, 256), BF)
     return kernel_call(
-        functools.partial(side_kernel, planes_of=planes_of), (w,), (planes, band), [shape, shape]
+        functools.partial(side_kernel, planes_of=planes_of), (w,), (planes, band), [shape, shape], rest=rest
     )
 
 
@@ -253,15 +284,9 @@
 
 
 def merge_kernel(
-    n_ref, w_ref, planes_ref, own_ref, got_ref, band_ref, merge_ref, pre_ref, act_ref, sum_ref, sum_b_ref,
-    rows_ref, weight_ref, sems
+    n_ref, w_ref, planes_ref, own_ref, got_ref, band_ref, merge_ref, pre_ref, act_ref, sum_ref, sum_b_ref, rows_ref
 ):
     n = n_ref[0]
-    copies = []
-    for b in range(8):
-        place = pl.ds(256 * b, 256)
-        copies.append(pltpu.make_async_copy(merge_ref.at[place], weight_ref.at[place], sems.at[b]))
-        copies[b].start()
     planes = arrived_planes(w_ref[0], planes_ref)
     wide_rows = fine_sum(n, planes, own_ref, got_ref, band_ref)
     rows_ref[0] = wide_rows[:, :128]
@@ -272,8 +297,7 @@
         pre_ref[b] = pre
         act = (pre * jax.nn.sigmoid(pre)).astype(BF)
         act_ref[b] = act
-        copies[b].wait()
-        part = nn_dot(act, weight_ref[256 * b : 256 * b + 256])
+        part = nn_dot(act, merge_ref[256 * b : 256 * b + 256])
         total = part if total is None else total + part
     sum_ref[...] = total
     sum_b_ref[...] = total.astype(BF)
@@ -287,9 +311,12 @@
         cot_ref[b] = jnp.concatenate([cell_rows(rows_ref.at[h], b) for h in range(2)], axis=1).astype(BF)
 
 
-def final_kernel(n_ref, w_ref, planes_ref, own_ref, got_ref, band_ref, out_ref):
+def final_kernel(n_ref, w_ref, planes_ref, own_ref, got_ref, band_ref, out_ref, cells_ref):
     planes = returned_planes(w_ref[0], planes_ref)
-    out_ref[...] = fine_sum(n_ref[0], planes, own_ref, got_ref, band_ref).astype(BF)
+    rows = fine_sum(n_ref[0], planes, own_ref, got_ref, band_ref).astype(BF)
+    for d in range(8):
+        cells_ref[pl.ds(d, 256, stride=8), :] = nt_dot(rows, lane_place(d))
+    out_ref[...] = cells_ref[...].astype(BF).reshape(8, 16, 16, 32)
 
 
 def put_columns(cols_ref, cells):
@@ -339,17 +366,9 @@
 
 
 def inner_forward_kernel(
-    n_ref, step_ref, mine_ref, got_ref, weight_ref, table_ref, gate_ref, sum_ref, sum_b_ref, cols_ref, bias_ref, sem
+    n_ref, mine_ref, got_ref, bias_ref, weight_ref, gate_ref, sum_ref, sum_b_ref, cols_ref
 ):
-    step = step_ref[0]
-    group = pl.ds(pl.multiple_of(step // 8 * 8, 8), 8)
-    fetch = pltpu.make_async_copy(table_ref.at[group], bias_ref, sem)
-    fetch.start()
-    fetch.wait()
-    rows = bias_ref[...]
-    chosen = lax.broadcasted_iota(jnp.int32, rows.shape, 0) == step % 8
-    bias = jnp.sum(jnp.where(chosen, rows, jnp.zeros_like(rows)), axis=0, keepdims=True)
-    gate = mine_ref[...] + got_ref[...] + bias
+    gate = mine_ref[...] + got_ref[...] + bias_ref[...]
     gate_ref[...] = gate
     put_columns(cols_ref, gate * jax.nn.sigmoid(gate))
     total = conv_sum(cols_ref, feature_columns(n_ref[0], weight_ref), False, nn_dot)
@@ -455,7 +474,7 @@
     cells, features = part.shape
     half_shape = shape_of((cells, features // 2), BF)
     total, mine, send = kernel_call(
-        features_kernel, (n,), terms, [shape_of(part.shape, F32), half_shape, half_shape], rest=rest
+        features_kernel, (n,), terms, [shape_of(part.shape, F32), half_shape, half_shape]
     )
     return total, mine, swap_narrow(send)
 
@@ -489,27 +508,29 @@
     w = lax.axis_index("wide").astype(jnp.int32).reshape(1)
     n = lax.axis_index("narrow").astype(jnp.int32).reshape(1)
 
-    def row_form(fine_field):
-        return fine_field.transpose(1, 2, 3, 0).reshape(8, 32, 256)
-
+    fine_cells = pltpu.VMEM((2048, 32), F32)
     (outgoing,) = kernel_call(
-        pack_kernel, (n, w, timestep), (row_form(volume), row_form(cotangent)), [shape_of((8, 128, 256), BF)]
+        pack_kernel, (n, w, timestep), (volume.transpose(1, 2, 3, 0), cotangent.transpose(1, 2, 3, 0)),
+        [shape_of((8, 128, 256), BF)], [fine_cells, fine_cells],
     )
     arrived = across_wide(outgoing)
-    band = banded(fine_weight, False)
-    sides, sent = side_call(w, arrived, band, arrived_planes)
+    band, bias = kernel_call(
+        band_and_bias_kernel, (timestep,), (fine_weight,),
+        [shape_of((1024, 768), BF), shape_of((1, hidden), F32)],
+        [pltpu.VMEM((8, hidden), F32), pltpu.SemaphoreType.DMA], cost=BESIDE, rest=(step_table,),
+    )
+    sides, sent = side_call(w, arrived, band, arrived_planes, (merge_weight,))
     fine_rows = pltpu.VMEM((2, 256, 128), F32)
     sum_shapes = [shape_of((32, features), F32), shape_of((32, features), BF)]
     pre_act, act, merged_part, merged_part_b = kernel_call(
         merge_kernel,
         (n, w),
-        (arrived, sides, swap_narrow(sent), band),
+        (arrived, sides, swap_narrow(sent), band, merge_weight),
         [shape_of((8, 32, 256), F32), shape_of((8, 32, 256), BF)] + sum_shapes,
-        [fine_rows, pltpu.VMEM(merge_weight.shape, BF), pltpu.SemaphoreType.DMA((8,))],
-        rest=(merge_weight,),
+        [fine_rows],
     )
     (cot,) = kernel_call(cot_kernel, (), (arrived,), [shape_of((8, 32, 256), BF)], [fine_rows])
-    merged, mine, got = to_feature_halves(n, merged_part, merged_part_b, (hidden_weight,))
+    merged, mine, got = to_feature_halves(n, merged_part, merged_part_b, (hidden_weight, output_weight))
 
     gate_shape = shape_of((64, hidden), F32)
     half_shapes = [shape_of((64, half), F32), shape_of((64, half), BF)]
@@ -522,8 +543,7 @@
     )
     gate_pre, branch_part, branch_part_b = kernel_call(
         inner_forward_kernel,
-        (n, timestep), (gate_part, swap_narrow(gate_part), output_weight), [gate_shape] + half_shapes,
-        inner_columns + [pltpu.VMEM((8, hidden), F32), pltpu.SemaphoreType.DMA], rest=(step_table,),
+        (n,), (gate_part, swap_narrow(gate_part), bias, output_weight), [gate_shape] + half_shapes, inner_columns,
     )
     mine, got = to_cell_halves(n, branch_part, branch_part_b)
     grad_comb, res_part, res_part_b = kernel_call(
@@ -553,9 +573,9 @@
     (result,) = kernel_call(
         final_kernel,
         (n, w), (returned, sides, swap_narrow(sent), band),
-        [shape_of((256, 256), BF)],
-    )
-    return result.reshape(8, 16, 16, 32).transpose(3, 0, 1, 2)
+        [shape_of((8, 16, 16, 32), BF)], [fine_cells],
+    )
+    return result.transpose(3, 0, 1, 2)
 
 
 def shards(

time: 122 us -> 119 us (0.975)
  local copies, waits for them, and re-layouts: 6.57 us -> 3.54 us
    reshape x3 -> x0, local copies, waits for them, and re-layouts: 3.91 us -> none  [the longest x2 2.88 us: row_form(): return fine_field.transpose(1, 2, 3, 0).reshape(8, 32, 256)]
    unnamed x24 -> x28, local copies, waits for them, and re-layouts: 2.66 us -> 3.54 us
  transfers between devices with their start and end apart: 26 -> 26, of which waited for: 21 -> 23; matrix products, arithmetic and copies ran while one was open for 0% -> 0% of each run, Pallas kernels for 2% -> 2%
where the time goes in v5:
time: 119 us; the launch traced here: 118 us
  waiting for transfers between devices  56.3 us (47%)
  starting transfers between devices  36.6 us (31%)
  Pallas kernels  21 us (18%)
  local copies, waits for them, and re-layouts  3.54 us (3%)
    ppermute x16, waiting for transfers between devices, partner(): return lax.ppermute(value, 'wide', [(i, i ^ mask) for i in range(8)])  26.4 us
    ppermute x16, starting transfers between devices, partner(): return lax.ppermute(value, 'wide', [(i, i ^ mask) for i in range(8)])  24.1 us
    pallas_call x22, Pallas kernels, kernel_call(): pl.pallas_call(kernel, in_specs=[SMEM] * len(places) + [VMEM] * len(array...  21 us
    all_to_all x2, waiting for transfers between devices, across_wide(): lax.all_to_all(value, 'wide', split_axis=0, concat_axis=0, tiled=True)  20.4 us
    all_to_all x2, starting transfers between devices, across_wide(): lax.all_to_all(value, 'wide', split_axis=0, concat_axis=0, tiled=True)  11.6 us
    ppermute x8, waiting for transfers between devices, swap_narrow(): return lax.ppermute(value, 'narrow', [(0, 1), (1, 0)])  9.55 us
    unnamed x28, local copies, waits for them, and re-layouts  3.54 us
  transfers between devices with their start and end apart: 26, of which 23 were waited for; matrix products, arithmetic and copies ran while one was open for 0% of the time, Pallas kernels for 2%

profile of v5, /device:TPU:0, one launch (start us, length us, event | category | flops | bytes accessed | tf_op | source)
XLA Modules:
  0.0 118.4 jit_solution(14061338020167978506)
XLA Ops:
  2.7 1.5 %shard_map.91 = bf16[8,128,256]{2,1,0:T(8,128)(2,1)} custom-call(s32[1]{0:T(128)} %bitcast.n_ref, s32[1]{0:T(128)} %bitcast.1.w_ref, s32[1]{0:T(128)S(6)} %copy.10.step_ref, bf16[8,16,16,32]{3,2,1,0:T(8,128)(2,1)S(1)} %bitcast.9, bf16[8,16,16,32]{3,2,1,0:T(8,128)(2,1)S(1)} %bitcast.10), custom_call_target="tpu_custom_call" | custom-call | tf_op jit(solution)/shard_map/pallas_call | solution.py:139
  4.2 7.3 %all-to-all-start = ((bf16[8,128,256]{2,1,0:T(8,128)(2,1)}), bf16[8,128,256]{2,1,0:T(8,128)(2,1)S(1)}, u32[]{:S(2)}, u32[]{:S(2)}) async-start(bf16[8,128,256]{2,1,0:T(8,128)(2,1)} %shard_map.91), calls=%async_computation | async-start | bytes 1048576 | tf_op jit(solution)/shard_map/all_to_all | solution.py:491
  13.4 12.6 %all-to-all-done.planes_ref = bf16[8,128,256]{2,1,0:T(8,128)(2,1)S(1)} async-done(((bf16[8,128,256]{2,1,0:T(8,128)(2,1)}), bf16[8,128,256]{2,1,0:T(8,128)(2,1)S(1)}, u32[]{:S(2)}, u32[]{:S(2)}) %all-to-all-start) | async-done | bytes 524320 | tf_op jit(solution)/shard_map/all_to_all | solution.py:491
  28.2 2.1 %shard_map.94 = (f32[8,32,256]{2,1,0:T(8,128)S(1)}, bf16[8,32,256]{2,1,0:T(8,128)(2,1)S(1)}, f32[32,1024]{1,0:T(8,128)S(1)}, bf16[32,1024]{1,0:T(8,128)(2,1)S(1)}) custom-call(s32[1]{0:T(128)} %bitcast.n_ref, s32[1]{0:T(128)} %bitcast.1.w_ref, bf16[8,128,256]{2,1,0:T(8,128)(2,1)S(1)} %all-to-all-done.planes_ref, ...), custom_call_target="tpu_custom_call" | custom-call | tf_op jit(solution)/shard_map/pallas_call | solution.py:139
  30.3 1.5 %collective-permute-start.1 = (bf16[32,1024]{1,0:T(8,128)(2,1)S(1)}, bf16[32,1024]{1,0:T(8,128)(2,1)S(1)}, u32[]{:S(2)}, u32[]{:S(2)}) collective-permute-start(bf16[32,1024]{1,0:T(8,128)(2,1)S(1)} %get-tuple-element.45), channel_id=1, source_target_pairs={{0,2},{2,0},{4,6},{6,4},{8,10},{10,8},{12,14},{14,12},{1,3},{3,1},... | collective-permute-start | bytes 196616 | tf_op jit(solution)/shard_map/ppermute | solution.py:463
  31.8 2.8 %collective-permute-done.1.got_ref = bf16[32,1024]{1,0:T(8,128)(2,1)S(1)} collective-permute-done((bf16[32,1024]{1,0:T(8,128)(2,1)S(1)}, bf16[32,1024]{1,0:T(8,128)(2,1)S(1)}, u32[]{:S(2)}, u32[]{:S(2)}) %collective-permute-start.1) | collective-permute-done | bytes 65568 | tf_op jit(solution)/shard_map/ppermute | solution.py:463
  36.5 2.6 %collective-permute-start.4 = (bf16[32,1024]{1,0:T(8,128)(2,1)S(1)}, bf16[32,1024]{1,0:T(8,128)(2,1)S(1)}, u32[]{:S(2)}, u32[]{:S(2)}) collective-permute-start(bf16[32,1024]{1,0:T(8,128)(2,1)S(1)} %get-tuple-element.47), channel_id=1, source_target_pairs={{0,12},{2,14},{4,8},{6,10},{8,4},{10,6},{12,0},{14,2},{1,13},{3,15... | collective-permute-start | bytes 196616 | tf_op jit(solution)/shard_map/ppermute | solution.py:463
  39.1 1.6 %collective-permute-done.3.two_ref = bf16[32,1024]{1,0:T(8,128)(2,1)S(1)} collective-permute-done((bf16[32,1024]{1,0:T(8,128)(2,1)S(1)}, bf16[32,1024]{1,0:T(8,128)(2,1)S(1)}, u32[]{:S(2)}, u32[]{:S(2)}) %collective-permute-start.3) | collective-permute-done | bytes 65568 | tf_op jit(solution)/shard_map/ppermute | solution.py:463
  40.7 1.9 %collective-permute-done.4.three_ref = bf16[32,1024]{1,0:T(8,128)(2,1)S(1)} collective-permute-done((bf16[32,1024]{1,0:T(8,128)(2,1)S(1)}, bf16[32,1024]{1,0:T(8,128)(2,1)S(1)}, u32[]{:S(2)}, u32[]{:S(2)}) %collective-permute-start.4) | collective-permute-done | bytes 65568 | tf_op jit(solution)/shard_map/ppermute | solution.py:463
  43.9 1.4 %shard_map.97.mine_ref = f32[64,256]{1,0:T(8,128)S(1)} custom-call(s32[1]{0:T(128)} %bitcast.n_ref, bf16[32,512]{1,0:T(8,128)(2,1)S(1)} %get-tuple-element.49.mine_ref, bf16[32,512]{1,0:T(8,128)(2,1)S(1)} %collective-permute-done.5.got_ref, bf16[27,1024,256]{2,1,0:T(8,128)(2,1)S(1)} %bitcast.8), custom_call_target="tpu_custom_call" | custom-call | tf_op jit(solution)/shard_map/pallas_call | solution.py:139
  48.0 1.8 %collective-permute-start.7 = (bf16[64,512]{1,0:T(8,128)(2,1)S(1)}, bf16[64,512]{1,0:T(8,128)(2,1)S(1)}, u32[]{:S(2)}, u32[]{:S(2)}) collective-permute-start(bf16[64,512]{1,0:T(8,128)(2,1)S(1)} %get-tuple-element.53), channel_id=1, source_target_pairs={{0,2},{2,0},{4,6},{6,4},{8,10},{10,8},{12,14},{14,12},{1,3},{3,1},... | collective-permute-start | bytes 196616 | tf_op jit(solution)/shard_map/ppermute | solution.py:463
  49.8 2.6 %collective-permute-done.7.got_ref = bf16[64,512]{1,0:T(8,128)(2,1)S(1)} collective-permute-done((bf16[64,512]{1,0:T(8,128)(2,1)S(1)}, bf16[64,512]{1,0:T(8,128)(2,1)S(1)}, u32[]{:S(2)}, u32[]{:S(2)}) %collective-permute-start.7) | collective-permute-done | bytes 65568 | tf_op jit(solution)/shard_map/ppermute | solution.py:463
  52.4 2.7 %collective-permute-start.10 = (bf16[64,512]{1,0:T(8,128)(2,1)S(1)}, bf16[64,512]{1,0:T(8,128)(2,1)S(1)}, u32[]{:S(2)}, u32[]{:S(2)}) collective-permute-start(bf16[64,512]{1,0:T(8,128)(2,1)S(1)} %get-tuple-element.55), channel_id=1, source_target_pairs={{0,12},{2,14},{4,8},{6,10},{8,4},{10,6},{12,0},{14,2},{1,13},{3,15... | collective-permute-start | bytes 196616 | tf_op jit(solution)/shard_map/ppermute | solution.py:463
  55.0 1.8 %collective-permute-start.9 = (bf16[64,512]{1,0:T(8,128)(2,1)S(1)}, bf16[64,512]{1,0:T(8,128)(2,1)S(1)}, u32[]{:S(2)}, u32[]{:S(2)}) collective-permute-start(bf16[64,512]{1,0:T(8,128)(2,1)S(1)} %get-tuple-element.55), channel_id=1, source_target_pairs={{0,8},{2,10},{4,12},{6,14},{8,0},{10,2},{12,4},{14,6},{1,9},{3,11}... | collective-permute-start | bytes 196616 | tf_op jit(solution)/shard_map/ppermute | solution.py:463
  56.8 1.9 %collective-permute-done.10.three_ref = bf16[64,512]{1,0:T(8,128)(2,1)S(1)} collective-permute-done((bf16[64,512]{1,0:T(8,128)(2,1)S(1)}, bf16[64,512]{1,0:T(8,128)(2,1)S(1)}, u32[]{:S(2)}, u32[]{:S(2)}) %collective-permute-start.10) | collective-permute-done | bytes 65568 | tf_op jit(solution)/shard_map/ppermute | solution.py:463
  61.7 2.7 %shard_map.102 = (bf16[8,32,256]{2,1,0:T(8,128)(2,1)S(1)}, f32[32,1024]{1,0:T(8,128)S(1)}, bf16[32,1024]{1,0:T(8,128)(2,1)S(1)}) custom-call(s32[1]{0:T(128)} %bitcast.n_ref, f32[32,1024]{1,0:T(8,128)S(1)} %get-tuple-element.48.merged_ref, f32[32,512]{1,0:T(8,128)S(1)} %get-tuple-element.56.mine_ref, bf16[32,512]{1,0:T(8,128)(2,1)S(1)} %collective-permute-done.11.got_ref, ...), custom_call_target="tpu_custom_call" | custom-call | tf_op jit(solution)/shard_map/pallas_call | solution.py:139
  64.4 1.5 %collective-permute-start.12 = (bf16[32,1024]{1,0:T(8,128)(2,1)S(1)}, bf16[32,1024]{1,0:T(8,128)(2,1)S(1)}, u32[]{:S(2)}, u32[]{:S(2)}) collective-permute-start(bf16[32,1024]{1,0:T(8,128)(2,1)S(1)} %get-tuple-element.60), channel_id=1, source_target_pairs={{0,2},{2,0},{4,6},{6,4},{8,10},{10,8},{12,14},{14,12},{1,3},{3,1},... | collective-permute-start | bytes 196616 | tf_op jit(solution)/shard_map/ppermute | solution.py:463
  65.9 2.8 %collective-permute-done.12.got_ref = bf16[32,1024]{1,0:T(8,128)(2,1)S(1)} collective-permute-done((bf16[32,1024]{1,0:T(8,128)(2,1)S(1)}, bf16[32,1024]{1,0:T(8,128)(2,1)S(1)}, u32[]{:S(2)}, u32[]{:S(2)}) %collective-permute-start.12) | collective-permute-done | bytes 65568 | tf_op jit(solution)/shard_map/ppermute | solution.py:463
  68.7 1.9 %collective-permute-start.13 = (bf16[32,1024]{1,0:T(8,128)(2,1)S(1)}, bf16[32,1024]{1,0:T(8,128)(2,1)S(1)}, u32[]{:S(2)}, u32[]{:S(2)}) collective-permute-start(bf16[32,1024]{1,0:T(8,128)(2,1)S(1)} %get-tuple-element.62), channel_id=1, source_target_pairs={{0,4},{2,6},{4,0},{6,2},{8,12},{10,14},{12,8},{14,10},{1,5},{3,7},... | collective-permute-start | bytes 196616 | tf_op jit(solution)/shard_map/ppermute | solution.py:463
  71.0 2.2 %collective-permute-start.15 = (bf16[32,1024]{1,0:T(8,128)(2,1)S(1)}, bf16[32,1024]{1,0:T(8,128)(2,1)S(1)}, u32[]{:S(2)}, u32[]{:S(2)}) collective-permute-start(bf16[32,1024]{1,0:T(8,128)(2,1)S(1)} %get-tuple-element.62), channel_id=1, source_target_pairs={{0,12},{2,14},{4,8},{6,10},{8,4},{10,6},{12,0},{14,2},{1,13},{3,15... | collective-permute-start | bytes 196616 | tf_op jit(solution)/shard_map/ppermute | solution.py:463
  73.2 4.4 %collective-permute-done.14.two_ref = bf16[32,1024]{1,0:T(8,128)(2,1)S(1)} collective-permute-done((bf16[32,1024]{1,0:T(8,128)(2,1)S(1)}, bf16[32,1024]{1,0:T(8,128)(2,1)S(1)}, u32[]{:S(2)}, u32[]{:S(2)}) %collective-permute-start.14) | collective-permute-done | bytes 65568 | tf_op jit(solution)/shard_map/ppermute | solution.py:463
  78.9 2.3 %shard_map.105.mine_ref = f32[64,256]{1,0:T(8,128)S(1)} custom-call(s32[1]{0:T(128)} %bitcast.n_ref, bf16[32,512]{1,0:T(8,128)(2,1)S(1)} %get-tuple-element.64.mine_ref, bf16[32,512]{1,0:T(8,128)(2,1)S(1)} %collective-permute-done.16.got_ref, bf16[27,256,1024]{2,1,0:T(8,128)(2,1)S(1)} %bitcast.6), custom_call_target="tpu_custom_call" | custom-call | tf_op jit(solution)/shard_map/pallas_call | solution.py:139
  82.5 2.2 %shard_map.106 = (f32[64,512]{1,0:T(8,128)S(1)}, bf16[64,512]{1,0:T(8,128)(2,1)S(1)}) custom-call(s32[1]{0:T(128)} %bitcast.n_ref, f32[64,256]{1,0:T(8,128)S(1)} %shard_map.105.mine_ref, f32[64,256]{1,0:T(8,128)S(1)} %collective-permute-done.17.got_ref, f32[64,256]{1,0:T(8,128)S(1)} %get-tuple-element.66.gate_ref, bf16[27,1024,256]{2,1,0:T(8,128)(2,1)S(1)} %bitcast.8), custom_call_target="tpu_custom_call" | custom-call | tf_op jit(solution)/shard_map/pallas_call | solution.py:139
  84.8 1.5 %collective-permute-start.18 = (bf16[64,512]{1,0:T(8,128)(2,1)S(1)}, bf16[64,512]{1,0:T(8,128)(2,1)S(1)}, u32[]{:S(2)}, u32[]{:S(2)}) collective-permute-start(bf16[64,512]{1,0:T(8,128)(2,1)S(1)} %get-tuple-element.68), channel_id=1, source_target_pairs={{0,2},{2,0},{4,6},{6,4},{8,10},{10,8},{12,14},{14,12},{1,3},{3,1},... | collective-permute-start | bytes 196616 | tf_op jit(solution)/shard_map/ppermute | solution.py:463
  86.3 2.8 %collective-permute-done.18.got_ref = bf16[64,512]{1,0:T(8,128)(2,1)S(1)} collective-permute-done((bf16[64,512]{1,0:T(8,128)(2,1)S(1)}, bf16[64,512]{1,0:T(8,128)(2,1)S(1)}, u32[]{:S(2)}, u32[]{:S(2)}) %collective-permute-start.18) | collective-permute-done | bytes 65568 | tf_op jit(solution)/shard_map/ppermute | solution.py:463
  91.4 2.1 %collective-permute-start.21 = (bf16[64,512]{1,0:T(8,128)(2,1)S(1)}, bf16[64,512]{1,0:T(8,128)(2,1)S(1)}, u32[]{:S(2)}, u32[]{:S(2)}) collective-permute-start(bf16[64,512]{1,0:T(8,128)(2,1)S(1)} %get-tuple-element.70), channel_id=1, source_target_pairs={{0,12},{2,14},{4,8},{6,10},{8,4},{10,6},{12,0},{14,2},{1,13},{3,15... | collective-permute-start | bytes 196616 | tf_op jit(solution)/shard_map/ppermute | solution.py:463
  93.7 3.2 %collective-permute-done.20.two_ref = bf16[64,512]{1,0:T(8,128)(2,1)S(1)} collective-permute-done((bf16[64,512]{1,0:T(8,128)(2,1)S(1)}, bf16[64,512]{1,0:T(8,128)(2,1)S(1)}, u32[]{:S(2)}, u32[]{:S(2)}) %collective-permute-start.20) | collective-permute-done | bytes 65568 | tf_op jit(solution)/shard_map/ppermute | solution.py:463
  98.9 2.1 %shard_map.109 = bf16[8,64,256]{2,1,0:T(8,128)(2,1)} custom-call(s32[1]{0:T(128)} %bitcast.n_ref, s32[1]{0:T(128)} %bitcast.1.w_ref, f32[32,1024]{1,0:T(8,128)S(1)} %get-tuple-element.63.res_ref, f32[32,512]{1,0:T(8,128)S(1)} %get-tuple-element.71.mine_ref, bf16[32,512]{1,0:T(8,128)(2,1)S(1)} %collective-permute-done.22.got_ref, ...), custom_call_target="tpu_custom_call" | custom-call | tf_op jit(solution)/shard_map/pallas_call | solution.py:139
  101.1 4.3 %all-to-all-start.1 = ((bf16[8,64,256]{2,1,0:T(8,128)(2,1)}), bf16[8,64,256]{2,1,0:T(8,128)(2,1)S(1)}, u32[]{:S(2)}, u32[]{:S(2)}) async-start(bf16[8,64,256]{2,1,0:T(8,128)(2,1)} %shard_map.109), calls=%async_computation.1 | async-start | bytes 524288 | tf_op jit(solution)/shard_map/all_to_all | solution.py:491
  105.4 1.4 %shard_map.110.band_ref = bf16[1024,768]{1,0:T(8,128)(2,1)S(1)} custom-call(bf16[27,32,32]{2,1,0:T(8,128)(2,1)S(1)} %copy-done.3), custom_call_target="tpu_custom_call" | custom-call | bytes 33554432 | tf_op jit(solution)/shard_map/pallas_call | solution.py:139
  106.8 7.8 %all-to-all-done.1.planes_ref = bf16[8,64,256]{2,1,0:T(8,128)(2,1)S(1)} async-done(((bf16[8,64,256]{2,1,0:T(8,128)(2,1)}), bf16[8,64,256]{2,1,0:T(8,128)(2,1)S(1)}, u32[]{:S(2)}, u32[]{:S(2)}) %all-to-all-start.1) | async-done | bytes 262176 | tf_op jit(solution)/shard_map/all_to_all | solution.py:491
  116.3 2.0 %shard_map.112 = bf16[8,16,16,32]{3,2,1,0:T(8,128)(2,1)} custom-call(s32[1]{0:T(128)} %bitcast.n_ref, s32[1]{0:T(128)} %bitcast.1.w_ref, bf16[8,64,256]{2,1,0:T(8,128)(2,1)S(1)} %all-to-all-done.1.planes_ref, bf16[256,256]{1,0:T(8,128)(2,1)S(1)} %get-tuple-element.75.own_ref, bf16[256,256]{1,0:T(8,128)(2,1)S(1)} %collective-permute-done.23.got_ref, ...), custom_call_target="tpu_custom_call" | custom-call | tf_op jit(solution)/shard_map/pallas_call | solution.py:139
  (72 shorter events, 24.0 us)
Async XLA Ops:
  4.2 21.8 %all-to-all-start = ((bf16[8,128,256]{2,1,0:T(8,128)(2,1)}), bf16[8,128,256]{2,1,0:T(8,128)(2,1)S(1)}, u32[]{:S(2)}, u32[]{:S(2)}) async-start(bf16[8,128,256]{2,1,0:T(8,128)(2,1)} %shard_map.91), calls=%async_computation | async-start | bytes 1048576 | tf_op jit(solution)/shard_map/all_to_all | solution.py:491
  26.0 17.9 %slice-start.4 = ((s8[14155776]{0:T(1024)(128)(4,1)}), s8[4194304]{0:T(1024)(128)(4,1)S(1)}, s32[]{:S(2)}) async-start(s8[14155776]{0:T(1024)(128)(4,1)} %bitcast.7), calls=%async_computation.6 | async-start | bytes 8388608
  26.3 1.4 %collective-permute-start = (bf16[256,256]{1,0:T(8,128)(2,1)S(1)}, bf16[256,256]{1,0:T(8,128)(2,1)S(1)}, u32[]{:S(2)}, u32[]{:S(2)}) collective-permute-start(bf16[256,256]{1,0:T(8,128)(2,1)S(1)} %get-tuple-element.43), channel_id=1, source_target_pairs={{0,1},{1,0},{2,3},{3,2},{4,5},{5,4},{6,7},{7,6},{8,9},{9,8},{10,11... | collective-permute-start | bytes 393224 | tf_op jit(solution)/shard_map/ppermute | solution.py:431
  28.2 15.7 %slice-start.5 = ((s8[14155776]{0:T(1024)(128)(4,1)}), s8[4194304]{0:T(1024)(128)(4,1)S(1)}, s32[]{:S(2)}) async-start(s8[14155776]{0:T(1024)(128)(4,1)} %bitcast.7), calls=%async_computation.7 | async-start | bytes 8388608
  30.3 4.3 %collective-permute-start.1 = (bf16[32,1024]{1,0:T(8,128)(2,1)S(1)}, bf16[32,1024]{1,0:T(8,128)(2,1)S(1)}, u32[]{:S(2)}, u32[]{:S(2)}) collective-permute-start(bf16[32,1024]{1,0:T(8,128)(2,1)S(1)} %get-tuple-element.45), channel_id=1, source_target_pairs={{0,2},{2,0},{4,6},{6,4},{8,10},{10,8},{12,14},{14,12},{1,3},{3,1},... | collective-permute-start | bytes 196616 | tf_op jit(solution)/shard_map/ppermute | solution.py:463
  34.6 12.0 %slice-start = ((s8[14155776]{0:T(1024)(128)(4,1)}), s8[4194304]{0:T(1024)(128)(4,1)S(1)}, s32[]{:S(2)}) async-start(s8[14155776]{0:T(1024)(128)(4,1)} %bitcast.5), calls=%async_computation.2 | async-start | bytes 8388608
  34.6 12.0 %slice-start.1 = ((s8[14155776]{0:T(1024)(128)(4,1)}), s8[4194304]{0:T(1024)(128)(4,1)S(1)}, s32[]{:S(2)}) async-start(s8[14155776]{0:T(1024)(128)(4,1)} %bitcast.5), calls=%async_computation.3 | async-start | bytes 8388608
  34.7 4.5 %collective-permute-start.2 = (bf16[32,1024]{1,0:T(8,128)(2,1)S(1)}, bf16[32,1024]{1,0:T(8,128)(2,1)S(1)}, u32[]{:S(2)}, u32[]{:S(2)}) collective-permute-start(bf16[32,1024]{1,0:T(8,128)(2,1)S(1)} %get-tuple-element.47), channel_id=1, source_target_pairs={{0,4},{2,6},{4,0},{6,2},{8,12},{10,14},{12,8},{14,10},{1,5},{3,7},... | collective-permute-start | bytes 196616 | tf_op jit(solution)/shard_map/ppermute | solution.py:463
  35.5 5.3 %collective-permute-start.3 = (bf16[32,1024]{1,0:T(8,128)(2,1)S(1)}, bf16[32,1024]{1,0:T(8,128)(2,1)S(1)}, u32[]{:S(2)}, u32[]{:S(2)}) collective-permute-start(bf16[32,1024]{1,0:T(8,128)(2,1)S(1)} %get-tuple-element.47), channel_id=1, source_target_pairs={{0,8},{2,10},{4,12},{6,14},{8,0},{10,2},{12,4},{14,6},{1,9},{3,11}... | collective-permute-start | bytes 196616 | tf_op jit(solution)/shard_map/ppermute | solution.py:463
  36.5 6.1 %collective-permute-start.4 = (bf16[32,1024]{1,0:T(8,128)(2,1)S(1)}, bf16[32,1024]{1,0:T(8,128)(2,1)S(1)}, u32[]{:S(2)}, u32[]{:S(2)}) collective-permute-start(bf16[32,1024]{1,0:T(8,128)(2,1)S(1)} %get-tuple-element.47), channel_id=1, source_target_pairs={{0,12},{2,14},{4,8},{6,10},{8,4},{10,6},{12,0},{14,2},{1,13},{3,15... | collective-permute-start | bytes 196616 | tf_op jit(solution)/shard_map/ppermute | solution.py:463
  42.6 1.3 %collective-permute-start.5 = (bf16[32,512]{1,0:T(8,128)(2,1)S(1)}, bf16[32,512]{1,0:T(8,128)(2,1)S(1)}, u32[]{:S(2)}, u32[]{:S(2)}) collective-permute-start(bf16[32,512]{1,0:T(8,128)(2,1)S(1)} %get-tuple-element.50), channel_id=1, source_target_pairs={{0,1},{1,0},{2,3},{3,2},{4,5},{5,4},{6,7},{7,6},{8,9},{9,8},{10,11... | collective-permute-start | bytes 98312 | tf_op jit(solution)/shard_map/ppermute | solution.py:431
  45.3 1.3 %collective-permute-start.6 = (f32[64,256]{1,0:T(8,128)S(1)}, f32[64,256]{1,0:T(8,128)S(1)}, u32[]{:S(2)}, u32[]{:S(2)}) collective-permute-start(f32[64,256]{1,0:T(8,128)S(1)} %shard_map.97.mine_ref), channel_id=1, source_target_pairs={{0,1},{1,0},{2,3},{3,2},{4,5},{5,4},{6,7},{7,6},{8,9},{9,8},{10,11... | collective-permute-start | bytes 196616 | tf_op jit(solution)/shard_map/ppermute | solution.py:431
  46.7 15.0 %copy-start.1 = (bf16[1024,2048]{1,0:T(8,128)(2,1)S(1)}, bf16[1024,2048]{1,0:T(8,128)(2,1)}, u32[]{:S(2)}) copy-start(bf16[1024,2048]{1,0:T(8,128)(2,1)} %expand_ref.1) | copy-start | bytes 12582916
  48.0 4.3 %collective-permute-start.7 = (bf16[64,512]{1,0:T(8,128)(2,1)S(1)}, bf16[64,512]{1,0:T(8,128)(2,1)S(1)}, u32[]{:S(2)}, u32[]{:S(2)}) collective-permute-start(bf16[64,512]{1,0:T(8,128)(2,1)S(1)} %get-tuple-element.53), channel_id=1, source_target_pairs={{0,2},{2,0},{4,6},{6,4},{8,10},{10,8},{12,14},{14,12},{1,3},{3,1},... | collective-permute-start | bytes 196616 | tf_op jit(solution)/shard_map/ppermute | solution.py:463
  52.4 6.4 %collective-permute-start.10 = (bf16[64,512]{1,0:T(8,128)(2,1)S(1)}, bf16[64,512]{1,0:T(8,128)(2,1)S(1)}, u32[]{:S(2)}, u32[]{:S(2)}) collective-permute-start(bf16[64,512]{1,0:T(8,128)(2,1)S(1)} %get-tuple-element.55), channel_id=1, source_target_pairs={{0,12},{2,14},{4,8},{6,10},{8,4},{10,6},{12,0},{14,2},{1,13},{3,15... | collective-permute-start | bytes 196616 | tf_op jit(solution)/shard_map/ppermute | solution.py:463
  55.0 4.4 %collective-permute-start.8 = (bf16[64,512]{1,0:T(8,128)(2,1)S(1)}, bf16[64,512]{1,0:T(8,128)(2,1)S(1)}, u32[]{:S(2)}, u32[]{:S(2)}) collective-permute-start(bf16[64,512]{1,0:T(8,128)(2,1)S(1)} %get-tuple-element.55), channel_id=1, source_target_pairs={{0,4},{2,6},{4,0},{6,2},{8,12},{10,14},{12,8},{14,10},{1,5},{3,7},... | collective-permute-start | bytes 196616 | tf_op jit(solution)/shard_map/ppermute | solution.py:463
  55.0 5.3 %collective-permute-start.9 = (bf16[64,512]{1,0:T(8,128)(2,1)S(1)}, bf16[64,512]{1,0:T(8,128)(2,1)S(1)}, u32[]{:S(2)}, u32[]{:S(2)}) collective-permute-start(bf16[64,512]{1,0:T(8,128)(2,1)S(1)} %get-tuple-element.55), channel_id=1, source_target_pairs={{0,8},{2,10},{4,12},{6,14},{8,0},{10,2},{12,4},{14,6},{1,9},{3,11}... | collective-permute-start | bytes 196616 | tf_op jit(solution)/shard_map/ppermute | solution.py:463
  60.4 1.3 %collective-permute-start.11 = (bf16[32,512]{1,0:T(8,128)(2,1)S(1)}, bf16[32,512]{1,0:T(8,128)(2,1)S(1)}, u32[]{:S(2)}, u32[]{:S(2)}) collective-permute-start(bf16[32,512]{1,0:T(8,128)(2,1)S(1)} %get-tuple-element.57), channel_id=1, source_target_pairs={{0,1},{1,0},{2,3},{3,2},{4,5},{5,4},{6,7},{7,6},{8,9},{9,8},{10,11... | collective-permute-start | bytes 98312 | tf_op jit(solution)/shard_map/ppermute | solution.py:431
  64.4 4.3 %collective-permute-start.12 = (bf16[32,1024]{1,0:T(8,128)(2,1)S(1)}, bf16[32,1024]{1,0:T(8,128)(2,1)S(1)}, u32[]{:S(2)}, u32[]{:S(2)}) collective-permute-start(bf16[32,1024]{1,0:T(8,128)(2,1)S(1)} %get-tuple-element.60), channel_id=1, source_target_pairs={{0,2},{2,0},{4,6},{6,4},{8,10},{10,8},{12,14},{14,12},{1,3},{3,1},... | collective-permute-start | bytes 196616 | tf_op jit(solution)/shard_map/ppermute | solution.py:463
  68.7 4.5 %collective-permute-start.13 = (bf16[32,1024]{1,0:T(8,128)(2,1)S(1)}, bf16[32,1024]{1,0:T(8,128)(2,1)S(1)}, u32[]{:S(2)}, u32[]{:S(2)}) collective-permute-start(bf16[32,1024]{1,0:T(8,128)(2,1)S(1)} %get-tuple-element.62), channel_id=1, source_target_pairs={{0,4},{2,6},{4,0},{6,2},{8,12},{10,14},{12,8},{14,10},{1,5},{3,7},... | collective-permute-start | bytes 196616 | tf_op jit(solution)/shard_map/ppermute | solution.py:463
  70.7 6.9 %collective-permute-start.14 = (bf16[32,1024]{1,0:T(8,128)(2,1)S(1)}, bf16[32,1024]{1,0:T(8,128)(2,1)S(1)}, u32[]{:S(2)}, u32[]{:S(2)}) collective-permute-start(bf16[32,1024]{1,0:T(8,128)(2,1)S(1)} %get-tuple-element.62), channel_id=1, source_target_pairs={{0,8},{2,10},{4,12},{6,14},{8,0},{10,2},{12,4},{14,6},{1,9},{3,11}... | collective-permute-start | bytes 196616 | tf_op jit(solution)/shard_map/ppermute | solution.py:463
  71.0 6.7 %collective-permute-start.15 = (bf16[32,1024]{1,0:T(8,128)(2,1)S(1)}, bf16[32,1024]{1,0:T(8,128)(2,1)S(1)}, u32[]{:S(2)}, u32[]{:S(2)}) collective-permute-start(bf16[32,1024]{1,0:T(8,128)(2,1)S(1)} %get-tuple-element.62), channel_id=1, source_target_pairs={{0,12},{2,14},{4,8},{6,10},{8,4},{10,6},{12,0},{14,2},{1,13},{3,15... | collective-permute-start | bytes 196616 | tf_op jit(solution)/shard_map/ppermute | solution.py:463
  77.7 1.3 %collective-permute-start.16 = (bf16[32,512]{1,0:T(8,128)(2,1)S(1)}, bf16[32,512]{1,0:T(8,128)(2,1)S(1)}, u32[]{:S(2)}, u32[]{:S(2)}) collective-permute-start(bf16[32,512]{1,0:T(8,128)(2,1)S(1)} %get-tuple-element.65), channel_id=1, source_target_pairs={{0,1},{1,0},{2,3},{3,2},{4,5},{5,4},{6,7},{7,6},{8,9},{9,8},{10,11... | collective-permute-start | bytes 98312 | tf_op jit(solution)/shard_map/ppermute | solution.py:431
  81.2 1.3 %collective-permute-start.17 = (f32[64,256]{1,0:T(8,128)S(1)}, f32[64,256]{1,0:T(8,128)S(1)}, u32[]{:S(2)}, u32[]{:S(2)}) collective-permute-start(f32[64,256]{1,0:T(8,128)S(1)} %shard_map.105.mine_ref), channel_id=1, source_target_pairs={{0,1},{1,0},{2,3},{3,2},{4,5},{5,4},{6,7},{7,6},{8,9},{9,8},{10,11... | collective-permute-start | bytes 196616 | tf_op jit(solution)/shard_map/ppermute | solution.py:431
  84.8 20.6 %copy-start.3 = (bf16[27,32,32]{2,1,0:T(8,128)(2,1)S(1)}, bf16[27,32,32]{2,1,0:T(8,128)(2,1)}, u32[]{:S(2)}) copy-start(bf16[27,32,32]{2,1,0:T(8,128)(2,1)} %weight_ref.11) | copy-start | bytes 165892
  84.8 4.3 %collective-permute-start.18 = (bf16[64,512]{1,0:T(8,128)(2,1)S(1)}, bf16[64,512]{1,0:T(8,128)(2,1)S(1)}, u32[]{:S(2)}, u32[]{:S(2)}) collective-permute-start(bf16[64,512]{1,0:T(8,128)(2,1)S(1)} %get-tuple-element.68), channel_id=1, source_target_pairs={{0,2},{2,0},{4,6},{6,4},{8,10},{10,8},{12,14},{14,12},{1,3},{3,1},... | collective-permute-start | bytes 196616 | tf_op jit(solution)/shard_map/ppermute | solution.py:463
  89.1 4.6 %collective-permute-start.19 = (bf16[64,512]{1,0:T(8,128)(2,1)S(1)}, bf16[64,512]{1,0:T(8,128)(2,1)S(1)}, u32[]{:S(2)}, u32[]{:S(2)}) collective-permute-start(bf16[64,512]{1,0:T(8,128)(2,1)S(1)} %get-tuple-element.70), channel_id=1, source_target_pairs={{0,4},{2,6},{4,0},{6,2},{8,12},{10,14},{12,8},{14,10},{1,5},{3,7},... | collective-permute-start | bytes 196616 | tf_op jit(solution)/shard_map/ppermute | solution.py:463
  90.5 6.4 %collective-permute-start.20 = (bf16[64,512]{1,0:T(8,128)(2,1)S(1)}, bf16[64,512]{1,0:T(8,128)(2,1)S(1)}, u32[]{:S(2)}, u32[]{:S(2)}) collective-permute-start(bf16[64,512]{1,0:T(8,128)(2,1)S(1)} %get-tuple-element.70), channel_id=1, source_target_pairs={{0,8},{2,10},{4,12},{6,14},{8,0},{10,2},{12,4},{14,6},{1,9},{3,11}... | collective-permute-start | bytes 196616 | tf_op jit(solution)/shard_map/ppermute | solution.py:463
  91.4 6.2 %collective-permute-start.21 = (bf16[64,512]{1,0:T(8,128)(2,1)S(1)}, bf16[64,512]{1,0:T(8,128)(2,1)S(1)}, u32[]{:S(2)}, u32[]{:S(2)}) collective-permute-start(bf16[64,512]{1,0:T(8,128)(2,1)S(1)} %get-tuple-element.70), channel_id=1, source_target_pairs={{0,12},{2,14},{4,8},{6,10},{8,4},{10,6},{12,0},{14,2},{1,13},{3,15... | collective-permute-start | bytes 196616 | tf_op jit(solution)/shard_map/ppermute | solution.py:463
  97.7 1.3 %collective-permute-start.22 = (bf16[32,512]{1,0:T(8,128)(2,1)S(1)}, bf16[32,512]{1,0:T(8,128)(2,1)S(1)}, u32[]{:S(2)}, u32[]{:S(2)}) collective-permute-start(bf16[32,512]{1,0:T(8,128)(2,1)S(1)} %get-tuple-element.72), channel_id=1, source_target_pairs={{0,1},{1,0},{2,3},{3,2},{4,5},{5,4},{6,7},{7,6},{8,9},{9,8},{10,11... | collective-permute-start | bytes 98312 | tf_op jit(solution)/shard_map/ppermute | solution.py:431
  101.1 13.6 %all-to-all-start.1 = ((bf16[8,64,256]{2,1,0:T(8,128)(2,1)}), bf16[8,64,256]{2,1,0:T(8,128)(2,1)S(1)}, u32[]{:S(2)}, u32[]{:S(2)}) async-start(bf16[8,64,256]{2,1,0:T(8,128)(2,1)} %shard_map.109), calls=%async_computation.1 | async-start | bytes 524288 | tf_op jit(solution)/shard_map/all_to_all | solution.py:491
  114.9 1.4 %collective-permute-start.23 = (bf16[256,256]{1,0:T(8,128)(2,1)S(1)}, bf16[256,256]{1,0:T(8,128)(2,1)S(1)}, u32[]{:S(2)}, u32[]{:S(2)}) collective-permute-start(bf16[256,256]{1,0:T(8,128)(2,1)S(1)} %get-tuple-element.76), channel_id=1, source_target_pairs={{0,1},{1,0},{2,3},{3,2},{4,5},{5,4},{6,7},{7,6},{8,9},{9,8},{10,11... | collective-permute-start | bytes 393224 | tf_op jit(solution)/shard_map/ppermute | solution.py:431
  (8 other events, 38.5 us)

commit v6 on v5

--- a/solution.py
+++ b/solution.py
@@ -206,19 +206,27 @@
     for d in range(8):
         part = nn_dot(cells_ref[pl.ds(d, 256, stride=8), :].astype(BF), lane_place(d))
         rows = part if rows is None else rows + part
-    return rows.astype(BF)
-
-
-def pack_kernel(n_ref, w_ref, step_ref, field_ref, cot_ref, out_ref, cells_ref, other_ref):
-    del n_ref, w_ref, step_ref
-    field = to_rows(field_ref, cells_ref)
-    cot = to_rows(cot_ref, other_ref)
-    for a in range(8):
-        before, after = (a + 7) % 8, (a + 1) % 8
-        out_ref[a, 0:32] = field[32 * before : 32 * before + 32]
-        out_ref[a, 32:64] = field[32 * a : 32 * a + 32]
-        out_ref[a, 64:96] = field[32 * after : 32 * after + 32]
-        out_ref[a, 96:128] = cot[32 * a : 32 * a + 32]
+    return rows.astype(BF).reshape(8, 32, 256)
+
+
+def pack_kernel(n_ref, w_ref, step_ref, volume_ref, cotangent_ref, *refs):
+    del n_ref, step_ref
+    out_refs = refs[:8]
+    volume_copy_ref, cotangent_copy_ref, cells_ref, other_ref, field_ref, cot_ref, sems = refs[8:]
+    first = pltpu.make_async_copy(volume_ref, volume_copy_ref, sems.at[0])
+    second = pltpu.make_async_copy(cotangent_ref, cotangent_copy_ref, sems.at[1])
+    first.start()
+    second.start()
+    first.wait()
+    field_ref[...] = to_rows(volume_copy_ref, cells_ref)
+    second.wait()
+    cot_ref[...] = to_rows(cotangent_copy_ref, other_ref)
+    for mask, out_ref in enumerate(out_refs):
+        a = w_ref[0] ^ mask
+        out_ref[0:32] = field_ref[(a + 7) & 7]
+        out_ref[32:64] = field_ref[a]
+        out_ref[64:96] = field_ref[(a + 1) & 7]
+        out_ref[96:128] = cot_ref[a]
 
 
 def arrived_planes(w, arrived_ref):
@@ -237,10 +245,19 @@
     return grown[0:256], grown[32:288], grown[64:320]
 
 
-def side_kernel(w_ref, planes_ref, band_ref, *refs, planes_of):
+def arrived_kernel(w_ref, *refs):
+    planes_ref, own_ref, send_ref = refs[-3:]
+    for mask in range(8):
+        planes_ref[w_ref[0] ^ mask] = refs[mask][...]
+    put_sides(arrived_planes(w_ref[0], planes_ref), own_ref, send_ref)
+
+
+def returned_kernel(w_ref, planes_ref, band_ref, own_ref, send_ref):
     del band_ref
-    own_ref, send_ref = refs[-2:]
-    planes = planes_of(w_ref[0], planes_ref)
+    put_sides(returned_planes(w_ref[0], planes_ref), own_ref, send_ref)
+
+
+def put_sides(planes, own_ref, send_ref):
     source = lax.broadcasted_iota(jnp.int32, (256, 256), 0)
     target = lax.broadcasted_iota(jnp.int32, (256, 256), 1)
     sides = None
@@ -258,24 +275,29 @@
     send_ref[...] = jnp.where(own, zero, sides).astype(BF)
 
 
-def side_call(w, planes, band, planes_of, rest=()):
-    shape = shape_of((256, 256), BF)
-    return kernel_call(
-        functools.partial(side_kernel, planes_of=planes_of), (w,), (planes, band), [shape, shape], rest=rest
-    )
-
-
-def fine_sum(n, planes, own_ref, got_ref, band_ref):
+def main_kernel(w_ref, planes_ref, band_ref, out_ref, *, planes_of):
+    lhs = jnp.concatenate(planes_of(w_ref[0], planes_ref), axis=1)
+    out_ref[...] = nn_dot(lhs, band_ref[0:768])
+
+
+def main_call(w, planes, band, planes_of):
+    (out,) = kernel_call(
+        functools.partial(main_kernel, planes_of=planes_of), (w,), (planes, band), [shape_of((256, 768), F32)]
+    )
+    return out
+
+
+def fine_sum(n, main_ref, own_ref, got_ref, band_ref):
     lane = lax.broadcasted_iota(jnp.int32, (256, 256), 1)
     keep = ((lane & 32) != 0) == (n == 0)
     got = jnp.where(keep, got_ref[...].astype(F32), jnp.zeros((256, 256), F32))
     sides = (own_ref[...].astype(F32) + got).astype(BF)
-    lhs = jnp.concatenate([*planes, sides], axis=1)
-    total = nn_dot(lhs, band_ref[:, 256:512])
+    shifts_y = main_ref[...] + nn_dot(sides, band_ref[768:1024])
     y = (lax.broadcasted_iota(jnp.int32, (256, 1), 0) >> 1) & 15
+    total = shifts_y[:, 256:512]
     zero = jnp.zeros_like(total)
-    below = pltpu.roll(nn_dot(lhs, band_ref[:, 0:256]), 2, 0)
-    above = pltpu.roll(nn_dot(lhs, band_ref[:, 512:768]), 254, 0)
+    below = pltpu.roll(shifts_y[:, 0:256], 2, 0)
+    above = pltpu.roll(shifts_y[:, 512:768], 254, 0)
     return total + jnp.where(y > 0, below, zero) + jnp.where(y < 15, above, zero)
 
 
@@ -284,11 +306,9 @@
 
 
 def merge_kernel(
-    n_ref, w_ref, planes_ref, own_ref, got_ref, band_ref, merge_ref, pre_ref, act_ref, sum_ref, sum_b_ref, rows_ref
+    n_ref, main_ref, own_ref, got_ref, band_ref, merge_ref, pre_ref, act_ref, sum_ref, sum_b_ref, rows_ref
 ):
-    n = n_ref[0]
-    planes = arrived_planes(w_ref[0], planes_ref)
-    wide_rows = fine_sum(n, planes, own_ref, got_ref, band_ref)
+    wide_rows = fine_sum(n_ref[0], main_ref, own_ref, got_ref, band_ref)
     rows_ref[0] = wide_rows[:, :128]
     rows_ref[1] = wide_rows[:, 128:]
     total = None
@@ -311,9 +331,8 @@
         cot_ref[b] = jnp.concatenate([cell_rows(rows_ref.at[h], b) for h in range(2)], axis=1).astype(BF)
 
 
-def final_kernel(n_ref, w_ref, planes_ref, own_ref, got_ref, band_ref, out_ref, cells_ref):
-    planes = returned_planes(w_ref[0], planes_ref)
-    rows = fine_sum(n_ref[0], planes, own_ref, got_ref, band_ref).astype(BF)
+def final_kernel(n_ref, main_ref, own_ref, got_ref, band_ref, out_ref, cells_ref):
+    rows = fine_sum(n_ref[0], main_ref, own_ref, got_ref, band_ref).astype(BF)
     for d in range(8):
         cells_ref[pl.ds(d, 256, stride=8), :] = nt_dot(rows, lane_place(d))
     out_ref[...] = cells_ref[...].astype(BF).reshape(8, 16, 16, 32)
@@ -487,8 +506,10 @@
     return mine, swap_narrow(send)
 
 
-def across_wide(value):
-    return lax.all_to_all(value, "wide", split_axis=0, concat_axis=0, tiled=True)
+def across_wide(messages):
+    return [messages[0]] + [
+        lax.ppermute(messages[mask], "wide", [(i, i ^ mask) for i in range(8)]) for mask in range(1, 8)
+    ]
 
 
 def eight_shards(
@@ -509,23 +530,30 @@
     n = lax.axis_index("narrow").astype(jnp.int32).reshape(1)
 
     fine_cells = pltpu.VMEM((2048, 32), F32)
-    (outgoing,) = kernel_call(
-        pack_kernel, (n, w, timestep), (volume.transpose(1, 2, 3, 0), cotangent.transpose(1, 2, 3, 0)),
-        [shape_of((8, 128, 256), BF)], [fine_cells, fine_cells],
-    )
-    arrived = across_wide(outgoing)
+    fine_field = pltpu.VMEM((8, 16, 16, 32), BF)
+    fine_blocks = pltpu.VMEM((8, 32, 256), BF)
+    outgoing = kernel_call(
+        pack_kernel, (n, w, timestep), (), [shape_of((128, 256), BF)] * 8,
+        [fine_field, fine_field, fine_cells, fine_cells, fine_blocks, fine_blocks, pltpu.SemaphoreType.DMA((2,))],
+        rest=(volume.transpose(1, 2, 3, 0), cotangent.transpose(1, 2, 3, 0)),
+    )
+    messages = across_wide(outgoing)
     band, bias = kernel_call(
         band_and_bias_kernel, (timestep,), (fine_weight,),
         [shape_of((1024, 768), BF), shape_of((1, hidden), F32)],
         [pltpu.VMEM((8, hidden), F32), pltpu.SemaphoreType.DMA], cost=BESIDE, rest=(step_table,),
     )
-    sides, sent = side_call(w, arrived, band, arrived_planes, (merge_weight,))
+    side_shape = shape_of((256, 256), BF)
+    arrived, sides, sent = kernel_call(
+        arrived_kernel, (w,), (*messages, band), [shape_of((8, 128, 256), BF), side_shape, side_shape],
+        rest=(merge_weight,),
+    )
     fine_rows = pltpu.VMEM((2, 256, 128), F32)
     sum_shapes = [shape_of((32, features), F32), shape_of((32, features), BF)]
     pre_act, act, merged_part, merged_part_b = kernel_call(
         merge_kernel,
-        (n, w),
-        (arrived, sides, swap_narrow(sent), band, merge_weight),
+        (n,),
+        (main_call(w, arrived, band, arrived_planes), sides, swap_narrow(sent), band, merge_weight),
         [shape_of((8, 32, 256), F32), shape_of((8, 32, 256), BF)] + sum_shapes,
         [fine_rows],
     )
@@ -567,12 +595,12 @@
         (n, w), (grad_res, mine, got, grad_comb, pre_act, merge_weight),
         [shape_of((8, 64, 256), BF)], [fine_rows],
     )
-    returned = across_wide(leaving)
+    returned = lax.all_to_all(leaving, "wide", split_axis=0, concat_axis=0, tiled=True)
     band = banded(fine_weight, True)
-    sides, sent = side_call(w, returned, band, returned_planes)
+    sides, sent = kernel_call(returned_kernel, (w,), (returned, band), [side_shape, side_shape])
     (result,) = kernel_call(
         final_kernel,
-        (n, w), (returned, sides, swap_narrow(sent), band),
+        (n,), (main_call(w, returned, band, returned_planes), sides, swap_narrow(sent), band),
         [shape_of((8, 16, 16, 32), BF)], [fine_cells],
     )
     return result.transpose(3, 0, 1, 2)

time: 119 us -> 114 us (0.958)
  waiting for transfers between devices: 56.3 us -> 53.5 us
  local copies, waits for them, and re-layouts: 3.54 us -> 1.45 us
    ppermute x0 -> x7, starting transfers between devices: none -> 12.5 us  [across_wide(): lax.ppermute(messages[mask], 'wide', [(i, i ^ mask) for i in range(8)])]
    all_to_all x2 -> x1, waiting for transfers between devices: 20.4 us -> 7.99 us  [eight_shards(): lax.all_to_all(leaving, 'wide', split_axis=0, concat_axis=0, tiled=True)]
    all_to_all x2 -> x1, starting transfers between devices: 11.6 us -> 3.43 us  [eight_shards(): lax.all_to_all(leaving, 'wide', split_axis=0, concat_axis=0, tiled=True)]
    ppermute x16, waiting for transfers between devices: 26.4 us -> 31.8 us  [partner(): return lax.ppermute(value, 'wide', [(i, i ^ mask) for i in range(8)])]
    ppermute x0 -> x7, waiting for transfers between devices: none -> 5.14 us  [across_wide(): lax.ppermute(messages[mask], 'wide', [(i, i ^ mask) for i in range(8)])]
    ppermute x16, starting transfers between devices: 24.1 us -> 20.3 us  [partner(): return lax.ppermute(value, 'wide', [(i, i ^ mask) for i in range(8)])]
    unnamed x28 -> x24, local copies, waits for them, and re-layouts: 3.54 us -> 1.45 us
    pallas_call x22 -> x24, Pallas kernels: 21 us -> 21.1 us  [kernel_call(): pl.pallas_call(kernel, in_specs=[SMEM] * len(places) + [VMEM] * len(array...]
  transfers between devices with their start and end apart: 26 -> 32, of which waited for: 23 -> 24; matrix products, arithmetic and copies ran while one was open for 0% -> 0% of each run, Pallas kernels for 2% -> 3%
where the time goes in v6:
time: 114 us
  waiting for transfers between devices  53.5 us (47%)
  starting transfers between devices  37.1 us (33%)
  Pallas kernels  21.1 us (19%)
  local copies, waits for them, and re-layouts  1.45 us (1%)
    ppermute x16, waiting for transfers between devices, partner(): return lax.ppermute(value, 'wide', [(i, i ^ mask) for i in range(8)])  31.8 us
    pallas_call x24, Pallas kernels, kernel_call(): pl.pallas_call(kernel, in_specs=[SMEM] * len(places) + [VMEM] * len(array...  21.1 us
    ppermute x16, starting transfers between devices, partner(): return lax.ppermute(value, 'wide', [(i, i ^ mask) for i in range(8)])  20.3 us
    ppermute x7, starting transfers between devices, across_wide(): lax.ppermute(messages[mask], 'wide', [(i, i ^ mask) for i in range(8)])  12.5 us
    ppermute x8, waiting for transfers between devices, swap_narrow(): return lax.ppermute(value, 'narrow', [(0, 1), (1, 0)])  8.57 us
    all_to_all x1, waiting for transfers between devices, eight_shards(): lax.all_to_all(leaving, 'wide', split_axis=0, concat_axis=0, tiled=True)  7.99 us
    ppermute x7, waiting for transfers between devices, across_wide(): lax.ppermute(messages[mask], 'wide', [(i, i ^ mask) for i in range(8)])  5.14 us
    all_to_all x1, starting transfers between devices, eight_shards(): lax.all_to_all(leaving, 'wide', split_axis=0, concat_axis=0, tiled=True)  3.43 us
  transfers between devices with their start and end apart: 32, of which 24 were waited for; matrix products, arithmetic and copies ran while one was open for 0% of the time, Pallas kernels for 3%

profile of v6, /device:TPU:0, one launch (start us, length us, event | category | flops | bytes accessed | tf_op | source)
XLA Modules:
  0.0 114.1 jit_solution(18147594415817900574)
XLA Ops:
  0.7 2.0 %shard_map.91 = (bf16[128,256]{1,0:T(8,128)(2,1)S(1)}, bf16[128,256]{1,0:T(8,128)(2,1)S(1)}, bf16[128,256]{1,0:T(8,128)(2,1)S(1)}, bf16[128,256]{1,0:T(8,128)(2,...) custom-call(s32[1]{0:T(128)} %bitcast.n_ref, ...), custom_call_target="tpu_custom_call" | custom-call | tf_op jit(solution)/shard_map/pallas_call | solution.py:139
  2.7 3.0 %collective-permute-start = (bf16[128,256]{1,0:T(8,128)(2,1)S(1)}, bf16[128,256]{1,0:T(8,128)(2,1)S(1)}, u32[]{:S(2)}, u32[]{:S(2)}) collective-permute-start(bf16[128,256]{1,0:T(8,128)(2,1)S(1)} %get-tuple-element.51), channel_id=1, source_target_pairs={{0,2},{2,0},{4,6},{6,4},{8,10},{10,8},{12,14},{14,12},{1,3},{3,1},... | collective-permute-start | bytes 196616 | tf_op jit(solution)/shard_map/ppermute | solution.py:511
  5.7 1.6 %collective-permute-start.1 = (bf16[128,256]{1,0:T(8,128)(2,1)S(1)}, bf16[128,256]{1,0:T(8,128)(2,1)S(1)}, u32[]{:S(2)}, u32[]{:S(2)}) collective-permute-start(bf16[128,256]{1,0:T(8,128)(2,1)S(1)} %get-tuple-element.52), channel_id=1, source_target_pairs={{0,4},{2,6},{4,0},{6,2},{8,12},{10,14},{12,8},{14,10},{1,5},{3,7},... | collective-permute-start | bytes 196616 | tf_op jit(solution)/shard_map/ppermute | solution.py:511
  7.3 3.0 %collective-permute-start.3 = (bf16[128,256]{1,0:T(8,128)(2,1)S(1)}, bf16[128,256]{1,0:T(8,128)(2,1)S(1)}, u32[]{:S(2)}, u32[]{:S(2)}) collective-permute-start(bf16[128,256]{1,0:T(8,128)(2,1)S(1)} %get-tuple-element.54), channel_id=1, source_target_pairs={{0,8},{2,10},{4,12},{6,14},{8,0},{10,2},{12,4},{14,6},{1,9},{3,11}... | collective-permute-start | bytes 196616 | tf_op jit(solution)/shard_map/ppermute | solution.py:511
  11.6 3.6 %collective-permute-start.5 = (bf16[128,256]{1,0:T(8,128)(2,1)S(1)}, bf16[128,256]{1,0:T(8,128)(2,1)S(1)}, u32[]{:S(2)}, u32[]{:S(2)}) collective-permute-start(bf16[128,256]{1,0:T(8,128)(2,1)S(1)} %get-tuple-element.56), channel_id=1, source_target_pairs={{0,12},{2,14},{4,8},{6,10},{8,4},{10,6},{12,0},{14,2},{1,13},{3,15... | collective-permute-start | bytes 196616 | tf_op jit(solution)/shard_map/ppermute | solution.py:511
  17.1 3.4 %collective-permute-done.4.refs_5_ = bf16[128,256]{1,0:T(8,128)(2,1)S(1)} collective-permute-done((bf16[128,256]{1,0:T(8,128)(2,1)S(1)}, bf16[128,256]{1,0:T(8,128)(2,1)S(1)}, u32[]{:S(2)}, u32[]{:S(2)}) %collective-permute-start.4) | collective-permute-done | bytes 65568 | tf_op jit(solution)/shard_map/ppermute | solution.py:511
  20.5 1.7 %collective-permute-done.6.refs_7_ = bf16[128,256]{1,0:T(8,128)(2,1)S(1)} collective-permute-done((bf16[128,256]{1,0:T(8,128)(2,1)S(1)}, bf16[128,256]{1,0:T(8,128)(2,1)S(1)}, u32[]{:S(2)}, u32[]{:S(2)}) %collective-permute-start.6) | collective-permute-done | bytes 65568 | tf_op jit(solution)/shard_map/ppermute | solution.py:511
  26.3 3.8 %collective-permute-done.8.got_ref = bf16[32,1024]{1,0:T(8,128)(2,1)S(1)} collective-permute-done((bf16[32,1024]{1,0:T(8,128)(2,1)S(1)}, bf16[32,1024]{1,0:T(8,128)(2,1)S(1)}, u32[]{:S(2)}, u32[]{:S(2)}) %collective-permute-start.8) | collective-permute-done | bytes 65568 | tf_op jit(solution)/shard_map/ppermute | solution.py:482
  30.1 2.8 %collective-permute-start.10 = (bf16[32,1024]{1,0:T(8,128)(2,1)S(1)}, bf16[32,1024]{1,0:T(8,128)(2,1)S(1)}, u32[]{:S(2)}, u32[]{:S(2)}) collective-permute-start(bf16[32,1024]{1,0:T(8,128)(2,1)S(1)} %get-tuple-element.65), channel_id=1, source_target_pairs={{0,8},{2,10},{4,12},{6,14},{8,0},{10,2},{12,4},{14,6},{1,9},{3,11}... | collective-permute-start | bytes 196616 | tf_op jit(solution)/shard_map/ppermute | solution.py:482
  35.4 3.7 %collective-permute-done.11.three_ref = bf16[32,1024]{1,0:T(8,128)(2,1)S(1)} collective-permute-done((bf16[32,1024]{1,0:T(8,128)(2,1)S(1)}, bf16[32,1024]{1,0:T(8,128)(2,1)S(1)}, u32[]{:S(2)}, u32[]{:S(2)}) %collective-permute-start.11) | collective-permute-done | bytes 65568 | tf_op jit(solution)/shard_map/ppermute | solution.py:482
  45.4 3.5 %collective-permute-done.14.got_ref = bf16[64,512]{1,0:T(8,128)(2,1)S(1)} collective-permute-done((bf16[64,512]{1,0:T(8,128)(2,1)S(1)}, bf16[64,512]{1,0:T(8,128)(2,1)S(1)}, u32[]{:S(2)}, u32[]{:S(2)}) %collective-permute-start.14) | collective-permute-done | bytes 65568 | tf_op jit(solution)/shard_map/ppermute | solution.py:482
  49.0 2.4 %collective-permute-start.16 = (bf16[64,512]{1,0:T(8,128)(2,1)S(1)}, bf16[64,512]{1,0:T(8,128)(2,1)S(1)}, u32[]{:S(2)}, u32[]{:S(2)}) collective-permute-start(bf16[64,512]{1,0:T(8,128)(2,1)S(1)} %get-tuple-element.73), channel_id=1, source_target_pairs={{0,8},{2,10},{4,12},{6,14},{8,0},{10,2},{12,4},{14,6},{1,9},{3,11}... | collective-permute-start | bytes 196616 | tf_op jit(solution)/shard_map/ppermute | solution.py:482
  51.4 2.0 %collective-permute-start.17 = (bf16[64,512]{1,0:T(8,128)(2,1)S(1)}, bf16[64,512]{1,0:T(8,128)(2,1)S(1)}, u32[]{:S(2)}, u32[]{:S(2)}) collective-permute-start(bf16[64,512]{1,0:T(8,128)(2,1)S(1)} %get-tuple-element.73), channel_id=1, source_target_pairs={{0,12},{2,14},{4,8},{6,10},{8,4},{10,6},{12,0},{14,2},{1,13},{3,15... | collective-permute-start | bytes 196616 | tf_op jit(solution)/shard_map/ppermute | solution.py:482
  53.4 2.7 %collective-permute-done.16.two_ref = bf16[64,512]{1,0:T(8,128)(2,1)S(1)} collective-permute-done((bf16[64,512]{1,0:T(8,128)(2,1)S(1)}, bf16[64,512]{1,0:T(8,128)(2,1)S(1)}, u32[]{:S(2)}, u32[]{:S(2)}) %collective-permute-start.16) | collective-permute-done | bytes 65568 | tf_op jit(solution)/shard_map/ppermute | solution.py:482
  58.8 2.7 %shard_map.103 = (bf16[8,32,256]{2,1,0:T(8,128)(2,1)S(1)}, f32[32,1024]{1,0:T(8,128)S(1)}, bf16[32,1024]{1,0:T(8,128)(2,1)S(1)}) custom-call(s32[1]{0:T(128)} %bitcast.n_ref, f32[32,1024]{1,0:T(8,128)S(1)} %get-tuple-element.66.merged_ref, f32[32,512]{1,0:T(8,128)S(1)} %get-tuple-element.74.mine_ref, bf16[32,512]{1,0:T(8,128)(2,1)S(1)} %collective-permute-done.18.got_ref, ...), custom_call_target="tpu_custom_call" | custom-call | tf_op jit(solution)/shard_map/pallas_call | solution.py:139
  62.3 3.6 %collective-permute-done.19.got_ref = bf16[32,1024]{1,0:T(8,128)(2,1)S(1)} collective-permute-done((bf16[32,1024]{1,0:T(8,128)(2,1)S(1)}, bf16[32,1024]{1,0:T(8,128)(2,1)S(1)}, u32[]{:S(2)}, u32[]{:S(2)}) %collective-permute-start.19) | collective-permute-done | bytes 65568 | tf_op jit(solution)/shard_map/ppermute | solution.py:482
  66.0 2.6 %collective-permute-start.21 = (bf16[32,1024]{1,0:T(8,128)(2,1)S(1)}, bf16[32,1024]{1,0:T(8,128)(2,1)S(1)}, u32[]{:S(2)}, u32[]{:S(2)}) collective-permute-start(bf16[32,1024]{1,0:T(8,128)(2,1)S(1)} %get-tuple-element.80), channel_id=1, source_target_pairs={{0,8},{2,10},{4,12},{6,14},{8,0},{10,2},{12,4},{14,6},{1,9},{3,11}... | collective-permute-start | bytes 196616 | tf_op jit(solution)/shard_map/ppermute | solution.py:482
  68.5 1.8 %collective-permute-start.22 = (bf16[32,1024]{1,0:T(8,128)(2,1)S(1)}, bf16[32,1024]{1,0:T(8,128)(2,1)S(1)}, u32[]{:S(2)}, u32[]{:S(2)}) collective-permute-start(bf16[32,1024]{1,0:T(8,128)(2,1)S(1)} %get-tuple-element.80), channel_id=1, source_target_pairs={{0,12},{2,14},{4,8},{6,10},{8,4},{10,6},{12,0},{14,2},{1,13},{3,15... | collective-permute-start | bytes 196616 | tf_op jit(solution)/shard_map/ppermute | solution.py:482
  70.3 2.5 %collective-permute-done.21.two_ref = bf16[32,1024]{1,0:T(8,128)(2,1)S(1)} collective-permute-done((bf16[32,1024]{1,0:T(8,128)(2,1)S(1)}, bf16[32,1024]{1,0:T(8,128)(2,1)S(1)}, u32[]{:S(2)}, u32[]{:S(2)}) %collective-permute-start.21) | collective-permute-done | bytes 65568 | tf_op jit(solution)/shard_map/ppermute | solution.py:482
  72.9 1.7 %collective-permute-done.22.three_ref = bf16[32,1024]{1,0:T(8,128)(2,1)S(1)} collective-permute-done((bf16[32,1024]{1,0:T(8,128)(2,1)S(1)}, bf16[32,1024]{1,0:T(8,128)(2,1)S(1)}, u32[]{:S(2)}, u32[]{:S(2)}) %collective-permute-start.22) | collective-permute-done | bytes 65568 | tf_op jit(solution)/shard_map/ppermute | solution.py:482
  75.9 2.3 %shard_map.106.mine_ref = f32[64,256]{1,0:T(8,128)S(1)} custom-call(s32[1]{0:T(128)} %bitcast.n_ref, bf16[32,512]{1,0:T(8,128)(2,1)S(1)} %get-tuple-element.82.mine_ref, bf16[32,512]{1,0:T(8,128)(2,1)S(1)} %collective-permute-done.23.got_ref, bf16[27,256,1024]{2,1,0:T(8,128)(2,1)S(1)} %bitcast.6), custom_call_target="tpu_custom_call" | custom-call | tf_op jit(solution)/shard_map/pallas_call | solution.py:139
  79.5 2.2 %shard_map.107 = (f32[64,512]{1,0:T(8,128)S(1)}, bf16[64,512]{1,0:T(8,128)(2,1)S(1)}) custom-call(s32[1]{0:T(128)} %bitcast.n_ref, f32[64,256]{1,0:T(8,128)S(1)} %shard_map.106.mine_ref, f32[64,256]{1,0:T(8,128)S(1)} %collective-permute-done.24.got_ref, f32[64,256]{1,0:T(8,128)S(1)} %get-tuple-element.84.gate_ref, bf16[27,1024,256]{2,1,0:T(8,128)(2,1)S(1)} %bitcast.8), custom_call_target="tpu_custom_call" | custom-call | tf_op jit(solution)/shard_map/pallas_call | solution.py:139
  82.5 3.6 %collective-permute-done.25.got_ref = bf16[64,512]{1,0:T(8,128)(2,1)S(1)} collective-permute-done((bf16[64,512]{1,0:T(8,128)(2,1)S(1)}, bf16[64,512]{1,0:T(8,128)(2,1)S(1)}, u32[]{:S(2)}, u32[]{:S(2)}) %collective-permute-start.25) | collective-permute-done | bytes 65568 | tf_op jit(solution)/shard_map/ppermute | solution.py:482
  86.2 2.4 %collective-permute-start.27 = (bf16[64,512]{1,0:T(8,128)(2,1)S(1)}, bf16[64,512]{1,0:T(8,128)(2,1)S(1)}, u32[]{:S(2)}, u32[]{:S(2)}) collective-permute-start(bf16[64,512]{1,0:T(8,128)(2,1)S(1)} %get-tuple-element.88), channel_id=1, source_target_pairs={{0,8},{2,10},{4,12},{6,14},{8,0},{10,2},{12,4},{14,6},{1,9},{3,11}... | collective-permute-start | bytes 196616 | tf_op jit(solution)/shard_map/ppermute | solution.py:482
  88.5 2.0 %collective-permute-start.28 = (bf16[64,512]{1,0:T(8,128)(2,1)S(1)}, bf16[64,512]{1,0:T(8,128)(2,1)S(1)}, u32[]{:S(2)}, u32[]{:S(2)}) collective-permute-start(bf16[64,512]{1,0:T(8,128)(2,1)S(1)} %get-tuple-element.88), channel_id=1, source_target_pairs={{0,12},{2,14},{4,8},{6,10},{8,4},{10,6},{12,0},{14,2},{1,13},{3,15... | collective-permute-start | bytes 196616 | tf_op jit(solution)/shard_map/ppermute | solution.py:482
  90.6 2.5 %collective-permute-done.27.two_ref = bf16[64,512]{1,0:T(8,128)(2,1)S(1)} collective-permute-done((bf16[64,512]{1,0:T(8,128)(2,1)S(1)}, bf16[64,512]{1,0:T(8,128)(2,1)S(1)}, u32[]{:S(2)}, u32[]{:S(2)}) %collective-permute-start.27) | collective-permute-done | bytes 65568 | tf_op jit(solution)/shard_map/ppermute | solution.py:482
  93.0 1.6 %collective-permute-done.28.three_ref = bf16[64,512]{1,0:T(8,128)(2,1)S(1)} collective-permute-done((bf16[64,512]{1,0:T(8,128)(2,1)S(1)}, bf16[64,512]{1,0:T(8,128)(2,1)S(1)}, u32[]{:S(2)}, u32[]{:S(2)}) %collective-permute-start.28) | collective-permute-done | bytes 65568 | tf_op jit(solution)/shard_map/ppermute | solution.py:482
  95.9 2.1 %shard_map.110 = bf16[8,64,256]{2,1,0:T(8,128)(2,1)} custom-call(s32[1]{0:T(128)} %bitcast.n_ref, s32[1]{0:T(128)} %bitcast.1.w_ref, f32[32,1024]{1,0:T(8,128)S(1)} %get-tuple-element.81.res_ref, f32[32,512]{1,0:T(8,128)S(1)} %get-tuple-element.89.mine_ref, bf16[32,512]{1,0:T(8,128)(2,1)S(1)} %collective-permute-done.29.got_ref, ...), custom_call_target="tpu_custom_call" | custom-call | tf_op jit(solution)/shard_map/pallas_call | solution.py:139
  98.0 3.4 %all-to-all-start = ((bf16[8,64,256]{2,1,0:T(8,128)(2,1)}), bf16[8,64,256]{2,1,0:T(8,128)(2,1)S(1)}, u32[]{:S(2)}, u32[]{:S(2)}) async-start(bf16[8,64,256]{2,1,0:T(8,128)(2,1)} %shard_map.110), calls=%async_computation | async-start | bytes 524288 | tf_op jit(solution)/shard_map/all_to_all | solution.py:598
  101.5 1.4 %shard_map.111.band_ref = bf16[1024,768]{1,0:T(8,128)(2,1)S(1)} custom-call(bf16[27,32,32]{2,1,0:T(8,128)(2,1)S(1)} %copy-done.3), custom_call_target="tpu_custom_call" | custom-call | bytes 33554432 | tf_op jit(solution)/shard_map/pallas_call | solution.py:139
  102.9 8.0 %all-to-all-done.planes_ref = bf16[8,64,256]{2,1,0:T(8,128)(2,1)S(1)} async-done(((bf16[8,64,256]{2,1,0:T(8,128)(2,1)}), bf16[8,64,256]{2,1,0:T(8,128)(2,1)S(1)}, u32[]{:S(2)}, u32[]{:S(2)}) %all-to-all-start) | async-done | bytes 262176 | tf_op jit(solution)/shard_map/all_to_all | solution.py:598
  112.6 1.5 %shard_map.114 = bf16[8,16,16,32]{3,2,1,0:T(8,128)(2,1)} custom-call(s32[1]{0:T(128)} %bitcast.n_ref, f32[256,768]{1,0:T(8,128)S(1)} %shard_map.112.main_ref, bf16[256,256]{1,0:T(8,128)(2,1)S(1)} %get-tuple-element.93.own_ref, bf16[256,256]{1,0:T(8,128)(2,1)S(1)} %collective-permute-done.30.got_ref, bf16[1024,768]{1,0:T(8,128)(2,1)S(1)} %shard_map.111.band_ref), custom_call_target="tpu_custom_call" | custom-call | tf_op jit(solution)/shard_map/pallas_call | solution.py:139
  (82 shorter events, 26.0 us)
Async XLA Ops:
  2.7 8.9 %collective-permute-start = (bf16[128,256]{1,0:T(8,128)(2,1)S(1)}, bf16[128,256]{1,0:T(8,128)(2,1)S(1)}, u32[]{:S(2)}, u32[]{:S(2)}) collective-permute-start(bf16[128,256]{1,0:T(8,128)(2,1)S(1)} %get-tuple-element.51), channel_id=1, source_target_pairs={{0,2},{2,0},{4,6},{6,4},{8,10},{10,8},{12,14},{14,12},{1,3},{3,1},... | collective-permute-start | bytes 196616 | tf_op jit(solution)/shard_map/ppermute | solution.py:511
  5.7 9.5 %collective-permute-start.1 = (bf16[128,256]{1,0:T(8,128)(2,1)S(1)}, bf16[128,256]{1,0:T(8,128)(2,1)S(1)}, u32[]{:S(2)}, u32[]{:S(2)}) collective-permute-start(bf16[128,256]{1,0:T(8,128)(2,1)S(1)} %get-tuple-element.52), channel_id=1, source_target_pairs={{0,4},{2,6},{4,0},{6,2},{8,12},{10,14},{12,8},{14,10},{1,5},{3,7},... | collective-permute-start | bytes 196616 | tf_op jit(solution)/shard_map/ppermute | solution.py:511
  7.3 9.8 %collective-permute-start.2 = (bf16[128,256]{1,0:T(8,128)(2,1)S(1)}, bf16[128,256]{1,0:T(8,128)(2,1)S(1)}, u32[]{:S(2)}, u32[]{:S(2)}) collective-permute-start(bf16[128,256]{1,0:T(8,128)(2,1)S(1)} %get-tuple-element.53), channel_id=1, source_target_pairs={{0,6},{2,4},{4,2},{6,0},{8,14},{10,12},{12,10},{14,8},{1,7},{3,5},... | collective-permute-start | bytes 196616 | tf_op jit(solution)/shard_map/ppermute | solution.py:511
  7.3 9.8 %collective-permute-start.3 = (bf16[128,256]{1,0:T(8,128)(2,1)S(1)}, bf16[128,256]{1,0:T(8,128)(2,1)S(1)}, u32[]{:S(2)}, u32[]{:S(2)}) collective-permute-start(bf16[128,256]{1,0:T(8,128)(2,1)S(1)} %get-tuple-element.54), channel_id=1, source_target_pairs={{0,8},{2,10},{4,12},{6,14},{8,0},{10,2},{12,4},{14,6},{1,9},{3,11}... | collective-permute-start | bytes 196616 | tf_op jit(solution)/shard_map/ppermute | solution.py:511
  10.3 10.2 %collective-permute-start.4 = (bf16[128,256]{1,0:T(8,128)(2,1)S(1)}, bf16[128,256]{1,0:T(8,128)(2,1)S(1)}, u32[]{:S(2)}, u32[]{:S(2)}) collective-permute-start(bf16[128,256]{1,0:T(8,128)(2,1)S(1)} %get-tuple-element.55), channel_id=1, source_target_pairs={{0,10},{2,8},{4,14},{6,12},{8,2},{10,0},{12,6},{14,4},{1,11},{3,9}... | collective-permute-start | bytes 196616 | tf_op jit(solution)/shard_map/ppermute | solution.py:511
  11.6 8.9 %collective-permute-start.5 = (bf16[128,256]{1,0:T(8,128)(2,1)S(1)}, bf16[128,256]{1,0:T(8,128)(2,1)S(1)}, u32[]{:S(2)}, u32[]{:S(2)}) collective-permute-start(bf16[128,256]{1,0:T(8,128)(2,1)S(1)} %get-tuple-element.56), channel_id=1, source_target_pairs={{0,12},{2,14},{4,8},{6,10},{8,4},{10,6},{12,0},{14,2},{1,13},{3,15... | collective-permute-start | bytes 196616 | tf_op jit(solution)/shard_map/ppermute | solution.py:511
  15.2 7.1 %collective-permute-start.6 = (bf16[128,256]{1,0:T(8,128)(2,1)S(1)}, bf16[128,256]{1,0:T(8,128)(2,1)S(1)}, u32[]{:S(2)}, u32[]{:S(2)}) collective-permute-start(bf16[128,256]{1,0:T(8,128)(2,1)S(1)} %get-tuple-element.57), channel_id=1, source_target_pairs={{0,14},{2,12},{4,10},{6,8},{8,6},{10,4},{12,2},{14,0},{1,15},{3,13... | collective-permute-start | bytes 196616 | tf_op jit(solution)/shard_map/ppermute | solution.py:511
  22.5 1.4 %collective-permute-start.7 = (bf16[256,256]{1,0:T(8,128)(2,1)S(1)}, bf16[256,256]{1,0:T(8,128)(2,1)S(1)}, u32[]{:S(2)}, u32[]{:S(2)}) collective-permute-start(bf16[256,256]{1,0:T(8,128)(2,1)S(1)} %get-tuple-element.61), channel_id=1, source_target_pairs={{0,1},{1,0},{2,3},{3,2},{4,5},{5,4},{6,7},{7,6},{8,9},{9,8},{10,11... | collective-permute-start | bytes 393224 | tf_op jit(solution)/shard_map/ppermute | solution.py:450
  25.7 4.3 %collective-permute-start.8 = (bf16[32,1024]{1,0:T(8,128)(2,1)S(1)}, bf16[32,1024]{1,0:T(8,128)(2,1)S(1)}, u32[]{:S(2)}, u32[]{:S(2)}) collective-permute-start(bf16[32,1024]{1,0:T(8,128)(2,1)S(1)} %get-tuple-element.63), channel_id=1, source_target_pairs={{0,2},{2,0},{4,6},{6,4},{8,10},{10,8},{12,14},{14,12},{1,3},{3,1},... | collective-permute-start | bytes 196616 | tf_op jit(solution)/shard_map/ppermute | solution.py:482
  30.1 5.3 %collective-permute-start.10 = (bf16[32,1024]{1,0:T(8,128)(2,1)S(1)}, bf16[32,1024]{1,0:T(8,128)(2,1)S(1)}, u32[]{:S(2)}, u32[]{:S(2)}) collective-permute-start(bf16[32,1024]{1,0:T(8,128)(2,1)S(1)} %get-tuple-element.65), channel_id=1, source_target_pairs={{0,8},{2,10},{4,12},{6,14},{8,0},{10,2},{12,4},{14,6},{1,9},{3,11}... | collective-permute-start | bytes 196616 | tf_op jit(solution)/shard_map/ppermute | solution.py:482
  32.9 6.2 %collective-permute-start.11 = (bf16[32,1024]{1,0:T(8,128)(2,1)S(1)}, bf16[32,1024]{1,0:T(8,128)(2,1)S(1)}, u32[]{:S(2)}, u32[]{:S(2)}) collective-permute-start(bf16[32,1024]{1,0:T(8,128)(2,1)S(1)} %get-tuple-element.65), channel_id=1, source_target_pairs={{0,12},{2,14},{4,8},{6,10},{8,4},{10,6},{12,0},{14,2},{1,13},{3,15... | collective-permute-start | bytes 196616 | tf_op jit(solution)/shard_map/ppermute | solution.py:482
  34.2 5.0 %collective-permute-start.9 = (bf16[32,1024]{1,0:T(8,128)(2,1)S(1)}, bf16[32,1024]{1,0:T(8,128)(2,1)S(1)}, u32[]{:S(2)}, u32[]{:S(2)}) collective-permute-start(bf16[32,1024]{1,0:T(8,128)(2,1)S(1)} %get-tuple-element.65), channel_id=1, source_target_pairs={{0,4},{2,6},{4,0},{6,2},{8,12},{10,14},{12,8},{14,10},{1,5},{3,7},... | collective-permute-start | bytes 196616 | tf_op jit(solution)/shard_map/ppermute | solution.py:482
  39.2 1.3 %collective-permute-start.12 = (bf16[32,512]{1,0:T(8,128)(2,1)S(1)}, bf16[32,512]{1,0:T(8,128)(2,1)S(1)}, u32[]{:S(2)}, u32[]{:S(2)}) collective-permute-start(bf16[32,512]{1,0:T(8,128)(2,1)S(1)} %get-tuple-element.68), channel_id=1, source_target_pairs={{0,1},{1,0},{2,3},{3,2},{4,5},{5,4},{6,7},{7,6},{8,9},{9,8},{10,11... | collective-permute-start | bytes 98312 | tf_op jit(solution)/shard_map/ppermute | solution.py:450
  41.8 1.3 %collective-permute-start.13 = (f32[64,256]{1,0:T(8,128)S(1)}, f32[64,256]{1,0:T(8,128)S(1)}, u32[]{:S(2)}, u32[]{:S(2)}) collective-permute-start(f32[64,256]{1,0:T(8,128)S(1)} %shard_map.98.mine_ref), channel_id=1, source_target_pairs={{0,1},{1,0},{2,3},{3,2},{4,5},{5,4},{6,7},{7,6},{8,9},{9,8},{10,11... | collective-permute-start | bytes 196616 | tf_op jit(solution)/shard_map/ppermute | solution.py:450
  44.6 4.3 %collective-permute-start.14 = (bf16[64,512]{1,0:T(8,128)(2,1)S(1)}, bf16[64,512]{1,0:T(8,128)(2,1)S(1)}, u32[]{:S(2)}, u32[]{:S(2)}) collective-permute-start(bf16[64,512]{1,0:T(8,128)(2,1)S(1)} %get-tuple-element.71), channel_id=1, source_target_pairs={{0,2},{2,0},{4,6},{6,4},{8,10},{10,8},{12,14},{14,12},{1,3},{3,1},... | collective-permute-start | bytes 196616 | tf_op jit(solution)/shard_map/ppermute | solution.py:482
  48.9 4.5 %collective-permute-start.15 = (bf16[64,512]{1,0:T(8,128)(2,1)S(1)}, bf16[64,512]{1,0:T(8,128)(2,1)S(1)}, u32[]{:S(2)}, u32[]{:S(2)}) collective-permute-start(bf16[64,512]{1,0:T(8,128)(2,1)S(1)} %get-tuple-element.73), channel_id=1, source_target_pairs={{0,4},{2,6},{4,0},{6,2},{8,12},{10,14},{12,8},{14,10},{1,5},{3,7},... | collective-permute-start | bytes 196616 | tf_op jit(solution)/shard_map/ppermute | solution.py:482
  49.0 7.1 %collective-permute-start.16 = (bf16[64,512]{1,0:T(8,128)(2,1)S(1)}, bf16[64,512]{1,0:T(8,128)(2,1)S(1)}, u32[]{:S(2)}, u32[]{:S(2)}) collective-permute-start(bf16[64,512]{1,0:T(8,128)(2,1)S(1)} %get-tuple-element.73), channel_id=1, source_target_pairs={{0,8},{2,10},{4,12},{6,14},{8,0},{10,2},{12,4},{14,6},{1,9},{3,11}... | collective-permute-start | bytes 196616 | tf_op jit(solution)/shard_map/ppermute | solution.py:482
  51.4 6.1 %collective-permute-start.17 = (bf16[64,512]{1,0:T(8,128)(2,1)S(1)}, bf16[64,512]{1,0:T(8,128)(2,1)S(1)}, u32[]{:S(2)}, u32[]{:S(2)}) collective-permute-start(bf16[64,512]{1,0:T(8,128)(2,1)S(1)} %get-tuple-element.73), channel_id=1, source_target_pairs={{0,12},{2,14},{4,8},{6,10},{8,4},{10,6},{12,0},{14,2},{1,13},{3,15... | collective-permute-start | bytes 196616 | tf_op jit(solution)/shard_map/ppermute | solution.py:482
  57.5 1.3 %collective-permute-start.18 = (bf16[32,512]{1,0:T(8,128)(2,1)S(1)}, bf16[32,512]{1,0:T(8,128)(2,1)S(1)}, u32[]{:S(2)}, u32[]{:S(2)}) collective-permute-start(bf16[32,512]{1,0:T(8,128)(2,1)S(1)} %get-tuple-element.75), channel_id=1, source_target_pairs={{0,1},{1,0},{2,3},{3,2},{4,5},{5,4},{6,7},{7,6},{8,9},{9,8},{10,11... | collective-permute-start | bytes 98312 | tf_op jit(solution)/shard_map/ppermute | solution.py:450
  61.5 4.3 %collective-permute-start.19 = (bf16[32,1024]{1,0:T(8,128)(2,1)S(1)}, bf16[32,1024]{1,0:T(8,128)(2,1)S(1)}, u32[]{:S(2)}, u32[]{:S(2)}) collective-permute-start(bf16[32,1024]{1,0:T(8,128)(2,1)S(1)} %get-tuple-element.78), channel_id=1, source_target_pairs={{0,2},{2,0},{4,6},{6,4},{8,10},{10,8},{12,14},{14,12},{1,3},{3,1},... | collective-permute-start | bytes 196616 | tf_op jit(solution)/shard_map/ppermute | solution.py:482
  65.9 4.5 %collective-permute-start.20 = (bf16[32,1024]{1,0:T(8,128)(2,1)S(1)}, bf16[32,1024]{1,0:T(8,128)(2,1)S(1)}, u32[]{:S(2)}, u32[]{:S(2)}) collective-permute-start(bf16[32,1024]{1,0:T(8,128)(2,1)S(1)} %get-tuple-element.80), channel_id=1, source_target_pairs={{0,4},{2,6},{4,0},{6,2},{8,12},{10,14},{12,8},{14,10},{1,5},{3,7},... | collective-permute-start | bytes 196616 | tf_op jit(solution)/shard_map/ppermute | solution.py:482
  66.0 6.9 %collective-permute-start.21 = (bf16[32,1024]{1,0:T(8,128)(2,1)S(1)}, bf16[32,1024]{1,0:T(8,128)(2,1)S(1)}, u32[]{:S(2)}, u32[]{:S(2)}) collective-permute-start(bf16[32,1024]{1,0:T(8,128)(2,1)S(1)} %get-tuple-element.80), channel_id=1, source_target_pairs={{0,8},{2,10},{4,12},{6,14},{8,0},{10,2},{12,4},{14,6},{1,9},{3,11}... | collective-permute-start | bytes 196616 | tf_op jit(solution)/shard_map/ppermute | solution.py:482
  68.5 6.1 %collective-permute-start.22 = (bf16[32,1024]{1,0:T(8,128)(2,1)S(1)}, bf16[32,1024]{1,0:T(8,128)(2,1)S(1)}, u32[]{:S(2)}, u32[]{:S(2)}) collective-permute-start(bf16[32,1024]{1,0:T(8,128)(2,1)S(1)} %get-tuple-element.80), channel_id=1, source_target_pairs={{0,12},{2,14},{4,8},{6,10},{8,4},{10,6},{12,0},{14,2},{1,13},{3,15... | collective-permute-start | bytes 196616 | tf_op jit(solution)/shard_map/ppermute | solution.py:482
  74.6 1.3 %collective-permute-start.23 = (bf16[32,512]{1,0:T(8,128)(2,1)S(1)}, bf16[32,512]{1,0:T(8,128)(2,1)S(1)}, u32[]{:S(2)}, u32[]{:S(2)}) collective-permute-start(bf16[32,512]{1,0:T(8,128)(2,1)S(1)} %get-tuple-element.83), channel_id=1, source_target_pairs={{0,1},{1,0},{2,3},{3,2},{4,5},{5,4},{6,7},{7,6},{8,9},{9,8},{10,11... | collective-permute-start | bytes 98312 | tf_op jit(solution)/shard_map/ppermute | solution.py:450
  78.2 1.3 %collective-permute-start.24 = (f32[64,256]{1,0:T(8,128)S(1)}, f32[64,256]{1,0:T(8,128)S(1)}, u32[]{:S(2)}, u32[]{:S(2)}) collective-permute-start(f32[64,256]{1,0:T(8,128)S(1)} %shard_map.106.mine_ref), channel_id=1, source_target_pairs={{0,1},{1,0},{2,3},{3,2},{4,5},{5,4},{6,7},{7,6},{8,9},{9,8},{10,11... | collective-permute-start | bytes 196616 | tf_op jit(solution)/shard_map/ppermute | solution.py:450
  81.7 4.3 %collective-permute-start.25 = (bf16[64,512]{1,0:T(8,128)(2,1)S(1)}, bf16[64,512]{1,0:T(8,128)(2,1)S(1)}, u32[]{:S(2)}, u32[]{:S(2)}) collective-permute-start(bf16[64,512]{1,0:T(8,128)(2,1)S(1)} %get-tuple-element.86), channel_id=1, source_target_pairs={{0,2},{2,0},{4,6},{6,4},{8,10},{10,8},{12,14},{14,12},{1,3},{3,1},... | collective-permute-start | bytes 196616 | tf_op jit(solution)/shard_map/ppermute | solution.py:482
  86.1 4.5 %collective-permute-start.26 = (bf16[64,512]{1,0:T(8,128)(2,1)S(1)}, bf16[64,512]{1,0:T(8,128)(2,1)S(1)}, u32[]{:S(2)}, u32[]{:S(2)}) collective-permute-start(bf16[64,512]{1,0:T(8,128)(2,1)S(1)} %get-tuple-element.88), channel_id=1, source_target_pairs={{0,4},{2,6},{4,0},{6,2},{8,12},{10,14},{12,8},{14,10},{1,5},{3,7},... | collective-permute-start | bytes 196616 | tf_op jit(solution)/shard_map/ppermute | solution.py:482
  86.2 6.8 %collective-permute-start.27 = (bf16[64,512]{1,0:T(8,128)(2,1)S(1)}, bf16[64,512]{1,0:T(8,128)(2,1)S(1)}, u32[]{:S(2)}, u32[]{:S(2)}) collective-permute-start(bf16[64,512]{1,0:T(8,128)(2,1)S(1)} %get-tuple-element.88), channel_id=1, source_target_pairs={{0,8},{2,10},{4,12},{6,14},{8,0},{10,2},{12,4},{14,6},{1,9},{3,11}... | collective-permute-start | bytes 196616 | tf_op jit(solution)/shard_map/ppermute | solution.py:482
  88.5 6.1 %collective-permute-start.28 = (bf16[64,512]{1,0:T(8,128)(2,1)S(1)}, bf16[64,512]{1,0:T(8,128)(2,1)S(1)}, u32[]{:S(2)}, u32[]{:S(2)}) collective-permute-start(bf16[64,512]{1,0:T(8,128)(2,1)S(1)} %get-tuple-element.88), channel_id=1, source_target_pairs={{0,12},{2,14},{4,8},{6,10},{8,4},{10,6},{12,0},{14,2},{1,13},{3,15... | collective-permute-start | bytes 196616 | tf_op jit(solution)/shard_map/ppermute | solution.py:482
  94.6 1.3 %collective-permute-start.29 = (bf16[32,512]{1,0:T(8,128)(2,1)S(1)}, bf16[32,512]{1,0:T(8,128)(2,1)S(1)}, u32[]{:S(2)}, u32[]{:S(2)}) collective-permute-start(bf16[32,512]{1,0:T(8,128)(2,1)S(1)} %get-tuple-element.90), channel_id=1, source_target_pairs={{0,1},{1,0},{2,3},{3,2},{4,5},{5,4},{6,7},{7,6},{8,9},{9,8},{10,11... | collective-permute-start | bytes 98312 | tf_op jit(solution)/shard_map/ppermute | solution.py:450
  98.0 12.9 %all-to-all-start = ((bf16[8,64,256]{2,1,0:T(8,128)(2,1)}), bf16[8,64,256]{2,1,0:T(8,128)(2,1)S(1)}, u32[]{:S(2)}, u32[]{:S(2)}) async-start(bf16[8,64,256]{2,1,0:T(8,128)(2,1)} %shard_map.110), calls=%async_computation | async-start | bytes 524288 | tf_op jit(solution)/shard_map/all_to_all | solution.py:598
  111.2 1.4 %collective-permute-start.30 = (bf16[256,256]{1,0:T(8,128)(2,1)S(1)}, bf16[256,256]{1,0:T(8,128)(2,1)S(1)}, u32[]{:S(2)}, u32[]{:S(2)}) collective-permute-start(bf16[256,256]{1,0:T(8,128)(2,1)S(1)} %get-tuple-element.94), channel_id=1, source_target_pairs={{0,1},{1,0},{2,3},{3,2},{4,5},{5,4},{6,7},{7,6},{8,9},{9,8},{10,11... | collective-permute-start | bytes 393224 | tf_op jit(solution)/shard_map/ppermute | solution.py:450
  (12 other events, 135.2 us)

commit v7 on v6

--- a/solution.py
+++ b/solution.py
@@ -119,6 +119,7 @@
 F32 = jnp.float32
 LIMIT = 10 * 1024 * 1024
 BESIDE = 32 * 1024 * 1024
+NEAR, FAR = (1,), (6, 2, 4)
 VMEM = pl.BlockSpec(memory_space=pltpu.VMEM)
 SMEM = pl.BlockSpec(memory_space=pltpu.SMEM)
 
@@ -450,9 +451,11 @@
     return lax.ppermute(value, "narrow", [(0, 1), (1, 0)])
 
 
-def pair_kernel(part_ref, got_ref, *refs):
+def near_kernel(part_ref, *refs, count):
     pair_ref, pair_b_ref = refs[-2:]
-    pair = part_ref[...] + got_ref[...].astype(F32)
+    pair = part_ref[...]
+    for got_ref in refs[:count]:
+        pair += got_ref[...].astype(F32)
     pair_ref[...] = pair
     pair_b_ref[...] = pair.astype(BF)
 
@@ -483,9 +486,10 @@
 
     shape = part.shape
     pair, pair_b = kernel_call(
-        pair_kernel, (), (part, partner(part_b, 1)), [shape_of(shape, F32), shape_of(shape, BF)], rest=rest
-    )
-    return (pair, *[partner(pair_b, mask) for mask in (2, 4, 6)])
+        functools.partial(near_kernel, count=len(NEAR)), (), (part, *[partner(part_b, mask) for mask in NEAR]),
+        [shape_of(shape, F32), shape_of(shape, BF)], rest=rest,
+    )
+    return (pair, *[partner(pair_b, mask) for mask in FAR])
 
 
 def to_feature_halves(n, part, part_b, rest=()):

time: 114 us -> 112 us (0.982)
  waiting for transfers between devices: 53.5 us -> 51.2 us
    ppermute x16, waiting for transfers between devices: 31.8 us -> 29.5 us  [partner(): return lax.ppermute(value, 'wide', [(i, i ^ mask) for i in range(8)])]
  transfers between devices with their start and end apart: 32 -> 32, of which waited for: 24 -> 27; matrix products, arithmetic and copies ran while one was open for 0% -> 0% of each run, Pallas kernels for 3% -> 3%
where the time goes in v7:
time: 112 us
  waiting for transfers between devices  51.2 us (46%)
  starting transfers between devices  36.9 us (33%)
  Pallas kernels  21.1 us (19%)
  local copies, waits for them, and re-layouts  1.45 us (1%)
    ppermute x16, waiting for transfers between devices, partner(): return lax.ppermute(value, 'wide', [(i, i ^ mask) for i in range(8)])  29.5 us
    pallas_call x24, Pallas kernels, kernel_call(): pl.pallas_call(kernel, in_specs=[SMEM] * len(places) + [VMEM] * len(array...  21.1 us
    ppermute x16, starting transfers between devices, partner(): return lax.ppermute(value, 'wide', [(i, i ^ mask) for i in range(8)])  20.2 us
    ppermute x7, starting transfers between devices, across_wide(): lax.ppermute(messages[mask], 'wide', [(i, i ^ mask) for i in range(8)])  12.5 us
    ppermute x8, waiting for transfers between devices, swap_narrow(): return lax.ppermute(value, 'narrow', [(0, 1), (1, 0)])  8.57 us
    all_to_all x1, waiting for transfers between devices, eight_shards(): lax.all_to_all(leaving, 'wide', split_axis=0, concat_axis=0, tiled=True)  7.99 us
    ppermute x7, waiting for transfers between devices, across_wide(): lax.ppermute(messages[mask], 'wide', [(i, i ^ mask) for i in range(8)])  5.14 us
    all_to_all x1, starting transfers between devices, eight_shards(): lax.all_to_all(leaving, 'wide', split_axis=0, concat_axis=0, tiled=True)  3.41 us
  transfers between devices with their start and end apart: 32, of which 27 were waited for; matrix products, arithmetic and copies ran while one was open for 0% of the time, Pallas kernels for 3%

profile of v7, /device:TPU:0, one launch (start us, length us, event | category | flops | bytes accessed | tf_op | source)
XLA Modules:
  0.0 111.7 jit_solution(4298233793320217151)
XLA Ops:
  0.7 2.0 %shard_map.91 = (bf16[128,256]{1,0:T(8,128)(2,1)S(1)}, bf16[128,256]{1,0:T(8,128)(2,1)S(1)}, bf16[128,256]{1,0:T(8,128)(2,1)S(1)}, bf16[128,256]{1,0:T(8,128)(2,...) custom-call(s32[1]{0:T(128)} %bitcast.n_ref, ...), custom_call_target="tpu_custom_call" | custom-call | tf_op jit(solution)/shard_map/pallas_call | solution.py:140
  2.7 3.0 %collective-permute-start = (bf16[128,256]{1,0:T(8,128)(2,1)S(1)}, bf16[128,256]{1,0:T(8,128)(2,1)S(1)}, u32[]{:S(2)}, u32[]{:S(2)}) collective-permute-start(bf16[128,256]{1,0:T(8,128)(2,1)S(1)} %get-tuple-element.51), channel_id=1, source_target_pairs={{0,2},{2,0},{4,6},{6,4},{8,10},{10,8},{12,14},{14,12},{1,3},{3,1},... | collective-permute-start | bytes 196616 | tf_op jit(solution)/shard_map/ppermute | solution.py:515
  5.7 1.6 %collective-permute-start.1 = (bf16[128,256]{1,0:T(8,128)(2,1)S(1)}, bf16[128,256]{1,0:T(8,128)(2,1)S(1)}, u32[]{:S(2)}, u32[]{:S(2)}) collective-permute-start(bf16[128,256]{1,0:T(8,128)(2,1)S(1)} %get-tuple-element.52), channel_id=1, source_target_pairs={{0,4},{2,6},{4,0},{6,2},{8,12},{10,14},{12,8},{14,10},{1,5},{3,7},... | collective-permute-start | bytes 196616 | tf_op jit(solution)/shard_map/ppermute | solution.py:515
  7.3 3.0 %collective-permute-start.3 = (bf16[128,256]{1,0:T(8,128)(2,1)S(1)}, bf16[128,256]{1,0:T(8,128)(2,1)S(1)}, u32[]{:S(2)}, u32[]{:S(2)}) collective-permute-start(bf16[128,256]{1,0:T(8,128)(2,1)S(1)} %get-tuple-element.54), channel_id=1, source_target_pairs={{0,8},{2,10},{4,12},{6,14},{8,0},{10,2},{12,4},{14,6},{1,9},{3,11}... | collective-permute-start | bytes 196616 | tf_op jit(solution)/shard_map/ppermute | solution.py:515
  11.6 3.6 %collective-permute-start.5 = (bf16[128,256]{1,0:T(8,128)(2,1)S(1)}, bf16[128,256]{1,0:T(8,128)(2,1)S(1)}, u32[]{:S(2)}, u32[]{:S(2)}) collective-permute-start(bf16[128,256]{1,0:T(8,128)(2,1)S(1)} %get-tuple-element.56), channel_id=1, source_target_pairs={{0,12},{2,14},{4,8},{6,10},{8,4},{10,6},{12,0},{14,2},{1,13},{3,15... | collective-permute-start | bytes 196616 | tf_op jit(solution)/shard_map/ppermute | solution.py:515
  17.1 3.4 %collective-permute-done.4.refs_5_ = bf16[128,256]{1,0:T(8,128)(2,1)S(1)} collective-permute-done((bf16[128,256]{1,0:T(8,128)(2,1)S(1)}, bf16[128,256]{1,0:T(8,128)(2,1)S(1)}, u32[]{:S(2)}, u32[]{:S(2)}) %collective-permute-start.4) | collective-permute-done | bytes 65568 | tf_op jit(solution)/shard_map/ppermute | solution.py:515
  20.5 1.7 %collective-permute-done.6.refs_7_ = bf16[128,256]{1,0:T(8,128)(2,1)S(1)} collective-permute-done((bf16[128,256]{1,0:T(8,128)(2,1)S(1)}, bf16[128,256]{1,0:T(8,128)(2,1)S(1)}, u32[]{:S(2)}, u32[]{:S(2)}) %collective-permute-start.6) | collective-permute-done | bytes 65568 | tf_op jit(solution)/shard_map/ppermute | solution.py:515
  26.3 3.8 %collective-permute-done.8.refs_0_ = bf16[32,1024]{1,0:T(8,128)(2,1)S(1)} collective-permute-done((bf16[32,1024]{1,0:T(8,128)(2,1)S(1)}, bf16[32,1024]{1,0:T(8,128)(2,1)S(1)}, u32[]{:S(2)}, u32[]{:S(2)}) %collective-permute-start.8) | collective-permute-done | bytes 65568 | tf_op jit(solution)/shard_map/ppermute | solution.py:485
  30.1 1.7 %collective-permute-start.10 = (bf16[32,1024]{1,0:T(8,128)(2,1)S(1)}, bf16[32,1024]{1,0:T(8,128)(2,1)S(1)}, u32[]{:S(2)}, u32[]{:S(2)}) collective-permute-start(bf16[32,1024]{1,0:T(8,128)(2,1)S(1)} %get-tuple-element.65), channel_id=1, source_target_pairs={{0,4},{2,6},{4,0},{6,2},{8,12},{10,14},{12,8},{14,10},{1,5},{3,7},... | collective-permute-start | bytes 196616 | tf_op jit(solution)/shard_map/ppermute | solution.py:485
  33.0 1.6 %collective-permute-start.9 = (bf16[32,1024]{1,0:T(8,128)(2,1)S(1)}, bf16[32,1024]{1,0:T(8,128)(2,1)S(1)}, u32[]{:S(2)}, u32[]{:S(2)}) collective-permute-start(bf16[32,1024]{1,0:T(8,128)(2,1)S(1)} %get-tuple-element.65), channel_id=1, source_target_pairs={{0,12},{2,14},{4,8},{6,10},{8,4},{10,6},{12,0},{14,2},{1,13},{3,15... | collective-permute-start | bytes 196616 | tf_op jit(solution)/shard_map/ppermute | solution.py:485
  34.9 3.0 %collective-permute-done.11.three_ref = bf16[32,1024]{1,0:T(8,128)(2,1)S(1)} collective-permute-done((bf16[32,1024]{1,0:T(8,128)(2,1)S(1)}, bf16[32,1024]{1,0:T(8,128)(2,1)S(1)}, u32[]{:S(2)}, u32[]{:S(2)}) %collective-permute-start.11) | collective-permute-done | bytes 65568 | tf_op jit(solution)/shard_map/ppermute | solution.py:485
  40.5 1.4 %shard_map.98.mine_ref = f32[64,256]{1,0:T(8,128)S(1)} custom-call(s32[1]{0:T(128)} %bitcast.n_ref, bf16[32,512]{1,0:T(8,128)(2,1)S(1)} %get-tuple-element.67.mine_ref, bf16[32,512]{1,0:T(8,128)(2,1)S(1)} %collective-permute-done.12.got_ref, bf16[27,1024,256]{2,1,0:T(8,128)(2,1)S(1)} %bitcast.8), custom_call_target="tpu_custom_call" | custom-call | tf_op jit(solution)/shard_map/pallas_call | solution.py:140
  45.2 3.7 %collective-permute-done.14.refs_0_ = bf16[64,512]{1,0:T(8,128)(2,1)S(1)} collective-permute-done((bf16[64,512]{1,0:T(8,128)(2,1)S(1)}, bf16[64,512]{1,0:T(8,128)(2,1)S(1)}, u32[]{:S(2)}, u32[]{:S(2)}) %collective-permute-start.14) | collective-permute-done | bytes 65568 | tf_op jit(solution)/shard_map/ppermute | solution.py:485
  48.9 1.7 %collective-permute-start.15 = (bf16[64,512]{1,0:T(8,128)(2,1)S(1)}, bf16[64,512]{1,0:T(8,128)(2,1)S(1)}, u32[]{:S(2)}, u32[]{:S(2)}) collective-permute-start(bf16[64,512]{1,0:T(8,128)(2,1)S(1)} %get-tuple-element.73), channel_id=1, source_target_pairs={{0,12},{2,14},{4,8},{6,10},{8,4},{10,6},{12,0},{14,2},{1,13},{3,15... | collective-permute-start | bytes 196616 | tf_op jit(solution)/shard_map/ppermute | solution.py:485
  51.0 2.3 %collective-permute-start.17 = (bf16[64,512]{1,0:T(8,128)(2,1)S(1)}, bf16[64,512]{1,0:T(8,128)(2,1)S(1)}, u32[]{:S(2)}, u32[]{:S(2)}) collective-permute-start(bf16[64,512]{1,0:T(8,128)(2,1)S(1)} %get-tuple-element.73), channel_id=1, source_target_pairs={{0,8},{2,10},{4,12},{6,14},{8,0},{10,2},{12,4},{14,6},{1,9},{3,11}... | collective-permute-start | bytes 196616 | tf_op jit(solution)/shard_map/ppermute | solution.py:485
  53.4 2.2 %collective-permute-done.15.one_ref = bf16[64,512]{1,0:T(8,128)(2,1)S(1)} collective-permute-done((bf16[64,512]{1,0:T(8,128)(2,1)S(1)}, bf16[64,512]{1,0:T(8,128)(2,1)S(1)}, u32[]{:S(2)}, u32[]{:S(2)}) %collective-permute-start.15) | collective-permute-done | bytes 65568 | tf_op jit(solution)/shard_map/ppermute | solution.py:485
  57.9 2.7 %shard_map.103 = (bf16[8,32,256]{2,1,0:T(8,128)(2,1)S(1)}, f32[32,1024]{1,0:T(8,128)S(1)}, bf16[32,1024]{1,0:T(8,128)(2,1)S(1)}) custom-call(s32[1]{0:T(128)} %bitcast.n_ref, f32[32,1024]{1,0:T(8,128)S(1)} %get-tuple-element.66.merged_ref, f32[32,512]{1,0:T(8,128)S(1)} %get-tuple-element.74.mine_ref, bf16[32,512]{1,0:T(8,128)(2,1)S(1)} %collective-permute-done.18.got_ref, ...), custom_call_target="tpu_custom_call" | custom-call | tf_op jit(solution)/shard_map/pallas_call | solution.py:140
  61.2 3.7 %collective-permute-done.19.refs_0_ = bf16[32,1024]{1,0:T(8,128)(2,1)S(1)} collective-permute-done((bf16[32,1024]{1,0:T(8,128)(2,1)S(1)}, bf16[32,1024]{1,0:T(8,128)(2,1)S(1)}, u32[]{:S(2)}, u32[]{:S(2)}) %collective-permute-start.19) | collective-permute-done | bytes 65568 | tf_op jit(solution)/shard_map/ppermute | solution.py:485
  65.0 1.9 %collective-permute-start.20 = (bf16[32,1024]{1,0:T(8,128)(2,1)S(1)}, bf16[32,1024]{1,0:T(8,128)(2,1)S(1)}, u32[]{:S(2)}, u32[]{:S(2)}) collective-permute-start(bf16[32,1024]{1,0:T(8,128)(2,1)S(1)} %get-tuple-element.80), channel_id=1, source_target_pairs={{0,12},{2,14},{4,8},{6,10},{8,4},{10,6},{12,0},{14,2},{1,13},{3,15... | collective-permute-start | bytes 196616 | tf_op jit(solution)/shard_map/ppermute | solution.py:485
  67.6 1.9 %collective-permute-start.22 = (bf16[32,1024]{1,0:T(8,128)(2,1)S(1)}, bf16[32,1024]{1,0:T(8,128)(2,1)S(1)}, u32[]{:S(2)}, u32[]{:S(2)}) collective-permute-start(bf16[32,1024]{1,0:T(8,128)(2,1)S(1)} %get-tuple-element.80), channel_id=1, source_target_pairs={{0,8},{2,10},{4,12},{6,14},{8,0},{10,2},{12,4},{14,6},{1,9},{3,11}... | collective-permute-start | bytes 196616 | tf_op jit(solution)/shard_map/ppermute | solution.py:485
  69.4 2.4 %collective-permute-done.20.one_ref = bf16[32,1024]{1,0:T(8,128)(2,1)S(1)} collective-permute-done((bf16[32,1024]{1,0:T(8,128)(2,1)S(1)}, bf16[32,1024]{1,0:T(8,128)(2,1)S(1)}, u32[]{:S(2)}, u32[]{:S(2)}) %collective-permute-start.20) | collective-permute-done | bytes 65568 | tf_op jit(solution)/shard_map/ppermute | solution.py:485
  74.1 2.3 %shard_map.106.mine_ref = f32[64,256]{1,0:T(8,128)S(1)} custom-call(s32[1]{0:T(128)} %bitcast.n_ref, bf16[32,512]{1,0:T(8,128)(2,1)S(1)} %get-tuple-element.82.mine_ref, bf16[32,512]{1,0:T(8,128)(2,1)S(1)} %collective-permute-done.23.got_ref, bf16[27,256,1024]{2,1,0:T(8,128)(2,1)S(1)} %bitcast.6), custom_call_target="tpu_custom_call" | custom-call | tf_op jit(solution)/shard_map/pallas_call | solution.py:140
  77.7 2.2 %shard_map.107 = (f32[64,512]{1,0:T(8,128)S(1)}, bf16[64,512]{1,0:T(8,128)(2,1)S(1)}) custom-call(s32[1]{0:T(128)} %bitcast.n_ref, f32[64,256]{1,0:T(8,128)S(1)} %shard_map.106.mine_ref, f32[64,256]{1,0:T(8,128)S(1)} %collective-permute-done.24.got_ref, f32[64,256]{1,0:T(8,128)S(1)} %get-tuple-element.84.gate_ref, bf16[27,1024,256]{2,1,0:T(8,128)(2,1)S(1)} %bitcast.8), custom_call_target="tpu_custom_call" | custom-call | tf_op jit(solution)/shard_map/pallas_call | solution.py:140
  80.6 3.7 %collective-permute-done.25.refs_0_ = bf16[64,512]{1,0:T(8,128)(2,1)S(1)} collective-permute-done((bf16[64,512]{1,0:T(8,128)(2,1)S(1)}, bf16[64,512]{1,0:T(8,128)(2,1)S(1)}, u32[]{:S(2)}, u32[]{:S(2)}) %collective-permute-start.25) | collective-permute-done | bytes 65568 | tf_op jit(solution)/shard_map/ppermute | solution.py:485
  84.3 1.9 %collective-permute-start.26 = (bf16[64,512]{1,0:T(8,128)(2,1)S(1)}, bf16[64,512]{1,0:T(8,128)(2,1)S(1)}, u32[]{:S(2)}, u32[]{:S(2)}) collective-permute-start(bf16[64,512]{1,0:T(8,128)(2,1)S(1)} %get-tuple-element.88), channel_id=1, source_target_pairs={{0,12},{2,14},{4,8},{6,10},{8,4},{10,6},{12,0},{14,2},{1,13},{3,15... | collective-permute-start | bytes 196616 | tf_op jit(solution)/shard_map/ppermute | solution.py:485
  86.7 2.1 %collective-permute-start.28 = (bf16[64,512]{1,0:T(8,128)(2,1)S(1)}, bf16[64,512]{1,0:T(8,128)(2,1)S(1)}, u32[]{:S(2)}, u32[]{:S(2)}) collective-permute-start(bf16[64,512]{1,0:T(8,128)(2,1)S(1)} %get-tuple-element.88), channel_id=1, source_target_pairs={{0,8},{2,10},{4,12},{6,14},{8,0},{10,2},{12,4},{14,6},{1,9},{3,11}... | collective-permute-start | bytes 196616 | tf_op jit(solution)/shard_map/ppermute | solution.py:485
  88.8 2.4 %collective-permute-done.26.one_ref = bf16[64,512]{1,0:T(8,128)(2,1)S(1)} collective-permute-done((bf16[64,512]{1,0:T(8,128)(2,1)S(1)}, bf16[64,512]{1,0:T(8,128)(2,1)S(1)}, u32[]{:S(2)}, u32[]{:S(2)}) %collective-permute-start.26) | collective-permute-done | bytes 65568 | tf_op jit(solution)/shard_map/ppermute | solution.py:485
  93.5 2.1 %shard_map.110 = bf16[8,64,256]{2,1,0:T(8,128)(2,1)} custom-call(s32[1]{0:T(128)} %bitcast.n_ref, s32[1]{0:T(128)} %bitcast.1.w_ref, f32[32,1024]{1,0:T(8,128)S(1)} %get-tuple-element.81.res_ref, f32[32,512]{1,0:T(8,128)S(1)} %get-tuple-element.89.mine_ref, bf16[32,512]{1,0:T(8,128)(2,1)S(1)} %collective-permute-done.29.got_ref, ...), custom_call_target="tpu_custom_call" | custom-call | tf_op jit(solution)/shard_map/pallas_call | solution.py:140
  95.6 3.4 %all-to-all-start = ((bf16[8,64,256]{2,1,0:T(8,128)(2,1)}), bf16[8,64,256]{2,1,0:T(8,128)(2,1)S(1)}, u32[]{:S(2)}, u32[]{:S(2)}) async-start(bf16[8,64,256]{2,1,0:T(8,128)(2,1)} %shard_map.110), calls=%async_computation | async-start | bytes 524288 | tf_op jit(solution)/shard_map/all_to_all | solution.py:602
  99.1 1.4 %shard_map.111.band_ref = bf16[1024,768]{1,0:T(8,128)(2,1)S(1)} custom-call(bf16[27,32,32]{2,1,0:T(8,128)(2,1)S(1)} %copy-done.3), custom_call_target="tpu_custom_call" | custom-call | bytes 33554432 | tf_op jit(solution)/shard_map/pallas_call | solution.py:140
  100.5 8.0 %all-to-all-done.planes_ref = bf16[8,64,256]{2,1,0:T(8,128)(2,1)S(1)} async-done(((bf16[8,64,256]{2,1,0:T(8,128)(2,1)}), bf16[8,64,256]{2,1,0:T(8,128)(2,1)S(1)}, u32[]{:S(2)}, u32[]{:S(2)}) %all-to-all-start) | async-done | bytes 262176 | tf_op jit(solution)/shard_map/all_to_all | solution.py:602
  110.2 1.5 %shard_map.114 = bf16[8,16,16,32]{3,2,1,0:T(8,128)(2,1)} custom-call(s32[1]{0:T(128)} %bitcast.n_ref, f32[256,768]{1,0:T(8,128)S(1)} %shard_map.112.main_ref, bf16[256,256]{1,0:T(8,128)(2,1)S(1)} %get-tuple-element.93.own_ref, bf16[256,256]{1,0:T(8,128)(2,1)S(1)} %collective-permute-done.30.got_ref, bf16[1024,768]{1,0:T(8,128)(2,1)S(1)} %shard_map.111.band_ref), custom_call_target="tpu_custom_call" | custom-call | tf_op jit(solution)/shard_map/pallas_call | solution.py:140
  (82 shorter events, 27.3 us)
Async XLA Ops:
  2.7 8.9 %collective-permute-start = (bf16[128,256]{1,0:T(8,128)(2,1)S(1)}, bf16[128,256]{1,0:T(8,128)(2,1)S(1)}, u32[]{:S(2)}, u32[]{:S(2)}) collective-permute-start(bf16[128,256]{1,0:T(8,128)(2,1)S(1)} %get-tuple-element.51), channel_id=1, source_target_pairs={{0,2},{2,0},{4,6},{6,4},{8,10},{10,8},{12,14},{14,12},{1,3},{3,1},... | collective-permute-start | bytes 196616 | tf_op jit(solution)/shard_map/ppermute | solution.py:515
  5.7 9.5 %collective-permute-start.1 = (bf16[128,256]{1,0:T(8,128)(2,1)S(1)}, bf16[128,256]{1,0:T(8,128)(2,1)S(1)}, u32[]{:S(2)}, u32[]{:S(2)}) collective-permute-start(bf16[128,256]{1,0:T(8,128)(2,1)S(1)} %get-tuple-element.52), channel_id=1, source_target_pairs={{0,4},{2,6},{4,0},{6,2},{8,12},{10,14},{12,8},{14,10},{1,5},{3,7},... | collective-permute-start | bytes 196616 | tf_op jit(solution)/shard_map/ppermute | solution.py:515
  7.3 9.8 %collective-permute-start.2 = (bf16[128,256]{1,0:T(8,128)(2,1)S(1)}, bf16[128,256]{1,0:T(8,128)(2,1)S(1)}, u32[]{:S(2)}, u32[]{:S(2)}) collective-permute-start(bf16[128,256]{1,0:T(8,128)(2,1)S(1)} %get-tuple-element.53), channel_id=1, source_target_pairs={{0,6},{2,4},{4,2},{6,0},{8,14},{10,12},{12,10},{14,8},{1,7},{3,5},... | collective-permute-start | bytes 196616 | tf_op jit(solution)/shard_map/ppermute | solution.py:515
  7.3 9.8 %collective-permute-start.3 = (bf16[128,256]{1,0:T(8,128)(2,1)S(1)}, bf16[128,256]{1,0:T(8,128)(2,1)S(1)}, u32[]{:S(2)}, u32[]{:S(2)}) collective-permute-start(bf16[128,256]{1,0:T(8,128)(2,1)S(1)} %get-tuple-element.54), channel_id=1, source_target_pairs={{0,8},{2,10},{4,12},{6,14},{8,0},{10,2},{12,4},{14,6},{1,9},{3,11}... | collective-permute-start | bytes 196616 | tf_op jit(solution)/shard_map/ppermute | solution.py:515
  10.3 10.2 %collective-permute-start.4 = (bf16[128,256]{1,0:T(8,128)(2,1)S(1)}, bf16[128,256]{1,0:T(8,128)(2,1)S(1)}, u32[]{:S(2)}, u32[]{:S(2)}) collective-permute-start(bf16[128,256]{1,0:T(8,128)(2,1)S(1)} %get-tuple-element.55), channel_id=1, source_target_pairs={{0,10},{2,8},{4,14},{6,12},{8,2},{10,0},{12,6},{14,4},{1,11},{3,9}... | collective-permute-start | bytes 196616 | tf_op jit(solution)/shard_map/ppermute | solution.py:515
  11.6 8.9 %collective-permute-start.5 = (bf16[128,256]{1,0:T(8,128)(2,1)S(1)}, bf16[128,256]{1,0:T(8,128)(2,1)S(1)}, u32[]{:S(2)}, u32[]{:S(2)}) collective-permute-start(bf16[128,256]{1,0:T(8,128)(2,1)S(1)} %get-tuple-element.56), channel_id=1, source_target_pairs={{0,12},{2,14},{4,8},{6,10},{8,4},{10,6},{12,0},{14,2},{1,13},{3,15... | collective-permute-start | bytes 196616 | tf_op jit(solution)/shard_map/ppermute | solution.py:515
  15.2 7.1 %collective-permute-start.6 = (bf16[128,256]{1,0:T(8,128)(2,1)S(1)}, bf16[128,256]{1,0:T(8,128)(2,1)S(1)}, u32[]{:S(2)}, u32[]{:S(2)}) collective-permute-start(bf16[128,256]{1,0:T(8,128)(2,1)S(1)} %get-tuple-element.57), channel_id=1, source_target_pairs={{0,14},{2,12},{4,10},{6,8},{8,6},{10,4},{12,2},{14,0},{1,15},{3,13... | collective-permute-start | bytes 196616 | tf_op jit(solution)/shard_map/ppermute | solution.py:515
  22.5 1.4 %collective-permute-start.7 = (bf16[256,256]{1,0:T(8,128)(2,1)S(1)}, bf16[256,256]{1,0:T(8,128)(2,1)S(1)}, u32[]{:S(2)}, u32[]{:S(2)}) collective-permute-start(bf16[256,256]{1,0:T(8,128)(2,1)S(1)} %get-tuple-element.61), channel_id=1, source_target_pairs={{0,1},{1,0},{2,3},{3,2},{4,5},{5,4},{6,7},{7,6},{8,9},{9,8},{10,11... | collective-permute-start | bytes 393224 | tf_op jit(solution)/shard_map/ppermute | solution.py:451
  25.7 4.3 %collective-permute-start.8 = (bf16[32,1024]{1,0:T(8,128)(2,1)S(1)}, bf16[32,1024]{1,0:T(8,128)(2,1)S(1)}, u32[]{:S(2)}, u32[]{:S(2)}) collective-permute-start(bf16[32,1024]{1,0:T(8,128)(2,1)S(1)} %get-tuple-element.63), channel_id=1, source_target_pairs={{0,2},{2,0},{4,6},{6,4},{8,10},{10,8},{12,14},{14,12},{1,3},{3,1},... | collective-permute-start | bytes 196616 | tf_op jit(solution)/shard_map/ppermute | solution.py:485
  30.1 4.9 %collective-permute-start.10 = (bf16[32,1024]{1,0:T(8,128)(2,1)S(1)}, bf16[32,1024]{1,0:T(8,128)(2,1)S(1)}, u32[]{:S(2)}, u32[]{:S(2)}) collective-permute-start(bf16[32,1024]{1,0:T(8,128)(2,1)S(1)} %get-tuple-element.65), channel_id=1, source_target_pairs={{0,4},{2,6},{4,0},{6,2},{8,12},{10,14},{12,8},{14,10},{1,5},{3,7},... | collective-permute-start | bytes 196616 | tf_op jit(solution)/shard_map/ppermute | solution.py:485
  31.8 6.1 %collective-permute-start.11 = (bf16[32,1024]{1,0:T(8,128)(2,1)S(1)}, bf16[32,1024]{1,0:T(8,128)(2,1)S(1)}, u32[]{:S(2)}, u32[]{:S(2)}) collective-permute-start(bf16[32,1024]{1,0:T(8,128)(2,1)S(1)} %get-tuple-element.65), channel_id=1, source_target_pairs={{0,8},{2,10},{4,12},{6,14},{8,0},{10,2},{12,4},{14,6},{1,9},{3,11}... | collective-permute-start | bytes 196616 | tf_op jit(solution)/shard_map/ppermute | solution.py:485
  33.0 6.2 %collective-permute-start.9 = (bf16[32,1024]{1,0:T(8,128)(2,1)S(1)}, bf16[32,1024]{1,0:T(8,128)(2,1)S(1)}, u32[]{:S(2)}, u32[]{:S(2)}) collective-permute-start(bf16[32,1024]{1,0:T(8,128)(2,1)S(1)} %get-tuple-element.65), channel_id=1, source_target_pairs={{0,12},{2,14},{4,8},{6,10},{8,4},{10,6},{12,0},{14,2},{1,13},{3,15... | collective-permute-start | bytes 196616 | tf_op jit(solution)/shard_map/ppermute | solution.py:485
  39.2 1.3 %collective-permute-start.12 = (bf16[32,512]{1,0:T(8,128)(2,1)S(1)}, bf16[32,512]{1,0:T(8,128)(2,1)S(1)}, u32[]{:S(2)}, u32[]{:S(2)}) collective-permute-start(bf16[32,512]{1,0:T(8,128)(2,1)S(1)} %get-tuple-element.68), channel_id=1, source_target_pairs={{0,1},{1,0},{2,3},{3,2},{4,5},{5,4},{6,7},{7,6},{8,9},{9,8},{10,11... | collective-permute-start | bytes 98312 | tf_op jit(solution)/shard_map/ppermute | solution.py:451
  41.9 1.3 %collective-permute-start.13 = (f32[64,256]{1,0:T(8,128)S(1)}, f32[64,256]{1,0:T(8,128)S(1)}, u32[]{:S(2)}, u32[]{:S(2)}) collective-permute-start(f32[64,256]{1,0:T(8,128)S(1)} %shard_map.98.mine_ref), channel_id=1, source_target_pairs={{0,1},{1,0},{2,3},{3,2},{4,5},{5,4},{6,7},{7,6},{8,9},{9,8},{10,11... | collective-permute-start | bytes 196616 | tf_op jit(solution)/shard_map/ppermute | solution.py:451
  44.6 4.3 %collective-permute-start.14 = (bf16[64,512]{1,0:T(8,128)(2,1)S(1)}, bf16[64,512]{1,0:T(8,128)(2,1)S(1)}, u32[]{:S(2)}, u32[]{:S(2)}) collective-permute-start(bf16[64,512]{1,0:T(8,128)(2,1)S(1)} %get-tuple-element.71), channel_id=1, source_target_pairs={{0,2},{2,0},{4,6},{6,4},{8,10},{10,8},{12,14},{14,12},{1,3},{3,1},... | collective-permute-start | bytes 196616 | tf_op jit(solution)/shard_map/ppermute | solution.py:485
  48.9 6.7 %collective-permute-start.15 = (bf16[64,512]{1,0:T(8,128)(2,1)S(1)}, bf16[64,512]{1,0:T(8,128)(2,1)S(1)}, u32[]{:S(2)}, u32[]{:S(2)}) collective-permute-start(bf16[64,512]{1,0:T(8,128)(2,1)S(1)} %get-tuple-element.73), channel_id=1, source_target_pairs={{0,12},{2,14},{4,8},{6,10},{8,4},{10,6},{12,0},{14,2},{1,13},{3,15... | collective-permute-start | bytes 196616 | tf_op jit(solution)/shard_map/ppermute | solution.py:485
  50.7 5.0 %collective-permute-start.16 = (bf16[64,512]{1,0:T(8,128)(2,1)S(1)}, bf16[64,512]{1,0:T(8,128)(2,1)S(1)}, u32[]{:S(2)}, u32[]{:S(2)}) collective-permute-start(bf16[64,512]{1,0:T(8,128)(2,1)S(1)} %get-tuple-element.73), channel_id=1, source_target_pairs={{0,4},{2,6},{4,0},{6,2},{8,12},{10,14},{12,8},{14,10},{1,5},{3,7},... | collective-permute-start | bytes 196616 | tf_op jit(solution)/shard_map/ppermute | solution.py:485
  51.0 5.6 %collective-permute-start.17 = (bf16[64,512]{1,0:T(8,128)(2,1)S(1)}, bf16[64,512]{1,0:T(8,128)(2,1)S(1)}, u32[]{:S(2)}, u32[]{:S(2)}) collective-permute-start(bf16[64,512]{1,0:T(8,128)(2,1)S(1)} %get-tuple-element.73), channel_id=1, source_target_pairs={{0,8},{2,10},{4,12},{6,14},{8,0},{10,2},{12,4},{14,6},{1,9},{3,11}... | collective-permute-start | bytes 196616 | tf_op jit(solution)/shard_map/ppermute | solution.py:485
  56.6 1.3 %collective-permute-start.18 = (bf16[32,512]{1,0:T(8,128)(2,1)S(1)}, bf16[32,512]{1,0:T(8,128)(2,1)S(1)}, u32[]{:S(2)}, u32[]{:S(2)}) collective-permute-start(bf16[32,512]{1,0:T(8,128)(2,1)S(1)} %get-tuple-element.75), channel_id=1, source_target_pairs={{0,1},{1,0},{2,3},{3,2},{4,5},{5,4},{6,7},{7,6},{8,9},{9,8},{10,11... | collective-permute-start | bytes 98312 | tf_op jit(solution)/shard_map/ppermute | solution.py:451
  60.7 4.3 %collective-permute-start.19 = (bf16[32,1024]{1,0:T(8,128)(2,1)S(1)}, bf16[32,1024]{1,0:T(8,128)(2,1)S(1)}, u32[]{:S(2)}, u32[]{:S(2)}) collective-permute-start(bf16[32,1024]{1,0:T(8,128)(2,1)S(1)} %get-tuple-element.78), channel_id=1, source_target_pairs={{0,2},{2,0},{4,6},{6,4},{8,10},{10,8},{12,14},{14,12},{1,3},{3,1},... | collective-permute-start | bytes 196616 | tf_op jit(solution)/shard_map/ppermute | solution.py:485
  65.0 6.8 %collective-permute-start.20 = (bf16[32,1024]{1,0:T(8,128)(2,1)S(1)}, bf16[32,1024]{1,0:T(8,128)(2,1)S(1)}, u32[]{:S(2)}, u32[]{:S(2)}) collective-permute-start(bf16[32,1024]{1,0:T(8,128)(2,1)S(1)} %get-tuple-element.80), channel_id=1, source_target_pairs={{0,12},{2,14},{4,8},{6,10},{8,4},{10,6},{12,0},{14,2},{1,13},{3,15... | collective-permute-start | bytes 196616 | tf_op jit(solution)/shard_map/ppermute | solution.py:485
  66.9 5.0 %collective-permute-start.21 = (bf16[32,1024]{1,0:T(8,128)(2,1)S(1)}, bf16[32,1024]{1,0:T(8,128)(2,1)S(1)}, u32[]{:S(2)}, u32[]{:S(2)}) collective-permute-start(bf16[32,1024]{1,0:T(8,128)(2,1)S(1)} %get-tuple-element.80), channel_id=1, source_target_pairs={{0,4},{2,6},{4,0},{6,2},{8,12},{10,14},{12,8},{14,10},{1,5},{3,7},... | collective-permute-start | bytes 196616 | tf_op jit(solution)/shard_map/ppermute | solution.py:485
  67.6 5.3 %collective-permute-start.22 = (bf16[32,1024]{1,0:T(8,128)(2,1)S(1)}, bf16[32,1024]{1,0:T(8,128)(2,1)S(1)}, u32[]{:S(2)}, u32[]{:S(2)}) collective-permute-start(bf16[32,1024]{1,0:T(8,128)(2,1)S(1)} %get-tuple-element.80), channel_id=1, source_target_pairs={{0,8},{2,10},{4,12},{6,14},{8,0},{10,2},{12,4},{14,6},{1,9},{3,11}... | collective-permute-start | bytes 196616 | tf_op jit(solution)/shard_map/ppermute | solution.py:485
  72.9 1.3 %collective-permute-start.23 = (bf16[32,512]{1,0:T(8,128)(2,1)S(1)}, bf16[32,512]{1,0:T(8,128)(2,1)S(1)}, u32[]{:S(2)}, u32[]{:S(2)}) collective-permute-start(bf16[32,512]{1,0:T(8,128)(2,1)S(1)} %get-tuple-element.83), channel_id=1, source_target_pairs={{0,1},{1,0},{2,3},{3,2},{4,5},{5,4},{6,7},{7,6},{8,9},{9,8},{10,11... | collective-permute-start | bytes 98312 | tf_op jit(solution)/shard_map/ppermute | solution.py:451
  76.4 1.3 %collective-permute-start.24 = (f32[64,256]{1,0:T(8,128)S(1)}, f32[64,256]{1,0:T(8,128)S(1)}, u32[]{:S(2)}, u32[]{:S(2)}) collective-permute-start(f32[64,256]{1,0:T(8,128)S(1)} %shard_map.106.mine_ref), channel_id=1, source_target_pairs={{0,1},{1,0},{2,3},{3,2},{4,5},{5,4},{6,7},{7,6},{8,9},{9,8},{10,11... | collective-permute-start | bytes 196616 | tf_op jit(solution)/shard_map/ppermute | solution.py:451
  80.0 4.3 %collective-permute-start.25 = (bf16[64,512]{1,0:T(8,128)(2,1)S(1)}, bf16[64,512]{1,0:T(8,128)(2,1)S(1)}, u32[]{:S(2)}, u32[]{:S(2)}) collective-permute-start(bf16[64,512]{1,0:T(8,128)(2,1)S(1)} %get-tuple-element.86), channel_id=1, source_target_pairs={{0,2},{2,0},{4,6},{6,4},{8,10},{10,8},{12,14},{14,12},{1,3},{3,1},... | collective-permute-start | bytes 196616 | tf_op jit(solution)/shard_map/ppermute | solution.py:485
  84.3 6.9 %collective-permute-start.26 = (bf16[64,512]{1,0:T(8,128)(2,1)S(1)}, bf16[64,512]{1,0:T(8,128)(2,1)S(1)}, u32[]{:S(2)}, u32[]{:S(2)}) collective-permute-start(bf16[64,512]{1,0:T(8,128)(2,1)S(1)} %get-tuple-element.88), channel_id=1, source_target_pairs={{0,12},{2,14},{4,8},{6,10},{8,4},{10,6},{12,0},{14,2},{1,13},{3,15... | collective-permute-start | bytes 196616 | tf_op jit(solution)/shard_map/ppermute | solution.py:485
  86.3 5.0 %collective-permute-start.27 = (bf16[64,512]{1,0:T(8,128)(2,1)S(1)}, bf16[64,512]{1,0:T(8,128)(2,1)S(1)}, u32[]{:S(2)}, u32[]{:S(2)}) collective-permute-start(bf16[64,512]{1,0:T(8,128)(2,1)S(1)} %get-tuple-element.88), channel_id=1, source_target_pairs={{0,4},{2,6},{4,0},{6,2},{8,12},{10,14},{12,8},{14,10},{1,5},{3,7},... | collective-permute-start | bytes 196616 | tf_op jit(solution)/shard_map/ppermute | solution.py:485
  86.7 5.4 %collective-permute-start.28 = (bf16[64,512]{1,0:T(8,128)(2,1)S(1)}, bf16[64,512]{1,0:T(8,128)(2,1)S(1)}, u32[]{:S(2)}, u32[]{:S(2)}) collective-permute-start(bf16[64,512]{1,0:T(8,128)(2,1)S(1)} %get-tuple-element.88), channel_id=1, source_target_pairs={{0,8},{2,10},{4,12},{6,14},{8,0},{10,2},{12,4},{14,6},{1,9},{3,11}... | collective-permute-start | bytes 196616 | tf_op jit(solution)/shard_map/ppermute | solution.py:485
  92.2 1.3 %collective-permute-start.29 = (bf16[32,512]{1,0:T(8,128)(2,1)S(1)}, bf16[32,512]{1,0:T(8,128)(2,1)S(1)}, u32[]{:S(2)}, u32[]{:S(2)}) collective-permute-start(bf16[32,512]{1,0:T(8,128)(2,1)S(1)} %get-tuple-element.90), channel_id=1, source_target_pairs={{0,1},{1,0},{2,3},{3,2},{4,5},{5,4},{6,7},{7,6},{8,9},{9,8},{10,11... | collective-permute-start | bytes 98312 | tf_op jit(solution)/shard_map/ppermute | solution.py:451
  95.6 12.9 %all-to-all-start = ((bf16[8,64,256]{2,1,0:T(8,128)(2,1)}), bf16[8,64,256]{2,1,0:T(8,128)(2,1)S(1)}, u32[]{:S(2)}, u32[]{:S(2)}) async-start(bf16[8,64,256]{2,1,0:T(8,128)(2,1)} %shard_map.110), calls=%async_computation | async-start | bytes 524288 | tf_op jit(solution)/shard_map/all_to_all | solution.py:602
  108.8 1.4 %collective-permute-start.30 = (bf16[256,256]{1,0:T(8,128)(2,1)S(1)}, bf16[256,256]{1,0:T(8,128)(2,1)S(1)}, u32[]{:S(2)}, u32[]{:S(2)}) collective-permute-start(bf16[256,256]{1,0:T(8,128)(2,1)S(1)} %get-tuple-element.94), channel_id=1, source_target_pairs={{0,1},{1,0},{2,3},{3,2},{4,5},{5,4},{6,7},{7,6},{8,9},{9,8},{10,11... | collective-permute-start | bytes 393224 | tf_op jit(solution)/shard_map/ppermute | solution.py:451
  (12 other events, 133.8 us)

commit v8 on v7

--- a/solution.py
+++ b/solution.py
@@ -361,12 +361,13 @@
     return jnp.concatenate([jnp.where(first, mine, got), jnp.where(first, got, mine)], axis=axis)
 
 
-def conv_sum(cols_ref, weight_of, flipped, dot):
+def conv_sum(cols_ref, weight_of, back):
     total = None
     for t in range(27):
-        part = dot(cols_ref[26 - t if flipped else t], weight_of(t))
+        cells = cols_ref[26 - t if back else t]
+        part = nt_dot(weight_of(t), cells) if back else nn_dot(cells, weight_of(t))
         total = part if total is None else total + part
-    return total
+    return total.T if back else total
 
 
 def feature_rows(n, ref):
@@ -379,10 +380,10 @@
     return lambda t: ref[t, :, pl.ds(pl.multiple_of(n * half, half), half)]
 
 
-def outer_kernel(n_ref, mine_ref, got_ref, weight_ref, sum_ref, cols_ref, *, flipped, dot, part_of):
+def outer_kernel(n_ref, mine_ref, got_ref, weight_ref, sum_ref, cols_ref, *, back, part_of):
     n = n_ref[0]
     put_columns(cols_ref, both_halves(n, mine_ref[...].astype(F32), got_ref[...].astype(F32), 0))
-    sum_ref[...] = conv_sum(cols_ref, part_of(n, weight_ref), flipped, dot)
+    sum_ref[...] = conv_sum(cols_ref, part_of(n, weight_ref), back)
 
 
 def inner_forward_kernel(
@@ -391,7 +392,7 @@
     gate = mine_ref[...] + got_ref[...] + bias_ref[...]
     gate_ref[...] = gate
     put_columns(cols_ref, gate * jax.nn.sigmoid(gate))
-    total = conv_sum(cols_ref, feature_columns(n_ref[0], weight_ref), False, nn_dot)
+    total = conv_sum(cols_ref, feature_columns(n_ref[0], weight_ref), False)
     sum_ref[...] = total
     sum_b_ref[...] = total.astype(BF)
 
@@ -400,7 +401,7 @@
     n_ref, mine_ref, got_ref, gate_ref, weight_ref, sum_ref, sum_b_ref, cols_ref
 ):
     put_columns(cols_ref, (mine_ref[...] + got_ref[...]) * silu_slope(gate_ref[...]))
-    total = conv_sum(cols_ref, feature_rows(n_ref[0], weight_ref), True, nt_dot)
+    total = conv_sum(cols_ref, feature_rows(n_ref[0], weight_ref), True)
     sum_ref[...] = total
     sum_b_ref[...] = total.astype(BF)
 
@@ -570,7 +571,7 @@
     inner_columns = [pltpu.VMEM((27, 64, hidden), BF)]
 
     (gate_part,) = kernel_call(
-        functools.partial(outer_kernel, flipped=False, dot=nn_dot, part_of=feature_rows),
+        functools.partial(outer_kernel, back=False, part_of=feature_rows),
         (n,), (mine, got, hidden_weight), [gate_shape], outer_columns,
     )
     gate_pre, branch_part, branch_part_b = kernel_call(
@@ -585,7 +586,7 @@
     )
     grad_res, mine, got = to_feature_halves(n, res_part, res_part_b)
     (hidden_part,) = kernel_call(
-        functools.partial(outer_kernel, flipped=True, dot=nt_dot, part_of=feature_columns),
+        functools.partial(outer_kernel, back=True, part_of=feature_columns),
         (n,), (mine, got, output_weight), [gate_shape], outer_columns,
     )
     conv_part, conv_part_b = kernel_call(

time: 112 us -> 112 us (level)
  no operation moved by 1% of the time
where the time goes in v8:
time: 112 us; the launch traced here: 111 us
  waiting for transfers between devices  51.2 us (46%)
  starting transfers between devices  36.9 us (33%)
  Pallas kernels  20.7 us (18%)
  local copies, waits for them, and re-layouts  1.45 us (1%)
    ppermute x16, waiting for transfers between devices, partner(): return lax.ppermute(value, 'wide', [(i, i ^ mask) for i in range(8)])  29.5 us
    pallas_call x24, Pallas kernels, kernel_call(): pl.pallas_call(kernel, in_specs=[SMEM] * len(places) + [VMEM] * len(array...  20.7 us
    ppermute x16, starting transfers between devices, partner(): return lax.ppermute(value, 'wide', [(i, i ^ mask) for i in range(8)])  20.2 us
    ppermute x7, starting transfers between devices, across_wide(): lax.ppermute(messages[mask], 'wide', [(i, i ^ mask) for i in range(8)])  12.5 us
    ppermute x8, waiting for transfers between devices, swap_narrow(): return lax.ppermute(value, 'narrow', [(0, 1), (1, 0)])  8.57 us
    all_to_all x1, waiting for transfers between devices, eight_shards(): lax.all_to_all(leaving, 'wide', split_axis=0, concat_axis=0, tiled=True)  8 us
    ppermute x7, waiting for transfers between devices, across_wide(): lax.ppermute(messages[mask], 'wide', [(i, i ^ mask) for i in range(8)])  5.14 us
    all_to_all x1, starting transfers between devices, eight_shards(): lax.all_to_all(leaving, 'wide', split_axis=0, concat_axis=0, tiled=True)  3.41 us
  transfers between devices with their start and end apart: 32, of which 27 were waited for; matrix products, arithmetic and copies ran while one was open for 0% of the time, Pallas kernels for 3%

profile of v8, /device:TPU:0, one launch (start us, length us, event | category | flops | bytes accessed | tf_op | source)
XLA Modules:
  0.0 111.3 jit_solution(10029838687100317802)
XLA Ops:
  0.7 2.0 %shard_map.91 = (bf16[128,256]{1,0:T(8,128)(2,1)S(1)}, bf16[128,256]{1,0:T(8,128)(2,1)S(1)}, bf16[128,256]{1,0:T(8,128)(2,1)S(1)}, bf16[128,256]{1,0:T(8,128)(2,...) custom-call(s32[1]{0:T(128)} %bitcast.n_ref, ...), custom_call_target="tpu_custom_call" | custom-call | tf_op jit(solution)/shard_map/pallas_call | solution.py:140
  2.7 3.0 %collective-permute-start = (bf16[128,256]{1,0:T(8,128)(2,1)S(1)}, bf16[128,256]{1,0:T(8,128)(2,1)S(1)}, u32[]{:S(2)}, u32[]{:S(2)}) collective-permute-start(bf16[128,256]{1,0:T(8,128)(2,1)S(1)} %get-tuple-element.51), channel_id=1, source_target_pairs={{0,2},{2,0},{4,6},{6,4},{8,10},{10,8},{12,14},{14,12},{1,3},{3,1},... | collective-permute-start | bytes 196616 | tf_op jit(solution)/shard_map/ppermute | solution.py:516
  5.7 1.6 %collective-permute-start.1 = (bf16[128,256]{1,0:T(8,128)(2,1)S(1)}, bf16[128,256]{1,0:T(8,128)(2,1)S(1)}, u32[]{:S(2)}, u32[]{:S(2)}) collective-permute-start(bf16[128,256]{1,0:T(8,128)(2,1)S(1)} %get-tuple-element.52), channel_id=1, source_target_pairs={{0,4},{2,6},{4,0},{6,2},{8,12},{10,14},{12,8},{14,10},{1,5},{3,7},... | collective-permute-start | bytes 196616 | tf_op jit(solution)/shard_map/ppermute | solution.py:516
  7.3 3.0 %collective-permute-start.3 = (bf16[128,256]{1,0:T(8,128)(2,1)S(1)}, bf16[128,256]{1,0:T(8,128)(2,1)S(1)}, u32[]{:S(2)}, u32[]{:S(2)}) collective-permute-start(bf16[128,256]{1,0:T(8,128)(2,1)S(1)} %get-tuple-element.54), channel_id=1, source_target_pairs={{0,8},{2,10},{4,12},{6,14},{8,0},{10,2},{12,4},{14,6},{1,9},{3,11}... | collective-permute-start | bytes 196616 | tf_op jit(solution)/shard_map/ppermute | solution.py:516
  11.6 3.6 %collective-permute-start.5 = (bf16[128,256]{1,0:T(8,128)(2,1)S(1)}, bf16[128,256]{1,0:T(8,128)(2,1)S(1)}, u32[]{:S(2)}, u32[]{:S(2)}) collective-permute-start(bf16[128,256]{1,0:T(8,128)(2,1)S(1)} %get-tuple-element.56), channel_id=1, source_target_pairs={{0,12},{2,14},{4,8},{6,10},{8,4},{10,6},{12,0},{14,2},{1,13},{3,15... | collective-permute-start | bytes 196616 | tf_op jit(solution)/shard_map/ppermute | solution.py:516
  17.1 3.4 %collective-permute-done.4.refs_5_ = bf16[128,256]{1,0:T(8,128)(2,1)S(1)} collective-permute-done((bf16[128,256]{1,0:T(8,128)(2,1)S(1)}, bf16[128,256]{1,0:T(8,128)(2,1)S(1)}, u32[]{:S(2)}, u32[]{:S(2)}) %collective-permute-start.4) | collective-permute-done | bytes 65568 | tf_op jit(solution)/shard_map/ppermute | solution.py:516
  20.5 1.7 %collective-permute-done.6.refs_7_ = bf16[128,256]{1,0:T(8,128)(2,1)S(1)} collective-permute-done((bf16[128,256]{1,0:T(8,128)(2,1)S(1)}, bf16[128,256]{1,0:T(8,128)(2,1)S(1)}, u32[]{:S(2)}, u32[]{:S(2)}) %collective-permute-start.6) | collective-permute-done | bytes 65568 | tf_op jit(solution)/shard_map/ppermute | solution.py:516
  26.3 3.8 %collective-permute-done.8.refs_0_ = bf16[32,1024]{1,0:T(8,128)(2,1)S(1)} collective-permute-done((bf16[32,1024]{1,0:T(8,128)(2,1)S(1)}, bf16[32,1024]{1,0:T(8,128)(2,1)S(1)}, u32[]{:S(2)}, u32[]{:S(2)}) %collective-permute-start.8) | collective-permute-done | bytes 65568 | tf_op jit(solution)/shard_map/ppermute | solution.py:486
  30.1 1.7 %collective-permute-start.10 = (bf16[32,1024]{1,0:T(8,128)(2,1)S(1)}, bf16[32,1024]{1,0:T(8,128)(2,1)S(1)}, u32[]{:S(2)}, u32[]{:S(2)}) collective-permute-start(bf16[32,1024]{1,0:T(8,128)(2,1)S(1)} %get-tuple-element.65), channel_id=1, source_target_pairs={{0,4},{2,6},{4,0},{6,2},{8,12},{10,14},{12,8},{14,10},{1,5},{3,7},... | collective-permute-start | bytes 196616 | tf_op jit(solution)/shard_map/ppermute | solution.py:486
  33.0 1.6 %collective-permute-start.9 = (bf16[32,1024]{1,0:T(8,128)(2,1)S(1)}, bf16[32,1024]{1,0:T(8,128)(2,1)S(1)}, u32[]{:S(2)}, u32[]{:S(2)}) collective-permute-start(bf16[32,1024]{1,0:T(8,128)(2,1)S(1)} %get-tuple-element.65), channel_id=1, source_target_pairs={{0,12},{2,14},{4,8},{6,10},{8,4},{10,6},{12,0},{14,2},{1,13},{3,15... | collective-permute-start | bytes 196616 | tf_op jit(solution)/shard_map/ppermute | solution.py:486
  34.9 3.0 %collective-permute-done.11.three_ref = bf16[32,1024]{1,0:T(8,128)(2,1)S(1)} collective-permute-done((bf16[32,1024]{1,0:T(8,128)(2,1)S(1)}, bf16[32,1024]{1,0:T(8,128)(2,1)S(1)}, u32[]{:S(2)}, u32[]{:S(2)}) %collective-permute-start.11) | collective-permute-done | bytes 65568 | tf_op jit(solution)/shard_map/ppermute | solution.py:486
  40.5 1.4 %shard_map.98.mine_ref = f32[64,256]{1,0:T(8,128)S(1)} custom-call(s32[1]{0:T(128)} %bitcast.n_ref, bf16[32,512]{1,0:T(8,128)(2,1)S(1)} %get-tuple-element.67.mine_ref, bf16[32,512]{1,0:T(8,128)(2,1)S(1)} %collective-permute-done.12.got_ref, bf16[27,1024,256]{2,1,0:T(8,128)(2,1)S(1)} %bitcast.8), custom_call_target="tpu_custom_call" | custom-call | tf_op jit(solution)/shard_map/pallas_call | solution.py:140
  45.2 3.7 %collective-permute-done.14.refs_0_ = bf16[64,512]{1,0:T(8,128)(2,1)S(1)} collective-permute-done((bf16[64,512]{1,0:T(8,128)(2,1)S(1)}, bf16[64,512]{1,0:T(8,128)(2,1)S(1)}, u32[]{:S(2)}, u32[]{:S(2)}) %collective-permute-start.14) | collective-permute-done | bytes 65568 | tf_op jit(solution)/shard_map/ppermute | solution.py:486
  48.9 1.7 %collective-permute-start.15 = (bf16[64,512]{1,0:T(8,128)(2,1)S(1)}, bf16[64,512]{1,0:T(8,128)(2,1)S(1)}, u32[]{:S(2)}, u32[]{:S(2)}) collective-permute-start(bf16[64,512]{1,0:T(8,128)(2,1)S(1)} %get-tuple-element.73), channel_id=1, source_target_pairs={{0,12},{2,14},{4,8},{6,10},{8,4},{10,6},{12,0},{14,2},{1,13},{3,15... | collective-permute-start | bytes 196616 | tf_op jit(solution)/shard_map/ppermute | solution.py:486
  51.0 2.3 %collective-permute-start.17 = (bf16[64,512]{1,0:T(8,128)(2,1)S(1)}, bf16[64,512]{1,0:T(8,128)(2,1)S(1)}, u32[]{:S(2)}, u32[]{:S(2)}) collective-permute-start(bf16[64,512]{1,0:T(8,128)(2,1)S(1)} %get-tuple-element.73), channel_id=1, source_target_pairs={{0,8},{2,10},{4,12},{6,14},{8,0},{10,2},{12,4},{14,6},{1,9},{3,11}... | collective-permute-start | bytes 196616 | tf_op jit(solution)/shard_map/ppermute | solution.py:486
  53.4 2.2 %collective-permute-done.15.one_ref = bf16[64,512]{1,0:T(8,128)(2,1)S(1)} collective-permute-done((bf16[64,512]{1,0:T(8,128)(2,1)S(1)}, bf16[64,512]{1,0:T(8,128)(2,1)S(1)}, u32[]{:S(2)}, u32[]{:S(2)}) %collective-permute-start.15) | collective-permute-done | bytes 65568 | tf_op jit(solution)/shard_map/ppermute | solution.py:486
  57.9 2.7 %shard_map.103 = (bf16[8,32,256]{2,1,0:T(8,128)(2,1)S(1)}, f32[32,1024]{1,0:T(8,128)S(1)}, bf16[32,1024]{1,0:T(8,128)(2,1)S(1)}) custom-call(s32[1]{0:T(128)} %bitcast.n_ref, f32[32,1024]{1,0:T(8,128)S(1)} %get-tuple-element.66.merged_ref, f32[32,512]{1,0:T(8,128)S(1)} %get-tuple-element.74.mine_ref, bf16[32,512]{1,0:T(8,128)(2,1)S(1)} %collective-permute-done.18.got_ref, ...), custom_call_target="tpu_custom_call" | custom-call | tf_op jit(solution)/shard_map/pallas_call | solution.py:140
  61.2 3.7 %collective-permute-done.19.refs_0_ = bf16[32,1024]{1,0:T(8,128)(2,1)S(1)} collective-permute-done((bf16[32,1024]{1,0:T(8,128)(2,1)S(1)}, bf16[32,1024]{1,0:T(8,128)(2,1)S(1)}, u32[]{:S(2)}, u32[]{:S(2)}) %collective-permute-start.19) | collective-permute-done | bytes 65568 | tf_op jit(solution)/shard_map/ppermute | solution.py:486
  65.0 1.9 %collective-permute-start.20 = (bf16[32,1024]{1,0:T(8,128)(2,1)S(1)}, bf16[32,1024]{1,0:T(8,128)(2,1)S(1)}, u32[]{:S(2)}, u32[]{:S(2)}) collective-permute-start(bf16[32,1024]{1,0:T(8,128)(2,1)S(1)} %get-tuple-element.80), channel_id=1, source_target_pairs={{0,12},{2,14},{4,8},{6,10},{8,4},{10,6},{12,0},{14,2},{1,13},{3,15... | collective-permute-start | bytes 196616 | tf_op jit(solution)/shard_map/ppermute | solution.py:486
  67.6 1.9 %collective-permute-start.22 = (bf16[32,1024]{1,0:T(8,128)(2,1)S(1)}, bf16[32,1024]{1,0:T(8,128)(2,1)S(1)}, u32[]{:S(2)}, u32[]{:S(2)}) collective-permute-start(bf16[32,1024]{1,0:T(8,128)(2,1)S(1)} %get-tuple-element.80), channel_id=1, source_target_pairs={{0,8},{2,10},{4,12},{6,14},{8,0},{10,2},{12,4},{14,6},{1,9},{3,11}... | collective-permute-start | bytes 196616 | tf_op jit(solution)/shard_map/ppermute | solution.py:486
  69.4 2.4 %collective-permute-done.20.one_ref = bf16[32,1024]{1,0:T(8,128)(2,1)S(1)} collective-permute-done((bf16[32,1024]{1,0:T(8,128)(2,1)S(1)}, bf16[32,1024]{1,0:T(8,128)(2,1)S(1)}, u32[]{:S(2)}, u32[]{:S(2)}) %collective-permute-start.20) | collective-permute-done | bytes 65568 | tf_op jit(solution)/shard_map/ppermute | solution.py:486
  74.1 2.0 %shard_map.106.mine_ref = f32[64,256]{1,0:T(8,128)S(1)} custom-call(s32[1]{0:T(128)} %bitcast.n_ref, bf16[32,512]{1,0:T(8,128)(2,1)S(1)} %get-tuple-element.82.mine_ref, bf16[32,512]{1,0:T(8,128)(2,1)S(1)} %collective-permute-done.23.got_ref, bf16[27,256,1024]{2,1,0:T(8,128)(2,1)S(1)} %bitcast.6), custom_call_target="tpu_custom_call" | custom-call | tf_op jit(solution)/shard_map/pallas_call | solution.py:140
  77.5 2.0 %shard_map.107 = (f32[64,512]{1,0:T(8,128)S(1)}, bf16[64,512]{1,0:T(8,128)(2,1)S(1)}) custom-call(s32[1]{0:T(128)} %bitcast.n_ref, f32[64,256]{1,0:T(8,128)S(1)} %shard_map.106.mine_ref, f32[64,256]{1,0:T(8,128)S(1)} %collective-permute-done.24.got_ref, f32[64,256]{1,0:T(8,128)S(1)} %get-tuple-element.84.gate_ref, bf16[27,1024,256]{2,1,0:T(8,128)(2,1)S(1)} %bitcast.8), custom_call_target="tpu_custom_call" | custom-call | tf_op jit(solution)/shard_map/pallas_call | solution.py:140
  80.2 3.7 %collective-permute-done.25.refs_0_ = bf16[64,512]{1,0:T(8,128)(2,1)S(1)} collective-permute-done((bf16[64,512]{1,0:T(8,128)(2,1)S(1)}, bf16[64,512]{1,0:T(8,128)(2,1)S(1)}, u32[]{:S(2)}, u32[]{:S(2)}) %collective-permute-start.25) | collective-permute-done | bytes 65568 | tf_op jit(solution)/shard_map/ppermute | solution.py:486
  83.9 1.9 %collective-permute-start.26 = (bf16[64,512]{1,0:T(8,128)(2,1)S(1)}, bf16[64,512]{1,0:T(8,128)(2,1)S(1)}, u32[]{:S(2)}, u32[]{:S(2)}) collective-permute-start(bf16[64,512]{1,0:T(8,128)(2,1)S(1)} %get-tuple-element.88), channel_id=1, source_target_pairs={{0,12},{2,14},{4,8},{6,10},{8,4},{10,6},{12,0},{14,2},{1,13},{3,15... | collective-permute-start | bytes 196616 | tf_op jit(solution)/shard_map/ppermute | solution.py:486
  86.3 2.1 %collective-permute-start.28 = (bf16[64,512]{1,0:T(8,128)(2,1)S(1)}, bf16[64,512]{1,0:T(8,128)(2,1)S(1)}, u32[]{:S(2)}, u32[]{:S(2)}) collective-permute-start(bf16[64,512]{1,0:T(8,128)(2,1)S(1)} %get-tuple-element.88), channel_id=1, source_target_pairs={{0,8},{2,10},{4,12},{6,14},{8,0},{10,2},{12,4},{14,6},{1,9},{3,11}... | collective-permute-start | bytes 196616 | tf_op jit(solution)/shard_map/ppermute | solution.py:486
  88.4 2.4 %collective-permute-done.26.one_ref = bf16[64,512]{1,0:T(8,128)(2,1)S(1)} collective-permute-done((bf16[64,512]{1,0:T(8,128)(2,1)S(1)}, bf16[64,512]{1,0:T(8,128)(2,1)S(1)}, u32[]{:S(2)}, u32[]{:S(2)}) %collective-permute-start.26) | collective-permute-done | bytes 65568 | tf_op jit(solution)/shard_map/ppermute | solution.py:486
  93.1 2.1 %shard_map.110 = bf16[8,64,256]{2,1,0:T(8,128)(2,1)} custom-call(s32[1]{0:T(128)} %bitcast.n_ref, s32[1]{0:T(128)} %bitcast.1.w_ref, f32[32,1024]{1,0:T(8,128)S(1)} %get-tuple-element.81.res_ref, f32[32,512]{1,0:T(8,128)S(1)} %get-tuple-element.89.mine_ref, bf16[32,512]{1,0:T(8,128)(2,1)S(1)} %collective-permute-done.29.got_ref, ...), custom_call_target="tpu_custom_call" | custom-call | tf_op jit(solution)/shard_map/pallas_call | solution.py:140
  95.2 3.4 %all-to-all-start = ((bf16[8,64,256]{2,1,0:T(8,128)(2,1)}), bf16[8,64,256]{2,1,0:T(8,128)(2,1)S(1)}, u32[]{:S(2)}, u32[]{:S(2)}) async-start(bf16[8,64,256]{2,1,0:T(8,128)(2,1)} %shard_map.110), calls=%async_computation | async-start | bytes 524288 | tf_op jit(solution)/shard_map/all_to_all | solution.py:603
  98.6 1.4 %shard_map.111.band_ref = bf16[1024,768]{1,0:T(8,128)(2,1)S(1)} custom-call(bf16[27,32,32]{2,1,0:T(8,128)(2,1)S(1)} %copy-done.3), custom_call_target="tpu_custom_call" | custom-call | bytes 33554432 | tf_op jit(solution)/shard_map/pallas_call | solution.py:140
  100.1 8.0 %all-to-all-done.planes_ref = bf16[8,64,256]{2,1,0:T(8,128)(2,1)S(1)} async-done(((bf16[8,64,256]{2,1,0:T(8,128)(2,1)}), bf16[8,64,256]{2,1,0:T(8,128)(2,1)S(1)}, u32[]{:S(2)}, u32[]{:S(2)}) %all-to-all-start) | async-done | bytes 262176 | tf_op jit(solution)/shard_map/all_to_all | solution.py:603
  109.8 1.5 %shard_map.114 = bf16[8,16,16,32]{3,2,1,0:T(8,128)(2,1)} custom-call(s32[1]{0:T(128)} %bitcast.n_ref, f32[256,768]{1,0:T(8,128)S(1)} %shard_map.112.main_ref, bf16[256,256]{1,0:T(8,128)(2,1)S(1)} %get-tuple-element.93.own_ref, bf16[256,256]{1,0:T(8,128)(2,1)S(1)} %collective-permute-done.30.got_ref, bf16[1024,768]{1,0:T(8,128)(2,1)S(1)} %shard_map.111.band_ref), custom_call_target="tpu_custom_call" | custom-call | tf_op jit(solution)/shard_map/pallas_call | solution.py:140
  (82 shorter events, 27.3 us)
Async XLA Ops:
  2.7 8.9 %collective-permute-start = (bf16[128,256]{1,0:T(8,128)(2,1)S(1)}, bf16[128,256]{1,0:T(8,128)(2,1)S(1)}, u32[]{:S(2)}, u32[]{:S(2)}) collective-permute-start(bf16[128,256]{1,0:T(8,128)(2,1)S(1)} %get-tuple-element.51), channel_id=1, source_target_pairs={{0,2},{2,0},{4,6},{6,4},{8,10},{10,8},{12,14},{14,12},{1,3},{3,1},... | collective-permute-start | bytes 196616 | tf_op jit(solution)/shard_map/ppermute | solution.py:516
  5.7 9.5 %collective-permute-start.1 = (bf16[128,256]{1,0:T(8,128)(2,1)S(1)}, bf16[128,256]{1,0:T(8,128)(2,1)S(1)}, u32[]{:S(2)}, u32[]{:S(2)}) collective-permute-start(bf16[128,256]{1,0:T(8,128)(2,1)S(1)} %get-tuple-element.52), channel_id=1, source_target_pairs={{0,4},{2,6},{4,0},{6,2},{8,12},{10,14},{12,8},{14,10},{1,5},{3,7},... | collective-permute-start | bytes 196616 | tf_op jit(solution)/shard_map/ppermute | solution.py:516
  7.3 9.8 %collective-permute-start.2 = (bf16[128,256]{1,0:T(8,128)(2,1)S(1)}, bf16[128,256]{1,0:T(8,128)(2,1)S(1)}, u32[]{:S(2)}, u32[]{:S(2)}) collective-permute-start(bf16[128,256]{1,0:T(8,128)(2,1)S(1)} %get-tuple-element.53), channel_id=1, source_target_pairs={{0,6},{2,4},{4,2},{6,0},{8,14},{10,12},{12,10},{14,8},{1,7},{3,5},... | collective-permute-start | bytes 196616 | tf_op jit(solution)/shard_map/ppermute | solution.py:516
  7.3 9.8 %collective-permute-start.3 = (bf16[128,256]{1,0:T(8,128)(2,1)S(1)}, bf16[128,256]{1,0:T(8,128)(2,1)S(1)}, u32[]{:S(2)}, u32[]{:S(2)}) collective-permute-start(bf16[128,256]{1,0:T(8,128)(2,1)S(1)} %get-tuple-element.54), channel_id=1, source_target_pairs={{0,8},{2,10},{4,12},{6,14},{8,0},{10,2},{12,4},{14,6},{1,9},{3,11}... | collective-permute-start | bytes 196616 | tf_op jit(solution)/shard_map/ppermute | solution.py:516
  10.3 10.2 %collective-permute-start.4 = (bf16[128,256]{1,0:T(8,128)(2,1)S(1)}, bf16[128,256]{1,0:T(8,128)(2,1)S(1)}, u32[]{:S(2)}, u32[]{:S(2)}) collective-permute-start(bf16[128,256]{1,0:T(8,128)(2,1)S(1)} %get-tuple-element.55), channel_id=1, source_target_pairs={{0,10},{2,8},{4,14},{6,12},{8,2},{10,0},{12,6},{14,4},{1,11},{3,9}... | collective-permute-start | bytes 196616 | tf_op jit(solution)/shard_map/ppermute | solution.py:516
  11.6 8.9 %collective-permute-start.5 = (bf16[128,256]{1,0:T(8,128)(2,1)S(1)}, bf16[128,256]{1,0:T(8,128)(2,1)S(1)}, u32[]{:S(2)}, u32[]{:S(2)}) collective-permute-start(bf16[128,256]{1,0:T(8,128)(2,1)S(1)} %get-tuple-element.56), channel_id=1, source_target_pairs={{0,12},{2,14},{4,8},{6,10},{8,4},{10,6},{12,0},{14,2},{1,13},{3,15... | collective-permute-start | bytes 196616 | tf_op jit(solution)/shard_map/ppermute | solution.py:516
  15.2 7.1 %collective-permute-start.6 = (bf16[128,256]{1,0:T(8,128)(2,1)S(1)}, bf16[128,256]{1,0:T(8,128)(2,1)S(1)}, u32[]{:S(2)}, u32[]{:S(2)}) collective-permute-start(bf16[128,256]{1,0:T(8,128)(2,1)S(1)} %get-tuple-element.57), channel_id=1, source_target_pairs={{0,14},{2,12},{4,10},{6,8},{8,6},{10,4},{12,2},{14,0},{1,15},{3,13... | collective-permute-start | bytes 196616 | tf_op jit(solution)/shard_map/ppermute | solution.py:516
  22.5 1.4 %collective-permute-start.7 = (bf16[256,256]{1,0:T(8,128)(2,1)S(1)}, bf16[256,256]{1,0:T(8,128)(2,1)S(1)}, u32[]{:S(2)}, u32[]{:S(2)}) collective-permute-start(bf16[256,256]{1,0:T(8,128)(2,1)S(1)} %get-tuple-element.61), channel_id=1, source_target_pairs={{0,1},{1,0},{2,3},{3,2},{4,5},{5,4},{6,7},{7,6},{8,9},{9,8},{10,11... | collective-permute-start | bytes 393224 | tf_op jit(solution)/shard_map/ppermute | solution.py:452
  25.7 4.3 %collective-permute-start.8 = (bf16[32,1024]{1,0:T(8,128)(2,1)S(1)}, bf16[32,1024]{1,0:T(8,128)(2,1)S(1)}, u32[]{:S(2)}, u32[]{:S(2)}) collective-permute-start(bf16[32,1024]{1,0:T(8,128)(2,1)S(1)} %get-tuple-element.63), channel_id=1, source_target_pairs={{0,2},{2,0},{4,6},{6,4},{8,10},{10,8},{12,14},{14,12},{1,3},{3,1},... | collective-permute-start | bytes 196616 | tf_op jit(solution)/shard_map/ppermute | solution.py:486
  30.1 4.9 %collective-permute-start.10 = (bf16[32,1024]{1,0:T(8,128)(2,1)S(1)}, bf16[32,1024]{1,0:T(8,128)(2,1)S(1)}, u32[]{:S(2)}, u32[]{:S(2)}) collective-permute-start(bf16[32,1024]{1,0:T(8,128)(2,1)S(1)} %get-tuple-element.65), channel_id=1, source_target_pairs={{0,4},{2,6},{4,0},{6,2},{8,12},{10,14},{12,8},{14,10},{1,5},{3,7},... | collective-permute-start | bytes 196616 | tf_op jit(solution)/shard_map/ppermute | solution.py:486
  31.8 6.1 %collective-permute-start.11 = (bf16[32,1024]{1,0:T(8,128)(2,1)S(1)}, bf16[32,1024]{1,0:T(8,128)(2,1)S(1)}, u32[]{:S(2)}, u32[]{:S(2)}) collective-permute-start(bf16[32,1024]{1,0:T(8,128)(2,1)S(1)} %get-tuple-element.65), channel_id=1, source_target_pairs={{0,8},{2,10},{4,12},{6,14},{8,0},{10,2},{12,4},{14,6},{1,9},{3,11}... | collective-permute-start | bytes 196616 | tf_op jit(solution)/shard_map/ppermute | solution.py:486
  33.0 6.2 %collective-permute-start.9 = (bf16[32,1024]{1,0:T(8,128)(2,1)S(1)}, bf16[32,1024]{1,0:T(8,128)(2,1)S(1)}, u32[]{:S(2)}, u32[]{:S(2)}) collective-permute-start(bf16[32,1024]{1,0:T(8,128)(2,1)S(1)} %get-tuple-element.65), channel_id=1, source_target_pairs={{0,12},{2,14},{4,8},{6,10},{8,4},{10,6},{12,0},{14,2},{1,13},{3,15... | collective-permute-start | bytes 196616 | tf_op jit(solution)/shard_map/ppermute | solution.py:486
  39.2 1.3 %collective-permute-start.12 = (bf16[32,512]{1,0:T(8,128)(2,1)S(1)}, bf16[32,512]{1,0:T(8,128)(2,1)S(1)}, u32[]{:S(2)}, u32[]{:S(2)}) collective-permute-start(bf16[32,512]{1,0:T(8,128)(2,1)S(1)} %get-tuple-element.68), channel_id=1, source_target_pairs={{0,1},{1,0},{2,3},{3,2},{4,5},{5,4},{6,7},{7,6},{8,9},{9,8},{10,11... | collective-permute-start | bytes 98312 | tf_op jit(solution)/shard_map/ppermute | solution.py:452
  41.9 1.3 %collective-permute-start.13 = (f32[64,256]{1,0:T(8,128)S(1)}, f32[64,256]{1,0:T(8,128)S(1)}, u32[]{:S(2)}, u32[]{:S(2)}) collective-permute-start(f32[64,256]{1,0:T(8,128)S(1)} %shard_map.98.mine_ref), channel_id=1, source_target_pairs={{0,1},{1,0},{2,3},{3,2},{4,5},{5,4},{6,7},{7,6},{8,9},{9,8},{10,11... | collective-permute-start | bytes 196616 | tf_op jit(solution)/shard_map/ppermute | solution.py:452
  44.6 4.3 %collective-permute-start.14 = (bf16[64,512]{1,0:T(8,128)(2,1)S(1)}, bf16[64,512]{1,0:T(8,128)(2,1)S(1)}, u32[]{:S(2)}, u32[]{:S(2)}) collective-permute-start(bf16[64,512]{1,0:T(8,128)(2,1)S(1)} %get-tuple-element.71), channel_id=1, source_target_pairs={{0,2},{2,0},{4,6},{6,4},{8,10},{10,8},{12,14},{14,12},{1,3},{3,1},... | collective-permute-start | bytes 196616 | tf_op jit(solution)/shard_map/ppermute | solution.py:486
  48.9 6.7 %collective-permute-start.15 = (bf16[64,512]{1,0:T(8,128)(2,1)S(1)}, bf16[64,512]{1,0:T(8,128)(2,1)S(1)}, u32[]{:S(2)}, u32[]{:S(2)}) collective-permute-start(bf16[64,512]{1,0:T(8,128)(2,1)S(1)} %get-tuple-element.73), channel_id=1, source_target_pairs={{0,12},{2,14},{4,8},{6,10},{8,4},{10,6},{12,0},{14,2},{1,13},{3,15... | collective-permute-start | bytes 196616 | tf_op jit(solution)/shard_map/ppermute | solution.py:486
  50.7 5.0 %collective-permute-start.16 = (bf16[64,512]{1,0:T(8,128)(2,1)S(1)}, bf16[64,512]{1,0:T(8,128)(2,1)S(1)}, u32[]{:S(2)}, u32[]{:S(2)}) collective-permute-start(bf16[64,512]{1,0:T(8,128)(2,1)S(1)} %get-tuple-element.73), channel_id=1, source_target_pairs={{0,4},{2,6},{4,0},{6,2},{8,12},{10,14},{12,8},{14,10},{1,5},{3,7},... | collective-permute-start | bytes 196616 | tf_op jit(solution)/shard_map/ppermute | solution.py:486
  51.0 5.6 %collective-permute-start.17 = (bf16[64,512]{1,0:T(8,128)(2,1)S(1)}, bf16[64,512]{1,0:T(8,128)(2,1)S(1)}, u32[]{:S(2)}, u32[]{:S(2)}) collective-permute-start(bf16[64,512]{1,0:T(8,128)(2,1)S(1)} %get-tuple-element.73), channel_id=1, source_target_pairs={{0,8},{2,10},{4,12},{6,14},{8,0},{10,2},{12,4},{14,6},{1,9},{3,11}... | collective-permute-start | bytes 196616 | tf_op jit(solution)/shard_map/ppermute | solution.py:486
  56.6 1.3 %collective-permute-start.18 = (bf16[32,512]{1,0:T(8,128)(2,1)S(1)}, bf16[32,512]{1,0:T(8,128)(2,1)S(1)}, u32[]{:S(2)}, u32[]{:S(2)}) collective-permute-start(bf16[32,512]{1,0:T(8,128)(2,1)S(1)} %get-tuple-element.75), channel_id=1, source_target_pairs={{0,1},{1,0},{2,3},{3,2},{4,5},{5,4},{6,7},{7,6},{8,9},{9,8},{10,11... | collective-permute-start | bytes 98312 | tf_op jit(solution)/shard_map/ppermute | solution.py:452
  60.7 4.3 %collective-permute-start.19 = (bf16[32,1024]{1,0:T(8,128)(2,1)S(1)}, bf16[32,1024]{1,0:T(8,128)(2,1)S(1)}, u32[]{:S(2)}, u32[]{:S(2)}) collective-permute-start(bf16[32,1024]{1,0:T(8,128)(2,1)S(1)} %get-tuple-element.78), channel_id=1, source_target_pairs={{0,2},{2,0},{4,6},{6,4},{8,10},{10,8},{12,14},{14,12},{1,3},{3,1},... | collective-permute-start | bytes 196616 | tf_op jit(solution)/shard_map/ppermute | solution.py:486
  65.0 6.8 %collective-permute-start.20 = (bf16[32,1024]{1,0:T(8,128)(2,1)S(1)}, bf16[32,1024]{1,0:T(8,128)(2,1)S(1)}, u32[]{:S(2)}, u32[]{:S(2)}) collective-permute-start(bf16[32,1024]{1,0:T(8,128)(2,1)S(1)} %get-tuple-element.80), channel_id=1, source_target_pairs={{0,12},{2,14},{4,8},{6,10},{8,4},{10,6},{12,0},{14,2},{1,13},{3,15... | collective-permute-start | bytes 196616 | tf_op jit(solution)/shard_map/ppermute | solution.py:486
  66.9 5.0 %collective-permute-start.21 = (bf16[32,1024]{1,0:T(8,128)(2,1)S(1)}, bf16[32,1024]{1,0:T(8,128)(2,1)S(1)}, u32[]{:S(2)}, u32[]{:S(2)}) collective-permute-start(bf16[32,1024]{1,0:T(8,128)(2,1)S(1)} %get-tuple-element.80), channel_id=1, source_target_pairs={{0,4},{2,6},{4,0},{6,2},{8,12},{10,14},{12,8},{14,10},{1,5},{3,7},... | collective-permute-start | bytes 196616 | tf_op jit(solution)/shard_map/ppermute | solution.py:486
  67.6 5.3 %collective-permute-start.22 = (bf16[32,1024]{1,0:T(8,128)(2,1)S(1)}, bf16[32,1024]{1,0:T(8,128)(2,1)S(1)}, u32[]{:S(2)}, u32[]{:S(2)}) collective-permute-start(bf16[32,1024]{1,0:T(8,128)(2,1)S(1)} %get-tuple-element.80), channel_id=1, source_target_pairs={{0,8},{2,10},{4,12},{6,14},{8,0},{10,2},{12,4},{14,6},{1,9},{3,11}... | collective-permute-start | bytes 196616 | tf_op jit(solution)/shard_map/ppermute | solution.py:486
  72.9 1.3 %collective-permute-start.23 = (bf16[32,512]{1,0:T(8,128)(2,1)S(1)}, bf16[32,512]{1,0:T(8,128)(2,1)S(1)}, u32[]{:S(2)}, u32[]{:S(2)}) collective-permute-start(bf16[32,512]{1,0:T(8,128)(2,1)S(1)} %get-tuple-element.83), channel_id=1, source_target_pairs={{0,1},{1,0},{2,3},{3,2},{4,5},{5,4},{6,7},{7,6},{8,9},{9,8},{10,11... | collective-permute-start | bytes 98312 | tf_op jit(solution)/shard_map/ppermute | solution.py:452
  76.2 1.3 %collective-permute-start.24 = (f32[64,256]{1,0:T(8,128)S(1)}, f32[64,256]{1,0:T(8,128)S(1)}, u32[]{:S(2)}, u32[]{:S(2)}) collective-permute-start(f32[64,256]{1,0:T(8,128)S(1)} %shard_map.106.mine_ref), channel_id=1, source_target_pairs={{0,1},{1,0},{2,3},{3,2},{4,5},{5,4},{6,7},{7,6},{8,9},{9,8},{10,11... | collective-permute-start | bytes 196616 | tf_op jit(solution)/shard_map/ppermute | solution.py:452
  79.6 4.3 %collective-permute-start.25 = (bf16[64,512]{1,0:T(8,128)(2,1)S(1)}, bf16[64,512]{1,0:T(8,128)(2,1)S(1)}, u32[]{:S(2)}, u32[]{:S(2)}) collective-permute-start(bf16[64,512]{1,0:T(8,128)(2,1)S(1)} %get-tuple-element.86), channel_id=1, source_target_pairs={{0,2},{2,0},{4,6},{6,4},{8,10},{10,8},{12,14},{14,12},{1,3},{3,1},... | collective-permute-start | bytes 196616 | tf_op jit(solution)/shard_map/ppermute | solution.py:486
  83.9 6.9 %collective-permute-start.26 = (bf16[64,512]{1,0:T(8,128)(2,1)S(1)}, bf16[64,512]{1,0:T(8,128)(2,1)S(1)}, u32[]{:S(2)}, u32[]{:S(2)}) collective-permute-start(bf16[64,512]{1,0:T(8,128)(2,1)S(1)} %get-tuple-element.88), channel_id=1, source_target_pairs={{0,12},{2,14},{4,8},{6,10},{8,4},{10,6},{12,0},{14,2},{1,13},{3,15... | collective-permute-start | bytes 196616 | tf_op jit(solution)/shard_map/ppermute | solution.py:486
  85.9 5.0 %collective-permute-start.27 = (bf16[64,512]{1,0:T(8,128)(2,1)S(1)}, bf16[64,512]{1,0:T(8,128)(2,1)S(1)}, u32[]{:S(2)}, u32[]{:S(2)}) collective-permute-start(bf16[64,512]{1,0:T(8,128)(2,1)S(1)} %get-tuple-element.88), channel_id=1, source_target_pairs={{0,4},{2,6},{4,0},{6,2},{8,12},{10,14},{12,8},{14,10},{1,5},{3,7},... | collective-permute-start | bytes 196616 | tf_op jit(solution)/shard_map/ppermute | solution.py:486
  86.3 5.4 %collective-permute-start.28 = (bf16[64,512]{1,0:T(8,128)(2,1)S(1)}, bf16[64,512]{1,0:T(8,128)(2,1)S(1)}, u32[]{:S(2)}, u32[]{:S(2)}) collective-permute-start(bf16[64,512]{1,0:T(8,128)(2,1)S(1)} %get-tuple-element.88), channel_id=1, source_target_pairs={{0,8},{2,10},{4,12},{6,14},{8,0},{10,2},{12,4},{14,6},{1,9},{3,11}... | collective-permute-start | bytes 196616 | tf_op jit(solution)/shard_map/ppermute | solution.py:486
  91.8 1.3 %collective-permute-start.29 = (bf16[32,512]{1,0:T(8,128)(2,1)S(1)}, bf16[32,512]{1,0:T(8,128)(2,1)S(1)}, u32[]{:S(2)}, u32[]{:S(2)}) collective-permute-start(bf16[32,512]{1,0:T(8,128)(2,1)S(1)} %get-tuple-element.90), channel_id=1, source_target_pairs={{0,1},{1,0},{2,3},{3,2},{4,5},{5,4},{6,7},{7,6},{8,9},{9,8},{10,11... | collective-permute-start | bytes 98312 | tf_op jit(solution)/shard_map/ppermute | solution.py:452
  95.2 12.9 %all-to-all-start = ((bf16[8,64,256]{2,1,0:T(8,128)(2,1)}), bf16[8,64,256]{2,1,0:T(8,128)(2,1)S(1)}, u32[]{:S(2)}, u32[]{:S(2)}) async-start(bf16[8,64,256]{2,1,0:T(8,128)(2,1)} %shard_map.110), calls=%async_computation | async-start | bytes 524288 | tf_op jit(solution)/shard_map/all_to_all | solution.py:603
  108.4 1.4 %collective-permute-start.30 = (bf16[256,256]{1,0:T(8,128)(2,1)S(1)}, bf16[256,256]{1,0:T(8,128)(2,1)S(1)}, u32[]{:S(2)}, u32[]{:S(2)}) collective-permute-start(bf16[256,256]{1,0:T(8,128)(2,1)S(1)} %get-tuple-element.94), channel_id=1, source_target_pairs={{0,1},{1,0},{2,3},{3,2},{4,5},{5,4},{6,7},{7,6},{8,9},{9,8},{10,11... | collective-permute-start | bytes 393224 | tf_op jit(solution)/shard_map/ppermute | solution.py:452
  (12 other events, 133.7 us)

commit v9 on v8

--- a/solution.py
+++ b/solution.py
@@ -380,16 +380,18 @@
     return lambda t: ref[t, :, pl.ds(pl.multiple_of(n * half, half), half)]
 
 
-def outer_kernel(n_ref, mine_ref, got_ref, weight_ref, sum_ref, cols_ref, *, back, part_of):
+def outer_kernel(n_ref, mine_ref, got_ref, weight_ref, sum_ref, sum_b_ref, cols_ref, *, back, part_of):
     n = n_ref[0]
     put_columns(cols_ref, both_halves(n, mine_ref[...].astype(F32), got_ref[...].astype(F32), 0))
-    sum_ref[...] = conv_sum(cols_ref, part_of(n, weight_ref), back)
+    total = conv_sum(cols_ref, part_of(n, weight_ref), back)
+    sum_ref[...] = total
+    sum_b_ref[...] = total.astype(BF)
 
 
 def inner_forward_kernel(
     n_ref, mine_ref, got_ref, bias_ref, weight_ref, gate_ref, sum_ref, sum_b_ref, cols_ref
 ):
-    gate = mine_ref[...] + got_ref[...] + bias_ref[...]
+    gate = mine_ref[...] + got_ref[...].astype(F32) + bias_ref[...]
     gate_ref[...] = gate
     put_columns(cols_ref, gate * jax.nn.sigmoid(gate))
     total = conv_sum(cols_ref, feature_columns(n_ref[0], weight_ref), False)
@@ -400,7 +402,7 @@
 def inner_backward_kernel(
     n_ref, mine_ref, got_ref, gate_ref, weight_ref, sum_ref, sum_b_ref, cols_ref
 ):
-    put_columns(cols_ref, (mine_ref[...] + got_ref[...]) * silu_slope(gate_ref[...]))
+    put_columns(cols_ref, (mine_ref[...] + got_ref[...].astype(F32)) * silu_slope(gate_ref[...]))
     total = conv_sum(cols_ref, feature_rows(n_ref[0], weight_ref), True)
     sum_ref[...] = total
     sum_b_ref[...] = total.astype(BF)
@@ -551,7 +553,7 @@
     side_shape = shape_of((256, 256), BF)
     arrived, sides, sent = kernel_call(
         arrived_kernel, (w,), (*messages, band), [shape_of((8, 128, 256), BF), side_shape, side_shape],
-        rest=(merge_weight,),
+        rest=(merge_weight, hidden_weight, output_weight),
     )
     fine_rows = pltpu.VMEM((2, 256, 128), F32)
     sum_shapes = [shape_of((32, features), F32), shape_of((32, features), BF)]
@@ -570,13 +572,13 @@
     outer_columns = [pltpu.VMEM((27, 64, half), BF)]
     inner_columns = [pltpu.VMEM((27, 64, hidden), BF)]
 
-    (gate_part,) = kernel_call(
+    gate_part, gate_part_b = kernel_call(
         functools.partial(outer_kernel, back=False, part_of=feature_rows),
-        (n,), (mine, got, hidden_weight), [gate_shape], outer_columns,
+        (n,), (mine, got, hidden_weight), [gate_shape, shape_of((64, hidden), BF)], outer_columns,
     )
     gate_pre, branch_part, branch_part_b = kernel_call(
         inner_forward_kernel,
-        (n,), (gate_part, swap_narrow(gate_part), bias, output_weight), [gate_shape] + half_shapes, inner_columns,
+        (n,), (gate_part, swap_narrow(gate_part_b), bias, output_weight), [gate_shape] + half_shapes, inner_columns,
     )
     mine, got = to_cell_halves(n, branch_part, branch_part_b)
     grad_comb, res_part, res_part_b = kernel_call(
@@ -585,13 +587,13 @@
         [shape_of((8, 32, 256), BF)] + sum_shapes,
     )
     grad_res, mine, got = to_feature_halves(n, res_part, res_part_b)
-    (hidden_part,) = kernel_call(
+    hidden_part, hidden_part_b = kernel_call(
         functools.partial(outer_kernel, back=True, part_of=feature_columns),
-        (n,), (mine, got, output_weight), [gate_shape], outer_columns,
+        (n,), (mine, got, output_weight), [gate_shape, shape_of((64, hidden), BF)], outer_columns,
     )
     conv_part, conv_part_b = kernel_call(
         inner_backward_kernel,
-        (n,), (hidden_part, swap_narrow(hidden_part), gate_pre, hidden_weight),
+        (n,), (hidden_part, swap_narrow(hidden_part_b), gate_pre, hidden_weight),
         half_shapes, inner_columns,
     )
     mine, got = to_cell_halves(n, conv_part, conv_part_b)

time: 112 us -> 112 us (level)
  no operation moved by 1% of the time
where the time goes in v9:
time: 112 us; the launch traced here: 111 us
  waiting for transfers between devices  51.2 us (46%)
  starting transfers between devices  36.9 us (33%)
  Pallas kernels  20.7 us (18%)
  local copies, waits for them, and re-layouts  1.45 us (1%)
    ppermute x16, waiting for transfers between devices, partner(): return lax.ppermute(value, 'wide', [(i, i ^ mask) for i in range(8)])  29.5 us
    pallas_call x24, Pallas kernels, kernel_call(): pl.pallas_call(kernel, in_specs=[SMEM] * len(places) + [VMEM] * len(array...  20.7 us
    ppermute x16, starting transfers between devices, partner(): return lax.ppermute(value, 'wide', [(i, i ^ mask) for i in range(8)])  20.2 us
    ppermute x7, starting transfers between devices, across_wide(): lax.ppermute(messages[mask], 'wide', [(i, i ^ mask) for i in range(8)])  12.5 us
    ppermute x8, waiting for transfers between devices, swap_narrow(): return lax.ppermute(value, 'narrow', [(0, 1), (1, 0)])  8.47 us
    all_to_all x1, waiting for transfers between devices, eight_shards(): lax.all_to_all(leaving, 'wide', split_axis=0, concat_axis=0, tiled=True)  8 us
    ppermute x7, waiting for transfers between devices, across_wide(): lax.ppermute(messages[mask], 'wide', [(i, i ^ mask) for i in range(8)])  5.14 us
    all_to_all x1, starting transfers between devices, eight_shards(): lax.all_to_all(leaving, 'wide', split_axis=0, concat_axis=0, tiled=True)  3.41 us
  transfers between devices with their start and end apart: 32, of which 27 were waited for; matrix products, arithmetic and copies ran while one was open for 0% of the time, Pallas kernels for 3%

profile of v9, /device:TPU:0, one launch (start us, length us, event | category | flops | bytes accessed | tf_op | source)
XLA Modules:
  0.0 111.2 jit_solution(7488027775625823295)
XLA Ops:
  0.7 2.0 %shard_map.91 = (bf16[128,256]{1,0:T(8,128)(2,1)S(1)}, bf16[128,256]{1,0:T(8,128)(2,1)S(1)}, bf16[128,256]{1,0:T(8,128)(2,1)S(1)}, bf16[128,256]{1,0:T(8,128)(2,...) custom-call(s32[1]{0:T(128)} %bitcast.n_ref, ...), custom_call_target="tpu_custom_call" | custom-call | tf_op jit(solution)/shard_map/pallas_call | solution.py:140
  2.7 3.0 %collective-permute-start = (bf16[128,256]{1,0:T(8,128)(2,1)S(1)}, bf16[128,256]{1,0:T(8,128)(2,1)S(1)}, u32[]{:S(2)}, u32[]{:S(2)}) collective-permute-start(bf16[128,256]{1,0:T(8,128)(2,1)S(1)} %get-tuple-element.55), channel_id=1, source_target_pairs={{0,2},{2,0},{4,6},{6,4},{8,10},{10,8},{12,14},{14,12},{1,3},{3,1},... | collective-permute-start | bytes 196616 | tf_op jit(solution)/shard_map/ppermute | solution.py:518
  5.7 1.6 %collective-permute-start.1 = (bf16[128,256]{1,0:T(8,128)(2,1)S(1)}, bf16[128,256]{1,0:T(8,128)(2,1)S(1)}, u32[]{:S(2)}, u32[]{:S(2)}) collective-permute-start(bf16[128,256]{1,0:T(8,128)(2,1)S(1)} %get-tuple-element.56), channel_id=1, source_target_pairs={{0,4},{2,6},{4,0},{6,2},{8,12},{10,14},{12,8},{14,10},{1,5},{3,7},... | collective-permute-start | bytes 196616 | tf_op jit(solution)/shard_map/ppermute | solution.py:518
  7.3 3.0 %collective-permute-start.3 = (bf16[128,256]{1,0:T(8,128)(2,1)S(1)}, bf16[128,256]{1,0:T(8,128)(2,1)S(1)}, u32[]{:S(2)}, u32[]{:S(2)}) collective-permute-start(bf16[128,256]{1,0:T(8,128)(2,1)S(1)} %get-tuple-element.58), channel_id=1, source_target_pairs={{0,8},{2,10},{4,12},{6,14},{8,0},{10,2},{12,4},{14,6},{1,9},{3,11}... | collective-permute-start | bytes 196616 | tf_op jit(solution)/shard_map/ppermute | solution.py:518
  11.6 3.6 %collective-permute-start.5 = (bf16[128,256]{1,0:T(8,128)(2,1)S(1)}, bf16[128,256]{1,0:T(8,128)(2,1)S(1)}, u32[]{:S(2)}, u32[]{:S(2)}) collective-permute-start(bf16[128,256]{1,0:T(8,128)(2,1)S(1)} %get-tuple-element.60), channel_id=1, source_target_pairs={{0,12},{2,14},{4,8},{6,10},{8,4},{10,6},{12,0},{14,2},{1,13},{3,15... | collective-permute-start | bytes 196616 | tf_op jit(solution)/shard_map/ppermute | solution.py:518
  17.1 3.4 %collective-permute-done.4.refs_5_ = bf16[128,256]{1,0:T(8,128)(2,1)S(1)} collective-permute-done((bf16[128,256]{1,0:T(8,128)(2,1)S(1)}, bf16[128,256]{1,0:T(8,128)(2,1)S(1)}, u32[]{:S(2)}, u32[]{:S(2)}) %collective-permute-start.4) | collective-permute-done | bytes 65568 | tf_op jit(solution)/shard_map/ppermute | solution.py:518
  20.5 1.7 %collective-permute-done.6.refs_7_ = bf16[128,256]{1,0:T(8,128)(2,1)S(1)} collective-permute-done((bf16[128,256]{1,0:T(8,128)(2,1)S(1)}, bf16[128,256]{1,0:T(8,128)(2,1)S(1)}, u32[]{:S(2)}, u32[]{:S(2)}) %collective-permute-start.6) | collective-permute-done | bytes 65568 | tf_op jit(solution)/shard_map/ppermute | solution.py:518
  26.3 3.8 %collective-permute-done.8.refs_0_ = bf16[32,1024]{1,0:T(8,128)(2,1)S(1)} collective-permute-done((bf16[32,1024]{1,0:T(8,128)(2,1)S(1)}, bf16[32,1024]{1,0:T(8,128)(2,1)S(1)}, u32[]{:S(2)}, u32[]{:S(2)}) %collective-permute-start.8) | collective-permute-done | bytes 65568 | tf_op jit(solution)/shard_map/ppermute | solution.py:488
  30.1 1.7 %collective-permute-start.10 = (bf16[32,1024]{1,0:T(8,128)(2,1)S(1)}, bf16[32,1024]{1,0:T(8,128)(2,1)S(1)}, u32[]{:S(2)}, u32[]{:S(2)}) collective-permute-start(bf16[32,1024]{1,0:T(8,128)(2,1)S(1)} %get-tuple-element.69), channel_id=1, source_target_pairs={{0,4},{2,6},{4,0},{6,2},{8,12},{10,14},{12,8},{14,10},{1,5},{3,7},... | collective-permute-start | bytes 196616 | tf_op jit(solution)/shard_map/ppermute | solution.py:488
  33.0 1.6 %collective-permute-start.9 = (bf16[32,1024]{1,0:T(8,128)(2,1)S(1)}, bf16[32,1024]{1,0:T(8,128)(2,1)S(1)}, u32[]{:S(2)}, u32[]{:S(2)}) collective-permute-start(bf16[32,1024]{1,0:T(8,128)(2,1)S(1)} %get-tuple-element.69), channel_id=1, source_target_pairs={{0,12},{2,14},{4,8},{6,10},{8,4},{10,6},{12,0},{14,2},{1,13},{3,15... | collective-permute-start | bytes 196616 | tf_op jit(solution)/shard_map/ppermute | solution.py:488
  34.9 3.0 %collective-permute-done.11.three_ref = bf16[32,1024]{1,0:T(8,128)(2,1)S(1)} collective-permute-done((bf16[32,1024]{1,0:T(8,128)(2,1)S(1)}, bf16[32,1024]{1,0:T(8,128)(2,1)S(1)}, u32[]{:S(2)}, u32[]{:S(2)}) %collective-permute-start.11) | collective-permute-done | bytes 65568 | tf_op jit(solution)/shard_map/ppermute | solution.py:488
  40.5 1.4 %shard_map.98 = (f32[64,256]{1,0:T(8,128)S(1)}, bf16[64,256]{1,0:T(8,128)(2,1)S(1)}) custom-call(s32[1]{0:T(128)} %bitcast.n_ref, bf16[32,512]{1,0:T(8,128)(2,1)S(1)} %get-tuple-element.71.mine_ref, bf16[32,512]{1,0:T(8,128)(2,1)S(1)} %collective-permute-done.12.got_ref, bf16[27,1024,256]{2,1,0:T(8,128)(2,1)S(1)} %bitcast.8), custom_call_target="tpu_custom_call" | custom-call | tf_op jit(solution)/shard_map/pallas_call | solution.py:140
  45.1 3.7 %collective-permute-done.14.refs_0_ = bf16[64,512]{1,0:T(8,128)(2,1)S(1)} collective-permute-done((bf16[64,512]{1,0:T(8,128)(2,1)S(1)}, bf16[64,512]{1,0:T(8,128)(2,1)S(1)}, u32[]{:S(2)}, u32[]{:S(2)}) %collective-permute-start.14) | collective-permute-done | bytes 65568 | tf_op jit(solution)/shard_map/ppermute | solution.py:488
  48.9 1.7 %collective-permute-start.15 = (bf16[64,512]{1,0:T(8,128)(2,1)S(1)}, bf16[64,512]{1,0:T(8,128)(2,1)S(1)}, u32[]{:S(2)}, u32[]{:S(2)}) collective-permute-start(bf16[64,512]{1,0:T(8,128)(2,1)S(1)} %get-tuple-element.79), channel_id=1, source_target_pairs={{0,12},{2,14},{4,8},{6,10},{8,4},{10,6},{12,0},{14,2},{1,13},{3,15... | collective-permute-start | bytes 196616 | tf_op jit(solution)/shard_map/ppermute | solution.py:488
  51.0 2.3 %collective-permute-start.17 = (bf16[64,512]{1,0:T(8,128)(2,1)S(1)}, bf16[64,512]{1,0:T(8,128)(2,1)S(1)}, u32[]{:S(2)}, u32[]{:S(2)}) collective-permute-start(bf16[64,512]{1,0:T(8,128)(2,1)S(1)} %get-tuple-element.79), channel_id=1, source_target_pairs={{0,8},{2,10},{4,12},{6,14},{8,0},{10,2},{12,4},{14,6},{1,9},{3,11}... | collective-permute-start | bytes 196616 | tf_op jit(solution)/shard_map/ppermute | solution.py:488
  53.3 2.2 %collective-permute-done.15.one_ref = bf16[64,512]{1,0:T(8,128)(2,1)S(1)} collective-permute-done((bf16[64,512]{1,0:T(8,128)(2,1)S(1)}, bf16[64,512]{1,0:T(8,128)(2,1)S(1)}, u32[]{:S(2)}, u32[]{:S(2)}) %collective-permute-start.15) | collective-permute-done | bytes 65568 | tf_op jit(solution)/shard_map/ppermute | solution.py:488
  57.9 2.7 %shard_map.103 = (bf16[8,32,256]{2,1,0:T(8,128)(2,1)S(1)}, f32[32,1024]{1,0:T(8,128)S(1)}, bf16[32,1024]{1,0:T(8,128)(2,1)S(1)}) custom-call(s32[1]{0:T(128)} %bitcast.n_ref, f32[32,1024]{1,0:T(8,128)S(1)} %get-tuple-element.70.merged_ref, f32[32,512]{1,0:T(8,128)S(1)} %get-tuple-element.80.mine_ref, bf16[32,512]{1,0:T(8,128)(2,1)S(1)} %collective-permute-done.18.got_ref, ...), custom_call_target="tpu_custom_call" | custom-call | tf_op jit(solution)/shard_map/pallas_call | solution.py:140
  61.2 3.7 %collective-permute-done.19.refs_0_ = bf16[32,1024]{1,0:T(8,128)(2,1)S(1)} collective-permute-done((bf16[32,1024]{1,0:T(8,128)(2,1)S(1)}, bf16[32,1024]{1,0:T(8,128)(2,1)S(1)}, u32[]{:S(2)}, u32[]{:S(2)}) %collective-permute-start.19) | collective-permute-done | bytes 65568 | tf_op jit(solution)/shard_map/ppermute | solution.py:488
  65.0 1.9 %collective-permute-start.20 = (bf16[32,1024]{1,0:T(8,128)(2,1)S(1)}, bf16[32,1024]{1,0:T(8,128)(2,1)S(1)}, u32[]{:S(2)}, u32[]{:S(2)}) collective-permute-start(bf16[32,1024]{1,0:T(8,128)(2,1)S(1)} %get-tuple-element.86), channel_id=1, source_target_pairs={{0,12},{2,14},{4,8},{6,10},{8,4},{10,6},{12,0},{14,2},{1,13},{3,15... | collective-permute-start | bytes 196616 | tf_op jit(solution)/shard_map/ppermute | solution.py:488
  67.5 1.9 %collective-permute-start.22 = (bf16[32,1024]{1,0:T(8,128)(2,1)S(1)}, bf16[32,1024]{1,0:T(8,128)(2,1)S(1)}, u32[]{:S(2)}, u32[]{:S(2)}) collective-permute-start(bf16[32,1024]{1,0:T(8,128)(2,1)S(1)} %get-tuple-element.86), channel_id=1, source_target_pairs={{0,8},{2,10},{4,12},{6,14},{8,0},{10,2},{12,4},{14,6},{1,9},{3,11}... | collective-permute-start | bytes 196616 | tf_op jit(solution)/shard_map/ppermute | solution.py:488
  69.4 2.4 %collective-permute-done.20.one_ref = bf16[32,1024]{1,0:T(8,128)(2,1)S(1)} collective-permute-done((bf16[32,1024]{1,0:T(8,128)(2,1)S(1)}, bf16[32,1024]{1,0:T(8,128)(2,1)S(1)}, u32[]{:S(2)}, u32[]{:S(2)}) %collective-permute-start.20) | collective-permute-done | bytes 65568 | tf_op jit(solution)/shard_map/ppermute | solution.py:488
  74.1 2.0 %shard_map.106 = (f32[64,256]{1,0:T(8,128)S(1)}, bf16[64,256]{1,0:T(8,128)(2,1)S(1)}) custom-call(s32[1]{0:T(128)} %bitcast.n_ref, bf16[32,512]{1,0:T(8,128)(2,1)S(1)} %get-tuple-element.88.mine_ref, bf16[32,512]{1,0:T(8,128)(2,1)S(1)} %collective-permute-done.23.got_ref, bf16[27,256,1024]{2,1,0:T(8,128)(2,1)S(1)} %bitcast.6), custom_call_target="tpu_custom_call" | custom-call | tf_op jit(solution)/shard_map/pallas_call | solution.py:140
  77.4 2.0 %shard_map.107 = (f32[64,512]{1,0:T(8,128)S(1)}, bf16[64,512]{1,0:T(8,128)(2,1)S(1)}) custom-call(s32[1]{0:T(128)} %bitcast.n_ref, f32[64,256]{1,0:T(8,128)S(1)} %get-tuple-element.90.mine_ref, bf16[64,256]{1,0:T(8,128)(2,1)S(1)} %collective-permute-done.24.got_ref, f32[64,256]{1,0:T(8,128)S(1)} %get-tuple-element.92.gate_ref, bf16[27,1024,256]{2,1,0:T(8,128)(2,1)S(1)} %bitcast.8), custom_call_target="tpu_custom_call" | custom-call | tf_op jit(solution)/shard_map/pallas_call | solution.py:140
  80.1 3.7 %collective-permute-done.25.refs_0_ = bf16[64,512]{1,0:T(8,128)(2,1)S(1)} collective-permute-done((bf16[64,512]{1,0:T(8,128)(2,1)S(1)}, bf16[64,512]{1,0:T(8,128)(2,1)S(1)}, u32[]{:S(2)}, u32[]{:S(2)}) %collective-permute-start.25) | collective-permute-done | bytes 65568 | tf_op jit(solution)/shard_map/ppermute | solution.py:488
  83.9 1.9 %collective-permute-start.26 = (bf16[64,512]{1,0:T(8,128)(2,1)S(1)}, bf16[64,512]{1,0:T(8,128)(2,1)S(1)}, u32[]{:S(2)}, u32[]{:S(2)}) collective-permute-start(bf16[64,512]{1,0:T(8,128)(2,1)S(1)} %get-tuple-element.96), channel_id=1, source_target_pairs={{0,12},{2,14},{4,8},{6,10},{8,4},{10,6},{12,0},{14,2},{1,13},{3,15... | collective-permute-start | bytes 196616 | tf_op jit(solution)/shard_map/ppermute | solution.py:488
  86.3 2.0 %collective-permute-start.28 = (bf16[64,512]{1,0:T(8,128)(2,1)S(1)}, bf16[64,512]{1,0:T(8,128)(2,1)S(1)}, u32[]{:S(2)}, u32[]{:S(2)}) collective-permute-start(bf16[64,512]{1,0:T(8,128)(2,1)S(1)} %get-tuple-element.96), channel_id=1, source_target_pairs={{0,8},{2,10},{4,12},{6,14},{8,0},{10,2},{12,4},{14,6},{1,9},{3,11}... | collective-permute-start | bytes 196616 | tf_op jit(solution)/shard_map/ppermute | solution.py:488
  88.3 2.4 %collective-permute-done.26.one_ref = bf16[64,512]{1,0:T(8,128)(2,1)S(1)} collective-permute-done((bf16[64,512]{1,0:T(8,128)(2,1)S(1)}, bf16[64,512]{1,0:T(8,128)(2,1)S(1)}, u32[]{:S(2)}, u32[]{:S(2)}) %collective-permute-start.26) | collective-permute-done | bytes 65568 | tf_op jit(solution)/shard_map/ppermute | solution.py:488
  93.0 2.1 %shard_map.110 = bf16[8,64,256]{2,1,0:T(8,128)(2,1)} custom-call(s32[1]{0:T(128)} %bitcast.n_ref, s32[1]{0:T(128)} %bitcast.1.w_ref, f32[32,1024]{1,0:T(8,128)S(1)} %get-tuple-element.87.res_ref, f32[32,512]{1,0:T(8,128)S(1)} %get-tuple-element.97.mine_ref, bf16[32,512]{1,0:T(8,128)(2,1)S(1)} %collective-permute-done.29.got_ref, ...), custom_call_target="tpu_custom_call" | custom-call | tf_op jit(solution)/shard_map/pallas_call | solution.py:140
  95.1 3.4 %all-to-all-start = ((bf16[8,64,256]{2,1,0:T(8,128)(2,1)}), bf16[8,64,256]{2,1,0:T(8,128)(2,1)S(1)}, u32[]{:S(2)}, u32[]{:S(2)}) async-start(bf16[8,64,256]{2,1,0:T(8,128)(2,1)} %shard_map.110), calls=%async_computation | async-start | bytes 524288 | tf_op jit(solution)/shard_map/all_to_all | solution.py:605
  98.6 1.4 %shard_map.111.band_ref = bf16[1024,768]{1,0:T(8,128)(2,1)S(1)} custom-call(bf16[27,32,32]{2,1,0:T(8,128)(2,1)S(1)} %copy-done.3), custom_call_target="tpu_custom_call" | custom-call | bytes 33554432 | tf_op jit(solution)/shard_map/pallas_call | solution.py:140
  100.0 8.0 %all-to-all-done.planes_ref = bf16[8,64,256]{2,1,0:T(8,128)(2,1)S(1)} async-done(((bf16[8,64,256]{2,1,0:T(8,128)(2,1)}), bf16[8,64,256]{2,1,0:T(8,128)(2,1)S(1)}, u32[]{:S(2)}, u32[]{:S(2)}) %all-to-all-start) | async-done | bytes 262176 | tf_op jit(solution)/shard_map/all_to_all | solution.py:605
  109.7 1.5 %shard_map.114 = bf16[8,16,16,32]{3,2,1,0:T(8,128)(2,1)} custom-call(s32[1]{0:T(128)} %bitcast.n_ref, f32[256,768]{1,0:T(8,128)S(1)} %shard_map.112.main_ref, bf16[256,256]{1,0:T(8,128)(2,1)S(1)} %get-tuple-element.101.own_ref, bf16[256,256]{1,0:T(8,128)(2,1)S(1)} %collective-permute-done.30.got_ref, bf16[1024,768]{1,0:T(8,128)(2,1)S(1)} %shard_map.111.band_ref), custom_call_target="tpu_custom_call" | custom-call | tf_op jit(solution)/shard_map/pallas_call | solution.py:140
  (82 shorter events, 27.2 us)
Async XLA Ops:
  2.7 8.9 %collective-permute-start = (bf16[128,256]{1,0:T(8,128)(2,1)S(1)}, bf16[128,256]{1,0:T(8,128)(2,1)S(1)}, u32[]{:S(2)}, u32[]{:S(2)}) collective-permute-start(bf16[128,256]{1,0:T(8,128)(2,1)S(1)} %get-tuple-element.55), channel_id=1, source_target_pairs={{0,2},{2,0},{4,6},{6,4},{8,10},{10,8},{12,14},{14,12},{1,3},{3,1},... | collective-permute-start | bytes 196616 | tf_op jit(solution)/shard_map/ppermute | solution.py:518
  5.7 9.5 %collective-permute-start.1 = (bf16[128,256]{1,0:T(8,128)(2,1)S(1)}, bf16[128,256]{1,0:T(8,128)(2,1)S(1)}, u32[]{:S(2)}, u32[]{:S(2)}) collective-permute-start(bf16[128,256]{1,0:T(8,128)(2,1)S(1)} %get-tuple-element.56), channel_id=1, source_target_pairs={{0,4},{2,6},{4,0},{6,2},{8,12},{10,14},{12,8},{14,10},{1,5},{3,7},... | collective-permute-start | bytes 196616 | tf_op jit(solution)/shard_map/ppermute | solution.py:518
  7.3 9.8 %collective-permute-start.2 = (bf16[128,256]{1,0:T(8,128)(2,1)S(1)}, bf16[128,256]{1,0:T(8,128)(2,1)S(1)}, u32[]{:S(2)}, u32[]{:S(2)}) collective-permute-start(bf16[128,256]{1,0:T(8,128)(2,1)S(1)} %get-tuple-element.57), channel_id=1, source_target_pairs={{0,6},{2,4},{4,2},{6,0},{8,14},{10,12},{12,10},{14,8},{1,7},{3,5},... | collective-permute-start | bytes 196616 | tf_op jit(solution)/shard_map/ppermute | solution.py:518
  7.3 9.8 %collective-permute-start.3 = (bf16[128,256]{1,0:T(8,128)(2,1)S(1)}, bf16[128,256]{1,0:T(8,128)(2,1)S(1)}, u32[]{:S(2)}, u32[]{:S(2)}) collective-permute-start(bf16[128,256]{1,0:T(8,128)(2,1)S(1)} %get-tuple-element.58), channel_id=1, source_target_pairs={{0,8},{2,10},{4,12},{6,14},{8,0},{10,2},{12,4},{14,6},{1,9},{3,11}... | collective-permute-start | bytes 196616 | tf_op jit(solution)/shard_map/ppermute | solution.py:518
  10.3 10.2 %collective-permute-start.4 = (bf16[128,256]{1,0:T(8,128)(2,1)S(1)}, bf16[128,256]{1,0:T(8,128)(2,1)S(1)}, u32[]{:S(2)}, u32[]{:S(2)}) collective-permute-start(bf16[128,256]{1,0:T(8,128)(2,1)S(1)} %get-tuple-element.59), channel_id=1, source_target_pairs={{0,10},{2,8},{4,14},{6,12},{8,2},{10,0},{12,6},{14,4},{1,11},{3,9}... | collective-permute-start | bytes 196616 | tf_op jit(solution)/shard_map/ppermute | solution.py:518
  11.6 8.9 %collective-permute-start.5 = (bf16[128,256]{1,0:T(8,128)(2,1)S(1)}, bf16[128,256]{1,0:T(8,128)(2,1)S(1)}, u32[]{:S(2)}, u32[]{:S(2)}) collective-permute-start(bf16[128,256]{1,0:T(8,128)(2,1)S(1)} %get-tuple-element.60), channel_id=1, source_target_pairs={{0,12},{2,14},{4,8},{6,10},{8,4},{10,6},{12,0},{14,2},{1,13},{3,15... | collective-permute-start | bytes 196616 | tf_op jit(solution)/shard_map/ppermute | solution.py:518
  15.2 7.1 %collective-permute-start.6 = (bf16[128,256]{1,0:T(8,128)(2,1)S(1)}, bf16[128,256]{1,0:T(8,128)(2,1)S(1)}, u32[]{:S(2)}, u32[]{:S(2)}) collective-permute-start(bf16[128,256]{1,0:T(8,128)(2,1)S(1)} %get-tuple-element.61), channel_id=1, source_target_pairs={{0,14},{2,12},{4,10},{6,8},{8,6},{10,4},{12,2},{14,0},{1,15},{3,13... | collective-permute-start | bytes 196616 | tf_op jit(solution)/shard_map/ppermute | solution.py:518
  22.5 1.4 %collective-permute-start.7 = (bf16[256,256]{1,0:T(8,128)(2,1)S(1)}, bf16[256,256]{1,0:T(8,128)(2,1)S(1)}, u32[]{:S(2)}, u32[]{:S(2)}) collective-permute-start(bf16[256,256]{1,0:T(8,128)(2,1)S(1)} %get-tuple-element.65), channel_id=1, source_target_pairs={{0,1},{1,0},{2,3},{3,2},{4,5},{5,4},{6,7},{7,6},{8,9},{9,8},{10,11... | collective-permute-start | bytes 393224 | tf_op jit(solution)/shard_map/ppermute | solution.py:454
  25.7 4.3 %collective-permute-start.8 = (bf16[32,1024]{1,0:T(8,128)(2,1)S(1)}, bf16[32,1024]{1,0:T(8,128)(2,1)S(1)}, u32[]{:S(2)}, u32[]{:S(2)}) collective-permute-start(bf16[32,1024]{1,0:T(8,128)(2,1)S(1)} %get-tuple-element.67), channel_id=1, source_target_pairs={{0,2},{2,0},{4,6},{6,4},{8,10},{10,8},{12,14},{14,12},{1,3},{3,1},... | collective-permute-start | bytes 196616 | tf_op jit(solution)/shard_map/ppermute | solution.py:488
  30.1 4.9 %collective-permute-start.10 = (bf16[32,1024]{1,0:T(8,128)(2,1)S(1)}, bf16[32,1024]{1,0:T(8,128)(2,1)S(1)}, u32[]{:S(2)}, u32[]{:S(2)}) collective-permute-start(bf16[32,1024]{1,0:T(8,128)(2,1)S(1)} %get-tuple-element.69), channel_id=1, source_target_pairs={{0,4},{2,6},{4,0},{6,2},{8,12},{10,14},{12,8},{14,10},{1,5},{3,7},... | collective-permute-start | bytes 196616 | tf_op jit(solution)/shard_map/ppermute | solution.py:488
  31.8 6.1 %collective-permute-start.11 = (bf16[32,1024]{1,0:T(8,128)(2,1)S(1)}, bf16[32,1024]{1,0:T(8,128)(2,1)S(1)}, u32[]{:S(2)}, u32[]{:S(2)}) collective-permute-start(bf16[32,1024]{1,0:T(8,128)(2,1)S(1)} %get-tuple-element.69), channel_id=1, source_target_pairs={{0,8},{2,10},{4,12},{6,14},{8,0},{10,2},{12,4},{14,6},{1,9},{3,11}... | collective-permute-start | bytes 196616 | tf_op jit(solution)/shard_map/ppermute | solution.py:488
  33.0 6.2 %collective-permute-start.9 = (bf16[32,1024]{1,0:T(8,128)(2,1)S(1)}, bf16[32,1024]{1,0:T(8,128)(2,1)S(1)}, u32[]{:S(2)}, u32[]{:S(2)}) collective-permute-start(bf16[32,1024]{1,0:T(8,128)(2,1)S(1)} %get-tuple-element.69), channel_id=1, source_target_pairs={{0,12},{2,14},{4,8},{6,10},{8,4},{10,6},{12,0},{14,2},{1,13},{3,15... | collective-permute-start | bytes 196616 | tf_op jit(solution)/shard_map/ppermute | solution.py:488
  39.2 1.3 %collective-permute-start.12 = (bf16[32,512]{1,0:T(8,128)(2,1)S(1)}, bf16[32,512]{1,0:T(8,128)(2,1)S(1)}, u32[]{:S(2)}, u32[]{:S(2)}) collective-permute-start(bf16[32,512]{1,0:T(8,128)(2,1)S(1)} %get-tuple-element.72), channel_id=1, source_target_pairs={{0,1},{1,0},{2,3},{3,2},{4,5},{5,4},{6,7},{7,6},{8,9},{9,8},{10,11... | collective-permute-start | bytes 98312 | tf_op jit(solution)/shard_map/ppermute | solution.py:454
  41.9 1.3 %collective-permute-start.13 = (bf16[64,256]{1,0:T(8,128)(2,1)S(1)}, bf16[64,256]{1,0:T(8,128)(2,1)S(1)}, u32[]{:S(2)}, u32[]{:S(2)}) collective-permute-start(bf16[64,256]{1,0:T(8,128)(2,1)S(1)} %get-tuple-element.74), channel_id=1, source_target_pairs={{0,1},{1,0},{2,3},{3,2},{4,5},{5,4},{6,7},{7,6},{8,9},{9,8},{10,11... | collective-permute-start | bytes 98312 | tf_op jit(solution)/shard_map/ppermute | solution.py:454
  44.5 4.3 %collective-permute-start.14 = (bf16[64,512]{1,0:T(8,128)(2,1)S(1)}, bf16[64,512]{1,0:T(8,128)(2,1)S(1)}, u32[]{:S(2)}, u32[]{:S(2)}) collective-permute-start(bf16[64,512]{1,0:T(8,128)(2,1)S(1)} %get-tuple-element.77), channel_id=1, source_target_pairs={{0,2},{2,0},{4,6},{6,4},{8,10},{10,8},{12,14},{14,12},{1,3},{3,1},... | collective-permute-start | bytes 196616 | tf_op jit(solution)/shard_map/ppermute | solution.py:488
  48.9 6.7 %collective-permute-start.15 = (bf16[64,512]{1,0:T(8,128)(2,1)S(1)}, bf16[64,512]{1,0:T(8,128)(2,1)S(1)}, u32[]{:S(2)}, u32[]{:S(2)}) collective-permute-start(bf16[64,512]{1,0:T(8,128)(2,1)S(1)} %get-tuple-element.79), channel_id=1, source_target_pairs={{0,12},{2,14},{4,8},{6,10},{8,4},{10,6},{12,0},{14,2},{1,13},{3,15... | collective-permute-start | bytes 196616 | tf_op jit(solution)/shard_map/ppermute | solution.py:488
  50.6 5.0 %collective-permute-start.16 = (bf16[64,512]{1,0:T(8,128)(2,1)S(1)}, bf16[64,512]{1,0:T(8,128)(2,1)S(1)}, u32[]{:S(2)}, u32[]{:S(2)}) collective-permute-start(bf16[64,512]{1,0:T(8,128)(2,1)S(1)} %get-tuple-element.79), channel_id=1, source_target_pairs={{0,4},{2,6},{4,0},{6,2},{8,12},{10,14},{12,8},{14,10},{1,5},{3,7},... | collective-permute-start | bytes 196616 | tf_op jit(solution)/shard_map/ppermute | solution.py:488
  51.0 5.6 %collective-permute-start.17 = (bf16[64,512]{1,0:T(8,128)(2,1)S(1)}, bf16[64,512]{1,0:T(8,128)(2,1)S(1)}, u32[]{:S(2)}, u32[]{:S(2)}) collective-permute-start(bf16[64,512]{1,0:T(8,128)(2,1)S(1)} %get-tuple-element.79), channel_id=1, source_target_pairs={{0,8},{2,10},{4,12},{6,14},{8,0},{10,2},{12,4},{14,6},{1,9},{3,11}... | collective-permute-start | bytes 196616 | tf_op jit(solution)/shard_map/ppermute | solution.py:488
  56.6 1.3 %collective-permute-start.18 = (bf16[32,512]{1,0:T(8,128)(2,1)S(1)}, bf16[32,512]{1,0:T(8,128)(2,1)S(1)}, u32[]{:S(2)}, u32[]{:S(2)}) collective-permute-start(bf16[32,512]{1,0:T(8,128)(2,1)S(1)} %get-tuple-element.81), channel_id=1, source_target_pairs={{0,1},{1,0},{2,3},{3,2},{4,5},{5,4},{6,7},{7,6},{8,9},{9,8},{10,11... | collective-permute-start | bytes 98312 | tf_op jit(solution)/shard_map/ppermute | solution.py:454
  60.6 4.3 %collective-permute-start.19 = (bf16[32,1024]{1,0:T(8,128)(2,1)S(1)}, bf16[32,1024]{1,0:T(8,128)(2,1)S(1)}, u32[]{:S(2)}, u32[]{:S(2)}) collective-permute-start(bf16[32,1024]{1,0:T(8,128)(2,1)S(1)} %get-tuple-element.84), channel_id=1, source_target_pairs={{0,2},{2,0},{4,6},{6,4},{8,10},{10,8},{12,14},{14,12},{1,3},{3,1},... | collective-permute-start | bytes 196616 | tf_op jit(solution)/shard_map/ppermute | solution.py:488
  65.0 6.8 %collective-permute-start.20 = (bf16[32,1024]{1,0:T(8,128)(2,1)S(1)}, bf16[32,1024]{1,0:T(8,128)(2,1)S(1)}, u32[]{:S(2)}, u32[]{:S(2)}) collective-permute-start(bf16[32,1024]{1,0:T(8,128)(2,1)S(1)} %get-tuple-element.86), channel_id=1, source_target_pairs={{0,12},{2,14},{4,8},{6,10},{8,4},{10,6},{12,0},{14,2},{1,13},{3,15... | collective-permute-start | bytes 196616 | tf_op jit(solution)/shard_map/ppermute | solution.py:488
  66.8 5.0 %collective-permute-start.21 = (bf16[32,1024]{1,0:T(8,128)(2,1)S(1)}, bf16[32,1024]{1,0:T(8,128)(2,1)S(1)}, u32[]{:S(2)}, u32[]{:S(2)}) collective-permute-start(bf16[32,1024]{1,0:T(8,128)(2,1)S(1)} %get-tuple-element.86), channel_id=1, source_target_pairs={{0,4},{2,6},{4,0},{6,2},{8,12},{10,14},{12,8},{14,10},{1,5},{3,7},... | collective-permute-start | bytes 196616 | tf_op jit(solution)/shard_map/ppermute | solution.py:488
  67.5 5.3 %collective-permute-start.22 = (bf16[32,1024]{1,0:T(8,128)(2,1)S(1)}, bf16[32,1024]{1,0:T(8,128)(2,1)S(1)}, u32[]{:S(2)}, u32[]{:S(2)}) collective-permute-start(bf16[32,1024]{1,0:T(8,128)(2,1)S(1)} %get-tuple-element.86), channel_id=1, source_target_pairs={{0,8},{2,10},{4,12},{6,14},{8,0},{10,2},{12,4},{14,6},{1,9},{3,11}... | collective-permute-start | bytes 196616 | tf_op jit(solution)/shard_map/ppermute | solution.py:488
  72.8 1.3 %collective-permute-start.23 = (bf16[32,512]{1,0:T(8,128)(2,1)S(1)}, bf16[32,512]{1,0:T(8,128)(2,1)S(1)}, u32[]{:S(2)}, u32[]{:S(2)}) collective-permute-start(bf16[32,512]{1,0:T(8,128)(2,1)S(1)} %get-tuple-element.89), channel_id=1, source_target_pairs={{0,1},{1,0},{2,3},{3,2},{4,5},{5,4},{6,7},{7,6},{8,9},{9,8},{10,11... | collective-permute-start | bytes 98312 | tf_op jit(solution)/shard_map/ppermute | solution.py:454
  76.2 1.3 %collective-permute-start.24 = (bf16[64,256]{1,0:T(8,128)(2,1)S(1)}, bf16[64,256]{1,0:T(8,128)(2,1)S(1)}, u32[]{:S(2)}, u32[]{:S(2)}) collective-permute-start(bf16[64,256]{1,0:T(8,128)(2,1)S(1)} %get-tuple-element.91), channel_id=1, source_target_pairs={{0,1},{1,0},{2,3},{3,2},{4,5},{5,4},{6,7},{7,6},{8,9},{9,8},{10,11... | collective-permute-start | bytes 98312 | tf_op jit(solution)/shard_map/ppermute | solution.py:454
  79.5 4.3 %collective-permute-start.25 = (bf16[64,512]{1,0:T(8,128)(2,1)S(1)}, bf16[64,512]{1,0:T(8,128)(2,1)S(1)}, u32[]{:S(2)}, u32[]{:S(2)}) collective-permute-start(bf16[64,512]{1,0:T(8,128)(2,1)S(1)} %get-tuple-element.94), channel_id=1, source_target_pairs={{0,2},{2,0},{4,6},{6,4},{8,10},{10,8},{12,14},{14,12},{1,3},{3,1},... | collective-permute-start | bytes 196616 | tf_op jit(solution)/shard_map/ppermute | solution.py:488
  83.9 6.9 %collective-permute-start.26 = (bf16[64,512]{1,0:T(8,128)(2,1)S(1)}, bf16[64,512]{1,0:T(8,128)(2,1)S(1)}, u32[]{:S(2)}, u32[]{:S(2)}) collective-permute-start(bf16[64,512]{1,0:T(8,128)(2,1)S(1)} %get-tuple-element.96), channel_id=1, source_target_pairs={{0,12},{2,14},{4,8},{6,10},{8,4},{10,6},{12,0},{14,2},{1,13},{3,15... | collective-permute-start | bytes 196616 | tf_op jit(solution)/shard_map/ppermute | solution.py:488
  85.8 5.0 %collective-permute-start.27 = (bf16[64,512]{1,0:T(8,128)(2,1)S(1)}, bf16[64,512]{1,0:T(8,128)(2,1)S(1)}, u32[]{:S(2)}, u32[]{:S(2)}) collective-permute-start(bf16[64,512]{1,0:T(8,128)(2,1)S(1)} %get-tuple-element.96), channel_id=1, source_target_pairs={{0,4},{2,6},{4,0},{6,2},{8,12},{10,14},{12,8},{14,10},{1,5},{3,7},... | collective-permute-start | bytes 196616 | tf_op jit(solution)/shard_map/ppermute | solution.py:488
  86.3 5.4 %collective-permute-start.28 = (bf16[64,512]{1,0:T(8,128)(2,1)S(1)}, bf16[64,512]{1,0:T(8,128)(2,1)S(1)}, u32[]{:S(2)}, u32[]{:S(2)}) collective-permute-start(bf16[64,512]{1,0:T(8,128)(2,1)S(1)} %get-tuple-element.96), channel_id=1, source_target_pairs={{0,8},{2,10},{4,12},{6,14},{8,0},{10,2},{12,4},{14,6},{1,9},{3,11}... | collective-permute-start | bytes 196616 | tf_op jit(solution)/shard_map/ppermute | solution.py:488
  91.7 1.3 %collective-permute-start.29 = (bf16[32,512]{1,0:T(8,128)(2,1)S(1)}, bf16[32,512]{1,0:T(8,128)(2,1)S(1)}, u32[]{:S(2)}, u32[]{:S(2)}) collective-permute-start(bf16[32,512]{1,0:T(8,128)(2,1)S(1)} %get-tuple-element.98), channel_id=1, source_target_pairs={{0,1},{1,0},{2,3},{3,2},{4,5},{5,4},{6,7},{7,6},{8,9},{9,8},{10,11... | collective-permute-start | bytes 98312 | tf_op jit(solution)/shard_map/ppermute | solution.py:454
  95.1 12.9 %all-to-all-start = ((bf16[8,64,256]{2,1,0:T(8,128)(2,1)}), bf16[8,64,256]{2,1,0:T(8,128)(2,1)S(1)}, u32[]{:S(2)}, u32[]{:S(2)}) async-start(bf16[8,64,256]{2,1,0:T(8,128)(2,1)} %shard_map.110), calls=%async_computation | async-start | bytes 524288 | tf_op jit(solution)/shard_map/all_to_all | solution.py:605
  108.3 1.4 %collective-permute-start.30 = (bf16[256,256]{1,0:T(8,128)(2,1)S(1)}, bf16[256,256]{1,0:T(8,128)(2,1)S(1)}, u32[]{:S(2)}, u32[]{:S(2)}) collective-permute-start(bf16[256,256]{1,0:T(8,128)(2,1)S(1)} %get-tuple-element.102), channel_id=1, source_target_pairs={{0,1},{1,0},{2,3},{3,2},{4,5},{5,4},{6,7},{7,6},{8,9},{9,8},{10,11... | collective-permute-start | bytes 393224 | tf_op jit(solution)/shard_map/ppermute | solution.py:454
  (12 other events, 133.6 us)
